TPU v7x, 32 devices: a whole 2x2x4 slice. The times are simulated.
32 devices in a mesh: shot: 2 (over core), space: 16 (over z, y, x).
Axes of the slice: x: 2, y: 2, z: 4, core: 2. Of those that a mesh axis runs over, the one named last changes fastest.
Arguments:
- wavefields: float32 [4, 2, 2, 64, 128, 256], P('shot', None, None, 'space'), may hold values from -6 to 6
- courant: float32 [64, 192, 256], P('space'), may hold values from 0.03 to 0.2
- offsets: int32 [4], P('shot'), may hold values from 0 to 64
- strip_lines: bfloat16 [4, 2048, 256], P('shot', 'space'), may hold values from -6 to 6
- strip_ids: int32 [4, 2048], P('shot', 'space'), may hold values from -1 to 1023, as said below
- receiver_pos: int32 [4, 1024], P('shot', 'space'), may hold values from 0 to 511
- traces: float32 [4, 4, 1024], P('shot', None, 'space'), may hold values from -12 to 12
Outputs:
- wavefields_out: float32 [4, 2, 2, 64, 128, 256], P('shot', None, None, 'space')
- image: float32 [64, 192, 256], P('space')
Inputs may be any that keep to these rules, and one draw needn't show every extreme that they name: `strip_ids`: -1 marks an empty slot. For each shot every line number from 0 to 64 times the devices of space, minus 1, appears exactly once. Of the 128 slots of one device (an aligned block), at most 8 hold lines of one owner o = j // 64, and in every draw some device holds exactly 8 lines of one owner.
All inputs are finite; a program needn't handle non-finite values.
Results may differ from a plain program's by a relative error of at most 0.00105.
Values may be sent and summed in bfloat16 or wider, within the bound.
No kernel may reach another device: no remote copies, remote signals or barrier semaphores. Data moves between devices by JAX's collectives and lax.ppermute only.
A program may use at most 128 MiB of HBM per device.

v0:
```python
import jax
import jax.numpy as jnp
from jax import lax
from jax.sharding import PartitionSpec as P

STEPS = 4
RDEPTH = 4


FAR_COEF = -1.0 / 12.0
NEAR_COEF = 4.0 / 3.0
MID_COEF = -2.5


def passed_along(value, axis, steps):
    count = lax.axis_size(axis)
    leading, last = (max(0, -steps), min(count, count - steps))
    return lax.ppermute(value, axis, [(source, source + steps) for source in range(leading, last)])


def second_diff(wavefield, direction):
    padding = [(0, 0)] * wavefield.ndim
    padding[direction] = (2, 2)
    padded = jnp.pad(wavefield, padding)
    length = wavefield.shape[direction]

    def shifted(offset_at):
        return lax.slice_in_dim(padded, offset_at, offset_at + length, axis=direction)

    return (
        FAR_COEF * (shifted(0) + shifted(4))
        + NEAR_COEF * (shifted(1) + shifted(3))
        + MID_COEF * wavefield
    )


def laplacian(current):
    layers = current.shape[2]
    below = passed_along(current[:, :, layers - 2 :].astype(jnp.bfloat16), "space", 1).astype(
        jnp.float32
    )
    above = passed_along(current[:, :, :2].astype(jnp.bfloat16), "space", -1).astype(jnp.float32)
    along_x = second_diff(current, 2)
    along_x = along_x.at[:, :, 0].add(FAR_COEF * below[:, :, 0] + NEAR_COEF * below[:, :, 1])
    along_x = along_x.at[:, :, 1].add(FAR_COEF * below[:, :, 1])
    along_x = along_x.at[:, :, layers - 2].add(FAR_COEF * above[:, :, 0])
    along_x = along_x.at[:, :, layers - 1].add(
        NEAR_COEF * above[:, :, 0] + FAR_COEF * above[:, :, 1]
    )
    return along_x + second_diff(current, 3) + second_diff(current, 4)


def deliver(strip_lines, strip_ids, per_owner):
    my_index = lax.axis_index("space")
    cells_z = strip_lines.shape[2]
    shots_here = strip_lines.shape[0]
    initial = jnp.zeros((shots_here, per_owner, cells_z), jnp.bfloat16)
    row_data = lax.all_gather(strip_lines, "space", axis=1, tiled=True)
    line_ids = lax.all_gather(strip_ids, "space", axis=1, tiled=True)
    local_slot = jnp.where(line_ids // per_owner == my_index, line_ids % per_owner, per_owner)

    def put_one(table, row_block, slot_block):
        return table.at[slot_block].set(row_block, mode="drop")

    return jax.vmap(put_one)(initial, row_data, local_slot)


def body(wavefields, courant, offsets, strip_lines, strip_ids, receiver_pos, traces):
    shots_here = wavefields.shape[0]
    layers = wavefields.shape[3]
    rows_y = wavefields.shape[4]
    cells_z = wavefields.shape[5]
    model_y = courant.shape[1]
    per_owner = STEPS * 4 * layers
    saved = deliver(strip_lines, strip_ids, per_owner).astype(jnp.float32)
    saved = saved.reshape(shots_here, STEPS, layers, 4, cells_z)
    zero_index = jnp.zeros((), jnp.int32)

    def cut_speed(start_y):
        return lax.dynamic_slice(
            courant, (zero_index, start_y, zero_index), (layers, rows_y, cells_z)
        )

    speed = jax.vmap(cut_speed)(offsets)[:, None]

    def spread(spots, values):
        return jnp.zeros((layers * rows_y,), jnp.float32).at[spots].add(values)

    current = wavefields[:, 0]
    previous = wavefields[:, 1]
    contrib = jnp.zeros((shots_here, layers, rows_y, cells_z), jnp.float32)
    for time_step in range(STEPS):
        plane = jax.vmap(spread)(receiver_pos, traces[:, time_step]).reshape(
            shots_here, layers, rows_y
        )
        growth = laplacian(current).at[:, 1, :, :, RDEPTH].add(plane)
        earlier = 2.0 * current - previous + speed * growth
        boundary = saved[:, time_step]
        earlier = earlier.at[:, 0, :, 0:2].set(boundary[:, :, 0:2])
        earlier = earlier.at[:, 0, :, rows_y - 2 :].set(boundary[:, :, 2:4])
        contrib = contrib + current[:, 0] * (earlier[:, 1] - 2.0 * current[:, 1] + previous[:, 1])
        previous = current
        current = earlier
    wavefields_out = jnp.stack([current, previous], axis=1)
    frame = jnp.zeros((layers, model_y, cells_z), jnp.float32)
    for shot_at in range(shots_here):
        start_y = offsets[shot_at]
        window = lax.dynamic_slice(
            frame, (zero_index, start_y, zero_index), (layers, rows_y, cells_z)
        )
        frame = lax.dynamic_update_slice(
            frame, window + contrib[shot_at], (zero_index, start_y, zero_index)
        )
    image = lax.psum(frame, "shot") * (1.0 / (shots_here * lax.axis_size("shot")))
    return (wavefields_out, image)


def solution(mesh):
    placed = (
        P("shot", None, None, "space", None, None),
        P("space", None, None),
        P("shot"),
        P("shot", "space", None),
        P("shot", "space"),
        P("shot", "space"),
        P("shot", None, "space"),
    )
    return jax.shard_map(
        body,
        mesh=mesh,
        in_specs=placed,
        out_specs=(P("shot", None, None, "space", None, None), P("space", None, None)),
        check_vma=False,
    )
```

profile of v0, /device:TPU:19, one launch (start us, length us, event | category | flops | bytes accessed | tf_op | source)
XLA Modules:
  0.0 314.1 jit_solution(17044817995992516458)
XLA Ops:
  7.2 4.0 %fusion.112 = (f32[2,1,2,4,128,256]{5,4,3,2,1,0:T(8,128)}, f32[2,1,2,4,128,256]{5,4,3,2,1,0:T(8,128)S(1)}) fusion(f32[2,2,2,4,128,256]{5,4,3,2,1,0:T(8,128)} %param.63), kind=kLoop, calls=%fused_computation.228 | loop fusion | bytes 8388608 | tf_op jit(solution)/shard_map/slice | solution.py:90
  12.6 3.1 collective-permute-start
  15.7 2.2 collective-permute-start.1
  19.7 6.9 %scatter_fusion = f32[2,512]{1,0:T(2,128)S(1)} fusion(f32[2,512]{1,0:T(2,128)S(1)} %broadcast.461.clone, s32[128]{0:T(128)S(1)} %reshape.1152, f32[128]{0:T(128)S(1)} %reshape.1154), kind=kCustom, calls=%fused_computation.1 | custom fusion | flops 128 | bytes 2560 | tf_op jit(solution)/shard_map/vmap()/scatter-add | solution.py:87
  28.4 2.1 gather_fusion
  31.9 26.2 %all_gather.6 = s32[2,2048]{1,0:T(2,128)S(1)} all-gather(s32[2,128]{1,0:T(2,128)S(1)} %copy-done.22), channel_id=1, replica_groups=mesh['shot'=2,'space'=16] {'space'}, dimensions={1}, use_global_device_ids=true | all-gather | bytes 17408 | tf_op jit(solution)/shard_map/all_gather | solution.py:59
  64.6 2.5 fusion.4
  68.7 2.6 scatter-add.101
  71.3 3.5 %multiply_add_fusion.3 = f32[2,2,4,128,256]{4,3,2,0,1:T(8,128)S(1)} fusion(f32[2,2,4,128,256]{4,3,2,0,1:T(8,128)} %scatter-add.101, f32[2,4,128,256]{3,2,1,0:T(8,128)S(1)} %copy.21, f32[2,1,2,4,128,256]{5,4,3,2,1,0:T(8,128)} %get-tuple-element.346, f32[2,1,2,4,128,256]{5,4,3,2,1,0:T(8,128)} %copy-done.5), kind=kLoop, calls=%fused_computation.99 | loop fusion | flops 2097152 | bytes 9437184 | tf_op jit(solution)/shard_map/add | solution.py:97
  74.8 6.2 %all-gather.2.cloned.1.call-done = bf16[2,2048,256]{2,1,0:T(8,128)(2,1)} async-done(((bf16[2,128,256]{2,1,0:T(8,128)(2,1)}), bf16[2,2048,256]{2,1,0:T(8,128)(2,1)}) %all-gather.2.cloned.1.call-update) | async-done | bytes 2097168 | tf_op jit(solution)/shard_map/all_gather | solution.py:58
  81.0 18.0 %scatter_custom_fusion.4 = bf16[128,256]{1,0:T(8,128)(2,1)S(1)} fusion(s32[4096]{0:T(1024)S(1)} %bitcast.150, bf16[4096,256]{1,0:T(8,128)(2,1)} %bitcast.151, bf16[]{:T(256)} %constant.676.clone.1), kind=kCustom, calls=%fused_computation.184 | custom fusion | bytes 66048
  105.3 3.1 collective-permute-start.2
  108.5 6.9 %scatter_fusion.1 = f32[2,512]{1,0:T(2,128)S(1)} fusion(f32[2,512]{1,0:T(2,128)S(1)} %broadcast.461.clone.1, s32[128]{0:T(128)S(1)} %reshape.1152, f32[128]{0:T(128)S(1)} %reshape.1160), kind=kCustom, calls=%fused_computation.2 | custom fusion | flops 128 | bytes 2560 | tf_op jit(solution)/shard_map/vmap()/scatter-add | solution.py:87
  116.5 2.3 collective-permute-start.3
  120.7 1.9 fusion.86
  124.5 6.7 %collective-permute-done.3 = bf16[2,2,2,128,256]{4,3,2,0,1:T(8,128)(2,1)S(1)} collective-permute-done((bf16[2,2,2,128,256]{4,3,2,0,1:T(8,128)(2,1)}, bf16[2,2,2,128,256]{4,3,2,0,1:T(8,128)(2,1)S(1)}, u32[]{:S(2)}, u32[]{:S(2)}) %collective-permute-start.3) | collective-permute-done | bytes 524320 | tf_op jit(solution)/shard_map/ppermute | solution.py:18
  133.3 2.0 fusion.81
  135.2 3.7 %fusion.11 = f32[2,2,4,128,256]{4,3,2,0,1:T(8,128)S(1)} fusion(f32[2,2,4,128,256]{4,3,2,0,1:T(8,128)S(1)} %scatter.36, f32[2,2,4,128,256]{4,3,2,0,1:T(8,128)} %fusion.81), kind=kLoop, calls=%fused_computation.50 | loop fusion | flops 7864320 | bytes 6291456 | tf_op jit(solution)/shard_map/add | solution.py:50
  141.3 2.7 scatter-add.111
  144.0 2.8 multiply_add_fusion.2
  150.1 2.8 scatter.40
  152.9 6.6 %fusion.114 = (bf16[2,2,4,128,256]{4,3,2,0,1:T(8,128)(2,1)S(1)}, f32[2,2,4,128,256]{4,3,2,0,1:T(8,128)}) fusion(f32[2,2,4,128,256]{4,3,2,0,1:T(8,128)} %scatter.40), kind=kLoop, calls=%fused_computation.230 | loop fusion | flops 4194304 | bytes 5242880 | tf_op jit(solution)/shard_map/convert.4
  160.6 3.6 %collective-permute-start.4 = (bf16[2,2,2,128,256]{4,3,2,0,1:T(8,128)(2,1)}, bf16[2,2,2,128,256]{4,3,2,0,1:T(8,128)(2,1)}, u32[]{:S(2)}, u32[]{:S(2)}) collective-permute-start(bf16[2,2,2,128,256]{4,3,2,0,1:T(8,128)(2,1)} %get-tuple-element.357), channel_id=1, source_target_pairs={{0,1},{1,2},{2,3},{3,4},{4,5},{5,6},{6,7},{7,8},{8,9},{9,10},{10,1... | collective-permute-start | bytes 1572872 | tf_op jit(solution)/shard_map/ppermute | solution.py:18
  164.3 6.9 %scatter_fusion.2 = f32[2,512]{1,0:T(2,128)S(1)} fusion(f32[2,512]{1,0:T(2,128)S(1)} %broadcast.461.clone.2, s32[128]{0:T(128)S(1)} %reshape.1152, f32[128]{0:T(128)S(1)} %reshape.1166), kind=kCustom, calls=%fused_computation.3 | custom fusion | flops 128 | bytes 2560 | tf_op jit(solution)/shard_map/vmap()/scatter-add | solution.py:87
  179.2 7.1 %collective-permute-done.5 = bf16[2,2,2,128,256]{4,3,2,0,1:T(8,128)(2,1)S(1)} collective-permute-done((bf16[2,2,2,128,256]{4,3,2,0,1:T(8,128)(2,1)}, bf16[2,2,2,128,256]{4,3,2,0,1:T(8,128)(2,1)S(1)}, u32[]{:S(2)}, u32[]{:S(2)}) %collective-permute-start.5) | collective-permute-done | bytes 524320 | tf_op jit(solution)/shard_map/ppermute | solution.py:18
  186.5 2.1 fusion.74
  188.5 2.0 fusion.73
  190.5 3.7 %fusion.18 = f32[2,2,4,128,256]{4,3,2,0,1:T(8,128)S(1)} fusion(f32[2,2,4,128,256]{4,3,2,0,1:T(8,128)S(1)} %copy-done.1, f32[2,2,4,128,256]{4,3,2,0,1:T(8,128)} %fusion.73), kind=kLoop, calls=%fused_computation.57 | loop fusion | flops 7864320 | bytes 6291456 | tf_op jit(solution)/shard_map/add | solution.py:50
  196.6 2.7 scatter-add.145
  199.2 2.8 multiply_add_fusion.1
  205.3 2.8 scatter.44
  208.1 6.4 %fusion.113 = (bf16[2,2,4,128,256]{4,3,2,0,1:T(8,128)(2,1)S(1)}, f32[2,2,4,128,256]{4,3,2,0,1:T(8,128)}) fusion(f32[2,2,4,128,256]{4,3,2,0,1:T(8,128)} %scatter.44), kind=kLoop, calls=%fused_computation.229 | loop fusion | flops 4194304 | bytes 5242880 | tf_op jit(solution)/shard_map/convert.2
  215.6 4.6 %collective-permute-start.6 = (bf16[2,2,2,128,256]{4,3,2,0,1:T(8,128)(2,1)}, bf16[2,2,2,128,256]{4,3,2,0,1:T(8,128)(2,1)}, u32[]{:S(2)}, u32[]{:S(2)}) collective-permute-start(bf16[2,2,2,128,256]{4,3,2,0,1:T(8,128)(2,1)} %get-tuple-element.355), channel_id=1, source_target_pairs={{0,1},{1,2},{2,3},{3,4},{4,5},{5,6},{6,7},{7,8},{8,9},{9,10},{10,1... | collective-permute-start | bytes 1572872 | tf_op jit(solution)/shard_map/ppermute | solution.py:18
  224.9 6.9 %scatter_fusion.3 = f32[2,512]{1,0:T(2,128)S(1)} fusion(f32[2,512]{1,0:T(2,128)S(1)} %broadcast.461.clone.3, s32[128]{0:T(128)S(1)} %reshape.1152, f32[128]{0:T(128)S(1)} %reshape.1172), kind=kCustom, calls=%fused_computation.4 | custom fusion | flops 128 | bytes 2560 | tf_op jit(solution)/shard_map/vmap()/scatter-add | solution.py:87
  234.2 2.1 collective-permute-start.7
  237.5 1.9 fusion.70
  241.3 5.0 %collective-permute-done.7 = bf16[2,2,2,128,256]{4,3,2,0,1:T(8,128)(2,1)S(1)} collective-permute-done((bf16[2,2,2,128,256]{4,3,2,0,1:T(8,128)(2,1)}, bf16[2,2,2,128,256]{4,3,2,0,1:T(8,128)(2,1)S(1)}, u32[]{:S(2)}, u32[]{:S(2)}) %collective-permute-start.7) | collective-permute-done | bytes 524320 | tf_op jit(solution)/shard_map/ppermute | solution.py:18
  246.4 2.1 fusion.66
  248.5 2.0 fusion.65
  250.5 3.7 %fusion.25 = f32[2,2,4,128,256]{4,3,2,0,1:T(8,128)S(1)} fusion(f32[2,2,4,128,256]{4,3,2,0,1:T(8,128)S(1)} %copy-done.3, f32[2,2,4,128,256]{4,3,2,0,1:T(8,128)} %fusion.65), kind=kLoop, calls=%fused_computation.64 | loop fusion | flops 7864320 | bytes 6291456 | tf_op jit(solution)/shard_map/add | solution.py:50
  256.5 2.7 scatter-add.151
  259.2 3.5 %multiply_add_fusion = f32[2,2,4,128,256]{4,3,2,0,1:T(8,128)S(1)} fusion(f32[2,2,4,128,256]{4,3,2,0,1:T(8,128)} %scatter-add.151, f32[2,2,4,128,256]{4,3,2,0,1:T(8,128)} %scatter.40, f32[2,2,4,128,256]{4,3,2,0,1:T(8,128)} %scatter.44, f32[2,4,128,256]{3,2,1,0:T(8,128)S(1)} %copy.21), kind=kLoop, calls=%fused_computation.93 | loop fusion | flops 2097152 | bytes 9437184 | tf_op jit(solution)/shard_map/add | solution.py:97
  265.9 2.8 scatter.55
  268.7 4.4 %fusion.55 = f32[2,4,128,256]{3,2,1,0:T(8,128)S(1)} fusion(f32[2,2,4,128,256]{4,3,2,0,1:T(8,128)} %scatter.55, f32[2,2,4,128,256]{4,3,2,0,1:T(8,128)} %scatter.44, f32[2,2,4,128,256]{4,3,2,0,1:T(8,128)} %scatter.40, f32[2,2,4,128,256]{4,3,2,0,1:T(8,128)S(1)} %scatter.36, f32[2,2,4,128,256]{4,3,2,0,1:T(8,128)} %bitcast.148, f32[2,2,4,128,256]{4,3,2,0,1:T(8,128)} %bitcast.144), kind=kLoop, calls=%fused_computation.105 | loop fusion | flops 4980736 | bytes 11534336 | tf_op jit(solution)/shard_map/add | solution.py:101
  279.4 2.0 pad_maximum_fusion
  281.4 2.4 copy.29
  283.8 21.4 %all-reduce.14.cloned.1.call-done = f32[4,192,256]{2,1,0:T(8,128)} async-done(((f32[4,192,256]{2,1,0:T(8,128)}), f32[4,192,256]{2,1,0:T(8,128)}) %all-reduce.14.cloned.1.call-update) | async-done | bytes 786448 | tf_op jit(solution)/shard_map/psum | solution.py:114
  305.2 2.1 broadcast_multiply_fusion
  (139 shorter events, 67.0 us)
Async XLA Ops:
  7.2 73.8 %all-gather.2.cloned.1.call-start = ((), (), s32[]{:S(2)}) async-start(), calls=%async_computation | async-start | bytes 2228224 | tf_op jit(solution)/shard_map/all_gather | solution.py:58
  11.2 6.8 %copy-start.5 = (f32[2,1,2,4,128,256]{5,4,3,2,1,0:T(8,128)}, f32[2,1,2,4,128,256]{5,4,3,2,1,0:T(8,128)S(1)}, u32[]{:S(2)}) copy-start(f32[2,1,2,4,128,256]{5,4,3,2,1,0:T(8,128)S(1)} %get-tuple-element.347) | copy-start | bytes 6291460
  11.2 6.7 %copy-start.23 = (s32[2,64]{1,0:T(2,128)S(1)}, s32[2,64]{1,0:T(2,128)}, u32[]{:S(2)}) copy-start(s32[2,64]{1,0:T(2,128)} %param.68) | copy-start | bytes 1540
  11.2 6.8 %copy-start.21 = (s32[2]{0:T(128)S(1)}, s32[2]{0:T(128)}, u32[]{:S(2)}) copy-start(s32[2]{0:T(128)} %param.65) | copy-start | bytes 28
  11.2 6.8 %copy-start.20 = (f32[2,4,64]{2,1,0:T(4,128)S(1)}, f32[2,4,64]{2,1,0:T(4,128)}, u32[]{:S(2)}) copy-start(f32[2,4,64]{2,1,0:T(4,128)} %param.69) | copy-start | bytes 6148
  12.6 49.0 %collective-permute-start = (bf16[2,2,2,128,256]{4,3,2,0,1:T(8,128)(2,1)}, bf16[2,2,2,128,256]{4,3,2,0,1:T(8,128)(2,1)}, u32[]{:S(2)}, u32[]{:S(2)}) collective-permute-start(bf16[2,2,2,128,256]{4,3,2,0,1:T(8,128)(2,1)} %get-tuple-element.361), channel_id=1, source_target_pairs={{0,1},{1,2},{2,3},{3,4},{4,5},{5,6},{6,7},{7,8},{8,9},{9,10},{10,1... | collective-permute-start | bytes 1572872 | tf_op jit(solution)/shard_map/ppermute | solution.py:18
  15.7 47.0 %collective-permute-start.1 = (bf16[2,2,2,128,256]{4,3,2,0,1:T(8,128)(2,1)}, bf16[2,2,2,128,256]{4,3,2,0,1:T(8,128)(2,1)}, u32[]{:S(2)}, u32[]{:S(2)}) collective-permute-start(bf16[2,2,2,128,256]{4,3,2,0,1:T(8,128)(2,1)} %get-tuple-element.360), channel_id=1, source_target_pairs={{1,0},{2,1},{3,2},{4,3},{5,4},{6,5},{7,6},{8,7},{9,8},{10,9},{11,1... | collective-permute-start | bytes 1572872 | tf_op jit(solution)/shard_map/ppermute | solution.py:18
  17.9 287.3 %all-reduce.14.cloned.1.call-start = ((), (), s32[]{:S(2)}) async-start(), calls=%async_computation.1 | async-start | bytes 1572864 | tf_op jit(solution)/shard_map/psum | solution.py:114
  19.6 8.2 %copy-start.19 = (f32[4,192,256]{2,1,0:T(8,128)S(1)}, f32[4,192,256]{2,1,0:T(8,128)}, u32[]{:S(2)}) copy-start(f32[4,192,256]{2,1,0:T(8,128)} %param.64) | copy-start | bytes 2359300
  28.3 3.6 %copy-start.22 = (s32[2,128]{1,0:T(2,128)S(1)}, s32[2,128]{1,0:T(2,128)}, u32[]{:S(2)}) copy-start(s32[2,128]{1,0:T(2,128)} %param.67) | copy-start | bytes 3076
  28.3 29.9 %copy-start.24 = (s32[2]{0:T(128)S(1)}, s32[2]{0:T(128)}, u32[]{:S(2)}) copy-start(s32[2]{0:T(128)} %constant.713) | copy-start | bytes 28
  28.3 30.0 %copy-start.25 = (s32[2]{0:T(128)S(1)}, s32[2]{0:T(128)}, u32[]{:S(2)}) copy-start(s32[2]{0:T(128)} %constant.716) | copy-start | bytes 28
  28.3 32.2 %copy-start.26 = (s32[5]{0:T(128)S(1)}, s32[5]{0:T(128)}, u32[]{:S(2)}) copy-start(s32[5]{0:T(128)} %constant.684.clone.1) | copy-start | bytes 64
  28.3 32.8 %copy-start.6 = (f32[2,1,2,4,128,256]{5,4,3,0,2,1:T(8,128)S(1)}, f32[2,1,2,4,128,256]{5,4,3,0,2,1:T(8,128)}, u32[]{:S(2)}) copy-start(f32[2,1,2,4,128,256]{5,4,3,0,2,1:T(8,128)} %copy.47) | copy-start | bytes 6291460
  64.6 3.9 %copy-start.15 = (f32[2,1,4,128,1]{4,3,2,0,1:T(8,128)S(1)}, f32[2,1,4,128,1]{4,3,2,0,1:T(8,128)}, u32[]{:S(2)}) copy-start(f32[2,1,4,128,1]{4,3,2,0,1:T(8,128)} %reshape.1192) | copy-start | bytes 12292
  67.1 1.3 copy-start.10
  105.3 14.2 %collective-permute-start.2 = (bf16[2,2,2,128,256]{4,3,2,0,1:T(8,128)(2,1)}, bf16[2,2,2,128,256]{4,3,2,0,1:T(8,128)(2,1)}, u32[]{:S(2)}, u32[]{:S(2)}) collective-permute-start(bf16[2,2,2,128,256]{4,3,2,0,1:T(8,128)(2,1)} %get-tuple-element.359), channel_id=1, source_target_pairs={{0,1},{1,2},{2,3},{3,4},{4,5},{5,6},{6,7},{7,8},{8,9},{9,10},{10,1... | collective-permute-start | bytes 1572872 | tf_op jit(solution)/shard_map/ppermute | solution.py:18
  116.5 14.7 %collective-permute-start.3 = (bf16[2,2,2,128,256]{4,3,2,0,1:T(8,128)(2,1)}, bf16[2,2,2,128,256]{4,3,2,0,1:T(8,128)(2,1)S(1)}, u32[]{:S(2)}, u32[]{:S(2)}) collective-permute-start(bf16[2,2,2,128,256]{4,3,2,0,1:T(8,128)(2,1)} %get-tuple-element.358), channel_id=1, source_target_pairs={{1,0},{2,1},{3,2},{4,3},{5,4},{6,5},{7,6},{8,7},{9,8},{10,9},{11,1... | collective-permute-start | bytes 1572872 | tf_op jit(solution)/shard_map/ppermute | solution.py:18
  135.2 5.1 %copy-start.17 = (f32[2,1,4,128,1]{4,3,2,0,1:T(8,128)S(1)}, f32[2,1,4,128,1]{4,3,2,0,1:T(8,128)}, u32[]{:S(2)}) copy-start(f32[2,1,4,128,1]{4,3,2,0,1:T(8,128)} %reshape.1193) | copy-start | bytes 12292
  139.0 1.3 copy-start.11
  146.9 1.3 copy-start
  160.6 13.7 %collective-permute-start.4 = (bf16[2,2,2,128,256]{4,3,2,0,1:T(8,128)(2,1)}, bf16[2,2,2,128,256]{4,3,2,0,1:T(8,128)(2,1)}, u32[]{:S(2)}, u32[]{:S(2)}) collective-permute-start(bf16[2,2,2,128,256]{4,3,2,0,1:T(8,128)(2,1)} %get-tuple-element.357), channel_id=1, source_target_pairs={{0,1},{1,2},{2,3},{3,4},{4,5},{5,6},{6,7},{7,8},{8,9},{9,10},{10,1... | collective-permute-start | bytes 1572872 | tf_op jit(solution)/shard_map/ppermute | solution.py:18
  172.3 14.1 %collective-permute-start.5 = (bf16[2,2,2,128,256]{4,3,2,0,1:T(8,128)(2,1)}, bf16[2,2,2,128,256]{4,3,2,0,1:T(8,128)(2,1)S(1)}, u32[]{:S(2)}, u32[]{:S(2)}) collective-permute-start(bf16[2,2,2,128,256]{4,3,2,0,1:T(8,128)(2,1)} %get-tuple-element.356), channel_id=1, source_target_pairs={{1,0},{2,1},{3,2},{4,3},{5,4},{6,5},{7,6},{8,7},{9,8},{10,9},{11,1... | collective-permute-start | bytes 1572872 | tf_op jit(solution)/shard_map/ppermute | solution.py:18
  186.5 4.0 %copy-start.1 = (f32[2,2,4,128,256]{4,3,2,0,1:T(8,128)S(1)}, f32[2,2,4,128,256]{4,3,2,0,1:T(8,128)}, u32[]{:S(2)}) copy-start(f32[2,2,4,128,256]{4,3,2,0,1:T(8,128)} %scatter.40) | copy-start | bytes 6291460
  190.5 5.1 %copy-start.18 = (f32[2,1,4,128,1]{4,3,2,0,1:T(8,128)S(1)}, f32[2,1,4,128,1]{4,3,2,0,1:T(8,128)}, u32[]{:S(2)}) copy-start(f32[2,1,4,128,1]{4,3,2,0,1:T(8,128)} %reshape.1194) | copy-start | bytes 12292
  194.2 1.3 copy-start.12
  202.0 1.4 copy-start.2
  214.6 5.7 %copy-start.7 = (f32[2,1,2,4,128,256]{5,4,3,2,1,0:T(8,128)S(1)}, f32[2,1,2,4,128,256]{5,4,3,2,1,0:T(8,128)}, u32[]{:S(2)}) copy-start(f32[2,1,2,4,128,256]{5,4,3,2,1,0:T(8,128)} %get-tuple-element.346) | copy-start | bytes 6291460
  215.6 20.7 %collective-permute-start.6 = (bf16[2,2,2,128,256]{4,3,2,0,1:T(8,128)(2,1)}, bf16[2,2,2,128,256]{4,3,2,0,1:T(8,128)(2,1)}, u32[]{:S(2)}, u32[]{:S(2)}) collective-permute-start(bf16[2,2,2,128,256]{4,3,2,0,1:T(8,128)(2,1)} %get-tuple-element.355), channel_id=1, source_target_pairs={{0,1},{1,2},{2,3},{3,4},{4,5},{5,6},{6,7},{7,8},{8,9},{9,10},{10,1... | collective-permute-start | bytes 1572872 | tf_op jit(solution)/shard_map/ppermute | solution.py:18
  234.2 12.1 %collective-permute-start.7 = (bf16[2,2,2,128,256]{4,3,2,0,1:T(8,128)(2,1)}, bf16[2,2,2,128,256]{4,3,2,0,1:T(8,128)(2,1)S(1)}, u32[]{:S(2)}, u32[]{:S(2)}) collective-permute-start(bf16[2,2,2,128,256]{4,3,2,0,1:T(8,128)(2,1)} %get-tuple-element.354), channel_id=1, source_target_pairs={{1,0},{2,1},{3,2},{4,3},{5,4},{6,5},{7,6},{8,7},{9,8},{10,9},{11,1... | collective-permute-start | bytes 1572872 | tf_op jit(solution)/shard_map/ppermute | solution.py:18
  246.4 4.0 %copy-start.3 = (f32[2,2,4,128,256]{4,3,2,0,1:T(8,128)S(1)}, f32[2,2,4,128,256]{4,3,2,0,1:T(8,128)}, u32[]{:S(2)}) copy-start(f32[2,2,4,128,256]{4,3,2,0,1:T(8,128)} %scatter.44) | copy-start | bytes 6291460
  250.5 5.1 %copy-start.16 = (f32[2,1,4,128,1]{4,3,2,0,1:T(8,128)S(1)}, f32[2,1,4,128,1]{4,3,2,0,1:T(8,128)}, u32[]{:S(2)}) copy-start(f32[2,1,4,128,1]{4,3,2,0,1:T(8,128)} %reshape.1195) | copy-start | bytes 12292
  254.2 1.3 copy-start.9
  262.7 1.3 copy-start.8
  273.1 1.0 copy-start.14
  274.2 5.2 %copy-start.4 = (f32[2,2,4,128,256]{4,3,2,0,1:T(8,128)S(1)}, f32[2,2,4,128,256]{4,3,2,0,1:T(8,128)}, u32[]{:S(2)}) copy-start(f32[2,2,4,128,256]{4,3,2,0,1:T(8,128)} %scatter.44) | copy-start | bytes 6291460
  278.5 0.9 copy-start.13
Sparse Core Ops, SparseCore 0:
  18.0 62.9 all-gather.1
  279.5 25.6 all-reduce.13
where the time goes:
time: 317 us; the launch traced here: 314 us
  other arithmetic  120 us (38%)
  local copies, waits for them, and re-layouts  78.7 us (25%)
  waiting for transfers between devices  47.1 us (15%)
  blocking collectives  26.2 us (8%)
  starting transfers between devices  23.1 us (7%)
  between operations  18.6 us (6%)
    unnamed x62, local copies, waits for them, and re-layouts  35.3 us
    scatter-add x5, other arithmetic, spread(): return jnp.zeros((layers * rows_y,), jnp.float32).at[spots].add(values)  27.5 us
    all_gather x1, blocking collectives, deliver(): line_ids = lax.all_gather(strip_ids, 'space', axis=1, tiled=True)  26.2 us
    ppermute x8, starting transfers between devices, passed_along(): lax.ppermute(value, axis, [(source, source + steps) for source in range(l...  23 us
    another operation x9, other arithmetic  22.9 us
    psum x1, waiting for transfers between devices, body(): lax.psum(frame, 'shot') * (1.0 / (shots_here * lax.axis_size('shot')))  21.4 us
    ppermute x8, waiting for transfers between devices, passed_along(): lax.ppermute(value, axis, [(source, source + steps) for source in range(l...  19.5 us
    add x4, other arithmetic, laplacian(): return along_x + second_diff(current, 3) + second_diff(current, 4)  13.8 us
  transfers between devices with their start and end apart: 10, of which 6 were waited for; matrix products, arithmetic and copies ran while one was open for 24% of the time, Pallas kernels for 0%

commit v1 on v0

v1 whole, which is shorter than its diff:
```python
import functools

import jax
import jax.numpy as jnp
from jax import lax
from jax.experimental import pallas as pl
from jax.experimental.pallas import tpu as pltpu
from jax.sharding import PartitionSpec as P

STEPS = 4
RDEPTH = 4
EDGE = 4
LANES = 128
VMEM_LIMIT = 40 * 1024 * 1024
VMEM = pltpu.VMEM
SMEM = pltpu.SMEM


def params():
    return pltpu.CompilerParams(vmem_limit_bytes=VMEM_LIMIT)


def cost(flops, moved):
    return pl.CostEstimate(flops=flops, bytes_accessed=moved, transcendentals=0)


def swap_pairs(value, first):
    count = lax.axis_size("space")
    routes = []
    for at in range(first, count - 1, 2):
        routes += [(at, at + 1), (at + 1, at)]
    return lax.ppermute(value, "space", routes)


def band(rows, centre):
    gap = jnp.abs(
        lax.broadcasted_iota(jnp.int32, (rows, rows), 0)
        - lax.broadcasted_iota(jnp.int32, (rows, rows), 1)
    )
    weights = jnp.where(gap == 0, centre, jnp.where(gap == 1, 16.0, jnp.where(gap == 2, -1.0, 0.0)))
    return weights.astype(jnp.bfloat16)


def mm(left, right, dims=((1,), (0,))):
    return lax.dot_general(left, right, (dims, ((), ())), preferred_element_type=jnp.float32)


def window_at(offset, model_y, rows_y):
    start = jnp.minimum(lax.div(offset, 8), (model_y - rows_y - 8) // 8) * 8
    return pl.multiple_of(start, 8), offset - start


def add_window(target_ref, lead, part, offset):
    rows_y = part.shape[0]
    start, gap = window_at(offset, target_ref.shape[-2], rows_y)
    moved = jnp.concatenate([part, jnp.zeros((8, part.shape[1]), part.dtype)], axis=0)
    at = lead + (pl.ds(start, rows_y + 8), slice(None))
    target_ref[at] = target_ref[at] + pltpu.roll(moved, gap, 0)


def is_odd():
    return lax.rem(lax.axis_index("space"), 2) == 1


def write_sends(field_ref, lead, send0_ref, send1_ref):
    odd = is_odd()
    for comp in range(2):
        for at in range(2):
            low = field_ref[lead + (comp, at)]
            high = field_ref[lead + (comp, at + field_ref.shape[-3] - 2)]
            send0_ref[comp, at] = jnp.where(odd, low, high).astype(jnp.bfloat16)
            send1_ref[comp, at] = jnp.where(odd, high, low).astype(jnp.bfloat16)


def pack_kernel(field_ref, send0_ref, send1_ref):
    write_sends(field_ref, (0, 0), send0_ref, send1_ref)


def pack_halo(wavefields, shot):
    _, _, comps, layers, rows_y, cells_z = wavefields.shape
    half = jax.ShapeDtypeStruct((comps, 2, rows_y, cells_z), jnp.bfloat16)
    whole = pl.BlockSpec(half.shape, lambda i: (0, 0, 0, 0))
    return pl.pallas_call(
        pack_kernel,
        grid=(1,),
        in_specs=[
            pl.BlockSpec((1, 1, comps, layers, rows_y, cells_z), lambda i: (shot, 0, 0, 0, 0, 0))
        ],
        out_specs=[whole, whole],
        out_shape=[half, half],
        compiler_params=params(),
        cost_estimate=cost(10**6, 2 * 2**20),
        name="pack_halo",
    )(wavefields)


def pack_lines_kernel(cap, per_owner, ids_ref, lines_ref, out_ref):
    shots, hold = ids_ref.shape
    total = shots * hold
    ids = jnp.concatenate([ids_ref[shot : shot + 1] for shot in range(shots)], axis=1)
    ids = ids.astype(jnp.float32)
    row_at = lax.broadcasted_iota(jnp.int32, (total, total), 0)
    col_at = lax.broadcasted_iota(jnp.int32, (total, total), 1)
    slot_at = lax.broadcasted_iota(jnp.int32, (1, total), 1)
    shot_of = jnp.zeros((1, total), jnp.float32)
    for shot in range(1, shots):
        shot_of = shot_of + (slot_at >= shot * hold).astype(jnp.float32)
    owner = jnp.floor((ids + 0.5) * (1.0 / per_owner))
    inside = ids - owner * per_owner
    used = ids >= 0.0
    key = jnp.where(used, owner * shots + shot_of, -1.0)
    wide_key = jnp.broadcast_to(key, (total, total))
    same = jnp.where(row_at == col_at, wide_key, 0.0)
    tall_key = jnp.sum(same, axis=1, keepdims=True)
    earlier_one = (tall_key == wide_key) & (row_at < col_at)
    rank = jnp.sum(earlier_one.astype(jnp.float32), axis=0, keepdims=True)
    target = jnp.where(used, key * cap + rank, -1.0)
    hot = jnp.where(row_at.astype(jnp.float32) == target, 1.0, 0.0)
    tags = jnp.sum(hot * (inside + 1.0), axis=1, keepdims=True)
    hot = hot.astype(jnp.bfloat16)
    cells_z = lines_ref.shape[2]
    rows = mm(hot[:, :hold], lines_ref[0])
    for shot in range(1, shots):
        rows = rows + mm(hot[:, shot * hold : (shot + 1) * hold], lines_ref[shot])
    out_ref[:, :cells_z] = rows.astype(jnp.bfloat16)
    out_ref[:, cells_z:] = jnp.broadcast_to(tags, (total, LANES)).astype(jnp.bfloat16)


def unpack_lines_kernel(cap, shots, per_owner, got_ref, out_ref):
    total = got_ref.shape[0]
    cells_z = out_ref.shape[1]
    tags = got_ref[:, cells_z : cells_z + LANES].astype(jnp.float32)[:, 0:1]
    row_at = lax.broadcasted_iota(jnp.int32, (total, 1), 0).astype(jnp.float32)
    block = jnp.floor((row_at + 0.5) * (1.0 / cap))
    shot_of = block - shots * jnp.floor((block + 0.5) * (1.0 / shots))
    target = jnp.where(tags > 0.5, tags - 1.0 + shot_of * per_owner, -1.0)
    line_at = lax.broadcasted_iota(jnp.int32, (total, shots * per_owner), 1).astype(jnp.float32)
    hot = jnp.where(line_at == target, 1.0, 0.0).astype(jnp.bfloat16)
    out_ref[...] = mm(hot, got_ref[:, :cells_z], ((0,), (0,)))


def deliver(strip_lines, strip_ids, per_owner):
    shots, hold, cells_z = strip_lines.shape
    holders = lax.axis_size("space")
    cap = hold // holders
    total = shots * hold
    wide = cells_z + LANES
    message = pl.pallas_call(
        functools.partial(pack_lines_kernel, cap, per_owner),
        out_shape=jax.ShapeDtypeStruct((total, wide), jnp.bfloat16),
        compiler_params=params(),
        cost_estimate=cost(10**6, 2**19),
        name="pack_lines",
    )(strip_ids, strip_lines)
    message = message.reshape(holders, shots * cap, wide)
    got = lax.all_to_all(message, "space", 0, 0, tiled=False)
    got = got.reshape(total, wide)
    return pl.pallas_call(
        functools.partial(unpack_lines_kernel, cap, shots, per_owner),
        out_shape=jax.ShapeDtypeStruct((shots * per_owner, cells_z), jnp.float32),
        compiler_params=params(),
        cost_estimate=cost(10**6, 2**19),
        name="unpack_lines",
    )(got)


def split3(value):
    parts = []
    for _ in range(3):
        part = value.astype(jnp.bfloat16)
        parts.append(part)
        value = value - part.astype(jnp.float32)
    return parts


def step_kernel(shot, step, first, last, *refs):
    refs = list(refs)
    take = lambda: refs.pop(0)
    offsets_ref = take() if first else None
    now_ref, later_ref = take(), take()
    got0_ref, got1_ref = take(), take()
    saved_ref, pos_ref, traces_ref = take(), take(), take()
    speed_from = take()
    contrib_from = None if first else take()
    if last and shot > 0:
        take()
    if last:
        out_ref, contrib_ref, new_ref, sems = take(), take(), take(), take()
    else:
        new_ref, send0_ref, send1_ref, contrib_ref = take(), take(), take(), take()
        speed_out = take() if first else None
    lead = (0, 0) if first else ()
    lead_later = (0, 0) if step < 2 else ()
    layers, rows_y, cells_z = new_ref.shape[-3:]
    if last:
        keep = pltpu.make_async_copy(now_ref, out_ref.at[shot, 1], sems.at[0])
        keep.start()
    odd = is_odd()
    across_z = band(cells_z, -90.0)
    across_y = band(rows_y, 0.0)
    trace_row = traces_ref[shot, step : step + 1, :]
    lane_of = lax.broadcasted_iota(jnp.int32, (LANES, trace_row.shape[1]), 0)
    trace_parts = [
        jnp.where(lane_of == RDEPTH, part.astype(jnp.float32), 0.0).astype(jnp.bfloat16)
        for part in split3(trace_row)
    ]
    spots = pos_ref[shot : shot + 1, :]
    cell_of = lax.broadcasted_iota(jnp.int32, (rows_y, trace_row.shape[1]), 0)

    for layer in range(layers):
        if first:
            start_y, gap = window_at(offsets_ref[shot], speed_from.shape[1], rows_y)
            speed = speed_from[layer, pl.ds(start_y, rows_y + 8), :]
            speed = pltpu.roll(speed, lax.rem(rows_y + 8 - gap, rows_y + 8), 0)[:rows_y]
            speed_out[layer] = speed
        else:
            speed = speed_from[layer]
        for comp in range(2):
            def layer_of(at):
                if at < 0:
                    both = (got1_ref[comp, 2 + at], got0_ref[comp, 2 + at])
                elif at >= layers:
                    both = (got0_ref[comp, at - layers], got1_ref[comp, at - layers])
                else:
                    return now_ref[lead + (comp, at)]
                even_one, odd_one = (part.astype(jnp.float32) for part in both)
                return jnp.where(odd, odd_one, even_one)

            here = layer_of(layer)
            high = here.astype(jnp.bfloat16)
            low = (here - high.astype(jnp.float32)).astype(jnp.bfloat16)
            growth = mm(high, across_z) + mm(low, across_z)
            growth = growth + (mm(across_y, high) + mm(across_y, low))
            growth = growth + 16.0 * (layer_of(layer - 1) + layer_of(layer + 1))
            growth = growth - (layer_of(layer - 2) + layer_of(layer + 2))
            growth = growth * (1.0 / 12.0)
            if comp == 1:
                hot = jnp.where(spots == cell_of + layer * rows_y, 1.0, 0.0).astype(jnp.bfloat16)
                plane = mm(hot, trace_parts[0], ((1,), (1,)))
                plane = plane + mm(hot, trace_parts[1], ((1,), (1,)))
                plane = plane + mm(hot, trace_parts[2], ((1,), (1,)))
                growth = jnp.concatenate(
                    [growth[:, :LANES] + plane, growth[:, LANES:]], axis=1
                )
            change = speed * growth
            new_ref[comp, layer] = 2.0 * here - later_ref[lead_later + (comp, layer)] + change
            if comp == 1:
                term = now_ref[lead + (0, layer)] * change
                contrib_ref[layer] = term if first else contrib_from[layer] + term
        per_step = layers * EDGE
        base = (shot * STEPS + step) * per_step + layer * EDGE
        new_ref[0, layer, 0:2, :] = saved_ref[base : base + 2, :]
        new_ref[0, layer, rows_y - 2 :, :] = saved_ref[base + 2 : base + 4, :]
    if last:
        give = pltpu.make_async_copy(new_ref, out_ref.at[shot, 0], sems.at[1])
        give.start()
        give.wait()
        keep.wait()
    else:
        write_sends(new_ref, (), send0_ref, send1_ref)


def one_step(shot, step, shots, offsets, now, later, got, saved, pos, traces, speed, contrib, out):
    first, last = step == 0, step == STEPS - 1
    comps, layers, rows_y, cells_z = now.shape[-4:]
    vmem = pl.BlockSpec(memory_space=VMEM)
    state = jax.ShapeDtypeStruct((comps, layers, rows_y, cells_z), jnp.float32)
    half = jax.ShapeDtypeStruct((comps, 2, rows_y, cells_z), jnp.bfloat16)
    image = jax.ShapeDtypeStruct((layers, rows_y, cells_z), jnp.float32)
    args, specs, aliases = [], [], {}
    scratch = []
    block = (1, 1) + state.shape
    if first:
        args.append(offsets)
        specs.append(pl.BlockSpec(memory_space=SMEM))
    for at, field in enumerate((now, later)):
        args.append(field)
        if field.ndim == 6:
            at = at if first else 0
            specs.append(pl.BlockSpec(block, lambda i, at=at: (shot, at, 0, 0, 0, 0)))
        else:
            specs.append(vmem)
    args += [*got, saved, pos, traces, speed]
    specs += [vmem] * 6
    if not first:
        args.append(contrib)
        specs.append(vmem)
    if last:
        shape_out = jax.ShapeDtypeStruct((shots, 2) + state.shape, jnp.float32)
        if shot > 0:
            aliases[len(args)] = 0
            args.append(out)
            specs.append(pl.BlockSpec(memory_space=pl.ANY))
        outs = [shape_out, image]
        out_specs = [pl.BlockSpec(memory_space=pl.ANY), vmem]
        scratch = [pltpu.VMEM(state.shape, jnp.float32), pltpu.SemaphoreType.DMA((2,))]
    else:
        outs = [state, half, half, image] + ([image] if first else [])
        out_specs = [vmem] * len(outs)
    return pl.pallas_call(
        functools.partial(step_kernel, shot, step, first, last),
        grid=(1,),
        in_specs=specs,
        out_specs=out_specs,
        out_shape=outs,
        scratch_shapes=scratch,
        input_output_aliases=aliases,
        compiler_params=params(),
        cost_estimate=cost(10**9, 5 * 2**20),
        name="step",
    )(*args)


def frame_kernel(scale, sides, offsets_ref, *refs):
    image_ref = refs[-1]
    shots = (len(refs) - 1) // sides
    layers = image_ref.shape[0]
    image_ref[...] = jnp.zeros_like(image_ref)
    for layer in range(layers):
        for shot in range(shots):
            add_window(image_ref, (layer,), refs[shot][layer], offsets_ref[shot])


def image_kernel(scale, offsets_ref, others_ref, *refs):
    image_ref, frame_ref = refs[-2:]
    shots = (len(refs) - 2) // 2
    layers = image_ref.shape[0]
    for layer in range(layers):
        for side, places in ((0, offsets_ref), (1, others_ref)):
            frame_ref[side] = jnp.zeros_like(frame_ref[side])
            for shot in range(shots):
                add_window(frame_ref, (side,), refs[side * shots + shot][layer], places[shot])
        image_ref[layer] = (frame_ref[0] + frame_ref[1]) * scale


def body(wavefields, courant, offsets, strip_lines, strip_ids, receiver_pos, traces):
    shots = wavefields.shape[0]
    layers, rows_y, cells_z = wavefields.shape[3:]
    model_y = courant.shape[1]
    per_owner = STEPS * EDGE * layers
    shot_devices = lax.axis_size("shot")
    scale = 1.0 / (shots * shot_devices)

    def exchange(sends):
        return swap_pairs(sends[0], 0), swap_pairs(sends[1], 1)

    got = [exchange(pack_halo(wavefields, shot)) for shot in range(shots)]
    saved = deliver(strip_lines, strip_ids, per_owner)
    swap = [(0, 1), (1, 0)]
    paired = shot_devices == 2
    if paired:
        others_at = lax.ppermute(offsets, "shot", swap)
    now = [wavefields] * shots
    later = [wavefields] * shots
    contrib = [None] * shots
    speed = [courant] * shots
    out = None
    others = []
    for step in range(STEPS):
        for shot in range(shots):
            made = one_step(
                shot, step, shots, offsets, now[shot], later[shot], got[shot], saved, receiver_pos,
                traces, speed[shot], contrib[shot], out,
            )
            if step == STEPS - 1:
                out, contrib[shot] = made
                if paired:
                    others.append(lax.ppermute(contrib[shot], "shot", swap))
                continue
            got[shot] = exchange(made[1:3])
            contrib[shot] = made[3]
            if step == 0:
                speed[shot] = made[4]
            later[shot], now[shot] = now[shot], made[0]
    smem, vmem = pl.BlockSpec(memory_space=SMEM), pl.BlockSpec(memory_space=VMEM)
    shape_out = jax.ShapeDtypeStruct((layers, model_y, cells_z), jnp.float32)
    if paired:
        image = pl.pallas_call(
            functools.partial(image_kernel, scale),
            in_specs=[smem, smem] + [vmem] * (2 * shots),
            out_specs=vmem,
            out_shape=shape_out,
            scratch_shapes=[pltpu.VMEM((2, model_y, cells_z), jnp.float32)],
            compiler_params=params(),
            cost_estimate=cost(10**6, 3 * 2**20),
            name="image",
        )(offsets, others_at, *contrib, *others)
    else:
        frame = pl.pallas_call(
            functools.partial(frame_kernel, scale, 1),
            in_specs=[smem] + [vmem] * shots,
            out_specs=vmem,
            out_shape=shape_out,
            compiler_params=params(),
            cost_estimate=cost(10**6, 3 * 2**20),
            name="frame",
        )(offsets, *contrib)
        image = lax.psum(frame, "shot") * scale
    return (out, image)


def solution(mesh):
    placed = (
        P("shot", None, None, "space", None, None),
        P("space", None, None),
        P("shot"),
        P("shot", "space", None),
        P("shot", "space"),
        P("shot", "space"),
        P("shot", None, "space"),
    )
    return jax.shard_map(
        body,
        mesh=mesh,
        in_specs=placed,
        out_specs=(P("shot", None, None, "space", None, None), P("space", None, None)),
        check_vma=False,
    )
```

time: 317 us -> 114 us (0.36)
  other arithmetic: 120 us -> 0 us
  local copies, waits for them, and re-layouts: 78.7 us -> 5.96 us
  blocking collectives: 26.2 us -> 0 us
  between operations: 18.6 us -> 0.89 us
  Pallas kernels: 0 us -> 16.6 us
  starting transfers between devices: 23.1 us -> 35.5 us
  waiting for transfers between devices: 47.1 us -> 54.4 us
    scatter-add x21 -> x0, other arithmetic: 51.8 us -> none  [the longest x5 27.5 us: spread(): return jnp.zeros((layers * rows_y,), jnp.float32).at[spots].add(values)]
    add x15 -> x0, other arithmetic: 35.5 us -> none  [the longest x4 13.8 us: laplacian(): return along_x + second_diff(current, 3) + second_diff(current, 4)]
    ppermute x8 -> x19, waiting for transfers between devices: 19.5 us -> 54.4 us  [the longest x16 52.6 us: swap_pairs(): return lax.ppermute(value, 'space', routes)]
    unnamed x62 -> x16, local copies, waits for them, and re-layouts: 35.3 us -> 5.96 us
    all_gather x1 -> x0, blocking collectives: 26.2 us -> none  [deliver(): line_ids = lax.all_gather(strip_ids, 'space', axis=1, tiled=True)]
    another operation x10 -> x0, other arithmetic: 24.9 us -> none
    psum x1 -> x0, waiting for transfers between devices: 21.4 us -> none  [body(): lax.psum(frame, 'shot') * (1.0 / (shots_here * lax.axis_size('shot')))]
    pallas_call x0 -> x13, Pallas kernels: none -> 16.6 us  [the longest x8 12.9 us: one_step(): pl.pallas_call(functools.partial(step_kernel, shot, step, first, last), g...]
  transfers between devices with their start and end apart: 10 -> 20, of which waited for: 6 -> 10; matrix products, arithmetic and copies ran while one was open for 24% -> 0% of each run, Pallas kernels for 0% -> 10%
where the time goes in v1:
time: 114 us; the launch traced here: 113 us
  waiting for transfers between devices  54.4 us (48%)
  starting transfers between devices  35.5 us (31%)
  Pallas kernels  16.6 us (15%)
  local copies, waits for them, and re-layouts  5.96 us (5%)
    ppermute x16, waiting for transfers between devices, swap_pairs(): return lax.ppermute(value, 'space', routes)  52.6 us
    ppermute x16, starting transfers between devices, swap_pairs(): return lax.ppermute(value, 'space', routes)  26.1 us
    pallas_call x8, Pallas kernels, one_step(): pl.pallas_call(functools.partial(step_kernel, shot, step, first, last), g...  12.9 us
    all_to_all x1, starting transfers between devices, deliver(): got = lax.all_to_all(message, 'space', 0, 0, tiled=False)  6.52 us
    unnamed x16, local copies, waits for them, and re-layouts  5.96 us
    ppermute x2, starting transfers between devices, body(): others.append(lax.ppermute(contrib[shot], 'shot', swap))  2.44 us
  transfers between devices with their start and end apart: 20, of which 10 were waited for; matrix products, arithmetic and copies ran while one was open for 0% of the time, Pallas kernels for 10%

profile of v1, /device:TPU:19, one launch (start us, length us, event | category | flops | bytes accessed | tf_op | source)
XLA Modules:
  0.0 113.3 jit_solution(17262384325590955112)
XLA Ops:
  0.6 0.9 copy-done.4
  1.5 0.7 copy-done.7
  2.2 1.0 pack_lines.1
  3.2 6.5 %all-to-all-start = ((bf16[16,16,384]{2,1,0:T(8,128)(2,1)}), bf16[16,16,384]{2,1,0:T(8,128)(2,1)S(1)}, u32[]{:S(2)}, u32[]{:S(2)}) async-start(bf16[16,16,384]{2,1,0:T(8,128)(2,1)} %bitcast), calls=%async_computation | async-start | bytes 393216 | tf_op jit(solution)/shard_map/all_to_all | solution.py:156
  9.8 2.2 %copy-done = f32[2,2,2,4,128,256]{5,4,3,2,1,0:T(8,128)S(1)} copy-done((f32[2,2,2,4,128,256]{5,4,3,2,1,0:T(8,128)S(1)}, f32[2,2,2,4,128,256]{5,4,3,2,1,0:T(8,128)}, u32[]{:S(2)}) %copy-start) | copy-done | bytes 4194328
  11.9 0.1 pack_halo.3
  12.0 0.3 collective-permute-start.8
  12.4 4.0 %collective-permute-start.9 = (bf16[2,2,128,256]{3,2,1,0:T(8,128)(2,1)S(1)}, bf16[2,2,128,256]{3,2,1,0:T(8,128)(2,1)S(1)}, u32[]{:S(2)}, u32[]{:S(2)}) collective-permute-start(bf16[2,2,128,256]{3,2,1,0:T(8,128)(2,1)S(1)} %get-tuple-element.52), channel_id=1, source_target_pairs={{1,2},{2,1},{3,4},{4,3},{5,6},{6,5},{7,8},{8,7},{9,10},{10,9},{11,... | collective-permute-start | bytes 786440 | tf_op jit(solution)/shard_map/ppermute | solution.py:32
  16.4 0.1 pack_halo.2
  16.5 0.3 collective-permute-start
  16.8 4.0 %collective-permute-start.1 = (bf16[2,2,128,256]{3,2,1,0:T(8,128)(2,1)S(1)}, bf16[2,2,128,256]{3,2,1,0:T(8,128)(2,1)S(1)}, u32[]{:S(2)}, u32[]{:S(2)}) collective-permute-start(bf16[2,2,128,256]{3,2,1,0:T(8,128)(2,1)S(1)} %get-tuple-element.37), channel_id=1, source_target_pairs={{1,2},{2,1},{3,4},{4,3},{5,6},{6,5},{7,8},{8,7},{9,10},{10,9},{11,... | collective-permute-start | bytes 786440 | tf_op jit(solution)/shard_map/ppermute | solution.py:32
  20.8 0.3 unpack_lines.1.refs_5_.refs_4_
  21.1 9.8 %collective-permute-done.8.refs_3_ = bf16[2,2,128,256]{3,2,1,0:T(8,128)(2,1)S(1)} collective-permute-done((bf16[2,2,128,256]{3,2,1,0:T(8,128)(2,1)S(1)}, bf16[2,2,128,256]{3,2,1,0:T(8,128)(2,1)S(1)}, u32[]{:S(2)}, u32[]{:S(2)}) %collective-permute-start.8) | collective-permute-done | bytes 262176 | tf_op jit(solution)/shard_map/ppermute | solution.py:32
  31.0 0.0 copy-start.1
  31.0 2.2 %copy-done.1 = f32[2,2,2,4,128,256]{5,4,3,2,1,0:T(8,128)S(1)} copy-done((f32[2,2,2,4,128,256]{5,4,3,2,1,0:T(8,128)S(1)}, f32[2,2,2,4,128,256]{5,4,3,2,1,0:T(8,128)}, u32[]{:S(2)}) %copy-start.1) | copy-done | bytes 4194328
  33.2 1.8 %step.11 = (f32[2,4,128,256]{3,2,1,0:T(8,128)S(1)}, bf16[2,2,128,256]{3,2,1,0:T(8,128)(2,1)S(1)}, bf16[2,2,128,256]{3,2,1,0:T(8,128)(2,1)S(1)}, f32[4,128,256]{2,1,0:T(8,128)S(1)}, f32[4,128,256]{2,1,0:T(8,128)S(1)}) custom-call(s32[2]{0:T(128)S(1)} %copy-done.6, f32[2,2,2,4,128,256]{5,4,3,2,1,0:T(8,128)S(1)} %copy-done.1, ...), custom_call_target="tpu_custom_call" | custom-call | flops 1000000000 | bytes 5242880 | tf_op jit(solution)/shard_map/step/pallas_call | solution.py:300
  34.9 0.1 collective-permute-start.10
  35.0 3.7 %collective-permute-start.11 = (bf16[2,2,128,256]{3,2,1,0:T(8,128)(2,1)S(1)}, bf16[2,2,128,256]{3,2,1,0:T(8,128)(2,1)S(1)}, u32[]{:S(2)}, u32[]{:S(2)}) collective-permute-start(bf16[2,2,128,256]{3,2,1,0:T(8,128)(2,1)S(1)} %get-tuple-element.55), channel_id=1, source_target_pairs={{1,2},{2,1},{3,4},{4,3},{5,6},{6,5},{7,8},{8,7},{9,10},{10,9},{11,... | collective-permute-start | bytes 786440 | tf_op jit(solution)/shard_map/ppermute | solution.py:32
  38.7 1.8 %step.8 = (f32[2,4,128,256]{3,2,1,0:T(8,128)S(1)}, bf16[2,2,128,256]{3,2,1,0:T(8,128)(2,1)S(1)}, bf16[2,2,128,256]{3,2,1,0:T(8,128)(2,1)S(1)}, f32[4,128,256]{2,1,0:T(8,128)S(1)}, f32[4,128,256]{2,1,0:T(8,128)S(1)}) custom-call(s32[2]{0:T(128)S(1)} %copy-done.6, f32[2,2,2,4,128,256]{5,4,3,2,1,0:T(8,128)S(1)} %copy-done.1, ...), custom_call_target="tpu_custom_call" | custom-call | flops 1000000000 | bytes 5242880 | tf_op jit(solution)/shard_map/step/pallas_call | solution.py:300
  40.5 1.2 %collective-permute-start.2 = (bf16[2,2,128,256]{3,2,1,0:T(8,128)(2,1)S(1)}, bf16[2,2,128,256]{3,2,1,0:T(8,128)(2,1)S(1)}, u32[]{:S(2)}, u32[]{:S(2)}) collective-permute-start(bf16[2,2,128,256]{3,2,1,0:T(8,128)(2,1)S(1)} %get-tuple-element.39), channel_id=1, source_target_pairs={{0,1},{1,0},{2,3},{3,2},{4,5},{5,4},{6,7},{7,6},{8,9},{9,8},{10,11... | collective-permute-start | bytes 786440 | tf_op jit(solution)/shard_map/ppermute | solution.py:32
  41.7 2.2 %collective-permute-start.3 = (bf16[2,2,128,256]{3,2,1,0:T(8,128)(2,1)S(1)}, bf16[2,2,128,256]{3,2,1,0:T(8,128)(2,1)S(1)}, u32[]{:S(2)}, u32[]{:S(2)}) collective-permute-start(bf16[2,2,128,256]{3,2,1,0:T(8,128)(2,1)S(1)} %get-tuple-element.40), channel_id=1, source_target_pairs={{1,2},{2,1},{3,4},{4,3},{5,6},{6,5},{7,8},{8,7},{9,10},{10,9},{11,... | collective-permute-start | bytes 786440 | tf_op jit(solution)/shard_map/ppermute | solution.py:32
  43.9 4.2 %collective-permute-done.11.refs_3_ = bf16[2,2,128,256]{3,2,1,0:T(8,128)(2,1)S(1)} collective-permute-done((bf16[2,2,128,256]{3,2,1,0:T(8,128)(2,1)S(1)}, bf16[2,2,128,256]{3,2,1,0:T(8,128)(2,1)S(1)}, u32[]{:S(2)}, u32[]{:S(2)}) %collective-permute-start.11) | collective-permute-done | bytes 262176 | tf_op jit(solution)/shard_map/ppermute | solution.py:32
  48.1 1.3 %step.12 = (f32[2,4,128,256]{3,2,1,0:T(8,128)S(1)}, bf16[2,2,128,256]{3,2,1,0:T(8,128)(2,1)S(1)}, bf16[2,2,128,256]{3,2,1,0:T(8,128)(2,1)S(1)}, f32[4,128,256]{2,1,0:T(8,128)S(1)}) custom-call(f32[2,4,128,256]{3,2,1,0:T(8,128)S(1)} %get-tuple-element.53.refs_0_.refs_1_, f32[2,2,2,4,128,256]{5,4,3,2,1,0:T(8,128)S(1)} %copy-done.1, ...), custom_call_target="tpu_custom_call" | custom-call | flops 1000000000 | bytes 5242880 | tf_op jit(solution)/shard_map/step/pallas_call | solution.py:300
  49.4 0.1 collective-permute-start.12
  49.5 2.1 %collective-permute-start.13 = (bf16[2,2,128,256]{3,2,1,0:T(8,128)(2,1)S(1)}, bf16[2,2,128,256]{3,2,1,0:T(8,128)(2,1)S(1)}, u32[]{:S(2)}, u32[]{:S(2)}) collective-permute-start(bf16[2,2,128,256]{3,2,1,0:T(8,128)(2,1)S(1)} %get-tuple-element.60), channel_id=1, source_target_pairs={{1,2},{2,1},{3,4},{4,3},{5,6},{6,5},{7,8},{8,7},{9,10},{10,9},{11,... | collective-permute-start | bytes 786440 | tf_op jit(solution)/shard_map/ppermute | solution.py:32
  51.6 10.5 %collective-permute-done.2.refs_2_ = bf16[2,2,128,256]{3,2,1,0:T(8,128)(2,1)S(1)} collective-permute-done((bf16[2,2,128,256]{3,2,1,0:T(8,128)(2,1)S(1)}, bf16[2,2,128,256]{3,2,1,0:T(8,128)(2,1)S(1)}, u32[]{:S(2)}, u32[]{:S(2)}) %collective-permute-start.2) | collective-permute-done | bytes 262176 | tf_op jit(solution)/shard_map/ppermute | solution.py:32
  62.1 1.3 %step.9 = (f32[2,4,128,256]{3,2,1,0:T(8,128)S(1)}, bf16[2,2,128,256]{3,2,1,0:T(8,128)(2,1)S(1)}, bf16[2,2,128,256]{3,2,1,0:T(8,128)(2,1)S(1)}, f32[4,128,256]{2,1,0:T(8,128)S(1)}) custom-call(f32[2,4,128,256]{3,2,1,0:T(8,128)S(1)} %get-tuple-element.38.refs_0_.refs_1_, f32[2,2,2,4,128,256]{5,4,3,2,1,0:T(8,128)S(1)} %copy-done.1, ...), custom_call_target="tpu_custom_call" | custom-call | flops 1000000000 | bytes 5242880 | tf_op jit(solution)/shard_map/step/pallas_call | solution.py:300
  63.3 0.1 collective-permute-start.4
  63.4 2.5 %collective-permute-start.5 = (bf16[2,2,128,256]{3,2,1,0:T(8,128)(2,1)S(1)}, bf16[2,2,128,256]{3,2,1,0:T(8,128)(2,1)S(1)}, u32[]{:S(2)}, u32[]{:S(2)}) collective-permute-start(bf16[2,2,128,256]{3,2,1,0:T(8,128)(2,1)S(1)} %get-tuple-element.45), channel_id=1, source_target_pairs={{1,2},{2,1},{3,4},{4,3},{5,6},{6,5},{7,8},{8,7},{9,10},{10,9},{11,... | collective-permute-start | bytes 786440 | tf_op jit(solution)/shard_map/ppermute | solution.py:32
  66.0 1.7 %collective-permute-done.12.refs_2_ = bf16[2,2,128,256]{3,2,1,0:T(8,128)(2,1)S(1)} collective-permute-done((bf16[2,2,128,256]{3,2,1,0:T(8,128)(2,1)S(1)}, bf16[2,2,128,256]{3,2,1,0:T(8,128)(2,1)S(1)}, u32[]{:S(2)}, u32[]{:S(2)}) %collective-permute-start.12) | collective-permute-done | bytes 262176 | tf_op jit(solution)/shard_map/ppermute | solution.py:32
  67.7 1.2 %collective-permute-done.13.refs_3_ = bf16[2,2,128,256]{3,2,1,0:T(8,128)(2,1)S(1)} collective-permute-done((bf16[2,2,128,256]{3,2,1,0:T(8,128)(2,1)S(1)}, bf16[2,2,128,256]{3,2,1,0:T(8,128)(2,1)S(1)}, u32[]{:S(2)}, u32[]{:S(2)}) %collective-permute-start.13) | collective-permute-done | bytes 262176 | tf_op jit(solution)/shard_map/ppermute | solution.py:32
  68.8 1.2 %step.13 = (f32[2,4,128,256]{3,2,1,0:T(8,128)S(1)}, bf16[2,2,128,256]{3,2,1,0:T(8,128)(2,1)S(1)}, bf16[2,2,128,256]{3,2,1,0:T(8,128)(2,1)S(1)}, f32[4,128,256]{2,1,0:T(8,128)S(1)}) custom-call(f32[2,4,128,256]{3,2,1,0:T(8,128)S(1)} %get-tuple-element.58.refs_0_.refs_1_, f32[2,4,128,256]{3,2,1,0:T(8,128)S(1)} %get-tuple-element.53.refs_0_.refs_1_, ...), custom_call_target="tpu_custom_call" | custom-call | flops 1000000000 | bytes 5242880 | tf_op jit(solution)/shard_map/step/pallas_call | solution.py:300
  70.1 0.1 collective-permute-start.14
  70.2 2.8 %collective-permute-start.15 = (bf16[2,2,128,256]{3,2,1,0:T(8,128)(2,1)S(1)}, bf16[2,2,128,256]{3,2,1,0:T(8,128)(2,1)S(1)}, u32[]{:S(2)}, u32[]{:S(2)}) collective-permute-start(bf16[2,2,128,256]{3,2,1,0:T(8,128)(2,1)S(1)} %get-tuple-element.64), channel_id=1, source_target_pairs={{1,2},{2,1},{3,4},{4,3},{5,6},{6,5},{7,8},{8,7},{9,10},{10,9},{11,... | collective-permute-start | bytes 786440 | tf_op jit(solution)/shard_map/ppermute | solution.py:32
  73.0 11.6 %collective-permute-done.4.refs_2_ = bf16[2,2,128,256]{3,2,1,0:T(8,128)(2,1)S(1)} collective-permute-done((bf16[2,2,128,256]{3,2,1,0:T(8,128)(2,1)S(1)}, bf16[2,2,128,256]{3,2,1,0:T(8,128)(2,1)S(1)}, u32[]{:S(2)}, u32[]{:S(2)}) %collective-permute-start.4) | collective-permute-done | bytes 262176 | tf_op jit(solution)/shard_map/ppermute | solution.py:32
  84.5 1.2 %step.10 = (f32[2,4,128,256]{3,2,1,0:T(8,128)S(1)}, bf16[2,2,128,256]{3,2,1,0:T(8,128)(2,1)S(1)}, bf16[2,2,128,256]{3,2,1,0:T(8,128)(2,1)S(1)}, f32[4,128,256]{2,1,0:T(8,128)S(1)}) custom-call(f32[2,4,128,256]{3,2,1,0:T(8,128)S(1)} %get-tuple-element.43.refs_0_.refs_1_, f32[2,4,128,256]{3,2,1,0:T(8,128)S(1)} %get-tuple-element.38.refs_0_.refs_1_, ...), custom_call_target="tpu_custom_call" | custom-call | flops 1000000000 | bytes 5242880 | tf_op jit(solution)/shard_map/step/pallas_call | solution.py:300
  85.8 0.1 collective-permute-start.6
  85.9 2.5 %collective-permute-start.7 = (bf16[2,2,128,256]{3,2,1,0:T(8,128)(2,1)S(1)}, bf16[2,2,128,256]{3,2,1,0:T(8,128)(2,1)S(1)}, u32[]{:S(2)}, u32[]{:S(2)}) collective-permute-start(bf16[2,2,128,256]{3,2,1,0:T(8,128)(2,1)S(1)} %get-tuple-element.49), channel_id=1, source_target_pairs={{1,2},{2,1},{3,4},{4,3},{5,6},{6,5},{7,8},{8,7},{9,10},{10,9},{11,... | collective-permute-start | bytes 786440 | tf_op jit(solution)/shard_map/ppermute | solution.py:32
  88.4 1.8 %collective-permute-done.14.refs_2_ = bf16[2,2,128,256]{3,2,1,0:T(8,128)(2,1)S(1)} collective-permute-done((bf16[2,2,128,256]{3,2,1,0:T(8,128)(2,1)S(1)}, bf16[2,2,128,256]{3,2,1,0:T(8,128)(2,1)S(1)}, u32[]{:S(2)}, u32[]{:S(2)}) %collective-permute-start.14) | collective-permute-done | bytes 262176 | tf_op jit(solution)/shard_map/ppermute | solution.py:32
  90.2 1.2 %collective-permute-done.15.refs_3_ = bf16[2,2,128,256]{3,2,1,0:T(8,128)(2,1)S(1)} collective-permute-done((bf16[2,2,128,256]{3,2,1,0:T(8,128)(2,1)S(1)}, bf16[2,2,128,256]{3,2,1,0:T(8,128)(2,1)S(1)}, u32[]{:S(2)}, u32[]{:S(2)}) %collective-permute-start.15) | collective-permute-done | bytes 262176 | tf_op jit(solution)/shard_map/ppermute | solution.py:32
  91.3 2.2 %step.14 = (f32[2,2,2,4,128,256]{5,4,3,2,1,0:T(8,128)}, f32[4,128,256]{2,1,0:T(8,128)S(1)}) custom-call(f32[2,4,128,256]{3,2,1,0:T(8,128)S(1)} %get-tuple-element.62.refs_0_, f32[2,4,128,256]{3,2,1,0:T(8,128)S(1)} %get-tuple-element.58.refs_0_.refs_1_, bf16[2,2,128,256]{3,2,1,0:T(8,128)(2,1)S(1)} %collective-permute-done.14.refs_2_, ...), custom_call_target="tpu_custom_call" | custom-call | flops 1000000000 | bytes 5242880 | tf_op jit(solution)/shard_map/step/pallas_call | solution.py:300
  93.5 10.7 %collective-permute-done.6.refs_2_ = bf16[2,2,128,256]{3,2,1,0:T(8,128)(2,1)S(1)} collective-permute-done((bf16[2,2,128,256]{3,2,1,0:T(8,128)(2,1)S(1)}, bf16[2,2,128,256]{3,2,1,0:T(8,128)(2,1)S(1)}, u32[]{:S(2)}, u32[]{:S(2)}) %collective-permute-start.6) | collective-permute-done | bytes 262176 | tf_op jit(solution)/shard_map/ppermute | solution.py:32
  104.2 2.2 %step.15 = (f32[2,2,2,4,128,256]{5,4,3,2,1,0:T(8,128)}, f32[4,128,256]{2,1,0:T(8,128)S(1)}) custom-call(f32[2,4,128,256]{3,2,1,0:T(8,128)S(1)} %get-tuple-element.47.refs_0_, f32[2,4,128,256]{3,2,1,0:T(8,128)S(1)} %get-tuple-element.43.refs_0_.refs_1_, bf16[2,2,128,256]{3,2,1,0:T(8,128)(2,1)S(1)} %collective-permute-done.6.refs_2_, ...), custom_call_target="tpu_custom_call", output_to_operand_aliasing={{0}: (9, {})} | custom-call | flops 1000000000 | bytes 5242880 | tf_op jit(solution)/shard_map/step/pallas_call | solution.py:300
  106.4 2.4 %collective-permute-start.18 = (f32[4,128,256]{2,1,0:T(8,128)S(1)}, f32[4,128,256]{2,1,0:T(8,128)S(1)}, u32[]{:S(2)}, u32[]{:S(2)}) collective-permute-start(f32[4,128,256]{2,1,0:T(8,128)S(1)} %get-tuple-element.69.refs_1_), channel_id=1, source_target_pairs={{0,16},{16,0},{1,17},{17,1},{2,18},{18,2},{3,19},{19,3},{4,20},{20... | collective-permute-start | bytes 1572872 | tf_op jit(solution)/shard_map/ppermute | solution.py:368
  108.7 0.1 collective-permute-start.17
  108.8 0.4 collective-permute-start.16
  109.3 1.8 %collective-permute-done.16.others_ref = s32[2]{0:T(128)S(1)} collective-permute-done((s32[2]{0:T(128)S(1)}, s32[2]{0:T(128)S(1)}, u32[]{:S(2)}, u32[]{:S(2)}) %collective-permute-start.16) | collective-permute-done | bytes 40 | tf_op jit(solution)/shard_map/ppermute | solution.py:352
  111.0 2.2 %image.1 = f32[4,192,256]{2,1,0:T(8,128)} custom-call(s32[2]{0:T(128)S(1)} %copy-done.6, s32[2]{0:T(128)S(1)} %collective-permute-done.16.others_ref, f32[4,128,256]{2,1,0:T(8,128)S(1)} %get-tuple-element.68.refs_0_, f32[4,128,256]{2,1,0:T(8,128)S(1)} %get-tuple-element.69.refs_1_, f32[4,128,256]{2,1,0:T(8,128)S(1)} %collective-permute-done.17.refs_2_, ...), custom_call_target="tpu_custom_call" | custom-call | flops 1000000 | bytes 3145728 | tf_op jit(solution)/shard_map/image/pallas_call | solution.py:378
  (21 shorter events, 0.0 us)
Async XLA Ops:
  0.6 0.9 copy-start.4
  1.5 0.7 copy-start.7
  3.2 17.6 %all-to-all-start = ((bf16[16,16,384]{2,1,0:T(8,128)(2,1)}), bf16[16,16,384]{2,1,0:T(8,128)(2,1)S(1)}, u32[]{:S(2)}, u32[]{:S(2)}) async-start(bf16[16,16,384]{2,1,0:T(8,128)(2,1)} %bitcast), calls=%async_computation | async-start | bytes 393216 | tf_op jit(solution)/shard_map/all_to_all | solution.py:156
  9.7 2.2 %copy-start = (f32[2,2,2,4,128,256]{5,4,3,2,1,0:T(8,128)S(1)}, f32[2,2,2,4,128,256]{5,4,3,2,1,0:T(8,128)}, u32[]{:S(2)}) copy-start(f32[2,2,2,4,128,256]{5,4,3,2,1,0:T(8,128)} %refs_1_.7) | copy-start | bytes 12582916
  11.9 19.0 %copy-start.2 = (f32[4,192,256]{2,1,0:T(8,128)S(1)}, f32[4,192,256]{2,1,0:T(8,128)}, u32[]{:S(2)}) copy-start(f32[4,192,256]{2,1,0:T(8,128)} %refs_8_.3) | copy-start | bytes 2359300
  11.9 19.0 %copy-start.3 = (f32[2,4,64]{2,1,0:T(4,128)S(1)}, f32[2,4,64]{2,1,0:T(4,128)}, u32[]{:S(2)}) copy-start(f32[2,4,64]{2,1,0:T(4,128)} %refs_6_.15) | copy-start | bytes 6148
  11.9 19.0 %copy-start.5 = (s32[2,64]{1,0:T(2,128)S(1)}, s32[2,64]{1,0:T(2,128)}, u32[]{:S(2)}) copy-start(s32[2,64]{1,0:T(2,128)} %refs_5_.11) | copy-start | bytes 1540
  11.9 19.0 %copy-start.6 = (s32[2]{0:T(128)S(1)}, s32[2]{0:T(128)}, u32[]{:S(2)}) copy-start(s32[2]{0:T(128)} %offsets_ref.1) | copy-start | bytes 28
  12.0 18.9 %collective-permute-start.8 = (bf16[2,2,128,256]{3,2,1,0:T(8,128)(2,1)S(1)}, bf16[2,2,128,256]{3,2,1,0:T(8,128)(2,1)S(1)}, u32[]{:S(2)}, u32[]{:S(2)}) collective-permute-start(bf16[2,2,128,256]{3,2,1,0:T(8,128)(2,1)S(1)} %get-tuple-element.51), channel_id=1, source_target_pairs={{0,1},{1,0},{2,3},{3,2},{4,5},{5,4},{6,7},{7,6},{8,9},{9,8},{10,11... | collective-permute-start | bytes 786440 | tf_op jit(solution)/shard_map/ppermute | solution.py:32
  12.4 18.6 %collective-permute-start.9 = (bf16[2,2,128,256]{3,2,1,0:T(8,128)(2,1)S(1)}, bf16[2,2,128,256]{3,2,1,0:T(8,128)(2,1)S(1)}, u32[]{:S(2)}, u32[]{:S(2)}) collective-permute-start(bf16[2,2,128,256]{3,2,1,0:T(8,128)(2,1)S(1)} %get-tuple-element.52), channel_id=1, source_target_pairs={{1,2},{2,1},{3,4},{4,3},{5,6},{6,5},{7,8},{8,7},{9,10},{10,9},{11,... | collective-permute-start | bytes 786440 | tf_op jit(solution)/shard_map/ppermute | solution.py:32
  16.5 22.2 %collective-permute-start = (bf16[2,2,128,256]{3,2,1,0:T(8,128)(2,1)S(1)}, bf16[2,2,128,256]{3,2,1,0:T(8,128)(2,1)S(1)}, u32[]{:S(2)}, u32[]{:S(2)}) collective-permute-start(bf16[2,2,128,256]{3,2,1,0:T(8,128)(2,1)S(1)} %get-tuple-element.36), channel_id=1, source_target_pairs={{0,1},{1,0},{2,3},{3,2},{4,5},{5,4},{6,7},{7,6},{8,9},{9,8},{10,11... | collective-permute-start | bytes 786440 | tf_op jit(solution)/shard_map/ppermute | solution.py:32
  16.8 21.9 %collective-permute-start.1 = (bf16[2,2,128,256]{3,2,1,0:T(8,128)(2,1)S(1)}, bf16[2,2,128,256]{3,2,1,0:T(8,128)(2,1)S(1)}, u32[]{:S(2)}, u32[]{:S(2)}) collective-permute-start(bf16[2,2,128,256]{3,2,1,0:T(8,128)(2,1)S(1)} %get-tuple-element.37), channel_id=1, source_target_pairs={{1,2},{2,1},{3,4},{4,3},{5,6},{6,5},{7,8},{8,7},{9,10},{10,9},{11,... | collective-permute-start | bytes 786440 | tf_op jit(solution)/shard_map/ppermute | solution.py:32
  31.0 2.2 %copy-start.1 = (f32[2,2,2,4,128,256]{5,4,3,2,1,0:T(8,128)S(1)}, f32[2,2,2,4,128,256]{5,4,3,2,1,0:T(8,128)}, u32[]{:S(2)}) copy-start(f32[2,2,2,4,128,256]{5,4,3,2,1,0:T(8,128)} %refs_1_.7) | copy-start | bytes 12582916
  34.9 9.0 %collective-permute-start.10 = (bf16[2,2,128,256]{3,2,1,0:T(8,128)(2,1)S(1)}, bf16[2,2,128,256]{3,2,1,0:T(8,128)(2,1)S(1)}, u32[]{:S(2)}, u32[]{:S(2)}) collective-permute-start(bf16[2,2,128,256]{3,2,1,0:T(8,128)(2,1)S(1)} %get-tuple-element.54), channel_id=1, source_target_pairs={{0,1},{1,0},{2,3},{3,2},{4,5},{5,4},{6,7},{7,6},{8,9},{9,8},{10,11... | collective-permute-start | bytes 786440 | tf_op jit(solution)/shard_map/ppermute | solution.py:32
  35.0 13.1 %collective-permute-start.11 = (bf16[2,2,128,256]{3,2,1,0:T(8,128)(2,1)S(1)}, bf16[2,2,128,256]{3,2,1,0:T(8,128)(2,1)S(1)}, u32[]{:S(2)}, u32[]{:S(2)}) collective-permute-start(bf16[2,2,128,256]{3,2,1,0:T(8,128)(2,1)S(1)} %get-tuple-element.55), channel_id=1, source_target_pairs={{1,2},{2,1},{3,4},{4,3},{5,6},{6,5},{7,8},{8,7},{9,10},{10,9},{11,... | collective-permute-start | bytes 786440 | tf_op jit(solution)/shard_map/ppermute | solution.py:32
  40.5 21.6 %collective-permute-start.2 = (bf16[2,2,128,256]{3,2,1,0:T(8,128)(2,1)S(1)}, bf16[2,2,128,256]{3,2,1,0:T(8,128)(2,1)S(1)}, u32[]{:S(2)}, u32[]{:S(2)}) collective-permute-start(bf16[2,2,128,256]{3,2,1,0:T(8,128)(2,1)S(1)} %get-tuple-element.39), channel_id=1, source_target_pairs={{0,1},{1,0},{2,3},{3,2},{4,5},{5,4},{6,7},{7,6},{8,9},{9,8},{10,11... | collective-permute-start | bytes 786440 | tf_op jit(solution)/shard_map/ppermute | solution.py:32
  41.7 20.4 %collective-permute-start.3 = (bf16[2,2,128,256]{3,2,1,0:T(8,128)(2,1)S(1)}, bf16[2,2,128,256]{3,2,1,0:T(8,128)(2,1)S(1)}, u32[]{:S(2)}, u32[]{:S(2)}) collective-permute-start(bf16[2,2,128,256]{3,2,1,0:T(8,128)(2,1)S(1)} %get-tuple-element.40), channel_id=1, source_target_pairs={{1,2},{2,1},{3,4},{4,3},{5,6},{6,5},{7,8},{8,7},{9,10},{10,9},{11,... | collective-permute-start | bytes 786440 | tf_op jit(solution)/shard_map/ppermute | solution.py:32
  49.4 18.3 %collective-permute-start.12 = (bf16[2,2,128,256]{3,2,1,0:T(8,128)(2,1)S(1)}, bf16[2,2,128,256]{3,2,1,0:T(8,128)(2,1)S(1)}, u32[]{:S(2)}, u32[]{:S(2)}) collective-permute-start(bf16[2,2,128,256]{3,2,1,0:T(8,128)(2,1)S(1)} %get-tuple-element.59), channel_id=1, source_target_pairs={{0,1},{1,0},{2,3},{3,2},{4,5},{5,4},{6,7},{7,6},{8,9},{9,8},{10,11... | collective-permute-start | bytes 786440 | tf_op jit(solution)/shard_map/ppermute | solution.py:32
  49.5 19.4 %collective-permute-start.13 = (bf16[2,2,128,256]{3,2,1,0:T(8,128)(2,1)S(1)}, bf16[2,2,128,256]{3,2,1,0:T(8,128)(2,1)S(1)}, u32[]{:S(2)}, u32[]{:S(2)}) collective-permute-start(bf16[2,2,128,256]{3,2,1,0:T(8,128)(2,1)S(1)} %get-tuple-element.60), channel_id=1, source_target_pairs={{1,2},{2,1},{3,4},{4,3},{5,6},{6,5},{7,8},{8,7},{9,10},{10,9},{11,... | collective-permute-start | bytes 786440 | tf_op jit(solution)/shard_map/ppermute | solution.py:32
  63.3 21.2 %collective-permute-start.4 = (bf16[2,2,128,256]{3,2,1,0:T(8,128)(2,1)S(1)}, bf16[2,2,128,256]{3,2,1,0:T(8,128)(2,1)S(1)}, u32[]{:S(2)}, u32[]{:S(2)}) collective-permute-start(bf16[2,2,128,256]{3,2,1,0:T(8,128)(2,1)S(1)} %get-tuple-element.44), channel_id=1, source_target_pairs={{0,1},{1,0},{2,3},{3,2},{4,5},{5,4},{6,7},{7,6},{8,9},{9,8},{10,11... | collective-permute-start | bytes 786440 | tf_op jit(solution)/shard_map/ppermute | solution.py:32
  63.4 21.1 %collective-permute-start.5 = (bf16[2,2,128,256]{3,2,1,0:T(8,128)(2,1)S(1)}, bf16[2,2,128,256]{3,2,1,0:T(8,128)(2,1)S(1)}, u32[]{:S(2)}, u32[]{:S(2)}) collective-permute-start(bf16[2,2,128,256]{3,2,1,0:T(8,128)(2,1)S(1)} %get-tuple-element.45), channel_id=1, source_target_pairs={{1,2},{2,1},{3,4},{4,3},{5,6},{6,5},{7,8},{8,7},{9,10},{10,9},{11,... | collective-permute-start | bytes 786440 | tf_op jit(solution)/shard_map/ppermute | solution.py:32
  70.1 20.1 %collective-permute-start.14 = (bf16[2,2,128,256]{3,2,1,0:T(8,128)(2,1)S(1)}, bf16[2,2,128,256]{3,2,1,0:T(8,128)(2,1)S(1)}, u32[]{:S(2)}, u32[]{:S(2)}) collective-permute-start(bf16[2,2,128,256]{3,2,1,0:T(8,128)(2,1)S(1)} %get-tuple-element.63), channel_id=1, source_target_pairs={{0,1},{1,0},{2,3},{3,2},{4,5},{5,4},{6,7},{7,6},{8,9},{9,8},{10,11... | collective-permute-start | bytes 786440 | tf_op jit(solution)/shard_map/ppermute | solution.py:32
  70.2 21.2 %collective-permute-start.15 = (bf16[2,2,128,256]{3,2,1,0:T(8,128)(2,1)S(1)}, bf16[2,2,128,256]{3,2,1,0:T(8,128)(2,1)S(1)}, u32[]{:S(2)}, u32[]{:S(2)}) collective-permute-start(bf16[2,2,128,256]{3,2,1,0:T(8,128)(2,1)S(1)} %get-tuple-element.64), channel_id=1, source_target_pairs={{1,2},{2,1},{3,4},{4,3},{5,6},{6,5},{7,8},{8,7},{9,10},{10,9},{11,... | collective-permute-start | bytes 786440 | tf_op jit(solution)/shard_map/ppermute | solution.py:32
  85.8 18.4 %collective-permute-start.6 = (bf16[2,2,128,256]{3,2,1,0:T(8,128)(2,1)S(1)}, bf16[2,2,128,256]{3,2,1,0:T(8,128)(2,1)S(1)}, u32[]{:S(2)}, u32[]{:S(2)}) collective-permute-start(bf16[2,2,128,256]{3,2,1,0:T(8,128)(2,1)S(1)} %get-tuple-element.48), channel_id=1, source_target_pairs={{0,1},{1,0},{2,3},{3,2},{4,5},{5,4},{6,7},{7,6},{8,9},{9,8},{10,11... | collective-permute-start | bytes 786440 | tf_op jit(solution)/shard_map/ppermute | solution.py:32
  85.9 18.3 %collective-permute-start.7 = (bf16[2,2,128,256]{3,2,1,0:T(8,128)(2,1)S(1)}, bf16[2,2,128,256]{3,2,1,0:T(8,128)(2,1)S(1)}, u32[]{:S(2)}, u32[]{:S(2)}) collective-permute-start(bf16[2,2,128,256]{3,2,1,0:T(8,128)(2,1)S(1)} %get-tuple-element.49), channel_id=1, source_target_pairs={{1,2},{2,1},{3,4},{4,3},{5,6},{6,5},{7,8},{8,7},{9,10},{10,9},{11,... | collective-permute-start | bytes 786440 | tf_op jit(solution)/shard_map/ppermute | solution.py:32
  106.4 4.7 %collective-permute-start.18 = (f32[4,128,256]{2,1,0:T(8,128)S(1)}, f32[4,128,256]{2,1,0:T(8,128)S(1)}, u32[]{:S(2)}, u32[]{:S(2)}) collective-permute-start(f32[4,128,256]{2,1,0:T(8,128)S(1)} %get-tuple-element.69.refs_1_), channel_id=1, source_target_pairs={{0,16},{16,0},{1,17},{17,1},{2,18},{18,2},{3,19},{19,3},{4,20},{20... | collective-permute-start | bytes 1572872 | tf_op jit(solution)/shard_map/ppermute | solution.py:368
  108.7 2.3 %collective-permute-start.17 = (f32[4,128,256]{2,1,0:T(8,128)S(1)}, f32[4,128,256]{2,1,0:T(8,128)S(1)}, u32[]{:S(2)}, u32[]{:S(2)}) collective-permute-start(f32[4,128,256]{2,1,0:T(8,128)S(1)} %get-tuple-element.68.refs_0_), channel_id=1, source_target_pairs={{0,16},{16,0},{1,17},{17,1},{2,18},{18,2},{3,19},{19,3},{4,20},{20... | collective-permute-start | bytes 1572872 | tf_op jit(solution)/shard_map/ppermute | solution.py:368
  108.8 2.2 %collective-permute-start.16 = (s32[2]{0:T(128)S(1)}, s32[2]{0:T(128)S(1)}, u32[]{:S(2)}, u32[]{:S(2)}) collective-permute-start(s32[2]{0:T(128)S(1)} %copy-done.6), channel_id=1, source_target_pairs={{0,16},{16,0},{1,17},{17,1},{2,18},{18,2},{3,19},{19,3},{4,20},{20... | collective-permute-start | bytes 32 | tf_op jit(solution)/shard_map/ppermute | solution.py:352

commit v2 on v1

v2 whole, which is shorter than its diff:
```python
import functools

import jax
import jax.numpy as jnp
from jax import lax
from jax.experimental import pallas as pl
from jax.experimental.pallas import tpu as pltpu
from jax.sharding import PartitionSpec as P

STEPS = 4
RDEPTH = 4
EDGE = 4
LANES = 128
VMEM_LIMIT = 24 * 1024 * 1024
VMEM = pltpu.VMEM
SMEM = pltpu.SMEM
HBM = pltpu.HBM
BOTH = ((0, 1),)
SPLIT = ((1,), (0,))
HEAVY = 10**13


def params():
    return pltpu.CompilerParams(vmem_limit_bytes=VMEM_LIMIT)


def cost(weight=0):
    return pl.CostEstimate(flops=1 + weight, bytes_accessed=1, transcendentals=0)


def swap_pairs(value, first):
    count = lax.axis_size("space")
    routes = []
    for at in range(first, count - 1, 2):
        routes += [(at, at + 1), (at + 1, at)]
    return lax.ppermute(value, "space", routes)


def band(rows, centre):
    gap = jnp.abs(
        lax.broadcasted_iota(jnp.int32, (rows, rows), 0)
        - lax.broadcasted_iota(jnp.int32, (rows, rows), 1)
    )
    weights = jnp.where(gap == 0, centre, jnp.where(gap == 1, 16.0, jnp.where(gap == 2, -1.0, 0.0)))
    return weights.astype(jnp.bfloat16)


def mm(left, right, dims=((1,), (0,))):
    return lax.dot_general(left, right, (dims, ((), ())), preferred_element_type=jnp.float32)


def window_at(offset, model_y, rows_y):
    start = jnp.minimum(lax.div(offset, 8), (model_y - rows_y - 8) // 8) * 8
    return pl.multiple_of(start, 8), offset - start


def add_window(target_ref, lead, part, offset):
    rows_y = part.shape[0]
    start, gap = window_at(offset, target_ref.shape[-2], rows_y)
    moved = jnp.concatenate([part, jnp.zeros((8, part.shape[1]), part.dtype)], axis=0)
    at = lead + (pl.ds(start, rows_y + 8), slice(None))
    target_ref[at] = target_ref[at] + pltpu.roll(moved, gap, 0)


def is_odd():
    return lax.rem(lax.axis_index("space"), 2) == 1


def write_sends(field_ref, groups, send_refs):
    odd = is_odd()
    for at_group, group in enumerate(groups):
        send0_ref, send1_ref = send_refs[2 * at_group : 2 * at_group + 2]
        for place, comp in enumerate(group):
            for at in range(2):
                low = field_ref[comp, at]
                high = field_ref[comp, at + field_ref.shape[-3] - 2]
                send0_ref[place, at] = jnp.where(odd, low, high).astype(jnp.bfloat16)
                send1_ref[place, at] = jnp.where(odd, high, low).astype(jnp.bfloat16)


def pack_kernel(shot, field_ref, *refs):
    send0_ref, send1_ref, own_ref, sem = refs[-4:]
    load = pltpu.make_async_copy(field_ref.at[shot, 0], own_ref, sem)
    load.start()
    load.wait()
    write_sends(own_ref, BOTH, (send0_ref, send1_ref))


def pack_halo(wavefields, shot, after):
    _, _, comps, layers, rows_y, cells_z = wavefields.shape
    half = jax.ShapeDtypeStruct((comps, 2, rows_y, cells_z), jnp.bfloat16)
    return pl.pallas_call(
        functools.partial(pack_kernel, shot),
        in_specs=[pl.BlockSpec(memory_space=HBM)] + [pl.BlockSpec(memory_space=pl.ANY)] * len(after),
        out_specs=[pl.BlockSpec(memory_space=VMEM)] * 2,
        out_shape=[half, half],
        scratch_shapes=[
            pltpu.VMEM((comps, layers, rows_y, cells_z), jnp.float32),
            pltpu.SemaphoreType.DMA,
        ],
        compiler_params=params(),
        cost_estimate=cost(),
        name="pack_halo",
    )(pltpu.with_memory_space_constraint(wavefields, HBM), *after)


def pack_lines_kernel(cap, per_owner, ids_ref, lines_ref, after_ref, out_ref):
    shots, hold = ids_ref.shape
    total = shots * hold
    ids = jnp.concatenate([ids_ref[shot : shot + 1] for shot in range(shots)], axis=1)
    ids = ids.astype(jnp.float32)
    row_at = lax.broadcasted_iota(jnp.int32, (total, total), 0)
    col_at = lax.broadcasted_iota(jnp.int32, (total, total), 1)
    slot_at = lax.broadcasted_iota(jnp.int32, (1, total), 1)
    shot_of = jnp.zeros((1, total), jnp.float32)
    for shot in range(1, shots):
        shot_of = shot_of + (slot_at >= shot * hold).astype(jnp.float32)
    owner = jnp.floor((ids + 0.5) * (1.0 / per_owner))
    inside = ids - owner * per_owner
    used = ids >= 0.0
    key = jnp.where(used, owner * shots + shot_of, -1.0)
    wide_key = jnp.broadcast_to(key, (total, total))
    same = jnp.where(row_at == col_at, wide_key, 0.0)
    tall_key = jnp.sum(same, axis=1, keepdims=True)
    earlier_one = (tall_key == wide_key) & (row_at < col_at)
    rank = jnp.sum(earlier_one.astype(jnp.float32), axis=0, keepdims=True)
    target = jnp.where(used, key * cap + rank, -1.0)
    hot = jnp.where(row_at.astype(jnp.float32) == target, 1.0, 0.0)
    tags = jnp.sum(hot * (inside + 1.0), axis=1, keepdims=True)
    hot = hot.astype(jnp.bfloat16)
    cells_z = lines_ref.shape[2]
    rows = mm(hot[:, :hold], lines_ref[0])
    for shot in range(1, shots):
        rows = rows + mm(hot[:, shot * hold : (shot + 1) * hold], lines_ref[shot])
    out_ref[:, :cells_z] = rows.astype(jnp.bfloat16)
    out_ref[:, cells_z:] = jnp.broadcast_to(tags, (total, LANES)).astype(jnp.bfloat16)


def unpack_lines_kernel(cap, shots, per_owner, got_ref, out_ref):
    total = got_ref.shape[0]
    cells_z = out_ref.shape[1]
    tags = got_ref[:, cells_z : cells_z + LANES].astype(jnp.float32)[:, 0:1]
    row_at = lax.broadcasted_iota(jnp.int32, (total, 1), 0).astype(jnp.float32)
    block = jnp.floor((row_at + 0.5) * (1.0 / cap))
    shot_of = block - shots * jnp.floor((block + 0.5) * (1.0 / shots))
    target = jnp.where(tags > 0.5, tags - 1.0 + shot_of * per_owner, -1.0)
    line_at = lax.broadcasted_iota(jnp.int32, (total, shots * per_owner), 1).astype(jnp.float32)
    hot = jnp.where(line_at == target, 1.0, 0.0).astype(jnp.bfloat16)
    out_ref[...] = mm(hot, got_ref[:, :cells_z], ((0,), (0,)))


def pack_lines(strip_lines, strip_ids, per_owner, cap, after):
    shots, hold, cells_z = strip_lines.shape
    vmem = pl.BlockSpec(memory_space=VMEM)
    return pl.pallas_call(
        functools.partial(pack_lines_kernel, cap, per_owner),
        in_specs=[vmem, vmem, pl.BlockSpec(memory_space=pl.ANY)],
        out_specs=vmem,
        out_shape=jax.ShapeDtypeStruct((shots * hold, cells_z + LANES), jnp.bfloat16),
        compiler_params=params(),
        cost_estimate=cost(),
        name="pack_lines",
    )(strip_ids, strip_lines, after)


def deliver(message, cap, shots, per_owner):
    total, wide = message.shape
    message = message.reshape(lax.axis_size("space"), shots * cap, wide)
    got = lax.all_to_all(message, "space", 0, 0, tiled=False)
    return pl.pallas_call(
        functools.partial(unpack_lines_kernel, cap, shots, per_owner),
        out_shape=jax.ShapeDtypeStruct((shots * per_owner, wide - LANES), jnp.float32),
        compiler_params=params(),
        cost_estimate=cost(),
        name="unpack_lines",
    )(got.reshape(total, wide))


def split3(value):
    parts = []
    for _ in range(3):
        part = value.astype(jnp.bfloat16)
        parts.append(part)
        value = value - part.astype(jnp.float32)
    return parts


def take_lines(new_ref, saved_ref, shot, step, layer):
    _, layers, rows_y, _ = new_ref.shape
    base = ((shot * STEPS + step) * layers + layer) * EDGE
    new_ref[0, layer, 0:2, :] = saved_ref[base : base + 2, :]
    new_ref[0, layer, rows_y - 2 :, :] = saved_ref[base + 2 : base + 4, :]


def finish_kernel(shot, new_from, saved_ref, new_ref, send0_ref, send1_ref):
    del new_from
    for layer in range(new_ref.shape[1]):
        take_lines(new_ref, saved_ref, shot, 0, layer)
    write_sends(new_ref, BOTH, (send0_ref, send1_ref))


def finish_first(shot, new, saved):
    comps, _, rows_y, cells_z = new.shape
    half = jax.ShapeDtypeStruct((comps, 2, rows_y, cells_z), jnp.bfloat16)
    vmem = pl.BlockSpec(memory_space=VMEM)
    return pl.pallas_call(
        functools.partial(finish_kernel, shot),
        in_specs=[vmem, vmem],
        out_specs=[vmem] * 3,
        out_shape=[jax.ShapeDtypeStruct(new.shape, new.dtype), half, half],
        input_output_aliases={0: 0},
        compiler_params=params(),
        cost_estimate=cost(),
        name="finish_first_%d" % shot,
    )(new, saved)


def step_kernel(shot, step, comps, got_groups, send_groups, create, lines, waits, *refs):
    refs = list(refs)

    def take(count):
        taken, refs[:] = refs[:count], refs[count:]
        return taken

    first, last = step == 0, step == STEPS - 1
    with_image = 1 in comps
    now_ref, later_ref = take(2)
    got_of = {}
    for group in got_groups:
        got0_ref, got1_ref = take(2)
        for place, comp in enumerate(group):
            got_of[comp] = (got0_ref, got1_ref, place)
    [saved_ref] = take(1) if lines else [None]
    pos_ref, traces_ref = take(2) if with_image else (None, None)
    framing = last and with_image
    [offsets_ref] = take(1) if first or framing else [None]
    [speed_from] = take(1)
    [contrib_from] = take(1) if with_image and not first else [None]
    [frame_from] = take(1) if framing and not create else [None]
    take(waits)
    if last:
        take(0 if create else 1)
        [out_ref] = take(1)
    else:
        [new_ref] = take(1)
        send_refs = take(2 * len(send_groups))
    [contrib_ref] = take(1) if with_image else [None]
    [speed_out] = take(1) if first else [None]
    if last:
        new_ref, out_sems = take(2)
    loads = []
    if first:
        state_ref, load_sems = take(2)
        loads = [pltpu.make_async_copy(now_ref.at[shot], state_ref, load_sems.at[0])]
        now_ref, later_ref = state_ref.at[0], state_ref.at[1]
    elif step == 1:
        state_ref, load_sems = take(2)
        loads = [pltpu.make_async_copy(later_ref.at[shot, 0], state_ref, load_sems.at[0])]
        later_ref = state_ref
    for load in loads:
        load.start()
    layers, rows_y, cells_z = new_ref.shape[-3:]
    stores = []
    if last and with_image:
        stores.append(pltpu.make_async_copy(now_ref, out_ref.at[shot, 1], out_sems.at[0]))
        stores[0].start()
    odd = is_odd()
    across_z = band(cells_z, -90.0)
    across_y = band(rows_y, 0.0)
    if with_image:
        trace_row = traces_ref[shot, step : step + 1, :]
        lane_of = lax.broadcasted_iota(jnp.int32, (LANES, trace_row.shape[1]), 0)
        trace_parts = [
            jnp.where(lane_of == RDEPTH, part.astype(jnp.float32), 0.0).astype(jnp.bfloat16)
            for part in split3(trace_row)
        ]
        spots = pos_ref[shot : shot + 1, :]
        cell_of = lax.broadcasted_iota(jnp.int32, (rows_y, trace_row.shape[1]), 0)
    for load in loads:
        load.wait()

    for comp in comps:
        got0_ref, got1_ref, place = got_of[comp]

        def layer_of(at):
            if at < 0:
                both = (got1_ref[place, 2 + at], got0_ref[place, 2 + at])
            elif at >= layers:
                both = (got0_ref[place, at - layers], got1_ref[place, at - layers])
            else:
                return now_ref[comp, at]
            even_one, odd_one = (part.astype(jnp.float32) for part in both)
            return jnp.where(odd, odd_one, even_one)

        for layer in range(layers):
            if first and comp == comps[0]:
                start_y, gap = window_at(offsets_ref[shot], speed_from.shape[1], rows_y)
                speed = speed_from[layer, pl.ds(start_y, rows_y + 8), :]
                speed = pltpu.roll(speed, lax.rem(rows_y + 8 - gap, rows_y + 8), 0)[:rows_y]
                speed_out[layer] = speed
            else:
                speed = (speed_out if first else speed_from)[layer]
            here = layer_of(layer)
            high = here.astype(jnp.bfloat16)
            low = (here - high.astype(jnp.float32)).astype(jnp.bfloat16)
            growth = mm(high, across_z) + mm(low, across_z)
            growth = growth + (mm(across_y, high) + mm(across_y, low))
            growth = growth + 16.0 * (layer_of(layer - 1) + layer_of(layer + 1))
            growth = growth - (layer_of(layer - 2) + layer_of(layer + 2))
            growth = growth * (1.0 / 12.0)
            if comp == 1:
                hot = jnp.where(spots == cell_of + layer * rows_y, 1.0, 0.0).astype(jnp.bfloat16)
                plane = mm(hot, trace_parts[0], ((1,), (1,)))
                plane = plane + mm(hot, trace_parts[1], ((1,), (1,)))
                plane = plane + mm(hot, trace_parts[2], ((1,), (1,)))
                growth = jnp.concatenate(
                    [growth[:, :LANES] + plane, growth[:, LANES:]], axis=1
                )
            change = speed * growth
            new_ref[comp, layer] = 2.0 * here - later_ref[comp, layer] + change
            if comp == 1:
                term = now_ref[0, layer] * change
                if not first:
                    term = contrib_from[layer] + term
                if framing:
                    if create:
                        contrib_ref[layer] = jnp.zeros_like(contrib_ref[layer])
                    else:
                        contrib_ref[layer] = frame_from[layer]
                    add_window(contrib_ref, (layer,), term, offsets_ref[shot])
                else:
                    contrib_ref[layer] = term
            elif lines:
                take_lines(new_ref, saved_ref, shot, step, layer)
        if last:
            stores.append(
                pltpu.make_async_copy(
                    new_ref.at[comp], out_ref.at[shot, 0, comp], out_sems.at[1 + comp]
                )
            )
            stores[-1].start()
    for store in stores:
        store.wait()
    if not last:
        write_sends(new_ref, send_groups, send_refs)


def one_step(
    shot, step, comps, got_groups, send_groups,
    wavefields, offsets, now, later, got, saved, pos, traces, speed, contrib, frame, out, after, heavy, model_y,
):
    first, last = step == 0, step == STEPS - 1
    with_image = 1 in comps
    shots = wavefields.shape[0]
    both, layers, rows_y, cells_z = wavefields.shape[2:]
    vmem, hbm = pl.BlockSpec(memory_space=VMEM), pl.BlockSpec(memory_space=HBM)
    state = jax.ShapeDtypeStruct((both, layers, rows_y, cells_z), jnp.float32)
    image = jax.ShapeDtypeStruct((layers, rows_y, cells_z), jnp.float32)
    aliases = {}
    scratch = []
    args = [
        pltpu.with_memory_space_constraint(field, HBM) if field is wavefields else field
        for field in (now, later)
    ]
    specs = [hbm if first else vmem, hbm if step < 2 else vmem]
    args += [value for pair in got for value in pair]
    specs += [vmem] * (2 * len(got))
    lines = saved is not None and 0 in comps
    if lines:
        args.append(saved)
        specs.append(vmem)
    if with_image:
        args += [pos, traces]
        specs += [vmem, vmem]
    framing = last and with_image
    if first or framing:
        args.append(offsets)
        specs.append(pl.BlockSpec(memory_space=SMEM))
    args.append(speed)
    specs.append(vmem)
    if with_image and not first:
        args.append(contrib)
        specs.append(vmem)
    if framing and out is not None:
        args.append(frame)
        specs.append(vmem)
    args += after
    specs += [pl.BlockSpec(memory_space=pl.ANY)] * len(after)
    if last:
        if out is not None:
            aliases[len(args)] = 0
            args.append(out)
            specs.append(hbm)
        outs = [jax.ShapeDtypeStruct((shots, 2) + state.shape, jnp.float32)]
        out_specs = [hbm]
        scratch = [pltpu.VMEM(state.shape, jnp.float32), pltpu.SemaphoreType.DMA((3,))]
    else:
        outs = [state]
        for group in send_groups:
            half = jax.ShapeDtypeStruct((len(group), 2, rows_y, cells_z), jnp.bfloat16)
            outs += [half, half]
        out_specs = [vmem] * len(outs)
    if framing:
        outs.append(jax.ShapeDtypeStruct((layers, model_y, cells_z), jnp.float32))
        out_specs.append(vmem)
    elif with_image:
        outs.append(image)
        out_specs.append(vmem)
    if first:
        outs.append(image)
        out_specs.append(vmem)
    if step < 2:
        lead = (2,) if first else ()
        scratch = [pltpu.VMEM(lead + state.shape, jnp.float32), pltpu.SemaphoreType.DMA((1,))]
    return pl.pallas_call(
        functools.partial(
            step_kernel, shot, step, comps, got_groups, send_groups, out is None, lines, len(after)
        ),
        in_specs=specs,
        out_specs=out_specs,
        out_shape=outs,
        scratch_shapes=scratch,
        input_output_aliases=aliases,
        compiler_params=params(),
        cost_estimate=cost(HEAVY if heavy else 0),
        name="step_%d_shot_%d" % (step, shot),
    )(*args)


def sum_kernel(scale, own_ref, other_ref, *refs):
    refs[-1][...] = (own_ref[...] + other_ref[...]) * scale


def sum_frames(own, other, scale, after):
    vmem, hbm = pl.BlockSpec(memory_space=VMEM), pl.BlockSpec(memory_space=HBM)
    return pl.pallas_call(
        functools.partial(sum_kernel, scale),
        in_specs=[vmem, vmem, hbm],
        out_specs=vmem,
        out_shape=jax.ShapeDtypeStruct(own.shape, jnp.float32),
        compiler_params=params(),
        cost_estimate=cost(),
        name="sum_frames",
    )(own, other, pltpu.with_memory_space_constraint(after, HBM))


def body(wavefields, courant, offsets, strip_lines, strip_ids, receiver_pos, traces):
    shots = wavefields.shape[0]
    layers = wavefields.shape[3]
    cells_z = wavefields.shape[5]
    model_y = courant.shape[1]
    per_owner = STEPS * EDGE * layers
    shot_devices = lax.axis_size("shot")
    scale = 1.0 / (shots * shot_devices)
    cap = strip_lines.shape[1] // lax.axis_size("space")

    def exchange(sends):
        return [
            (swap_pairs(sends[at], 0), swap_pairs(sends[at + 1], 1)) for at in range(0, len(sends), 2)
        ]

    sends = pack_halo(wavefields, 0, [])
    got = [exchange(sends)]
    message = pack_lines(strip_lines, strip_ids, per_owner, cap, sends[0])
    saved = deliver(message, cap, shots, per_owner)
    for shot in range(1, shots):
        got.append(exchange(pack_halo(wavefields, shot, [message])))
    groups = [BOTH] * shots
    now = [wavefields] * shots
    later = [wavefields] * shots
    contrib = [None] * shots
    speed = [courant] * shots
    out = None
    frame = None
    after = []
    for step in range(STEPS):
        for shot in range(shots):
            split = shot == shots - 1
            send_groups = SPLIT if split and step == STEPS - 2 else BOTH
            common = (wavefields, offsets, now[shot], later[shot])
            fixed = (receiver_pos, traces, speed[shot])
            if step < STEPS - 1:
                early = step == 0 and shot == 0
                made = one_step(
                    shot, step, BOTH[0], groups[shot], () if early else send_groups, *common,
                    got[shot], None if early else saved, *fixed, contrib[shot], None, None, after, early,
                    model_y,
                )
                later[shot], now[shot] = now[shot], made[0]
                if early:
                    made = [*finish_first(shot, made[0], saved), *made[1:]]
                    now[shot] = made[0]
                ends = 1 + 2 * len(send_groups)
                got[shot] = exchange(made[1:ends])
                groups[shot] = send_groups
                contrib[shot] = made[ends]
                if step == 0:
                    speed[shot] = made[ends + 1]
                after = [made[1]]
                continue
            for part, group in enumerate(groups[shot]):
                made = one_step(
                    shot, step, group, (group,), (), *common, got[shot][part : part + 1], saved,
                    *fixed, contrib[shot], frame, out, after, part > 0, model_y,
                )
                out = made[0]
                if 1 in group:
                    frame = made[1]
                    after = [frame]
    if shot_devices == 2:
        other = lax.ppermute(frame, "shot", [(0, 1), (1, 0)])
        image = sum_frames(frame, other, scale, out)
    else:
        image = lax.psum(frame, "shot") * scale
    return (out, image)


def solution(mesh):
    placed = (
        P("shot", None, None, "space", None, None),
        P("space", None, None),
        P("shot"),
        P("shot", "space", None),
        P("shot", "space"),
        P("shot", "space"),
        P("shot", None, "space"),
    )
    return jax.shard_map(
        body,
        mesh=mesh,
        in_specs=placed,
        out_specs=(P("shot", None, None, "space", None, None), P("space", None, None)),
        check_vma=False,
    )
```

time: 114 us -> 110 us (0.965)
  waiting for transfers between devices: 54.4 us -> 36.7 us
  Pallas kernels: 16.6 us -> 30.1 us
  starting transfers between devices: 35.5 us -> 41.5 us
  local copies, waits for them, and re-layouts: 5.96 us -> 0.03 us
    ppermute x16 -> x18, waiting for transfers between devices: 52.6 us -> 35.9 us  [swap_pairs(): return lax.ppermute(value, 'space', routes)]
    pallas_call x12 -> x14, Pallas kernels: 16.3 us -> 28.9 us  [the longest x9 21.9 us: one_step(): pl.pallas_call(functools.partial(step_kernel, shot, step, comps, got_grou...]
    ppermute x16 -> x18, starting transfers between devices: 26.1 us -> 35.2 us  [swap_pairs(): return lax.ppermute(value, 'space', routes)]
    unnamed x16 -> x12, local copies, waits for them, and re-layouts: 5.96 us -> 0.03 us
    ppermute x3 -> x1, starting transfers between devices: 2.88 us -> 0.65 us  [body(): other = lax.ppermute(frame, 'shot', [(0, 1), (1, 0)])]
  transfers between devices with their start and end apart: 20 -> 20, of which waited for: 10 -> 8; matrix products, arithmetic and copies ran while one was open for 0% -> 0% of each run, Pallas kernels for 10% -> 24%
where the time goes in v2:
time: 110 us; the launch traced here: 109 us
  starting transfers between devices  41.5 us (38%)
  waiting for transfers between devices  36.7 us (33%)
  Pallas kernels  30.1 us (27%)
    ppermute x18, waiting for transfers between devices, swap_pairs(): return lax.ppermute(value, 'space', routes)  35.9 us
    ppermute x18, starting transfers between devices, swap_pairs(): return lax.ppermute(value, 'space', routes)  35.2 us
    pallas_call x9, Pallas kernels, one_step(): pl.pallas_call(functools.partial(step_kernel, shot, step, comps, got_grou...  21.9 us
    all_to_all x1, starting transfers between devices, deliver(): got = lax.all_to_all(message, 'space', 0, 0, tiled=False)  5.63 us
    pallas_call x2, Pallas kernels, pack_halo(): pl.pallas_call(functools.partial(pack_kernel, shot), in_specs=[pl.BlockSp...  3.48 us
    pallas_call x1, Pallas kernels, sum_frames(): pl.pallas_call(functools.partial(sum_kernel, scale), in_specs=[vmem, vmem...  2.33 us
  transfers between devices with their start and end apart: 20, of which 8 were waited for; matrix products, arithmetic and copies ran while one was open for 0% of the time, Pallas kernels for 24%

profile of v2, /device:TPU:19, one launch (start us, length us, event | category | flops | bytes accessed | tf_op | source)
XLA Modules:
  0.0 109.2 jit_solution(15062997559999471836)
XLA Ops:
  0.7 1.4 %pack_halo.2 = (bf16[2,2,128,256]{3,2,1,0:T(8,128)(2,1)S(1)}, bf16[2,2,128,256]{3,2,1,0:T(8,128)(2,1)S(1)}) custom-call(f32[2,2,2,4,128,256]{5,4,3,2,1,0:T(8,128)} %refs_1_.7), custom_call_target="tpu_custom_call" | custom-call | flops 1 | bytes 1 | tf_op jit(solution)/shard_map/pack_halo/pallas_call | solution.py:92
  2.1 3.1 %collective-permute-start.3 = (bf16[2,2,128,256]{3,2,1,0:T(8,128)(2,1)S(1)}, bf16[2,2,128,256]{3,2,1,0:T(8,128)(2,1)S(1)}, u32[]{:S(2)}, u32[]{:S(2)}) collective-permute-start(bf16[2,2,128,256]{3,2,1,0:T(8,128)(2,1)S(1)} %get-tuple-element.42), channel_id=1, source_target_pairs={{1,2},{2,1},{3,4},{4,3},{5,6},{6,5},{7,8},{8,7},{9,10},{10,9},{11,... | collective-permute-start | bytes 786440 | tf_op jit(solution)/shard_map/ppermute | solution.py:36
  5.2 1.2 %collective-permute-start.2 = (bf16[2,2,128,256]{3,2,1,0:T(8,128)(2,1)S(1)}, bf16[2,2,128,256]{3,2,1,0:T(8,128)(2,1)S(1)}, u32[]{:S(2)}, u32[]{:S(2)}) collective-permute-start(bf16[2,2,128,256]{3,2,1,0:T(8,128)(2,1)S(1)} %get-tuple-element.39.after_ref), channel_id=1, source_target_pairs={{0,1},{1,0},{2,3},{3,2},{4,5},{5,4},{6,7},{7,6},{8,9},{9,8},{10,11... | collective-permute-start | bytes 786440 | tf_op jit(solution)/shard_map/ppermute | solution.py:36
  6.4 1.0 pack_lines.1.refs_0_
  7.4 5.6 %all-to-all-start = ((bf16[16,16,384]{2,1,0:T(8,128)(2,1)}), bf16[16,16,384]{2,1,0:T(8,128)(2,1)}, u32[]{:S(2)}, u32[]{:S(2)}) async-start(bf16[16,16,384]{2,1,0:T(8,128)(2,1)} %bitcast), calls=%async_computation | async-start | bytes 393216 | tf_op jit(solution)/shard_map/all_to_all | solution.py:169
  13.0 2.1 %pack_halo.3 = (bf16[2,2,128,256]{3,2,1,0:T(8,128)(2,1)}, bf16[2,2,128,256]{3,2,1,0:T(8,128)(2,1)}) custom-call(f32[2,2,2,4,128,256]{5,4,3,2,1,0:T(8,128)} %refs_1_.7, bf16[256,384]{1,0:T(8,128)(2,1)} %pack_lines.1.refs_0_), custom_call_target="tpu_custom_call" | custom-call | flops 1 | bytes 1 | tf_op jit(solution)/shard_map/pack_halo/pallas_call | solution.py:92
  15.1 0.3 collective-permute-start
  15.5 4.0 %collective-permute-start.1 = (bf16[2,2,128,256]{3,2,1,0:T(8,128)(2,1)}, bf16[2,2,128,256]{3,2,1,0:T(8,128)(2,1)}, u32[]{:S(2)}, u32[]{:S(2)}) collective-permute-start(bf16[2,2,128,256]{3,2,1,0:T(8,128)(2,1)} %get-tuple-element.41), channel_id=1, source_target_pairs={{1,2},{2,1},{3,4},{4,3},{5,6},{6,5},{7,8},{8,7},{9,10},{10,9},{11,... | collective-permute-start | bytes 786440 | tf_op jit(solution)/shard_map/ppermute | solution.py:36
  19.5 0.6 collective-permute-done.2.refs_2_
  20.1 3.3 %step_0_shot_0.1 = (f32[2,4,128,256]{3,2,1,0:T(8,128)S(1)}, f32[4,128,256]{2,1,0:T(8,128)S(1)}, f32[4,128,256]{2,1,0:T(8,128)S(1)}) custom-call(f32[2,2,2,4,128,256]{5,4,3,2,1,0:T(8,128)} %refs_1_.7, f32[2,2,2,4,128,256]{5,4,3,2,1,0:T(8,128)} %refs_1_.7, bf16[2,2,128,256]{3,2,1,0:T(8,128)(2,1)S(1)} %collective-permute-done.2.refs_2_, ...), custom_call_target="tpu_custom_call" | custom-call | flops 9999999827968 | bytes 1 | tf_op jit(solution)/shard_map/step_0_shot_0/pallas_call | solution.py:415
  23.4 0.0 all-to-all-done
  23.4 1.2 %unpack_lines.1.saved_ref.refs_4_ = f32[128,256]{1,0:T(8,128)S(1)} custom-call(bf16[256,384]{1,0:T(8,128)(2,1)} %bitcast.1.got_ref), custom_call_target="tpu_custom_call" | custom-call | flops 1 | bytes 1 | tf_op jit(solution)/shard_map/unpack_lines/pallas_call | solution.py:170
  24.7 0.1 finish_first_0.1
  24.8 3.3 %collective-permute-start.7 = (bf16[2,2,128,256]{3,2,1,0:T(8,128)(2,1)S(1)}, bf16[2,2,128,256]{3,2,1,0:T(8,128)(2,1)S(1)}, u32[]{:S(2)}, u32[]{:S(2)}) collective-permute-start(bf16[2,2,128,256]{3,2,1,0:T(8,128)(2,1)S(1)} %get-tuple-element.51), channel_id=1, source_target_pairs={{1,2},{2,1},{3,4},{4,3},{5,6},{6,5},{7,8},{8,7},{9,10},{10,9},{11,... | collective-permute-start | bytes 786440 | tf_op jit(solution)/shard_map/ppermute | solution.py:36
  28.1 0.5 collective-permute-start.6
  28.5 9.0 %collective-permute-done.refs_2_ = bf16[2,2,128,256]{3,2,1,0:T(8,128)(2,1)} collective-permute-done((bf16[2,2,128,256]{3,2,1,0:T(8,128)(2,1)}, bf16[2,2,128,256]{3,2,1,0:T(8,128)(2,1)}, u32[]{:S(2)}, u32[]{:S(2)}) %collective-permute-start) | collective-permute-done | bytes 262176 | tf_op jit(solution)/shard_map/ppermute | solution.py:36
  37.6 0.0 collective-permute-done.1.refs_3_
  37.6 3.8 %step_0_shot_1.1 = (f32[2,4,128,256]{3,2,1,0:T(8,128)S(1)}, bf16[2,2,128,256]{3,2,1,0:T(8,128)(2,1)S(1)}, bf16[2,2,128,256]{3,2,1,0:T(8,128)(2,1)S(1)}, f32[4,128,256]{2,1,0:T(8,128)S(1)}, f32[4,128,256]{2,1,0:T(8,128)S(1)}) custom-call(f32[2,2,2,4,128,256]{5,4,3,2,1,0:T(8,128)} %refs_1_.7, f32[2,2,2,4,128,256]{5,4,3,2,1,0:T(8,128)} %refs_1_.7, ...), custom_call_target="tpu_custom_call" | custom-call | flops 1 | bytes 1 | tf_op jit(solution)/shard_map/step_0_shot_1/pallas_call | solution.py:415
  41.4 3.3 %collective-permute-start.5 = (bf16[2,2,128,256]{3,2,1,0:T(8,128)(2,1)S(1)}, bf16[2,2,128,256]{3,2,1,0:T(8,128)(2,1)S(1)}, u32[]{:S(2)}, u32[]{:S(2)}) collective-permute-start(bf16[2,2,128,256]{3,2,1,0:T(8,128)(2,1)S(1)} %get-tuple-element.47), channel_id=1, source_target_pairs={{1,2},{2,1},{3,4},{4,3},{5,6},{6,5},{7,8},{8,7},{9,10},{10,9},{11,... | collective-permute-start | bytes 786440 | tf_op jit(solution)/shard_map/ppermute | solution.py:36
  44.7 0.1 collective-permute-start.4
  44.8 0.0 collective-permute-done.7.refs_3_
  44.8 2.4 %step_1_shot_0.1 = (f32[2,4,128,256]{3,2,1,0:T(8,128)S(1)}, bf16[2,2,128,256]{3,2,1,0:T(8,128)(2,1)S(1)}, bf16[2,2,128,256]{3,2,1,0:T(8,128)(2,1)S(1)}, f32[4,128,256]{2,1,0:T(8,128)S(1)}) custom-call(f32[2,4,128,256]{3,2,1,0:T(8,128)S(1)} %get-tuple-element.50.refs_0_.refs_1_, f32[2,2,2,4,128,256]{5,4,3,2,1,0:T(8,128)} %refs_1_.7, ...), custom_call_target="tpu_custom_call" | custom-call | flops 1 | bytes 1 | tf_op jit(solution)/shard_map/step_1_shot_0/pallas_call | solution.py:415
  47.2 2.9 %collective-permute-start.11 = (bf16[2,2,128,256]{3,2,1,0:T(8,128)(2,1)S(1)}, bf16[2,2,128,256]{3,2,1,0:T(8,128)(2,1)S(1)}, u32[]{:S(2)}, u32[]{:S(2)}) collective-permute-start(bf16[2,2,128,256]{3,2,1,0:T(8,128)(2,1)S(1)} %get-tuple-element.60), channel_id=1, source_target_pairs={{1,2},{2,1},{3,4},{4,3},{5,6},{6,5},{7,8},{8,7},{9,10},{10,9},{11,... | collective-permute-start | bytes 786440 | tf_op jit(solution)/shard_map/ppermute | solution.py:36
  50.1 1.4 %collective-permute-start.10 = (bf16[2,2,128,256]{3,2,1,0:T(8,128)(2,1)S(1)}, bf16[2,2,128,256]{3,2,1,0:T(8,128)(2,1)S(1)}, u32[]{:S(2)}, u32[]{:S(2)}) collective-permute-start(bf16[2,2,128,256]{3,2,1,0:T(8,128)(2,1)S(1)} %get-tuple-element.54.refs_9_), channel_id=1, source_target_pairs={{0,1},{1,0},{2,3},{3,2},{4,5},{5,4},{6,7},{7,6},{8,9},{9,8},{10,11... | collective-permute-start | bytes 786440 | tf_op jit(solution)/shard_map/ppermute | solution.py:36
  51.5 11.3 %collective-permute-done.4.refs_2_ = bf16[2,2,128,256]{3,2,1,0:T(8,128)(2,1)S(1)} collective-permute-done((bf16[2,2,128,256]{3,2,1,0:T(8,128)(2,1)S(1)}, bf16[2,2,128,256]{3,2,1,0:T(8,128)(2,1)S(1)}, u32[]{:S(2)}, u32[]{:S(2)}) %collective-permute-start.4) | collective-permute-done | bytes 262176 | tf_op jit(solution)/shard_map/ppermute | solution.py:36
  62.9 2.5 %step_1_shot_1.1 = (f32[2,4,128,256]{3,2,1,0:T(8,128)S(1)}, bf16[2,2,128,256]{3,2,1,0:T(8,128)(2,1)S(1)}, bf16[2,2,128,256]{3,2,1,0:T(8,128)(2,1)S(1)}, f32[4,128,256]{2,1,0:T(8,128)S(1)}) custom-call(f32[2,4,128,256]{3,2,1,0:T(8,128)S(1)} %get-tuple-element.45.refs_0_.refs_1_, f32[2,2,2,4,128,256]{5,4,3,2,1,0:T(8,128)} %refs_1_.7, ...), custom_call_target="tpu_custom_call" | custom-call | flops 1 | bytes 1 | tf_op jit(solution)/shard_map/step_1_shot_1/pallas_call | solution.py:415
  65.3 2.9 %collective-permute-start.9 = (bf16[2,2,128,256]{3,2,1,0:T(8,128)(2,1)S(1)}, bf16[2,2,128,256]{3,2,1,0:T(8,128)(2,1)S(1)}, u32[]{:S(2)}, u32[]{:S(2)}) collective-permute-start(bf16[2,2,128,256]{3,2,1,0:T(8,128)(2,1)S(1)} %get-tuple-element.57), channel_id=1, source_target_pairs={{1,2},{2,1},{3,4},{4,3},{5,6},{6,5},{7,8},{8,7},{9,10},{10,9},{11,... | collective-permute-start | bytes 786440 | tf_op jit(solution)/shard_map/ppermute | solution.py:36
  68.2 0.1 collective-permute-start.8
  68.3 0.1 collective-permute-done.10.refs_2_
  68.5 1.2 %step_2_shot_0.1 = (f32[2,4,128,256]{3,2,1,0:T(8,128)S(1)}, bf16[2,2,128,256]{3,2,1,0:T(8,128)(2,1)S(1)}, bf16[2,2,128,256]{3,2,1,0:T(8,128)(2,1)S(1)}, f32[4,128,256]{2,1,0:T(8,128)S(1)}) custom-call(f32[2,4,128,256]{3,2,1,0:T(8,128)S(1)} %get-tuple-element.59.refs_0_.refs_1_, f32[2,4,128,256]{3,2,1,0:T(8,128)S(1)} %get-tuple-element.50.refs_0_.refs_1_, ...), custom_call_target="tpu_custom_call" | custom-call | flops 1 | bytes 1 | tf_op jit(solution)/shard_map/step_2_shot_0/pallas_call | solution.py:415
  69.7 3.2 %collective-permute-start.17 = (bf16[2,2,128,256]{3,2,1,0:T(8,128)(2,1)S(1)}, bf16[2,2,128,256]{3,2,1,0:T(8,128)(2,1)S(1)}, u32[]{:S(2)}, u32[]{:S(2)}) collective-permute-start(bf16[2,2,128,256]{3,2,1,0:T(8,128)(2,1)S(1)} %get-tuple-element.70), channel_id=1, source_target_pairs={{1,2},{2,1},{3,4},{4,3},{5,6},{6,5},{7,8},{8,7},{9,10},{10,9},{11,... | collective-permute-start | bytes 786440 | tf_op jit(solution)/shard_map/ppermute | solution.py:36
  72.9 1.4 %collective-permute-start.16 = (bf16[2,2,128,256]{3,2,1,0:T(8,128)(2,1)S(1)}, bf16[2,2,128,256]{3,2,1,0:T(8,128)(2,1)S(1)}, u32[]{:S(2)}, u32[]{:S(2)}) collective-permute-start(bf16[2,2,128,256]{3,2,1,0:T(8,128)(2,1)S(1)} %get-tuple-element.62.refs_9_), channel_id=1, source_target_pairs={{0,1},{1,0},{2,3},{3,2},{4,5},{5,4},{6,7},{7,6},{8,9},{9,8},{10,11... | collective-permute-start | bytes 786440 | tf_op jit(solution)/shard_map/ppermute | solution.py:36
  74.3 1.1 %collective-permute-done.9.refs_3_ = bf16[2,2,128,256]{3,2,1,0:T(8,128)(2,1)S(1)} collective-permute-done((bf16[2,2,128,256]{3,2,1,0:T(8,128)(2,1)S(1)}, bf16[2,2,128,256]{3,2,1,0:T(8,128)(2,1)S(1)}, u32[]{:S(2)}, u32[]{:S(2)}) %collective-permute-start.9) | collective-permute-done | bytes 262176 | tf_op jit(solution)/shard_map/ppermute | solution.py:36
  75.4 11.0 %collective-permute-done.8.refs_2_ = bf16[2,2,128,256]{3,2,1,0:T(8,128)(2,1)S(1)} collective-permute-done((bf16[2,2,128,256]{3,2,1,0:T(8,128)(2,1)S(1)}, bf16[2,2,128,256]{3,2,1,0:T(8,128)(2,1)S(1)}, u32[]{:S(2)}, u32[]{:S(2)}) %collective-permute-start.8) | collective-permute-done | bytes 262176 | tf_op jit(solution)/shard_map/ppermute | solution.py:36
  86.4 1.2 %step_2_shot_1.1 = (f32[2,4,128,256]{3,2,1,0:T(8,128)S(1)}, bf16[1,2,128,256]{3,2,1,0:T(8,128)(2,1)S(1)}, bf16[1,2,128,256]{3,2,1,0:T(8,128)(2,1)S(1)}, bf16[1,2...) custom-call(f32[2,4,128,256]{3,2,1,0:T(8,128)S(1)} %get-tuple-element.55.refs_0_.refs_, ...), custom_call_target="tpu_custom_call" | custom-call | flops 1 | bytes 1 | tf_op jit(solution)/shard_map/step_2_shot_1/pallas_call | solution.py:415
  87.6 3.3 %collective-permute-start.15 = (bf16[1,2,128,256]{3,2,1,0:T(8,128)(2,1)S(1)}, bf16[1,2,128,256]{3,2,1,0:T(8,128)(2,1)S(1)}, u32[]{:S(2)}, u32[]{:S(2)}) collective-permute-start(bf16[1,2,128,256]{3,2,1,0:T(8,128)(2,1)S(1)} %get-tuple-element.67), channel_id=1, source_target_pairs={{1,2},{2,1},{3,4},{4,3},{5,6},{6,5},{7,8},{8,7},{9,10},{10,9},{11,... | collective-permute-start | bytes 393224 | tf_op jit(solution)/shard_map/ppermute | solution.py:36
  90.9 0.1 collective-permute-start.14
  91.0 1.5 %collective-permute-start.12 = (bf16[1,2,128,256]{3,2,1,0:T(8,128)(2,1)S(1)}, bf16[1,2,128,256]{3,2,1,0:T(8,128)(2,1)S(1)}, u32[]{:S(2)}, u32[]{:S(2)}) collective-permute-start(bf16[1,2,128,256]{3,2,1,0:T(8,128)(2,1)S(1)} %get-tuple-element.64), channel_id=1, source_target_pairs={{0,1},{1,0},{2,3},{3,2},{4,5},{5,4},{6,7},{7,6},{8,9},{9,8},{10,11... | collective-permute-start | bytes 393224 | tf_op jit(solution)/shard_map/ppermute | solution.py:36
  92.4 0.0 collective-permute-done.17.refs_3_
  92.4 2.9 %collective-permute-start.13 = (bf16[1,2,128,256]{3,2,1,0:T(8,128)(2,1)S(1)}, bf16[1,2,128,256]{3,2,1,0:T(8,128)(2,1)S(1)}, u32[]{:S(2)}, u32[]{:S(2)}) collective-permute-start(bf16[1,2,128,256]{3,2,1,0:T(8,128)(2,1)S(1)} %get-tuple-element.65), channel_id=1, source_target_pairs={{1,2},{2,1},{3,4},{4,3},{5,6},{6,5},{7,8},{8,7},{9,10},{10,9},{11,... | collective-permute-start | bytes 393224 | tf_op jit(solution)/shard_map/ppermute | solution.py:36
  95.4 2.7 %step_3_shot_0.1 = (f32[2,2,2,4,128,256]{5,4,3,2,1,0:T(8,128)}, f32[4,192,256]{2,1,0:T(8,128)S(1)}) custom-call(f32[2,4,128,256]{3,2,1,0:T(8,128)S(1)} %get-tuple-element.69.refs_0_, f32[2,4,128,256]{3,2,1,0:T(8,128)S(1)} %get-tuple-element.59.refs_0_.refs_1_, bf16[2,2,128,256]{3,2,1,0:T(8,128)(2,1)S(1)} %collective-permute-done.16.refs_2_, ...), custom_call_target="tpu_custom_call" | custom-call | flops 1 | bytes 1 | tf_op jit(solution)/shard_map/step_3_shot_0/pallas_call | solution.py:415
  98.0 0.0 collective-permute-done.15.refs_3_
  98.1 2.6 %collective-permute-done.14.refs_2_ = bf16[1,2,128,256]{3,2,1,0:T(8,128)(2,1)S(1)} collective-permute-done((bf16[1,2,128,256]{3,2,1,0:T(8,128)(2,1)S(1)}, bf16[1,2,128,256]{3,2,1,0:T(8,128)(2,1)S(1)}, u32[]{:S(2)}, u32[]{:S(2)}) %collective-permute-start.14) | collective-permute-done | bytes 131104 | tf_op jit(solution)/shard_map/ppermute | solution.py:36
  100.6 3.4 %step_3_shot_1.2 = (f32[2,2,2,4,128,256]{5,4,3,2,1,0:T(8,128)}, f32[4,192,256]{2,1,0:T(8,128)}) custom-call(f32[2,4,128,256]{3,2,1,0:T(8,128)S(1)} %get-tuple-element.63.refs_0_, f32[2,4,128,256]{3,2,1,0:T(8,128)S(1)} %get-tuple-element.55.refs_0_.refs_1_, ...), custom_call_target="tpu_custom_call", output_to_operand_aliasing={{0}: (11, {})} | custom-call | flops 1 | bytes 1 | tf_op jit(solution)/shard_map/step_3_shot_1/pallas_call | solution.py:415
  104.0 0.7 collective-permute-start.18
  104.7 1.4 %step_3_shot_1.3.refs_0_ = f32[2,2,2,4,128,256]{5,4,3,2,1,0:T(8,128)} custom-call(f32[2,4,128,256]{3,2,1,0:T(8,128)S(1)} %get-tuple-element.63.refs_0_, f32[2,4,128,256]{3,2,1,0:T(8,128)S(1)} %get-tuple-element.55.refs_0_.refs_1_, bf16[1,2,128,256]{3,2,1,0:T(8,128)(2,1)S(1)} %collective-permute-done.12.refs_2_, ...), custom_call_target="tpu_custom_call", output_to_operand_aliasing={{}: (7, {})} | custom-call | flops 9999999827968 | bytes 1 | tf_op jit(solution)/shard_map/step_3_shot_1/pallas_call | solution.py:415
  106.1 0.8 collective-permute-done.18.other_ref
  106.9 2.3 %sum_frames.1 = f32[4,192,256]{2,1,0:T(8,128)} custom-call(f32[4,192,256]{2,1,0:T(8,128)} %get-tuple-element.74.refs_6_.own_ref, f32[4,192,256]{2,1,0:T(8,128)} %collective-permute-done.18.other_ref, f32[2,2,2,4,128,256]{5,4,3,2,1,0:T(8,128)} %step_3_shot_1.3.refs_0_), custom_call_target="tpu_custom_call" | custom-call | flops 1 | bytes 1 | tf_op jit(solution)/shard_map/sum_frames/pallas_call | solution.py:436
  (19 shorter events, 0.0 us)
Async XLA Ops:
  0.6 5.8 %copy-start.5 = (s32[2,128]{1,0:T(2,128)S(1)}, s32[2,128]{1,0:T(2,128)}, u32[]{:S(2)}) copy-start(s32[2,128]{1,0:T(2,128)} %ids_ref.1) | copy-start | bytes 3076
  0.6 5.7 %copy-start.2 = (bf16[2,128,256]{2,1,0:T(8,128)(2,1)S(1)}, bf16[2,128,256]{2,1,0:T(8,128)(2,1)}, u32[]{:S(2)}) copy-start(bf16[2,128,256]{2,1,0:T(8,128)(2,1)} %lines_ref.1) | copy-start | bytes 393220
  0.7 19.4 %copy-start.1 = (f32[2,4,64]{2,1,0:T(4,128)S(1)}, f32[2,4,64]{2,1,0:T(4,128)}, u32[]{:S(2)}) copy-start(f32[2,4,64]{2,1,0:T(4,128)} %refs_5_.15) | copy-start | bytes 6148
  0.7 19.4 %copy-start.3 = (s32[2,64]{1,0:T(2,128)S(1)}, s32[2,64]{1,0:T(2,128)}, u32[]{:S(2)}) copy-start(s32[2,64]{1,0:T(2,128)} %refs_4_.3) | copy-start | bytes 1540
  0.7 19.4 %copy-start.4 = (s32[2]{0:T(128)S(1)}, s32[2]{0:T(128)}, u32[]{:S(2)}) copy-start(s32[2]{0:T(128)} %refs_6_.15) | copy-start | bytes 28
  0.7 19.4 %copy-start = (f32[4,192,256]{2,1,0:T(8,128)S(1)}, f32[4,192,256]{2,1,0:T(8,128)}, u32[]{:S(2)}) copy-start(f32[4,192,256]{2,1,0:T(8,128)} %refs_8_.1) | copy-start | bytes 2359300
  2.1 17.4 %collective-permute-start.3 = (bf16[2,2,128,256]{3,2,1,0:T(8,128)(2,1)S(1)}, bf16[2,2,128,256]{3,2,1,0:T(8,128)(2,1)S(1)}, u32[]{:S(2)}, u32[]{:S(2)}) collective-permute-start(bf16[2,2,128,256]{3,2,1,0:T(8,128)(2,1)S(1)} %get-tuple-element.42), channel_id=1, source_target_pairs={{1,2},{2,1},{3,4},{4,3},{5,6},{6,5},{7,8},{8,7},{9,10},{10,9},{11,... | collective-permute-start | bytes 786440 | tf_op jit(solution)/shard_map/ppermute | solution.py:36
  5.2 14.9 %collective-permute-start.2 = (bf16[2,2,128,256]{3,2,1,0:T(8,128)(2,1)S(1)}, bf16[2,2,128,256]{3,2,1,0:T(8,128)(2,1)S(1)}, u32[]{:S(2)}, u32[]{:S(2)}) collective-permute-start(bf16[2,2,128,256]{3,2,1,0:T(8,128)(2,1)S(1)} %get-tuple-element.39.after_ref), channel_id=1, source_target_pairs={{0,1},{1,0},{2,3},{3,2},{4,5},{5,4},{6,7},{7,6},{8,9},{9,8},{10,11... | collective-permute-start | bytes 786440 | tf_op jit(solution)/shard_map/ppermute | solution.py:36
  7.4 16.0 %all-to-all-start = ((bf16[16,16,384]{2,1,0:T(8,128)(2,1)}), bf16[16,16,384]{2,1,0:T(8,128)(2,1)}, u32[]{:S(2)}, u32[]{:S(2)}) async-start(bf16[16,16,384]{2,1,0:T(8,128)(2,1)} %bitcast), calls=%async_computation | async-start | bytes 393216 | tf_op jit(solution)/shard_map/all_to_all | solution.py:169
  15.1 22.5 %collective-permute-start = (bf16[2,2,128,256]{3,2,1,0:T(8,128)(2,1)}, bf16[2,2,128,256]{3,2,1,0:T(8,128)(2,1)}, u32[]{:S(2)}, u32[]{:S(2)}) collective-permute-start(bf16[2,2,128,256]{3,2,1,0:T(8,128)(2,1)} %get-tuple-element.40), channel_id=1, source_target_pairs={{0,1},{1,0},{2,3},{3,2},{4,5},{5,4},{6,7},{7,6},{8,9},{9,8},{10,11... | collective-permute-start | bytes 786440 | tf_op jit(solution)/shard_map/ppermute | solution.py:36
  15.5 22.1 %collective-permute-start.1 = (bf16[2,2,128,256]{3,2,1,0:T(8,128)(2,1)}, bf16[2,2,128,256]{3,2,1,0:T(8,128)(2,1)}, u32[]{:S(2)}, u32[]{:S(2)}) collective-permute-start(bf16[2,2,128,256]{3,2,1,0:T(8,128)(2,1)} %get-tuple-element.41), channel_id=1, source_target_pairs={{1,2},{2,1},{3,4},{4,3},{5,6},{6,5},{7,8},{8,7},{9,10},{10,9},{11,... | collective-permute-start | bytes 786440 | tf_op jit(solution)/shard_map/ppermute | solution.py:36
  24.8 20.0 %collective-permute-start.7 = (bf16[2,2,128,256]{3,2,1,0:T(8,128)(2,1)S(1)}, bf16[2,2,128,256]{3,2,1,0:T(8,128)(2,1)S(1)}, u32[]{:S(2)}, u32[]{:S(2)}) collective-permute-start(bf16[2,2,128,256]{3,2,1,0:T(8,128)(2,1)S(1)} %get-tuple-element.51), channel_id=1, source_target_pairs={{1,2},{2,1},{3,4},{4,3},{5,6},{6,5},{7,8},{8,7},{9,10},{10,9},{11,... | collective-permute-start | bytes 786440 | tf_op jit(solution)/shard_map/ppermute | solution.py:36
  28.1 16.7 %collective-permute-start.6 = (bf16[2,2,128,256]{3,2,1,0:T(8,128)(2,1)S(1)}, bf16[2,2,128,256]{3,2,1,0:T(8,128)(2,1)S(1)}, u32[]{:S(2)}, u32[]{:S(2)}) collective-permute-start(bf16[2,2,128,256]{3,2,1,0:T(8,128)(2,1)S(1)} %get-tuple-element.44.refs_9_), channel_id=1, source_target_pairs={{0,1},{1,0},{2,3},{3,2},{4,5},{5,4},{6,7},{7,6},{8,9},{9,8},{10,11... | collective-permute-start | bytes 786440 | tf_op jit(solution)/shard_map/ppermute | solution.py:36
  41.4 10.1 %collective-permute-start.5 = (bf16[2,2,128,256]{3,2,1,0:T(8,128)(2,1)S(1)}, bf16[2,2,128,256]{3,2,1,0:T(8,128)(2,1)S(1)}, u32[]{:S(2)}, u32[]{:S(2)}) collective-permute-start(bf16[2,2,128,256]{3,2,1,0:T(8,128)(2,1)S(1)} %get-tuple-element.47), channel_id=1, source_target_pairs={{1,2},{2,1},{3,4},{4,3},{5,6},{6,5},{7,8},{8,7},{9,10},{10,9},{11,... | collective-permute-start | bytes 786440 | tf_op jit(solution)/shard_map/ppermute | solution.py:36
  44.7 18.1 %collective-permute-start.4 = (bf16[2,2,128,256]{3,2,1,0:T(8,128)(2,1)S(1)}, bf16[2,2,128,256]{3,2,1,0:T(8,128)(2,1)S(1)}, u32[]{:S(2)}, u32[]{:S(2)}) collective-permute-start(bf16[2,2,128,256]{3,2,1,0:T(8,128)(2,1)S(1)} %get-tuple-element.46.refs_9_), channel_id=1, source_target_pairs={{0,1},{1,0},{2,3},{3,2},{4,5},{5,4},{6,7},{7,6},{8,9},{9,8},{10,11... | collective-permute-start | bytes 786440 | tf_op jit(solution)/shard_map/ppermute | solution.py:36
  47.2 21.1 %collective-permute-start.11 = (bf16[2,2,128,256]{3,2,1,0:T(8,128)(2,1)S(1)}, bf16[2,2,128,256]{3,2,1,0:T(8,128)(2,1)S(1)}, u32[]{:S(2)}, u32[]{:S(2)}) collective-permute-start(bf16[2,2,128,256]{3,2,1,0:T(8,128)(2,1)S(1)} %get-tuple-element.60), channel_id=1, source_target_pairs={{1,2},{2,1},{3,4},{4,3},{5,6},{6,5},{7,8},{8,7},{9,10},{10,9},{11,... | collective-permute-start | bytes 786440 | tf_op jit(solution)/shard_map/ppermute | solution.py:36
  50.1 18.4 %collective-permute-start.10 = (bf16[2,2,128,256]{3,2,1,0:T(8,128)(2,1)S(1)}, bf16[2,2,128,256]{3,2,1,0:T(8,128)(2,1)S(1)}, u32[]{:S(2)}, u32[]{:S(2)}) collective-permute-start(bf16[2,2,128,256]{3,2,1,0:T(8,128)(2,1)S(1)} %get-tuple-element.54.refs_9_), channel_id=1, source_target_pairs={{0,1},{1,0},{2,3},{3,2},{4,5},{5,4},{6,7},{7,6},{8,9},{9,8},{10,11... | collective-permute-start | bytes 786440 | tf_op jit(solution)/shard_map/ppermute | solution.py:36
  65.3 10.1 %collective-permute-start.9 = (bf16[2,2,128,256]{3,2,1,0:T(8,128)(2,1)S(1)}, bf16[2,2,128,256]{3,2,1,0:T(8,128)(2,1)S(1)}, u32[]{:S(2)}, u32[]{:S(2)}) collective-permute-start(bf16[2,2,128,256]{3,2,1,0:T(8,128)(2,1)S(1)} %get-tuple-element.57), channel_id=1, source_target_pairs={{1,2},{2,1},{3,4},{4,3},{5,6},{6,5},{7,8},{8,7},{9,10},{10,9},{11,... | collective-permute-start | bytes 786440 | tf_op jit(solution)/shard_map/ppermute | solution.py:36
  68.2 18.1 %collective-permute-start.8 = (bf16[2,2,128,256]{3,2,1,0:T(8,128)(2,1)S(1)}, bf16[2,2,128,256]{3,2,1,0:T(8,128)(2,1)S(1)}, u32[]{:S(2)}, u32[]{:S(2)}) collective-permute-start(bf16[2,2,128,256]{3,2,1,0:T(8,128)(2,1)S(1)} %get-tuple-element.56.refs_9_), channel_id=1, source_target_pairs={{0,1},{1,0},{2,3},{3,2},{4,5},{5,4},{6,7},{7,6},{8,9},{9,8},{10,11... | collective-permute-start | bytes 786440 | tf_op jit(solution)/shard_map/ppermute | solution.py:36
  69.7 22.7 %collective-permute-start.17 = (bf16[2,2,128,256]{3,2,1,0:T(8,128)(2,1)S(1)}, bf16[2,2,128,256]{3,2,1,0:T(8,128)(2,1)S(1)}, u32[]{:S(2)}, u32[]{:S(2)}) collective-permute-start(bf16[2,2,128,256]{3,2,1,0:T(8,128)(2,1)S(1)} %get-tuple-element.70), channel_id=1, source_target_pairs={{1,2},{2,1},{3,4},{4,3},{5,6},{6,5},{7,8},{8,7},{9,10},{10,9},{11,... | collective-permute-start | bytes 786440 | tf_op jit(solution)/shard_map/ppermute | solution.py:36
  72.9 22.5 %collective-permute-start.16 = (bf16[2,2,128,256]{3,2,1,0:T(8,128)(2,1)S(1)}, bf16[2,2,128,256]{3,2,1,0:T(8,128)(2,1)S(1)}, u32[]{:S(2)}, u32[]{:S(2)}) collective-permute-start(bf16[2,2,128,256]{3,2,1,0:T(8,128)(2,1)S(1)} %get-tuple-element.62.refs_9_), channel_id=1, source_target_pairs={{0,1},{1,0},{2,3},{3,2},{4,5},{5,4},{6,7},{7,6},{8,9},{9,8},{10,11... | collective-permute-start | bytes 786440 | tf_op jit(solution)/shard_map/ppermute | solution.py:36
  87.6 10.4 %collective-permute-start.15 = (bf16[1,2,128,256]{3,2,1,0:T(8,128)(2,1)S(1)}, bf16[1,2,128,256]{3,2,1,0:T(8,128)(2,1)S(1)}, u32[]{:S(2)}, u32[]{:S(2)}) collective-permute-start(bf16[1,2,128,256]{3,2,1,0:T(8,128)(2,1)S(1)} %get-tuple-element.67), channel_id=1, source_target_pairs={{1,2},{2,1},{3,4},{4,3},{5,6},{6,5},{7,8},{8,7},{9,10},{10,9},{11,... | collective-permute-start | bytes 393224 | tf_op jit(solution)/shard_map/ppermute | solution.py:36
  90.9 9.7 %collective-permute-start.14 = (bf16[1,2,128,256]{3,2,1,0:T(8,128)(2,1)S(1)}, bf16[1,2,128,256]{3,2,1,0:T(8,128)(2,1)S(1)}, u32[]{:S(2)}, u32[]{:S(2)}) collective-permute-start(bf16[1,2,128,256]{3,2,1,0:T(8,128)(2,1)S(1)} %get-tuple-element.66.refs_10_), channel_id=1, source_target_pairs={{0,1},{1,0},{2,3},{3,2},{4,5},{5,4},{6,7},{7,6},{8,9},{9,8},{10,11... | collective-permute-start | bytes 393224 | tf_op jit(solution)/shard_map/ppermute | solution.py:36
  91.0 13.7 %collective-permute-start.12 = (bf16[1,2,128,256]{3,2,1,0:T(8,128)(2,1)S(1)}, bf16[1,2,128,256]{3,2,1,0:T(8,128)(2,1)S(1)}, u32[]{:S(2)}, u32[]{:S(2)}) collective-permute-start(bf16[1,2,128,256]{3,2,1,0:T(8,128)(2,1)S(1)} %get-tuple-element.64), channel_id=1, source_target_pairs={{0,1},{1,0},{2,3},{3,2},{4,5},{5,4},{6,7},{7,6},{8,9},{9,8},{10,11... | collective-permute-start | bytes 393224 | tf_op jit(solution)/shard_map/ppermute | solution.py:36
  92.4 12.2 %collective-permute-start.13 = (bf16[1,2,128,256]{3,2,1,0:T(8,128)(2,1)S(1)}, bf16[1,2,128,256]{3,2,1,0:T(8,128)(2,1)S(1)}, u32[]{:S(2)}, u32[]{:S(2)}) collective-permute-start(bf16[1,2,128,256]{3,2,1,0:T(8,128)(2,1)S(1)} %get-tuple-element.65), channel_id=1, source_target_pairs={{1,2},{2,1},{3,4},{4,3},{5,6},{6,5},{7,8},{8,7},{9,10},{10,9},{11,... | collective-permute-start | bytes 393224 | tf_op jit(solution)/shard_map/ppermute | solution.py:36
  104.0 2.9 %collective-permute-start.18 = (f32[4,192,256]{2,1,0:T(8,128)}, f32[4,192,256]{2,1,0:T(8,128)}, u32[]{:S(2)}, u32[]{:S(2)}) collective-permute-start(f32[4,192,256]{2,1,0:T(8,128)} %get-tuple-element.74.refs_6_.own_ref), channel_id=1, source_target_pairs={{0,16},{16,0},{1,17},{17,1},{2,18},{18,2},{3,19},{19,3},{4,20},{20... | collective-permute-start | bytes 2359304 | tf_op jit(solution)/shard_map/ppermute | solution.py:511

commit v3 on v2

--- a/solution.py
+++ b/solution.py
@@ -79,11 +79,17 @@
 
 
 def pack_kernel(shot, field_ref, *refs):
-    send0_ref, send1_ref, own_ref, sem = refs[-4:]
-    load = pltpu.make_async_copy(field_ref.at[shot, 0], own_ref, sem)
-    load.start()
-    load.wait()
-    write_sends(own_ref, BOTH, (send0_ref, send1_ref))
+    send0_ref, send1_ref, own_ref, sems = refs[-4:]
+    comps = own_ref.shape[0]
+    loads = [
+        pltpu.make_async_copy(field_ref.at[shot, 0, comp], own_ref.at[comp], sems.at[comp])
+        for comp in range(comps)
+    ]
+    for load in loads:
+        load.start()
+    for comp, load in enumerate(loads):
+        load.wait()
+        write_sends(own_ref, ((comp,),), (send0_ref.at[comp : comp + 1], send1_ref.at[comp : comp + 1]))
 
 
 def pack_halo(wavefields, shot, after):
@@ -96,7 +102,7 @@
         out_shape=[half, half],
         scratch_shapes=[
             pltpu.VMEM((comps, layers, rows_y, cells_z), jnp.float32),
-            pltpu.SemaphoreType.DMA,
+            pltpu.SemaphoreType.DMA((comps,)),
         ],
         compiler_params=params(),
         cost_estimate=cost(),
@@ -215,7 +221,7 @@
     )(new, saved)
 
 
-def step_kernel(shot, step, comps, got_groups, send_groups, create, lines, waits, *refs):
+def step_kernel(shot, step, comps, got_groups, send_groups, create, framed, lines, waits, keeps, *refs):
     refs = list(refs)
 
     def take(count):
@@ -236,9 +242,14 @@
     [offsets_ref] = take(1) if first or framing else [None]
     [speed_from] = take(1)
     [contrib_from] = take(1) if with_image and not first else [None]
-    [frame_from] = take(1) if framing and not create else [None]
+    [frame_from] = take(1) if framing and framed else [None]
+    keep_refs = take(len(keeps))
+    held = last and comps == (1,)
+    [field_from] = take(1) if last and comps == (0,) else [None]
     take(waits)
-    if last:
+    if held:
+        [field_ref] = take(1)
+    elif last:
         take(0 if create else 1)
         [out_ref] = take(1)
     else:
@@ -246,7 +257,7 @@
         send_refs = take(2 * len(send_groups))
     [contrib_ref] = take(1) if with_image else [None]
     [speed_out] = take(1) if first else [None]
-    if last:
+    if last and not held:
         new_ref, out_sems = take(2)
     loads = []
     if first:
@@ -259,11 +270,17 @@
         later_ref = state_ref
     for load in loads:
         load.start()
-    layers, rows_y, cells_z = new_ref.shape[-3:]
+    layers, rows_y, cells_z = (field_ref if held else new_ref).shape[-3:]
     stores = []
-    if last and with_image:
-        stores.append(pltpu.make_async_copy(now_ref, out_ref.at[shot, 1], out_sems.at[0]))
-        stores[0].start()
+
+    def store(source_ref, target_ref):
+        stores.append(pltpu.make_async_copy(source_ref, target_ref, out_sems.at[len(stores)]))
+        stores[-1].start()
+
+    for keep, keep_ref in zip(keeps, keep_refs):
+        store(keep_ref, out_ref.at[keep, 1])
+    if field_from is not None:
+        store(field_from, out_ref.at[shot, 0, 1])
     odd = is_odd()
     across_z = band(cells_z, -90.0)
     across_y = band(rows_y, 0.0)
@@ -317,13 +334,17 @@
                     [growth[:, :LANES] + plane, growth[:, LANES:]], axis=1
                 )
             change = speed * growth
-            new_ref[comp, layer] = 2.0 * here - later_ref[comp, layer] + change
+            moved = 2.0 * here - later_ref[comp, layer] + change
+            if held:
+                field_ref[layer] = moved
+            else:
+                new_ref[comp, layer] = moved
             if comp == 1:
                 term = now_ref[0, layer] * change
                 if not first:
                     term = contrib_from[layer] + term
                 if framing:
-                    if create:
+                    if not framed:
                         contrib_ref[layer] = jnp.zeros_like(contrib_ref[layer])
                     else:
                         contrib_ref[layer] = frame_from[layer]
@@ -332,22 +353,17 @@
                     contrib_ref[layer] = term
             elif lines:
                 take_lines(new_ref, saved_ref, shot, step, layer)
-        if last:
-            stores.append(
-                pltpu.make_async_copy(
-                    new_ref.at[comp], out_ref.at[shot, 0, comp], out_sems.at[1 + comp]
-                )
-            )
-            stores[-1].start()
-    for store in stores:
-        store.wait()
+            if last and not held:
+                store(new_ref.at[comp, layer], out_ref.at[shot, 0, comp, layer])
+    for started in stores:
+        started.wait()
     if not last:
         write_sends(new_ref, send_groups, send_refs)
 
 
 def one_step(
     shot, step, comps, got_groups, send_groups,
-    wavefields, offsets, now, later, got, saved, pos, traces, speed, contrib, frame, out, after, heavy, model_y,
+    wavefields, offsets, now, later, got, saved, pos, traces, speed, contrib, frame, out, after, heavy, model_y, keeps=(), field=None,
 ):
     first, last = step == 0, step == STEPS - 1
     with_image = 1 in comps
@@ -381,19 +397,31 @@
     if with_image and not first:
         args.append(contrib)
         specs.append(vmem)
-    if framing and out is not None:
+    if framing and frame is not None:
         args.append(frame)
+        specs.append(vmem)
+    args += [value for _, value in keeps]
+    specs += [vmem] * len(keeps)
+    held = last and comps == (1,)
+    if last and comps == (0,):
+        args.append(field)
         specs.append(vmem)
     args += after
     specs += [pl.BlockSpec(memory_space=pl.ANY)] * len(after)
-    if last:
+    if held:
+        outs = [image]
+        out_specs = [vmem]
+    elif last:
         if out is not None:
             aliases[len(args)] = 0
             args.append(out)
             specs.append(hbm)
         outs = [jax.ShapeDtypeStruct((shots, 2) + state.shape, jnp.float32)]
         out_specs = [hbm]
-        scratch = [pltpu.VMEM(state.shape, jnp.float32), pltpu.SemaphoreType.DMA((3,))]
+        scratch = [
+            pltpu.VMEM(state.shape, jnp.float32),
+            pltpu.SemaphoreType.DMA((1 + len(keeps) + both * layers,)),
+        ]
     else:
         outs = [state]
         for group in send_groups:
@@ -414,7 +442,8 @@
         scratch = [pltpu.VMEM(lead + state.shape, jnp.float32), pltpu.SemaphoreType.DMA((1,))]
     return pl.pallas_call(
         functools.partial(
-            step_kernel, shot, step, comps, got_groups, send_groups, out is None, lines, len(after)
+            step_kernel, shot, step, comps, got_groups, send_groups, out is None, frame is not None,
+            lines, len(after), tuple(keep for keep, _ in keeps),
         ),
         in_specs=specs,
         out_specs=out_specs,
@@ -432,11 +461,13 @@
 
 
 def sum_frames(own, other, scale, after):
-    vmem, hbm = pl.BlockSpec(memory_space=VMEM), pl.BlockSpec(memory_space=HBM)
+    layers, model_y, cells_z = own.shape
+    block = pl.BlockSpec((1, model_y, cells_z), lambda i: (i, 0, 0))
     return pl.pallas_call(
         functools.partial(sum_kernel, scale),
-        in_specs=[vmem, vmem, hbm],
-        out_specs=vmem,
+        grid=(layers,),
+        in_specs=[block, block, pl.BlockSpec(memory_space=HBM)],
+        out_specs=block,
         out_shape=jax.ShapeDtypeStruct(own.shape, jnp.float32),
         compiler_params=params(),
         cost_estimate=cost(),
@@ -498,12 +529,21 @@
                     speed[shot] = made[ends + 1]
                 after = [made[1]]
                 continue
-            for part, group in enumerate(groups[shot]):
+            keeps = [] if split and shots > 1 else [(shot, now[shot])]
+            if shot == 0 and shots > 1:
+                keeps.append((shots - 1, now[shots - 1]))
+            field = None
+            for group in groups[shot]:
                 made = one_step(
-                    shot, step, group, (group,), (), *common, got[shot][part : part + 1], saved,
-                    *fixed, contrib[shot], frame, out, after, part > 0, model_y,
+                    shot, step, group, (group,), (), *common, got[shot][:1], saved, *fixed,
+                    contrib[shot], frame, out, after, group == (0,), model_y,
+                    () if group == (1,) else keeps, field,
                 )
-                out = made[0]
+                got[shot] = got[shot][1:]
+                if group == (1,):
+                    field = made[0]
+                else:
+                    out = made[0]
                 if 1 in group:
                     frame = made[1]
                     after = [frame]

time: 110 us -> 110 us (level)
    pallas_call x9, Pallas kernels: 21.9 us -> 20.7 us  [one_step(): pl.pallas_call(functools.partial(step_kernel, shot, step, comps, got_grou...]
    pallas_call x1, Pallas kernels: 2.33 us -> 3.48 us  [sum_frames(): pl.pallas_call(functools.partial(sum_kernel, scale), grid=(layers,), in_s...]
  transfers between devices with their start and end apart: 20 -> 20, of which waited for: 8 -> 9; matrix products, arithmetic and copies ran while one was open for 0% -> 0% of each run, Pallas kernels for 24% -> 23%
where the time goes in v3:
time: 110 us; the launch traced here: 109 us
  starting transfers between devices  41.4 us (38%)
  waiting for transfers between devices  36.9 us (34%)
  Pallas kernels  29.9 us (27%)
    ppermute x18, waiting for transfers between devices, swap_pairs(): return lax.ppermute(value, 'space', routes)  36.2 us
    ppermute x18, starting transfers between devices, swap_pairs(): return lax.ppermute(value, 'space', routes)  35.1 us
    pallas_call x9, Pallas kernels, one_step(): pl.pallas_call(functools.partial(step_kernel, shot, step, comps, got_grou...  20.7 us
    all_to_all x1, starting transfers between devices, deliver(): got = lax.all_to_all(message, 'space', 0, 0, tiled=False)  5.63 us
    pallas_call x1, Pallas kernels, sum_frames(): pl.pallas_call(functools.partial(sum_kernel, scale), grid=(layers,), in_s...  3.48 us
    pallas_call x2, Pallas kernels, pack_halo(): pl.pallas_call(functools.partial(pack_kernel, shot), in_specs=[pl.BlockSp...  3.37 us
  transfers between devices with their start and end apart: 20, of which 9 were waited for; matrix products, arithmetic and copies ran while one was open for 0% of the time, Pallas kernels for 23%

profile of v3, /device:TPU:19, one launch (start us, length us, event | category | flops | bytes accessed | tf_op | source)
XLA Modules:
  0.0 109.2 jit_solution(3241392595731000614)
XLA Ops:
  0.7 1.3 %pack_halo.2 = (bf16[2,2,128,256]{3,2,1,0:T(8,128)(2,1)S(1)}, bf16[2,2,128,256]{3,2,1,0:T(8,128)(2,1)S(1)}) custom-call(f32[2,2,2,4,128,256]{5,4,3,2,1,0:T(8,128)} %refs_1_.7), custom_call_target="tpu_custom_call" | custom-call | flops 1 | bytes 1 | tf_op jit(solution)/shard_map/pack_halo/pallas_call | solution.py:98
  2.0 3.1 %collective-permute-start.3 = (bf16[2,2,128,256]{3,2,1,0:T(8,128)(2,1)S(1)}, bf16[2,2,128,256]{3,2,1,0:T(8,128)(2,1)S(1)}, u32[]{:S(2)}, u32[]{:S(2)}) collective-permute-start(bf16[2,2,128,256]{3,2,1,0:T(8,128)(2,1)S(1)} %get-tuple-element.42), channel_id=1, source_target_pairs={{1,2},{2,1},{3,4},{4,3},{5,6},{6,5},{7,8},{8,7},{9,10},{10,9},{11,... | collective-permute-start | bytes 786440 | tf_op jit(solution)/shard_map/ppermute | solution.py:36
  5.2 1.2 %collective-permute-start.2 = (bf16[2,2,128,256]{3,2,1,0:T(8,128)(2,1)S(1)}, bf16[2,2,128,256]{3,2,1,0:T(8,128)(2,1)S(1)}, u32[]{:S(2)}, u32[]{:S(2)}) collective-permute-start(bf16[2,2,128,256]{3,2,1,0:T(8,128)(2,1)S(1)} %get-tuple-element.39.after_ref), channel_id=1, source_target_pairs={{0,1},{1,0},{2,3},{3,2},{4,5},{5,4},{6,7},{7,6},{8,9},{9,8},{10,11... | collective-permute-start | bytes 786440 | tf_op jit(solution)/shard_map/ppermute | solution.py:36
  6.3 1.0 pack_lines.1.refs_0_
  7.3 5.6 %all-to-all-start = ((bf16[16,16,384]{2,1,0:T(8,128)(2,1)}), bf16[16,16,384]{2,1,0:T(8,128)(2,1)}, u32[]{:S(2)}, u32[]{:S(2)}) async-start(bf16[16,16,384]{2,1,0:T(8,128)(2,1)} %bitcast), calls=%async_computation | async-start | bytes 393216 | tf_op jit(solution)/shard_map/all_to_all | solution.py:175
  13.0 2.0 %pack_halo.3 = (bf16[2,2,128,256]{3,2,1,0:T(8,128)(2,1)}, bf16[2,2,128,256]{3,2,1,0:T(8,128)(2,1)}) custom-call(f32[2,2,2,4,128,256]{5,4,3,2,1,0:T(8,128)} %refs_1_.7, bf16[256,384]{1,0:T(8,128)(2,1)} %pack_lines.1.refs_0_), custom_call_target="tpu_custom_call" | custom-call | flops 1 | bytes 1 | tf_op jit(solution)/shard_map/pack_halo/pallas_call | solution.py:98
  15.0 0.3 collective-permute-start
  15.4 4.0 %collective-permute-start.1 = (bf16[2,2,128,256]{3,2,1,0:T(8,128)(2,1)}, bf16[2,2,128,256]{3,2,1,0:T(8,128)(2,1)}, u32[]{:S(2)}, u32[]{:S(2)}) collective-permute-start(bf16[2,2,128,256]{3,2,1,0:T(8,128)(2,1)} %get-tuple-element.41), channel_id=1, source_target_pairs={{1,2},{2,1},{3,4},{4,3},{5,6},{6,5},{7,8},{8,7},{9,10},{10,9},{11,... | collective-permute-start | bytes 786440 | tf_op jit(solution)/shard_map/ppermute | solution.py:36
  19.3 0.0 collective-permute-done.3.refs_3_
  19.4 0.7 collective-permute-done.2.refs_2_
  20.1 3.3 %step_0_shot_0.1 = (f32[2,4,128,256]{3,2,1,0:T(8,128)S(1)}, f32[4,128,256]{2,1,0:T(8,128)S(1)}, f32[4,128,256]{2,1,0:T(8,128)S(1)}) custom-call(f32[2,2,2,4,128,256]{5,4,3,2,1,0:T(8,128)} %refs_1_.7, f32[2,2,2,4,128,256]{5,4,3,2,1,0:T(8,128)} %refs_1_.7, bf16[2,2,128,256]{3,2,1,0:T(8,128)(2,1)S(1)} %collective-permute-done.2.refs_2_, ...), custom_call_target="tpu_custom_call" | custom-call | flops 9999999827968 | bytes 1 | tf_op jit(solution)/shard_map/step_0_shot_0/pallas_call | solution.py:443
  23.4 0.0 all-to-all-done
  23.4 1.2 %unpack_lines.1.saved_ref.refs_4_ = f32[128,256]{1,0:T(8,128)S(1)} custom-call(bf16[256,384]{1,0:T(8,128)(2,1)} %bitcast.1.got_ref), custom_call_target="tpu_custom_call" | custom-call | flops 1 | bytes 1 | tf_op jit(solution)/shard_map/unpack_lines/pallas_call | solution.py:176
  24.6 0.1 finish_first_0.1
  24.7 3.3 %collective-permute-start.7 = (bf16[2,2,128,256]{3,2,1,0:T(8,128)(2,1)S(1)}, bf16[2,2,128,256]{3,2,1,0:T(8,128)(2,1)S(1)}, u32[]{:S(2)}, u32[]{:S(2)}) collective-permute-start(bf16[2,2,128,256]{3,2,1,0:T(8,128)(2,1)S(1)} %get-tuple-element.51), channel_id=1, source_target_pairs={{1,2},{2,1},{3,4},{4,3},{5,6},{6,5},{7,8},{8,7},{9,10},{10,9},{11,... | collective-permute-start | bytes 786440 | tf_op jit(solution)/shard_map/ppermute | solution.py:36
  28.0 0.4 collective-permute-start.6
  28.4 9.1 %collective-permute-done.refs_2_ = bf16[2,2,128,256]{3,2,1,0:T(8,128)(2,1)} collective-permute-done((bf16[2,2,128,256]{3,2,1,0:T(8,128)(2,1)}, bf16[2,2,128,256]{3,2,1,0:T(8,128)(2,1)}, u32[]{:S(2)}, u32[]{:S(2)}) %collective-permute-start) | collective-permute-done | bytes 262176 | tf_op jit(solution)/shard_map/ppermute | solution.py:36
  37.5 3.8 %step_0_shot_1.1 = (f32[2,4,128,256]{3,2,1,0:T(8,128)S(1)}, bf16[2,2,128,256]{3,2,1,0:T(8,128)(2,1)S(1)}, bf16[2,2,128,256]{3,2,1,0:T(8,128)(2,1)S(1)}, f32[4,128,256]{2,1,0:T(8,128)S(1)}, f32[4,128,256]{2,1,0:T(8,128)S(1)}) custom-call(f32[2,2,2,4,128,256]{5,4,3,2,1,0:T(8,128)} %refs_1_.7, f32[2,2,2,4,128,256]{5,4,3,2,1,0:T(8,128)} %refs_1_.7, ...), custom_call_target="tpu_custom_call" | custom-call | flops 1 | bytes 1 | tf_op jit(solution)/shard_map/step_0_shot_1/pallas_call | solution.py:443
  41.4 3.3 %collective-permute-start.5 = (bf16[2,2,128,256]{3,2,1,0:T(8,128)(2,1)S(1)}, bf16[2,2,128,256]{3,2,1,0:T(8,128)(2,1)S(1)}, u32[]{:S(2)}, u32[]{:S(2)}) collective-permute-start(bf16[2,2,128,256]{3,2,1,0:T(8,128)(2,1)S(1)} %get-tuple-element.47), channel_id=1, source_target_pairs={{1,2},{2,1},{3,4},{4,3},{5,6},{6,5},{7,8},{8,7},{9,10},{10,9},{11,... | collective-permute-start | bytes 786440 | tf_op jit(solution)/shard_map/ppermute | solution.py:36
  44.7 0.1 collective-permute-start.4
  44.7 0.0 collective-permute-done.7.refs_3_
  44.8 2.4 %step_1_shot_0.1 = (f32[2,4,128,256]{3,2,1,0:T(8,128)S(1)}, bf16[2,2,128,256]{3,2,1,0:T(8,128)(2,1)S(1)}, bf16[2,2,128,256]{3,2,1,0:T(8,128)(2,1)S(1)}, f32[4,128,256]{2,1,0:T(8,128)S(1)}) custom-call(f32[2,4,128,256]{3,2,1,0:T(8,128)S(1)} %get-tuple-element.50.refs_0_.refs_1_, f32[2,2,2,4,128,256]{5,4,3,2,1,0:T(8,128)} %refs_1_.7, ...), custom_call_target="tpu_custom_call" | custom-call | flops 1 | bytes 1 | tf_op jit(solution)/shard_map/step_1_shot_0/pallas_call | solution.py:443
  47.1 2.9 %collective-permute-start.11 = (bf16[2,2,128,256]{3,2,1,0:T(8,128)(2,1)S(1)}, bf16[2,2,128,256]{3,2,1,0:T(8,128)(2,1)S(1)}, u32[]{:S(2)}, u32[]{:S(2)}) collective-permute-start(bf16[2,2,128,256]{3,2,1,0:T(8,128)(2,1)S(1)} %get-tuple-element.60), channel_id=1, source_target_pairs={{1,2},{2,1},{3,4},{4,3},{5,6},{6,5},{7,8},{8,7},{9,10},{10,9},{11,... | collective-permute-start | bytes 786440 | tf_op jit(solution)/shard_map/ppermute | solution.py:36
  50.1 1.4 %collective-permute-start.10 = (bf16[2,2,128,256]{3,2,1,0:T(8,128)(2,1)S(1)}, bf16[2,2,128,256]{3,2,1,0:T(8,128)(2,1)S(1)}, u32[]{:S(2)}, u32[]{:S(2)}) collective-permute-start(bf16[2,2,128,256]{3,2,1,0:T(8,128)(2,1)S(1)} %get-tuple-element.54.refs_9_), channel_id=1, source_target_pairs={{0,1},{1,0},{2,3},{3,2},{4,5},{5,4},{6,7},{7,6},{8,9},{9,8},{10,11... | collective-permute-start | bytes 786440 | tf_op jit(solution)/shard_map/ppermute | solution.py:36
  51.4 11.3 %collective-permute-done.4.refs_2_ = bf16[2,2,128,256]{3,2,1,0:T(8,128)(2,1)S(1)} collective-permute-done((bf16[2,2,128,256]{3,2,1,0:T(8,128)(2,1)S(1)}, bf16[2,2,128,256]{3,2,1,0:T(8,128)(2,1)S(1)}, u32[]{:S(2)}, u32[]{:S(2)}) %collective-permute-start.4) | collective-permute-done | bytes 262176 | tf_op jit(solution)/shard_map/ppermute | solution.py:36
  62.8 2.5 %step_1_shot_1.1 = (f32[2,4,128,256]{3,2,1,0:T(8,128)S(1)}, bf16[2,2,128,256]{3,2,1,0:T(8,128)(2,1)S(1)}, bf16[2,2,128,256]{3,2,1,0:T(8,128)(2,1)S(1)}, f32[4,128,256]{2,1,0:T(8,128)S(1)}) custom-call(f32[2,4,128,256]{3,2,1,0:T(8,128)S(1)} %get-tuple-element.45.refs_0_.refs_1_, f32[2,2,2,4,128,256]{5,4,3,2,1,0:T(8,128)} %refs_1_.7, ...), custom_call_target="tpu_custom_call" | custom-call | flops 1 | bytes 1 | tf_op jit(solution)/shard_map/step_1_shot_1/pallas_call | solution.py:443
  65.3 2.9 %collective-permute-start.9 = (bf16[2,2,128,256]{3,2,1,0:T(8,128)(2,1)S(1)}, bf16[2,2,128,256]{3,2,1,0:T(8,128)(2,1)S(1)}, u32[]{:S(2)}, u32[]{:S(2)}) collective-permute-start(bf16[2,2,128,256]{3,2,1,0:T(8,128)(2,1)S(1)} %get-tuple-element.57), channel_id=1, source_target_pairs={{1,2},{2,1},{3,4},{4,3},{5,6},{6,5},{7,8},{8,7},{9,10},{10,9},{11,... | collective-permute-start | bytes 786440 | tf_op jit(solution)/shard_map/ppermute | solution.py:36
  68.2 0.1 collective-permute-start.8
  68.3 0.0 collective-permute-done.11.refs_3_
  68.3 0.1 collective-permute-done.10.refs_2_
  68.4 1.2 %step_2_shot_0.1 = (f32[2,4,128,256]{3,2,1,0:T(8,128)S(1)}, bf16[2,2,128,256]{3,2,1,0:T(8,128)(2,1)S(1)}, bf16[2,2,128,256]{3,2,1,0:T(8,128)(2,1)S(1)}, f32[4,128,256]{2,1,0:T(8,128)S(1)}) custom-call(f32[2,4,128,256]{3,2,1,0:T(8,128)S(1)} %get-tuple-element.59.refs_0_.refs_1_, f32[2,4,128,256]{3,2,1,0:T(8,128)S(1)} %get-tuple-element.50.refs_0_.refs_1_, ...), custom_call_target="tpu_custom_call" | custom-call | flops 1 | bytes 1 | tf_op jit(solution)/shard_map/step_2_shot_0/pallas_call | solution.py:443
  69.6 3.1 %collective-permute-start.17 = (bf16[2,2,128,256]{3,2,1,0:T(8,128)(2,1)S(1)}, bf16[2,2,128,256]{3,2,1,0:T(8,128)(2,1)S(1)}, u32[]{:S(2)}, u32[]{:S(2)}) collective-permute-start(bf16[2,2,128,256]{3,2,1,0:T(8,128)(2,1)S(1)} %get-tuple-element.70), channel_id=1, source_target_pairs={{1,2},{2,1},{3,4},{4,3},{5,6},{6,5},{7,8},{8,7},{9,10},{10,9},{11,... | collective-permute-start | bytes 786440 | tf_op jit(solution)/shard_map/ppermute | solution.py:36
  72.8 1.4 %collective-permute-start.16 = (bf16[2,2,128,256]{3,2,1,0:T(8,128)(2,1)S(1)}, bf16[2,2,128,256]{3,2,1,0:T(8,128)(2,1)S(1)}, u32[]{:S(2)}, u32[]{:S(2)}) collective-permute-start(bf16[2,2,128,256]{3,2,1,0:T(8,128)(2,1)S(1)} %get-tuple-element.62.refs_9_), channel_id=1, source_target_pairs={{0,1},{1,0},{2,3},{3,2},{4,5},{5,4},{6,7},{7,6},{8,9},{9,8},{10,11... | collective-permute-start | bytes 786440 | tf_op jit(solution)/shard_map/ppermute | solution.py:36
  74.2 1.1 %collective-permute-done.9.refs_3_ = bf16[2,2,128,256]{3,2,1,0:T(8,128)(2,1)S(1)} collective-permute-done((bf16[2,2,128,256]{3,2,1,0:T(8,128)(2,1)S(1)}, bf16[2,2,128,256]{3,2,1,0:T(8,128)(2,1)S(1)}, u32[]{:S(2)}, u32[]{:S(2)}) %collective-permute-start.9) | collective-permute-done | bytes 262176 | tf_op jit(solution)/shard_map/ppermute | solution.py:36
  75.3 11.0 %collective-permute-done.8.refs_2_ = bf16[2,2,128,256]{3,2,1,0:T(8,128)(2,1)S(1)} collective-permute-done((bf16[2,2,128,256]{3,2,1,0:T(8,128)(2,1)S(1)}, bf16[2,2,128,256]{3,2,1,0:T(8,128)(2,1)S(1)}, u32[]{:S(2)}, u32[]{:S(2)}) %collective-permute-start.8) | collective-permute-done | bytes 262176 | tf_op jit(solution)/shard_map/ppermute | solution.py:36
  86.3 1.2 %step_2_shot_1.1 = (f32[2,4,128,256]{3,2,1,0:T(8,128)S(1)}, bf16[1,2,128,256]{3,2,1,0:T(8,128)(2,1)S(1)}, bf16[1,2,128,256]{3,2,1,0:T(8,128)(2,1)S(1)}, bf16[1,2...) custom-call(f32[2,4,128,256]{3,2,1,0:T(8,128)S(1)} %get-tuple-element.55.refs_0_.refs_, ...), custom_call_target="tpu_custom_call" | custom-call | flops 1 | bytes 1 | tf_op jit(solution)/shard_map/step_2_shot_1/pallas_call | solution.py:443
  87.5 3.3 %collective-permute-start.15 = (bf16[1,2,128,256]{3,2,1,0:T(8,128)(2,1)S(1)}, bf16[1,2,128,256]{3,2,1,0:T(8,128)(2,1)S(1)}, u32[]{:S(2)}, u32[]{:S(2)}) collective-permute-start(bf16[1,2,128,256]{3,2,1,0:T(8,128)(2,1)S(1)} %get-tuple-element.67), channel_id=1, source_target_pairs={{1,2},{2,1},{3,4},{4,3},{5,6},{6,5},{7,8},{8,7},{9,10},{10,9},{11,... | collective-permute-start | bytes 393224 | tf_op jit(solution)/shard_map/ppermute | solution.py:36
  90.8 0.1 collective-permute-start.14
  90.9 1.5 %collective-permute-start.12 = (bf16[1,2,128,256]{3,2,1,0:T(8,128)(2,1)S(1)}, bf16[1,2,128,256]{3,2,1,0:T(8,128)(2,1)S(1)}, u32[]{:S(2)}, u32[]{:S(2)}) collective-permute-start(bf16[1,2,128,256]{3,2,1,0:T(8,128)(2,1)S(1)} %get-tuple-element.64), channel_id=1, source_target_pairs={{0,1},{1,0},{2,3},{3,2},{4,5},{5,4},{6,7},{7,6},{8,9},{9,8},{10,11... | collective-permute-start | bytes 393224 | tf_op jit(solution)/shard_map/ppermute | solution.py:36
  92.4 2.9 %collective-permute-start.13 = (bf16[1,2,128,256]{3,2,1,0:T(8,128)(2,1)S(1)}, bf16[1,2,128,256]{3,2,1,0:T(8,128)(2,1)S(1)}, u32[]{:S(2)}, u32[]{:S(2)}) collective-permute-start(bf16[1,2,128,256]{3,2,1,0:T(8,128)(2,1)S(1)} %get-tuple-element.65), channel_id=1, source_target_pairs={{1,2},{2,1},{3,4},{4,3},{5,6},{6,5},{7,8},{8,7},{9,10},{10,9},{11,... | collective-permute-start | bytes 393224 | tf_op jit(solution)/shard_map/ppermute | solution.py:36
  95.3 2.6 %step_3_shot_0.1 = (f32[2,2,2,4,128,256]{5,4,3,2,1,0:T(8,128)}, f32[4,192,256]{2,1,0:T(8,128)S(1)}) custom-call(f32[2,4,128,256]{3,2,1,0:T(8,128)S(1)} %get-tuple-element.69.refs_0_.refs_10_, f32[2,4,128,256]{3,2,1,0:T(8,128)S(1)} %get-tuple-element.59.refs_0_.refs_1_, bf16[2,2,128,256]{3,2,1,0:T(8,128)(2,1)S(1)} %collective-permute-done.16.refs_2_, ...), custom_call_target="tpu_custom_call" | custom-call | flops 1 | bytes 1 | tf_op jit(solution)/shard_map/step_3_shot_0/pallas_call | solution.py:443
  97.9 2.6 %collective-permute-done.14.refs_2_ = bf16[1,2,128,256]{3,2,1,0:T(8,128)(2,1)S(1)} collective-permute-done((bf16[1,2,128,256]{3,2,1,0:T(8,128)(2,1)S(1)}, bf16[1,2,128,256]{3,2,1,0:T(8,128)(2,1)S(1)}, u32[]{:S(2)}, u32[]{:S(2)}) %collective-permute-start.14) | collective-permute-done | bytes 131104 | tf_op jit(solution)/shard_map/ppermute | solution.py:36
  100.5 2.3 %step_3_shot_1.2 = (f32[4,128,256]{2,1,0:T(8,128)S(1)}, f32[4,192,256]{2,1,0:T(8,128)}) custom-call(f32[2,4,128,256]{3,2,1,0:T(8,128)S(1)} %get-tuple-element.63.refs_11_.refs_0_, f32[2,4,128,256]{3,2,1,0:T(8,128)S(1)} %get-tuple-element.55.refs_0_.refs_1_, bf16[1,2,128,256]{3,2,1,0:T(8,128)(2,1)S(1)} %collective-permute-done.14.refs_2_, ...), custom_call_target="tpu_custom_call" | custom-call | flops 1 | bytes 1 | tf_op jit(solution)/shard_map/step_3_shot_1/pallas_call | solution.py:443
  102.8 0.6 collective-permute-start.18
  103.4 0.2 collective-permute-done.13.refs_3_
  103.6 1.4 %step_3_shot_1.3.refs_0_ = f32[2,2,2,4,128,256]{5,4,3,2,1,0:T(8,128)} custom-call(f32[2,4,128,256]{3,2,1,0:T(8,128)S(1)} %get-tuple-element.63.refs_11_.refs_0_, f32[2,4,128,256]{3,2,1,0:T(8,128)S(1)} %get-tuple-element.55.refs_0_.refs_1_, bf16[1,2,128,256]{3,2,1,0:T(8,128)(2,1)S(1)} %collective-permute-done.12.refs_2_, ...), custom_call_target="tpu_custom_call", output_to_operand_aliasing={{}: (8, {})} | custom-call | flops 9999999827968 | bytes 1 | tf_op jit(solution)/shard_map/step_3_shot_1/pallas_call | solution.py:443
  105.0 0.7 collective-permute-done.18.other_ref
  105.7 3.5 %sum_frames.1 = f32[4,192,256]{2,1,0:T(8,128)} custom-call(f32[4,192,256]{2,1,0:T(8,128)} %get-tuple-element.74.refs_7_.own_ref, f32[4,192,256]{2,1,0:T(8,128)} %collective-permute-done.18.other_ref, f32[2,2,2,4,128,256]{5,4,3,2,1,0:T(8,128)} %step_3_shot_1.3.refs_0_), custom_call_target="tpu_custom_call" | custom-call | flops 1 | bytes 1 | tf_op jit(solution)/shard_map/sum_frames/pallas_call | solution.py:466
  (19 shorter events, 0.0 us)
Async XLA Ops:
  0.6 5.7 %copy-start.5 = (s32[2,128]{1,0:T(2,128)S(1)}, s32[2,128]{1,0:T(2,128)}, u32[]{:S(2)}) copy-start(s32[2,128]{1,0:T(2,128)} %ids_ref.1) | copy-start | bytes 3076
  0.6 5.7 %copy-start.2 = (bf16[2,128,256]{2,1,0:T(8,128)(2,1)S(1)}, bf16[2,128,256]{2,1,0:T(8,128)(2,1)}, u32[]{:S(2)}) copy-start(bf16[2,128,256]{2,1,0:T(8,128)(2,1)} %lines_ref.1) | copy-start | bytes 393220
  0.7 19.4 %copy-start.1 = (f32[2,4,64]{2,1,0:T(4,128)S(1)}, f32[2,4,64]{2,1,0:T(4,128)}, u32[]{:S(2)}) copy-start(f32[2,4,64]{2,1,0:T(4,128)} %refs_5_.15) | copy-start | bytes 6148
  0.7 19.4 %copy-start.3 = (s32[2,64]{1,0:T(2,128)S(1)}, s32[2,64]{1,0:T(2,128)}, u32[]{:S(2)}) copy-start(s32[2,64]{1,0:T(2,128)} %refs_4_.3) | copy-start | bytes 1540
  0.7 19.4 %copy-start.4 = (s32[2]{0:T(128)S(1)}, s32[2]{0:T(128)}, u32[]{:S(2)}) copy-start(s32[2]{0:T(128)} %refs_6_.15) | copy-start | bytes 28
  0.7 19.4 %copy-start = (f32[4,192,256]{2,1,0:T(8,128)S(1)}, f32[4,192,256]{2,1,0:T(8,128)}, u32[]{:S(2)}) copy-start(f32[4,192,256]{2,1,0:T(8,128)} %refs_8_.1) | copy-start | bytes 2359300
  2.0 17.3 %collective-permute-start.3 = (bf16[2,2,128,256]{3,2,1,0:T(8,128)(2,1)S(1)}, bf16[2,2,128,256]{3,2,1,0:T(8,128)(2,1)S(1)}, u32[]{:S(2)}, u32[]{:S(2)}) collective-permute-start(bf16[2,2,128,256]{3,2,1,0:T(8,128)(2,1)S(1)} %get-tuple-element.42), channel_id=1, source_target_pairs={{1,2},{2,1},{3,4},{4,3},{5,6},{6,5},{7,8},{8,7},{9,10},{10,9},{11,... | collective-permute-start | bytes 786440 | tf_op jit(solution)/shard_map/ppermute | solution.py:36
  5.2 14.9 %collective-permute-start.2 = (bf16[2,2,128,256]{3,2,1,0:T(8,128)(2,1)S(1)}, bf16[2,2,128,256]{3,2,1,0:T(8,128)(2,1)S(1)}, u32[]{:S(2)}, u32[]{:S(2)}) collective-permute-start(bf16[2,2,128,256]{3,2,1,0:T(8,128)(2,1)S(1)} %get-tuple-element.39.after_ref), channel_id=1, source_target_pairs={{0,1},{1,0},{2,3},{3,2},{4,5},{5,4},{6,7},{7,6},{8,9},{9,8},{10,11... | collective-permute-start | bytes 786440 | tf_op jit(solution)/shard_map/ppermute | solution.py:36
  7.3 16.0 %all-to-all-start = ((bf16[16,16,384]{2,1,0:T(8,128)(2,1)}), bf16[16,16,384]{2,1,0:T(8,128)(2,1)}, u32[]{:S(2)}, u32[]{:S(2)}) async-start(bf16[16,16,384]{2,1,0:T(8,128)(2,1)} %bitcast), calls=%async_computation | async-start | bytes 393216 | tf_op jit(solution)/shard_map/all_to_all | solution.py:175
  15.0 22.5 %collective-permute-start = (bf16[2,2,128,256]{3,2,1,0:T(8,128)(2,1)}, bf16[2,2,128,256]{3,2,1,0:T(8,128)(2,1)}, u32[]{:S(2)}, u32[]{:S(2)}) collective-permute-start(bf16[2,2,128,256]{3,2,1,0:T(8,128)(2,1)} %get-tuple-element.40), channel_id=1, source_target_pairs={{0,1},{1,0},{2,3},{3,2},{4,5},{5,4},{6,7},{7,6},{8,9},{9,8},{10,11... | collective-permute-start | bytes 786440 | tf_op jit(solution)/shard_map/ppermute | solution.py:36
  15.4 22.2 %collective-permute-start.1 = (bf16[2,2,128,256]{3,2,1,0:T(8,128)(2,1)}, bf16[2,2,128,256]{3,2,1,0:T(8,128)(2,1)}, u32[]{:S(2)}, u32[]{:S(2)}) collective-permute-start(bf16[2,2,128,256]{3,2,1,0:T(8,128)(2,1)} %get-tuple-element.41), channel_id=1, source_target_pairs={{1,2},{2,1},{3,4},{4,3},{5,6},{6,5},{7,8},{8,7},{9,10},{10,9},{11,... | collective-permute-start | bytes 786440 | tf_op jit(solution)/shard_map/ppermute | solution.py:36
  24.7 20.0 %collective-permute-start.7 = (bf16[2,2,128,256]{3,2,1,0:T(8,128)(2,1)S(1)}, bf16[2,2,128,256]{3,2,1,0:T(8,128)(2,1)S(1)}, u32[]{:S(2)}, u32[]{:S(2)}) collective-permute-start(bf16[2,2,128,256]{3,2,1,0:T(8,128)(2,1)S(1)} %get-tuple-element.51), channel_id=1, source_target_pairs={{1,2},{2,1},{3,4},{4,3},{5,6},{6,5},{7,8},{8,7},{9,10},{10,9},{11,... | collective-permute-start | bytes 786440 | tf_op jit(solution)/shard_map/ppermute | solution.py:36
  28.0 16.7 %collective-permute-start.6 = (bf16[2,2,128,256]{3,2,1,0:T(8,128)(2,1)S(1)}, bf16[2,2,128,256]{3,2,1,0:T(8,128)(2,1)S(1)}, u32[]{:S(2)}, u32[]{:S(2)}) collective-permute-start(bf16[2,2,128,256]{3,2,1,0:T(8,128)(2,1)S(1)} %get-tuple-element.44.refs_9_), channel_id=1, source_target_pairs={{0,1},{1,0},{2,3},{3,2},{4,5},{5,4},{6,7},{7,6},{8,9},{9,8},{10,11... | collective-permute-start | bytes 786440 | tf_op jit(solution)/shard_map/ppermute | solution.py:36
  41.4 10.1 %collective-permute-start.5 = (bf16[2,2,128,256]{3,2,1,0:T(8,128)(2,1)S(1)}, bf16[2,2,128,256]{3,2,1,0:T(8,128)(2,1)S(1)}, u32[]{:S(2)}, u32[]{:S(2)}) collective-permute-start(bf16[2,2,128,256]{3,2,1,0:T(8,128)(2,1)S(1)} %get-tuple-element.47), channel_id=1, source_target_pairs={{1,2},{2,1},{3,4},{4,3},{5,6},{6,5},{7,8},{8,7},{9,10},{10,9},{11,... | collective-permute-start | bytes 786440 | tf_op jit(solution)/shard_map/ppermute | solution.py:36
  44.7 18.1 %collective-permute-start.4 = (bf16[2,2,128,256]{3,2,1,0:T(8,128)(2,1)S(1)}, bf16[2,2,128,256]{3,2,1,0:T(8,128)(2,1)S(1)}, u32[]{:S(2)}, u32[]{:S(2)}) collective-permute-start(bf16[2,2,128,256]{3,2,1,0:T(8,128)(2,1)S(1)} %get-tuple-element.46.refs_9_), channel_id=1, source_target_pairs={{0,1},{1,0},{2,3},{3,2},{4,5},{5,4},{6,7},{7,6},{8,9},{9,8},{10,11... | collective-permute-start | bytes 786440 | tf_op jit(solution)/shard_map/ppermute | solution.py:36
  47.1 21.1 %collective-permute-start.11 = (bf16[2,2,128,256]{3,2,1,0:T(8,128)(2,1)S(1)}, bf16[2,2,128,256]{3,2,1,0:T(8,128)(2,1)S(1)}, u32[]{:S(2)}, u32[]{:S(2)}) collective-permute-start(bf16[2,2,128,256]{3,2,1,0:T(8,128)(2,1)S(1)} %get-tuple-element.60), channel_id=1, source_target_pairs={{1,2},{2,1},{3,4},{4,3},{5,6},{6,5},{7,8},{8,7},{9,10},{10,9},{11,... | collective-permute-start | bytes 786440 | tf_op jit(solution)/shard_map/ppermute | solution.py:36
  50.1 18.4 %collective-permute-start.10 = (bf16[2,2,128,256]{3,2,1,0:T(8,128)(2,1)S(1)}, bf16[2,2,128,256]{3,2,1,0:T(8,128)(2,1)S(1)}, u32[]{:S(2)}, u32[]{:S(2)}) collective-permute-start(bf16[2,2,128,256]{3,2,1,0:T(8,128)(2,1)S(1)} %get-tuple-element.54.refs_9_), channel_id=1, source_target_pairs={{0,1},{1,0},{2,3},{3,2},{4,5},{5,4},{6,7},{7,6},{8,9},{9,8},{10,11... | collective-permute-start | bytes 786440 | tf_op jit(solution)/shard_map/ppermute | solution.py:36
  65.3 10.1 %collective-permute-start.9 = (bf16[2,2,128,256]{3,2,1,0:T(8,128)(2,1)S(1)}, bf16[2,2,128,256]{3,2,1,0:T(8,128)(2,1)S(1)}, u32[]{:S(2)}, u32[]{:S(2)}) collective-permute-start(bf16[2,2,128,256]{3,2,1,0:T(8,128)(2,1)S(1)} %get-tuple-element.57), channel_id=1, source_target_pairs={{1,2},{2,1},{3,4},{4,3},{5,6},{6,5},{7,8},{8,7},{9,10},{10,9},{11,... | collective-permute-start | bytes 786440 | tf_op jit(solution)/shard_map/ppermute | solution.py:36
  68.2 18.1 %collective-permute-start.8 = (bf16[2,2,128,256]{3,2,1,0:T(8,128)(2,1)S(1)}, bf16[2,2,128,256]{3,2,1,0:T(8,128)(2,1)S(1)}, u32[]{:S(2)}, u32[]{:S(2)}) collective-permute-start(bf16[2,2,128,256]{3,2,1,0:T(8,128)(2,1)S(1)} %get-tuple-element.56.refs_9_), channel_id=1, source_target_pairs={{0,1},{1,0},{2,3},{3,2},{4,5},{5,4},{6,7},{7,6},{8,9},{9,8},{10,11... | collective-permute-start | bytes 786440 | tf_op jit(solution)/shard_map/ppermute | solution.py:36
  69.6 22.7 %collective-permute-start.17 = (bf16[2,2,128,256]{3,2,1,0:T(8,128)(2,1)S(1)}, bf16[2,2,128,256]{3,2,1,0:T(8,128)(2,1)S(1)}, u32[]{:S(2)}, u32[]{:S(2)}) collective-permute-start(bf16[2,2,128,256]{3,2,1,0:T(8,128)(2,1)S(1)} %get-tuple-element.70), channel_id=1, source_target_pairs={{1,2},{2,1},{3,4},{4,3},{5,6},{6,5},{7,8},{8,7},{9,10},{10,9},{11,... | collective-permute-start | bytes 786440 | tf_op jit(solution)/shard_map/ppermute | solution.py:36
  72.8 22.5 %collective-permute-start.16 = (bf16[2,2,128,256]{3,2,1,0:T(8,128)(2,1)S(1)}, bf16[2,2,128,256]{3,2,1,0:T(8,128)(2,1)S(1)}, u32[]{:S(2)}, u32[]{:S(2)}) collective-permute-start(bf16[2,2,128,256]{3,2,1,0:T(8,128)(2,1)S(1)} %get-tuple-element.62.refs_9_), channel_id=1, source_target_pairs={{0,1},{1,0},{2,3},{3,2},{4,5},{5,4},{6,7},{7,6},{8,9},{9,8},{10,11... | collective-permute-start | bytes 786440 | tf_op jit(solution)/shard_map/ppermute | solution.py:36
  87.5 10.4 %collective-permute-start.15 = (bf16[1,2,128,256]{3,2,1,0:T(8,128)(2,1)S(1)}, bf16[1,2,128,256]{3,2,1,0:T(8,128)(2,1)S(1)}, u32[]{:S(2)}, u32[]{:S(2)}) collective-permute-start(bf16[1,2,128,256]{3,2,1,0:T(8,128)(2,1)S(1)} %get-tuple-element.67), channel_id=1, source_target_pairs={{1,2},{2,1},{3,4},{4,3},{5,6},{6,5},{7,8},{8,7},{9,10},{10,9},{11,... | collective-permute-start | bytes 393224 | tf_op jit(solution)/shard_map/ppermute | solution.py:36
  90.8 9.7 %collective-permute-start.14 = (bf16[1,2,128,256]{3,2,1,0:T(8,128)(2,1)S(1)}, bf16[1,2,128,256]{3,2,1,0:T(8,128)(2,1)S(1)}, u32[]{:S(2)}, u32[]{:S(2)}) collective-permute-start(bf16[1,2,128,256]{3,2,1,0:T(8,128)(2,1)S(1)} %get-tuple-element.66.refs_12_), channel_id=1, source_target_pairs={{0,1},{1,0},{2,3},{3,2},{4,5},{5,4},{6,7},{7,6},{8,9},{9,8},{10,11... | collective-permute-start | bytes 393224 | tf_op jit(solution)/shard_map/ppermute | solution.py:36
  90.9 12.5 %collective-permute-start.12 = (bf16[1,2,128,256]{3,2,1,0:T(8,128)(2,1)S(1)}, bf16[1,2,128,256]{3,2,1,0:T(8,128)(2,1)S(1)}, u32[]{:S(2)}, u32[]{:S(2)}) collective-permute-start(bf16[1,2,128,256]{3,2,1,0:T(8,128)(2,1)S(1)} %get-tuple-element.64), channel_id=1, source_target_pairs={{0,1},{1,0},{2,3},{3,2},{4,5},{5,4},{6,7},{7,6},{8,9},{9,8},{10,11... | collective-permute-start | bytes 393224 | tf_op jit(solution)/shard_map/ppermute | solution.py:36
  92.4 11.2 %collective-permute-start.13 = (bf16[1,2,128,256]{3,2,1,0:T(8,128)(2,1)S(1)}, bf16[1,2,128,256]{3,2,1,0:T(8,128)(2,1)S(1)}, u32[]{:S(2)}, u32[]{:S(2)}) collective-permute-start(bf16[1,2,128,256]{3,2,1,0:T(8,128)(2,1)S(1)} %get-tuple-element.65), channel_id=1, source_target_pairs={{1,2},{2,1},{3,4},{4,3},{5,6},{6,5},{7,8},{8,7},{9,10},{10,9},{11,... | collective-permute-start | bytes 393224 | tf_op jit(solution)/shard_map/ppermute | solution.py:36
  102.8 2.8 %collective-permute-start.18 = (f32[4,192,256]{2,1,0:T(8,128)}, f32[4,192,256]{2,1,0:T(8,128)}, u32[]{:S(2)}, u32[]{:S(2)}) collective-permute-start(f32[4,192,256]{2,1,0:T(8,128)} %get-tuple-element.74.refs_7_.own_ref), channel_id=1, source_target_pairs={{0,16},{16,0},{1,17},{17,1},{2,18},{18,2},{3,19},{19,3},{4,20},{20... | collective-permute-start | bytes 2359304 | tf_op jit(solution)/shard_map/ppermute | solution.py:551

commit v4 on v3

--- a/solution.py
+++ b/solution.py
@@ -456,19 +456,30 @@
     )(*args)
 
 
-def sum_kernel(scale, own_ref, other_ref, *refs):
-    refs[-1][...] = (own_ref[...] + other_ref[...]) * scale
+def sum_kernel(scale, own_ref, other_ref, after_ref, image_ref, sum_ref, sems):
+    del after_ref
+    stores = []
+    for layer in range(sum_ref.shape[0]):
+        sum_ref[layer] = (own_ref[layer] + other_ref[layer]) * scale
+        stores.append(
+            pltpu.make_async_copy(sum_ref.at[layer], image_ref.at[layer], sems.at[layer])
+        )
+        stores[-1].start()
+    for started in stores:
+        started.wait()
 
 
 def sum_frames(own, other, scale, after):
-    layers, model_y, cells_z = own.shape
-    block = pl.BlockSpec((1, model_y, cells_z), lambda i: (i, 0, 0))
+    vmem, hbm = pl.BlockSpec(memory_space=VMEM), pl.BlockSpec(memory_space=HBM)
     return pl.pallas_call(
         functools.partial(sum_kernel, scale),
-        grid=(layers,),
-        in_specs=[block, block, pl.BlockSpec(memory_space=HBM)],
-        out_specs=block,
+        in_specs=[vmem, vmem, hbm],
+        out_specs=hbm,
         out_shape=jax.ShapeDtypeStruct(own.shape, jnp.float32),
+        scratch_shapes=[
+            pltpu.VMEM(own.shape, jnp.float32),
+            pltpu.SemaphoreType.DMA((own.shape[0],)),
+        ],
         compiler_params=params(),
         cost_estimate=cost(),
         name="sum_frames",
@@ -492,10 +503,11 @@
 
     sends = pack_halo(wavefields, 0, [])
     got = [exchange(sends)]
+    for shot in range(1, shots):
+        sends = pack_halo(wavefields, shot, [sends[0]])
+        got.append(exchange(sends))
     message = pack_lines(strip_lines, strip_ids, per_owner, cap, sends[0])
     saved = deliver(message, cap, shots, per_owner)
-    for shot in range(1, shots):
-        got.append(exchange(pack_halo(wavefields, shot, [message])))
     groups = [BOTH] * shots
     now = [wavefields] * shots
     later = [wavefields] * shots

time: 110 us -> 113 us (1.027)
  waiting for transfers between devices: 36.9 us -> 39.7 us
  starting transfers between devices: 41.4 us -> 43.3 us
  Pallas kernels: 29.9 us -> 28.7 us
    all_to_all x1, waiting for transfers between devices: 0.01 us -> 9.33 us  [deliver(): got = lax.all_to_all(message, 'space', 0, 0, tiled=False)]
    ppermute x18, waiting for transfers between devices: 36.2 us -> 29.5 us  [swap_pairs(): return lax.ppermute(value, 'space', routes)]
    ppermute x1, starting transfers between devices: 0.59 us -> 3.03 us  [body(): other = lax.ppermute(frame, 'shot', [(0, 1), (1, 0)])]
    pallas_call x1, Pallas kernels: 3.48 us -> 2.29 us  [sum_frames(): pl.pallas_call(functools.partial(sum_kernel, scale), in_specs=[vmem, vmem...]
  transfers between devices with their start and end apart: 20 -> 20, of which waited for: 9 -> 6; matrix products, arithmetic and copies ran while one was open for 0% -> 0% of each run, Pallas kernels for 23% -> 22%
where the time goes in v4:
time: 113 us
  starting transfers between devices  43.3 us (38%)
  waiting for transfers between devices  39.7 us (35%)
  Pallas kernels  28.7 us (25%)
    ppermute x18, starting transfers between devices, swap_pairs(): return lax.ppermute(value, 'space', routes)  34.7 us
    ppermute x18, waiting for transfers between devices, swap_pairs(): return lax.ppermute(value, 'space', routes)  29.5 us
    pallas_call x9, Pallas kernels, one_step(): pl.pallas_call(functools.partial(step_kernel, shot, step, comps, got_grou...  20.7 us
    all_to_all x1, waiting for transfers between devices, deliver(): got = lax.all_to_all(message, 'space', 0, 0, tiled=False)  9.33 us
    all_to_all x1, starting transfers between devices, deliver(): got = lax.all_to_all(message, 'space', 0, 0, tiled=False)  5.57 us
    pallas_call x2, Pallas kernels, pack_halo(): pl.pallas_call(functools.partial(pack_kernel, shot), in_specs=[pl.BlockSp...  3.37 us
    ppermute x1, starting transfers between devices, body(): other = lax.ppermute(frame, 'shot', [(0, 1), (1, 0)])  3.03 us
    pallas_call x1, Pallas kernels, sum_frames(): pl.pallas_call(functools.partial(sum_kernel, scale), in_specs=[vmem, vmem...  2.29 us
  transfers between devices with their start and end apart: 20, of which 6 were waited for; matrix products, arithmetic and copies ran while one was open for 0% of the time, Pallas kernels for 22%

profile of v4, /device:TPU:19, one launch (start us, length us, event | category | flops | bytes accessed | tf_op | source)
XLA Modules:
  0.0 112.7 jit_solution(12879392655281939967)
XLA Ops:
  0.7 1.3 %pack_halo.2 = (bf16[2,2,128,256]{3,2,1,0:T(8,128)(2,1)S(1)}, bf16[2,2,128,256]{3,2,1,0:T(8,128)(2,1)S(1)}) custom-call(f32[2,2,2,4,128,256]{5,4,3,2,1,0:T(8,128)} %refs_1_.7), custom_call_target="tpu_custom_call" | custom-call | flops 1 | bytes 1 | tf_op jit(solution)/shard_map/pack_halo/pallas_call | solution.py:98
  2.0 3.1 %collective-permute-start.3 = (bf16[2,2,128,256]{3,2,1,0:T(8,128)(2,1)S(1)}, bf16[2,2,128,256]{3,2,1,0:T(8,128)(2,1)S(1)}, u32[]{:S(2)}, u32[]{:S(2)}) collective-permute-start(bf16[2,2,128,256]{3,2,1,0:T(8,128)(2,1)S(1)} %get-tuple-element.42), channel_id=1, source_target_pairs={{1,2},{2,1},{3,4},{4,3},{5,6},{6,5},{7,8},{8,7},{9,10},{10,9},{11,... | collective-permute-start | bytes 786440 | tf_op jit(solution)/shard_map/ppermute | solution.py:36
  5.2 1.2 %collective-permute-start.2 = (bf16[2,2,128,256]{3,2,1,0:T(8,128)(2,1)S(1)}, bf16[2,2,128,256]{3,2,1,0:T(8,128)(2,1)S(1)}, u32[]{:S(2)}, u32[]{:S(2)}) collective-permute-start(bf16[2,2,128,256]{3,2,1,0:T(8,128)(2,1)S(1)} %get-tuple-element.39.refs_0_), channel_id=1, source_target_pairs={{0,1},{1,0},{2,3},{3,2},{4,5},{5,4},{6,7},{7,6},{8,9},{9,8},{10,11... | collective-permute-start | bytes 786440 | tf_op jit(solution)/shard_map/ppermute | solution.py:36
  6.3 2.0 %pack_halo.3 = (bf16[2,2,128,256]{3,2,1,0:T(8,128)(2,1)}, bf16[2,2,128,256]{3,2,1,0:T(8,128)(2,1)}) custom-call(f32[2,2,2,4,128,256]{5,4,3,2,1,0:T(8,128)} %refs_1_.7, bf16[2,2,128,256]{3,2,1,0:T(8,128)(2,1)S(1)} %get-tuple-element.39.refs_0_), custom_call_target="tpu_custom_call" | custom-call | flops 1 | bytes 1 | tf_op jit(solution)/shard_map/pack_halo/pallas_call | solution.py:98
  8.4 0.4 collective-permute-start
  8.8 1.0 pack_lines.1
  9.8 5.6 %all-to-all-start = ((bf16[16,16,384]{2,1,0:T(8,128)(2,1)}), bf16[16,16,384]{2,1,0:T(8,128)(2,1)}, u32[]{:S(2)}, u32[]{:S(2)}) async-start(bf16[16,16,384]{2,1,0:T(8,128)(2,1)} %bitcast), calls=%async_computation | async-start | bytes 393216 | tf_op jit(solution)/shard_map/all_to_all | solution.py:175
  15.4 3.1 %collective-permute-start.1 = (bf16[2,2,128,256]{3,2,1,0:T(8,128)(2,1)}, bf16[2,2,128,256]{3,2,1,0:T(8,128)(2,1)}, u32[]{:S(2)}, u32[]{:S(2)}) collective-permute-start(bf16[2,2,128,256]{3,2,1,0:T(8,128)(2,1)} %get-tuple-element.41), channel_id=1, source_target_pairs={{1,2},{2,1},{3,4},{4,3},{5,6},{6,5},{7,8},{8,7},{9,10},{10,9},{11,... | collective-permute-start | bytes 786440 | tf_op jit(solution)/shard_map/ppermute | solution.py:36
  18.5 0.0 collective-permute-done.3.refs_3_
  18.5 0.5 collective-permute-done.2.refs_2_
  19.0 3.3 %step_0_shot_0.1 = (f32[2,4,128,256]{3,2,1,0:T(8,128)S(1)}, f32[4,128,256]{2,1,0:T(8,128)S(1)}, f32[4,128,256]{2,1,0:T(8,128)S(1)}) custom-call(f32[2,2,2,4,128,256]{5,4,3,2,1,0:T(8,128)} %refs_1_.7, f32[2,2,2,4,128,256]{5,4,3,2,1,0:T(8,128)} %refs_1_.7, bf16[2,2,128,256]{3,2,1,0:T(8,128)(2,1)S(1)} %collective-permute-done.2.refs_2_, ...), custom_call_target="tpu_custom_call" | custom-call | flops 9999999827968 | bytes 1 | tf_op jit(solution)/shard_map/step_0_shot_0/pallas_call | solution.py:443
  22.3 9.3 %all-to-all-done = bf16[16,16,384]{2,1,0:T(8,128)(2,1)} async-done(((bf16[16,16,384]{2,1,0:T(8,128)(2,1)}), bf16[16,16,384]{2,1,0:T(8,128)(2,1)}, u32[]{:S(2)}, u32[]{:S(2)}) %all-to-all-start) | async-done | bytes 196640 | tf_op jit(solution)/shard_map/all_to_all | solution.py:175
  31.6 1.2 %unpack_lines.1.saved_ref.refs_4_ = f32[128,256]{1,0:T(8,128)S(1)} custom-call(bf16[256,384]{1,0:T(8,128)(2,1)} %bitcast.1.got_ref), custom_call_target="tpu_custom_call" | custom-call | flops 1 | bytes 1 | tf_op jit(solution)/shard_map/unpack_lines/pallas_call | solution.py:176
  32.9 0.1 finish_first_0.1
  33.0 3.5 %collective-permute-start.7 = (bf16[2,2,128,256]{3,2,1,0:T(8,128)(2,1)S(1)}, bf16[2,2,128,256]{3,2,1,0:T(8,128)(2,1)S(1)}, u32[]{:S(2)}, u32[]{:S(2)}) collective-permute-start(bf16[2,2,128,256]{3,2,1,0:T(8,128)(2,1)S(1)} %get-tuple-element.51), channel_id=1, source_target_pairs={{1,2},{2,1},{3,4},{4,3},{5,6},{6,5},{7,8},{8,7},{9,10},{10,9},{11,... | collective-permute-start | bytes 786440 | tf_op jit(solution)/shard_map/ppermute | solution.py:36
  36.6 0.7 collective-permute-start.6
  37.2 0.0 collective-permute-done.1.refs_3_
  37.2 3.8 %step_0_shot_1.1 = (f32[2,4,128,256]{3,2,1,0:T(8,128)S(1)}, bf16[2,2,128,256]{3,2,1,0:T(8,128)(2,1)S(1)}, bf16[2,2,128,256]{3,2,1,0:T(8,128)(2,1)S(1)}, f32[4,128,256]{2,1,0:T(8,128)S(1)}, f32[4,128,256]{2,1,0:T(8,128)S(1)}) custom-call(f32[2,2,2,4,128,256]{5,4,3,2,1,0:T(8,128)} %refs_1_.7, f32[2,2,2,4,128,256]{5,4,3,2,1,0:T(8,128)} %refs_1_.7, ...), custom_call_target="tpu_custom_call" | custom-call | flops 1 | bytes 1 | tf_op jit(solution)/shard_map/step_0_shot_1/pallas_call | solution.py:443
  41.1 4.4 %collective-permute-start.5 = (bf16[2,2,128,256]{3,2,1,0:T(8,128)(2,1)S(1)}, bf16[2,2,128,256]{3,2,1,0:T(8,128)(2,1)S(1)}, u32[]{:S(2)}, u32[]{:S(2)}) collective-permute-start(bf16[2,2,128,256]{3,2,1,0:T(8,128)(2,1)S(1)} %get-tuple-element.47), channel_id=1, source_target_pairs={{1,2},{2,1},{3,4},{4,3},{5,6},{6,5},{7,8},{8,7},{9,10},{10,9},{11,... | collective-permute-start | bytes 786440 | tf_op jit(solution)/shard_map/ppermute | solution.py:36
  45.5 0.1 collective-permute-start.4
  45.6 0.0 collective-permute-done.7.refs_3_
  45.6 10.4 %collective-permute-done.6.refs_2_ = bf16[2,2,128,256]{3,2,1,0:T(8,128)(2,1)S(1)} collective-permute-done((bf16[2,2,128,256]{3,2,1,0:T(8,128)(2,1)S(1)}, bf16[2,2,128,256]{3,2,1,0:T(8,128)(2,1)S(1)}, u32[]{:S(2)}, u32[]{:S(2)}) %collective-permute-start.6) | collective-permute-done | bytes 262176 | tf_op jit(solution)/shard_map/ppermute | solution.py:36
  56.0 2.4 %step_1_shot_0.1 = (f32[2,4,128,256]{3,2,1,0:T(8,128)S(1)}, bf16[2,2,128,256]{3,2,1,0:T(8,128)(2,1)S(1)}, bf16[2,2,128,256]{3,2,1,0:T(8,128)(2,1)S(1)}, f32[4,128,256]{2,1,0:T(8,128)S(1)}) custom-call(f32[2,4,128,256]{3,2,1,0:T(8,128)S(1)} %get-tuple-element.50.refs_0_.refs_1_, f32[2,2,2,4,128,256]{5,4,3,2,1,0:T(8,128)} %refs_1_.7, ...), custom_call_target="tpu_custom_call" | custom-call | flops 1 | bytes 1 | tf_op jit(solution)/shard_map/step_1_shot_0/pallas_call | solution.py:443
  58.4 3.4 %collective-permute-start.11 = (bf16[2,2,128,256]{3,2,1,0:T(8,128)(2,1)S(1)}, bf16[2,2,128,256]{3,2,1,0:T(8,128)(2,1)S(1)}, u32[]{:S(2)}, u32[]{:S(2)}) collective-permute-start(bf16[2,2,128,256]{3,2,1,0:T(8,128)(2,1)S(1)} %get-tuple-element.60), channel_id=1, source_target_pairs={{1,2},{2,1},{3,4},{4,3},{5,6},{6,5},{7,8},{8,7},{9,10},{10,9},{11,... | collective-permute-start | bytes 786440 | tf_op jit(solution)/shard_map/ppermute | solution.py:36
  61.8 0.1 collective-permute-start.10
  61.9 0.0 collective-permute-done.5.refs_3_
  61.9 2.5 %step_1_shot_1.1 = (f32[2,4,128,256]{3,2,1,0:T(8,128)S(1)}, bf16[2,2,128,256]{3,2,1,0:T(8,128)(2,1)S(1)}, bf16[2,2,128,256]{3,2,1,0:T(8,128)(2,1)S(1)}, f32[4,128,256]{2,1,0:T(8,128)S(1)}) custom-call(f32[2,4,128,256]{3,2,1,0:T(8,128)S(1)} %get-tuple-element.45.refs_0_.refs_1_, f32[2,2,2,4,128,256]{5,4,3,2,1,0:T(8,128)} %refs_1_.7, ...), custom_call_target="tpu_custom_call" | custom-call | flops 1 | bytes 1 | tf_op jit(solution)/shard_map/step_1_shot_1/pallas_call | solution.py:443
  64.4 3.1 %collective-permute-start.9 = (bf16[2,2,128,256]{3,2,1,0:T(8,128)(2,1)S(1)}, bf16[2,2,128,256]{3,2,1,0:T(8,128)(2,1)S(1)}, u32[]{:S(2)}, u32[]{:S(2)}) collective-permute-start(bf16[2,2,128,256]{3,2,1,0:T(8,128)(2,1)S(1)} %get-tuple-element.57), channel_id=1, source_target_pairs={{1,2},{2,1},{3,4},{4,3},{5,6},{6,5},{7,8},{8,7},{9,10},{10,9},{11,... | collective-permute-start | bytes 786440 | tf_op jit(solution)/shard_map/ppermute | solution.py:36
  67.5 1.0 collective-permute-start.8
  68.6 0.0 collective-permute-done.11.refs_3_
  68.6 11.4 %collective-permute-done.10.refs_2_ = bf16[2,2,128,256]{3,2,1,0:T(8,128)(2,1)S(1)} collective-permute-done((bf16[2,2,128,256]{3,2,1,0:T(8,128)(2,1)S(1)}, bf16[2,2,128,256]{3,2,1,0:T(8,128)(2,1)S(1)}, u32[]{:S(2)}, u32[]{:S(2)}) %collective-permute-start.10) | collective-permute-done | bytes 262176 | tf_op jit(solution)/shard_map/ppermute | solution.py:36
  80.0 1.2 %step_2_shot_0.1 = (f32[2,4,128,256]{3,2,1,0:T(8,128)S(1)}, bf16[2,2,128,256]{3,2,1,0:T(8,128)(2,1)S(1)}, bf16[2,2,128,256]{3,2,1,0:T(8,128)(2,1)S(1)}, f32[4,128,256]{2,1,0:T(8,128)S(1)}) custom-call(f32[2,4,128,256]{3,2,1,0:T(8,128)S(1)} %get-tuple-element.59.refs_0_.refs_1_, f32[2,4,128,256]{3,2,1,0:T(8,128)S(1)} %get-tuple-element.50.refs_0_.refs_1_, ...), custom_call_target="tpu_custom_call" | custom-call | flops 1 | bytes 1 | tf_op jit(solution)/shard_map/step_2_shot_0/pallas_call | solution.py:443
  81.2 2.8 %collective-permute-start.17 = (bf16[2,2,128,256]{3,2,1,0:T(8,128)(2,1)S(1)}, bf16[2,2,128,256]{3,2,1,0:T(8,128)(2,1)S(1)}, u32[]{:S(2)}, u32[]{:S(2)}) collective-permute-start(bf16[2,2,128,256]{3,2,1,0:T(8,128)(2,1)S(1)} %get-tuple-element.70), channel_id=1, source_target_pairs={{1,2},{2,1},{3,4},{4,3},{5,6},{6,5},{7,8},{8,7},{9,10},{10,9},{11,... | collective-permute-start | bytes 786440 | tf_op jit(solution)/shard_map/ppermute | solution.py:36
  84.0 0.1 collective-permute-start.16
  84.1 0.0 collective-permute-done.9.refs_3_
  84.1 7.1 %collective-permute-done.8.refs_2_ = bf16[2,2,128,256]{3,2,1,0:T(8,128)(2,1)S(1)} collective-permute-done((bf16[2,2,128,256]{3,2,1,0:T(8,128)(2,1)S(1)}, bf16[2,2,128,256]{3,2,1,0:T(8,128)(2,1)S(1)}, u32[]{:S(2)}, u32[]{:S(2)}) %collective-permute-start.8) | collective-permute-done | bytes 262176 | tf_op jit(solution)/shard_map/ppermute | solution.py:36
  91.2 1.2 %step_2_shot_1.1 = (f32[2,4,128,256]{3,2,1,0:T(8,128)S(1)}, bf16[1,2,128,256]{3,2,1,0:T(8,128)(2,1)S(1)}, bf16[1,2,128,256]{3,2,1,0:T(8,128)(2,1)S(1)}, bf16[1,2...) custom-call(f32[2,4,128,256]{3,2,1,0:T(8,128)S(1)} %get-tuple-element.55.refs_0_.refs_, ...), custom_call_target="tpu_custom_call" | custom-call | flops 1 | bytes 1 | tf_op jit(solution)/shard_map/step_2_shot_1/pallas_call | solution.py:443
  92.4 1.9 %collective-permute-start.15 = (bf16[1,2,128,256]{3,2,1,0:T(8,128)(2,1)S(1)}, bf16[1,2,128,256]{3,2,1,0:T(8,128)(2,1)S(1)}, u32[]{:S(2)}, u32[]{:S(2)}) collective-permute-start(bf16[1,2,128,256]{3,2,1,0:T(8,128)(2,1)S(1)} %get-tuple-element.67), channel_id=1, source_target_pairs={{1,2},{2,1},{3,4},{4,3},{5,6},{6,5},{7,8},{8,7},{9,10},{10,9},{11,... | collective-permute-start | bytes 393224 | tf_op jit(solution)/shard_map/ppermute | solution.py:36
  94.4 0.1 collective-permute-start.14
  94.4 1.5 %collective-permute-start.12 = (bf16[1,2,128,256]{3,2,1,0:T(8,128)(2,1)S(1)}, bf16[1,2,128,256]{3,2,1,0:T(8,128)(2,1)S(1)}, u32[]{:S(2)}, u32[]{:S(2)}) collective-permute-start(bf16[1,2,128,256]{3,2,1,0:T(8,128)(2,1)S(1)} %get-tuple-element.64), channel_id=1, source_target_pairs={{0,1},{1,0},{2,3},{3,2},{4,5},{5,4},{6,7},{7,6},{8,9},{9,8},{10,11... | collective-permute-start | bytes 393224 | tf_op jit(solution)/shard_map/ppermute | solution.py:36
  95.9 0.0 collective-permute-done.17.refs_3_
  95.9 4.2 %collective-permute-start.13 = (bf16[1,2,128,256]{3,2,1,0:T(8,128)(2,1)S(1)}, bf16[1,2,128,256]{3,2,1,0:T(8,128)(2,1)S(1)}, u32[]{:S(2)}, u32[]{:S(2)}) collective-permute-start(bf16[1,2,128,256]{3,2,1,0:T(8,128)(2,1)S(1)} %get-tuple-element.65), channel_id=1, source_target_pairs={{1,2},{2,1},{3,4},{4,3},{5,6},{6,5},{7,8},{8,7},{9,10},{10,9},{11,... | collective-permute-start | bytes 393224 | tf_op jit(solution)/shard_map/ppermute | solution.py:36
  100.2 2.6 %step_3_shot_0.1 = (f32[2,2,2,4,128,256]{5,4,3,2,1,0:T(8,128)}, f32[4,192,256]{2,1,0:T(8,128)S(1)}) custom-call(f32[2,4,128,256]{3,2,1,0:T(8,128)S(1)} %get-tuple-element.69.refs_0_.refs_10_, f32[2,4,128,256]{3,2,1,0:T(8,128)S(1)} %get-tuple-element.59.refs_0_.refs_1_, bf16[2,2,128,256]{3,2,1,0:T(8,128)(2,1)S(1)} %collective-permute-done.16.refs_2_, ...), custom_call_target="tpu_custom_call" | custom-call | flops 1 | bytes 1 | tf_op jit(solution)/shard_map/step_3_shot_0/pallas_call | solution.py:443
  102.8 2.3 %step_3_shot_1.2 = (f32[4,128,256]{2,1,0:T(8,128)S(1)}, f32[4,192,256]{2,1,0:T(8,128)}) custom-call(f32[2,4,128,256]{3,2,1,0:T(8,128)S(1)} %get-tuple-element.63.refs_11_.refs_0_, f32[2,4,128,256]{3,2,1,0:T(8,128)S(1)} %get-tuple-element.55.refs_0_.refs_1_, bf16[1,2,128,256]{3,2,1,0:T(8,128)(2,1)S(1)} %collective-permute-done.14.refs_2_, ...), custom_call_target="tpu_custom_call" | custom-call | flops 1 | bytes 1 | tf_op jit(solution)/shard_map/step_3_shot_1/pallas_call | solution.py:443
  105.1 3.0 %collective-permute-start.18 = (f32[4,192,256]{2,1,0:T(8,128)}, f32[4,192,256]{2,1,0:T(8,128)}, u32[]{:S(2)}, u32[]{:S(2)}) collective-permute-start(f32[4,192,256]{2,1,0:T(8,128)} %get-tuple-element.74.refs_7_.own_ref), channel_id=1, source_target_pairs={{0,16},{16,0},{1,17},{17,1},{2,18},{18,2},{3,19},{19,3},{4,20},{20... | collective-permute-start | bytes 2359304 | tf_op jit(solution)/shard_map/ppermute | solution.py:563
  108.1 1.4 %step_3_shot_1.3.after_ref = f32[2,2,2,4,128,256]{5,4,3,2,1,0:T(8,128)} custom-call(f32[2,4,128,256]{3,2,1,0:T(8,128)S(1)} %get-tuple-element.63.refs_11_.refs_0_, f32[2,4,128,256]{3,2,1,0:T(8,128)S(1)} %get-tuple-element.55.refs_0_.refs_1_, bf16[1,2,128,256]{3,2,1,0:T(8,128)(2,1)S(1)} %collective-permute-done.12.refs_2_, ...), custom_call_target="tpu_custom_call", output_to_operand_aliasing={{}: (8, {})} | custom-call | flops 9999999827968 | bytes 1 | tf_op jit(solution)/shard_map/step_3_shot_1/pallas_call | solution.py:443
  109.5 0.9 collective-permute-done.18.other_ref
  110.4 2.3 %sum_frames.1 = f32[4,192,256]{2,1,0:T(8,128)} custom-call(f32[4,192,256]{2,1,0:T(8,128)} %get-tuple-element.74.refs_7_.own_ref, f32[4,192,256]{2,1,0:T(8,128)} %collective-permute-done.18.other_ref, f32[2,2,2,4,128,256]{5,4,3,2,1,0:T(8,128)} %step_3_shot_1.3.after_ref), custom_call_target="tpu_custom_call" | custom-call | flops 1 | bytes 1 | tf_op jit(solution)/shard_map/sum_frames/pallas_call | solution.py:474
  (19 shorter events, 0.0 us)
Async XLA Ops:
  0.6 8.2 %copy-start.5 = (s32[2,128]{1,0:T(2,128)S(1)}, s32[2,128]{1,0:T(2,128)}, u32[]{:S(2)}) copy-start(s32[2,128]{1,0:T(2,128)} %ids_ref.1) | copy-start | bytes 3076
  0.6 8.2 %copy-start.2 = (bf16[2,128,256]{2,1,0:T(8,128)(2,1)S(1)}, bf16[2,128,256]{2,1,0:T(8,128)(2,1)}, u32[]{:S(2)}) copy-start(bf16[2,128,256]{2,1,0:T(8,128)(2,1)} %lines_ref.1) | copy-start | bytes 393220
  0.7 18.3 %copy-start.1 = (f32[2,4,64]{2,1,0:T(4,128)S(1)}, f32[2,4,64]{2,1,0:T(4,128)}, u32[]{:S(2)}) copy-start(f32[2,4,64]{2,1,0:T(4,128)} %refs_5_.15) | copy-start | bytes 6148
  0.7 18.3 %copy-start.3 = (s32[2,64]{1,0:T(2,128)S(1)}, s32[2,64]{1,0:T(2,128)}, u32[]{:S(2)}) copy-start(s32[2,64]{1,0:T(2,128)} %refs_4_.3) | copy-start | bytes 1540
  0.7 18.3 %copy-start.4 = (s32[2]{0:T(128)S(1)}, s32[2]{0:T(128)}, u32[]{:S(2)}) copy-start(s32[2]{0:T(128)} %refs_6_.15) | copy-start | bytes 28
  0.7 18.3 %copy-start = (f32[4,192,256]{2,1,0:T(8,128)S(1)}, f32[4,192,256]{2,1,0:T(8,128)}, u32[]{:S(2)}) copy-start(f32[4,192,256]{2,1,0:T(8,128)} %refs_8_.1) | copy-start | bytes 2359300
  2.0 16.4 %collective-permute-start.3 = (bf16[2,2,128,256]{3,2,1,0:T(8,128)(2,1)S(1)}, bf16[2,2,128,256]{3,2,1,0:T(8,128)(2,1)S(1)}, u32[]{:S(2)}, u32[]{:S(2)}) collective-permute-start(bf16[2,2,128,256]{3,2,1,0:T(8,128)(2,1)S(1)} %get-tuple-element.42), channel_id=1, source_target_pairs={{1,2},{2,1},{3,4},{4,3},{5,6},{6,5},{7,8},{8,7},{9,10},{10,9},{11,... | collective-permute-start | bytes 786440 | tf_op jit(solution)/shard_map/ppermute | solution.py:36
  5.2 13.8 %collective-permute-start.2 = (bf16[2,2,128,256]{3,2,1,0:T(8,128)(2,1)S(1)}, bf16[2,2,128,256]{3,2,1,0:T(8,128)(2,1)S(1)}, u32[]{:S(2)}, u32[]{:S(2)}) collective-permute-start(bf16[2,2,128,256]{3,2,1,0:T(8,128)(2,1)S(1)} %get-tuple-element.39.refs_0_), channel_id=1, source_target_pairs={{0,1},{1,0},{2,3},{3,2},{4,5},{5,4},{6,7},{7,6},{8,9},{9,8},{10,11... | collective-permute-start | bytes 786440 | tf_op jit(solution)/shard_map/ppermute | solution.py:36
  8.4 28.9 %collective-permute-start = (bf16[2,2,128,256]{3,2,1,0:T(8,128)(2,1)}, bf16[2,2,128,256]{3,2,1,0:T(8,128)(2,1)}, u32[]{:S(2)}, u32[]{:S(2)}) collective-permute-start(bf16[2,2,128,256]{3,2,1,0:T(8,128)(2,1)} %get-tuple-element.40.after_ref), channel_id=1, source_target_pairs={{0,1},{1,0},{2,3},{3,2},{4,5},{5,4},{6,7},{7,6},{8,9},{9,8},{10,11... | collective-permute-start | bytes 786440 | tf_op jit(solution)/shard_map/ppermute | solution.py:36
  9.8 21.8 %all-to-all-start = ((bf16[16,16,384]{2,1,0:T(8,128)(2,1)}), bf16[16,16,384]{2,1,0:T(8,128)(2,1)}, u32[]{:S(2)}, u32[]{:S(2)}) async-start(bf16[16,16,384]{2,1,0:T(8,128)(2,1)} %bitcast), calls=%async_computation | async-start | bytes 393216 | tf_op jit(solution)/shard_map/all_to_all | solution.py:175
  15.4 21.8 %collective-permute-start.1 = (bf16[2,2,128,256]{3,2,1,0:T(8,128)(2,1)}, bf16[2,2,128,256]{3,2,1,0:T(8,128)(2,1)}, u32[]{:S(2)}, u32[]{:S(2)}) collective-permute-start(bf16[2,2,128,256]{3,2,1,0:T(8,128)(2,1)} %get-tuple-element.41), channel_id=1, source_target_pairs={{1,2},{2,1},{3,4},{4,3},{5,6},{6,5},{7,8},{8,7},{9,10},{10,9},{11,... | collective-permute-start | bytes 786440 | tf_op jit(solution)/shard_map/ppermute | solution.py:36
  33.0 12.6 %collective-permute-start.7 = (bf16[2,2,128,256]{3,2,1,0:T(8,128)(2,1)S(1)}, bf16[2,2,128,256]{3,2,1,0:T(8,128)(2,1)S(1)}, u32[]{:S(2)}, u32[]{:S(2)}) collective-permute-start(bf16[2,2,128,256]{3,2,1,0:T(8,128)(2,1)S(1)} %get-tuple-element.51), channel_id=1, source_target_pairs={{1,2},{2,1},{3,4},{4,3},{5,6},{6,5},{7,8},{8,7},{9,10},{10,9},{11,... | collective-permute-start | bytes 786440 | tf_op jit(solution)/shard_map/ppermute | solution.py:36
  36.6 19.5 %collective-permute-start.6 = (bf16[2,2,128,256]{3,2,1,0:T(8,128)(2,1)S(1)}, bf16[2,2,128,256]{3,2,1,0:T(8,128)(2,1)S(1)}, u32[]{:S(2)}, u32[]{:S(2)}) collective-permute-start(bf16[2,2,128,256]{3,2,1,0:T(8,128)(2,1)S(1)} %get-tuple-element.44.refs_9_), channel_id=1, source_target_pairs={{0,1},{1,0},{2,3},{3,2},{4,5},{5,4},{6,7},{7,6},{8,9},{9,8},{10,11... | collective-permute-start | bytes 786440 | tf_op jit(solution)/shard_map/ppermute | solution.py:36
  41.1 20.9 %collective-permute-start.5 = (bf16[2,2,128,256]{3,2,1,0:T(8,128)(2,1)S(1)}, bf16[2,2,128,256]{3,2,1,0:T(8,128)(2,1)S(1)}, u32[]{:S(2)}, u32[]{:S(2)}) collective-permute-start(bf16[2,2,128,256]{3,2,1,0:T(8,128)(2,1)S(1)} %get-tuple-element.47), channel_id=1, source_target_pairs={{1,2},{2,1},{3,4},{4,3},{5,6},{6,5},{7,8},{8,7},{9,10},{10,9},{11,... | collective-permute-start | bytes 786440 | tf_op jit(solution)/shard_map/ppermute | solution.py:36
  45.5 16.4 %collective-permute-start.4 = (bf16[2,2,128,256]{3,2,1,0:T(8,128)(2,1)S(1)}, bf16[2,2,128,256]{3,2,1,0:T(8,128)(2,1)S(1)}, u32[]{:S(2)}, u32[]{:S(2)}) collective-permute-start(bf16[2,2,128,256]{3,2,1,0:T(8,128)(2,1)S(1)} %get-tuple-element.46.refs_9_), channel_id=1, source_target_pairs={{0,1},{1,0},{2,3},{3,2},{4,5},{5,4},{6,7},{7,6},{8,9},{9,8},{10,11... | collective-permute-start | bytes 786440 | tf_op jit(solution)/shard_map/ppermute | solution.py:36
  58.4 10.2 %collective-permute-start.11 = (bf16[2,2,128,256]{3,2,1,0:T(8,128)(2,1)S(1)}, bf16[2,2,128,256]{3,2,1,0:T(8,128)(2,1)S(1)}, u32[]{:S(2)}, u32[]{:S(2)}) collective-permute-start(bf16[2,2,128,256]{3,2,1,0:T(8,128)(2,1)S(1)} %get-tuple-element.60), channel_id=1, source_target_pairs={{1,2},{2,1},{3,4},{4,3},{5,6},{6,5},{7,8},{8,7},{9,10},{10,9},{11,... | collective-permute-start | bytes 786440 | tf_op jit(solution)/shard_map/ppermute | solution.py:36
  61.8 18.1 %collective-permute-start.10 = (bf16[2,2,128,256]{3,2,1,0:T(8,128)(2,1)S(1)}, bf16[2,2,128,256]{3,2,1,0:T(8,128)(2,1)S(1)}, u32[]{:S(2)}, u32[]{:S(2)}) collective-permute-start(bf16[2,2,128,256]{3,2,1,0:T(8,128)(2,1)S(1)} %get-tuple-element.54.refs_9_), channel_id=1, source_target_pairs={{0,1},{1,0},{2,3},{3,2},{4,5},{5,4},{6,7},{7,6},{8,9},{9,8},{10,11... | collective-permute-start | bytes 786440 | tf_op jit(solution)/shard_map/ppermute | solution.py:36
  64.4 19.7 %collective-permute-start.9 = (bf16[2,2,128,256]{3,2,1,0:T(8,128)(2,1)S(1)}, bf16[2,2,128,256]{3,2,1,0:T(8,128)(2,1)S(1)}, u32[]{:S(2)}, u32[]{:S(2)}) collective-permute-start(bf16[2,2,128,256]{3,2,1,0:T(8,128)(2,1)S(1)} %get-tuple-element.57), channel_id=1, source_target_pairs={{1,2},{2,1},{3,4},{4,3},{5,6},{6,5},{7,8},{8,7},{9,10},{10,9},{11,... | collective-permute-start | bytes 786440 | tf_op jit(solution)/shard_map/ppermute | solution.py:36
  67.5 23.7 %collective-permute-start.8 = (bf16[2,2,128,256]{3,2,1,0:T(8,128)(2,1)S(1)}, bf16[2,2,128,256]{3,2,1,0:T(8,128)(2,1)S(1)}, u32[]{:S(2)}, u32[]{:S(2)}) collective-permute-start(bf16[2,2,128,256]{3,2,1,0:T(8,128)(2,1)S(1)} %get-tuple-element.56.refs_9_), channel_id=1, source_target_pairs={{0,1},{1,0},{2,3},{3,2},{4,5},{5,4},{6,7},{7,6},{8,9},{9,8},{10,11... | collective-permute-start | bytes 786440 | tf_op jit(solution)/shard_map/ppermute | solution.py:36
  81.2 14.7 %collective-permute-start.17 = (bf16[2,2,128,256]{3,2,1,0:T(8,128)(2,1)S(1)}, bf16[2,2,128,256]{3,2,1,0:T(8,128)(2,1)S(1)}, u32[]{:S(2)}, u32[]{:S(2)}) collective-permute-start(bf16[2,2,128,256]{3,2,1,0:T(8,128)(2,1)S(1)} %get-tuple-element.70), channel_id=1, source_target_pairs={{1,2},{2,1},{3,4},{4,3},{5,6},{6,5},{7,8},{8,7},{9,10},{10,9},{11,... | collective-permute-start | bytes 786440 | tf_op jit(solution)/shard_map/ppermute | solution.py:36
  84.0 16.2 %collective-permute-start.16 = (bf16[2,2,128,256]{3,2,1,0:T(8,128)(2,1)S(1)}, bf16[2,2,128,256]{3,2,1,0:T(8,128)(2,1)S(1)}, u32[]{:S(2)}, u32[]{:S(2)}) collective-permute-start(bf16[2,2,128,256]{3,2,1,0:T(8,128)(2,1)S(1)} %get-tuple-element.62.refs_9_), channel_id=1, source_target_pairs={{0,1},{1,0},{2,3},{3,2},{4,5},{5,4},{6,7},{7,6},{8,9},{9,8},{10,11... | collective-permute-start | bytes 786440 | tf_op jit(solution)/shard_map/ppermute | solution.py:36
  92.4 10.3 %collective-permute-start.15 = (bf16[1,2,128,256]{3,2,1,0:T(8,128)(2,1)S(1)}, bf16[1,2,128,256]{3,2,1,0:T(8,128)(2,1)S(1)}, u32[]{:S(2)}, u32[]{:S(2)}) collective-permute-start(bf16[1,2,128,256]{3,2,1,0:T(8,128)(2,1)S(1)} %get-tuple-element.67), channel_id=1, source_target_pairs={{1,2},{2,1},{3,4},{4,3},{5,6},{6,5},{7,8},{8,7},{9,10},{10,9},{11,... | collective-permute-start | bytes 393224 | tf_op jit(solution)/shard_map/ppermute | solution.py:36
  94.4 8.4 %collective-permute-start.14 = (bf16[1,2,128,256]{3,2,1,0:T(8,128)(2,1)S(1)}, bf16[1,2,128,256]{3,2,1,0:T(8,128)(2,1)S(1)}, u32[]{:S(2)}, u32[]{:S(2)}) collective-permute-start(bf16[1,2,128,256]{3,2,1,0:T(8,128)(2,1)S(1)} %get-tuple-element.66.refs_12_), channel_id=1, source_target_pairs={{0,1},{1,0},{2,3},{3,2},{4,5},{5,4},{6,7},{7,6},{8,9},{9,8},{10,11... | collective-permute-start | bytes 393224 | tf_op jit(solution)/shard_map/ppermute | solution.py:36
  94.4 13.7 %collective-permute-start.12 = (bf16[1,2,128,256]{3,2,1,0:T(8,128)(2,1)S(1)}, bf16[1,2,128,256]{3,2,1,0:T(8,128)(2,1)S(1)}, u32[]{:S(2)}, u32[]{:S(2)}) collective-permute-start(bf16[1,2,128,256]{3,2,1,0:T(8,128)(2,1)S(1)} %get-tuple-element.64), channel_id=1, source_target_pairs={{0,1},{1,0},{2,3},{3,2},{4,5},{5,4},{6,7},{7,6},{8,9},{9,8},{10,11... | collective-permute-start | bytes 393224 | tf_op jit(solution)/shard_map/ppermute | solution.py:36
  95.9 12.2 %collective-permute-start.13 = (bf16[1,2,128,256]{3,2,1,0:T(8,128)(2,1)S(1)}, bf16[1,2,128,256]{3,2,1,0:T(8,128)(2,1)S(1)}, u32[]{:S(2)}, u32[]{:S(2)}) collective-permute-start(bf16[1,2,128,256]{3,2,1,0:T(8,128)(2,1)S(1)} %get-tuple-element.65), channel_id=1, source_target_pairs={{1,2},{2,1},{3,4},{4,3},{5,6},{6,5},{7,8},{8,7},{9,10},{10,9},{11,... | collective-permute-start | bytes 393224 | tf_op jit(solution)/shard_map/ppermute | solution.py:36
  105.1 5.3 %collective-permute-start.18 = (f32[4,192,256]{2,1,0:T(8,128)}, f32[4,192,256]{2,1,0:T(8,128)}, u32[]{:S(2)}, u32[]{:S(2)}) collective-permute-start(f32[4,192,256]{2,1,0:T(8,128)} %get-tuple-element.74.refs_7_.own_ref), channel_id=1, source_target_pairs={{0,16},{16,0},{1,17},{17,1},{2,18},{18,2},{3,19},{19,3},{4,20},{20... | collective-permute-start | bytes 2359304 | tf_op jit(solution)/shard_map/ppermute | solution.py:563

commit v5 on v4

--- a/solution.py
+++ b/solution.py
@@ -54,12 +54,22 @@
     return pl.multiple_of(start, 8), offset - start
 
 
-def add_window(target_ref, lead, part, offset):
-    rows_y = part.shape[0]
-    start, gap = window_at(offset, target_ref.shape[-2], rows_y)
-    moved = jnp.concatenate([part, jnp.zeros((8, part.shape[1]), part.dtype)], axis=0)
-    at = lead + (pl.ds(start, rows_y + 8), slice(None))
-    target_ref[at] = target_ref[at] + pltpu.roll(moved, gap, 0)
+def add_window(target_ref, layer, part, offset):
+    rows_y, cells_z = part.shape
+    groups = rows_y // 8
+    start = pl.multiple_of(lax.div(offset, 8) * 8, 8)
+    gap = lax.rem(offset, 8)
+    turned = pltpu.roll(part.reshape(groups, 8, cells_z), gap, 1)
+    before = lax.broadcasted_iota(jnp.int32, (8, cells_z), 0) < gap
+    body = [jnp.where(before, 0.0, turned[0])]
+    body += [jnp.where(before, turned[at - 1], turned[at]) for at in range(1, groups)]
+    at = pl.ds(start, rows_y)
+    target_ref[layer, at, :] = target_ref[layer, at, :] + jnp.concatenate(body, axis=0)
+
+    @pl.when(gap > 0)
+    def _():
+        rest = pl.ds(pl.multiple_of(start + rows_y, 8), 8)
+        target_ref[layer, rest, :] = target_ref[layer, rest, :] + jnp.where(before, turned[-1], 0.0)
 
 
 def is_odd():
@@ -348,7 +358,7 @@
                         contrib_ref[layer] = jnp.zeros_like(contrib_ref[layer])
                     else:
                         contrib_ref[layer] = frame_from[layer]
-                    add_window(contrib_ref, (layer,), term, offsets_ref[shot])
+                    add_window(contrib_ref, layer, term, offsets_ref[shot])
                 else:
                     contrib_ref[layer] = term
             elif lines:
@@ -503,11 +513,10 @@
 
     sends = pack_halo(wavefields, 0, [])
     got = [exchange(sends)]
-    for shot in range(1, shots):
-        sends = pack_halo(wavefields, shot, [sends[0]])
-        got.append(exchange(sends))
     message = pack_lines(strip_lines, strip_ids, per_owner, cap, sends[0])
     saved = deliver(message, cap, shots, per_owner)
+    for shot in range(1, shots):
+        got.append(exchange(pack_halo(wavefields, shot, [message])))
     groups = [BOTH] * shots
     now = [wavefields] * shots
     later = [wavefields] * shots

time: 113 us -> 109 us (0.965)
  waiting for transfers between devices: 39.7 us -> 36.5 us
  starting transfers between devices: 43.3 us -> 41.4 us
    all_to_all x1, waiting for transfers between devices: 9.33 us -> 0.01 us  [deliver(): got = lax.all_to_all(message, 'space', 0, 0, tiled=False)]
    ppermute x18, waiting for transfers between devices: 29.5 us -> 35.6 us  [swap_pairs(): return lax.ppermute(value, 'space', routes)]
    ppermute x1, starting transfers between devices: 3.03 us -> 0.6 us  [body(): other = lax.ppermute(frame, 'shot', [(0, 1), (1, 0)])]
  transfers between devices with their start and end apart: 20 -> 20, of which waited for: 6 -> 8; matrix products, arithmetic and copies ran while one was open for 0% -> 0% of each run, Pallas kernels for 22% -> 24%
where the time goes in v5:
time: 109 us; the launch traced here: 108 us
  starting transfers between devices  41.4 us (38%)
  waiting for transfers between devices  36.5 us (33%)
  Pallas kernels  29.7 us (27%)
    ppermute x18, waiting for transfers between devices, swap_pairs(): return lax.ppermute(value, 'space', routes)  35.6 us
    ppermute x18, starting transfers between devices, swap_pairs(): return lax.ppermute(value, 'space', routes)  35.1 us
    pallas_call x9, Pallas kernels, one_step(): pl.pallas_call(functools.partial(step_kernel, shot, step, comps, got_grou...  21.6 us
    all_to_all x1, starting transfers between devices, deliver(): got = lax.all_to_all(message, 'space', 0, 0, tiled=False)  5.63 us
    pallas_call x2, Pallas kernels, pack_halo(): pl.pallas_call(functools.partial(pack_kernel, shot), in_specs=[pl.BlockSp...  3.37 us
    pallas_call x1, Pallas kernels, sum_frames(): pl.pallas_call(functools.partial(sum_kernel, scale), in_specs=[vmem, vmem...  2.29 us
  transfers between devices with their start and end apart: 20, of which 8 were waited for; matrix products, arithmetic and copies ran while one was open for 0% of the time, Pallas kernels for 24%

profile of v5, /device:TPU:19, one launch (start us, length us, event | category | flops | bytes accessed | tf_op | source)
XLA Modules:
  0.0 108.5 jit_solution(1333097414235729156)
XLA Ops:
  0.7 1.3 %pack_halo.2 = (bf16[2,2,128,256]{3,2,1,0:T(8,128)(2,1)S(1)}, bf16[2,2,128,256]{3,2,1,0:T(8,128)(2,1)S(1)}) custom-call(f32[2,2,2,4,128,256]{5,4,3,2,1,0:T(8,128)} %refs_1_.7), custom_call_target="tpu_custom_call" | custom-call | flops 1 | bytes 1 | tf_op jit(solution)/shard_map/pack_halo/pallas_call | solution.py:108
  2.0 3.1 %collective-permute-start.3 = (bf16[2,2,128,256]{3,2,1,0:T(8,128)(2,1)S(1)}, bf16[2,2,128,256]{3,2,1,0:T(8,128)(2,1)S(1)}, u32[]{:S(2)}, u32[]{:S(2)}) collective-permute-start(bf16[2,2,128,256]{3,2,1,0:T(8,128)(2,1)S(1)} %get-tuple-element.42), channel_id=1, source_target_pairs={{1,2},{2,1},{3,4},{4,3},{5,6},{6,5},{7,8},{8,7},{9,10},{10,9},{11,... | collective-permute-start | bytes 786440 | tf_op jit(solution)/shard_map/ppermute | solution.py:36
  5.2 1.2 %collective-permute-start.2 = (bf16[2,2,128,256]{3,2,1,0:T(8,128)(2,1)S(1)}, bf16[2,2,128,256]{3,2,1,0:T(8,128)(2,1)S(1)}, u32[]{:S(2)}, u32[]{:S(2)}) collective-permute-start(bf16[2,2,128,256]{3,2,1,0:T(8,128)(2,1)S(1)} %get-tuple-element.39.after_ref), channel_id=1, source_target_pairs={{0,1},{1,0},{2,3},{3,2},{4,5},{5,4},{6,7},{7,6},{8,9},{9,8},{10,11... | collective-permute-start | bytes 786440 | tf_op jit(solution)/shard_map/ppermute | solution.py:36
  6.3 1.0 pack_lines.1.refs_0_
  7.3 5.6 %all-to-all-start = ((bf16[16,16,384]{2,1,0:T(8,128)(2,1)}), bf16[16,16,384]{2,1,0:T(8,128)(2,1)}, u32[]{:S(2)}, u32[]{:S(2)}) async-start(bf16[16,16,384]{2,1,0:T(8,128)(2,1)} %bitcast), calls=%async_computation | async-start | bytes 393216 | tf_op jit(solution)/shard_map/all_to_all | solution.py:185
  13.0 2.0 %pack_halo.3 = (bf16[2,2,128,256]{3,2,1,0:T(8,128)(2,1)}, bf16[2,2,128,256]{3,2,1,0:T(8,128)(2,1)}) custom-call(f32[2,2,2,4,128,256]{5,4,3,2,1,0:T(8,128)} %refs_1_.7, bf16[256,384]{1,0:T(8,128)(2,1)} %pack_lines.1.refs_0_), custom_call_target="tpu_custom_call" | custom-call | flops 1 | bytes 1 | tf_op jit(solution)/shard_map/pack_halo/pallas_call | solution.py:108
  15.0 0.3 collective-permute-start
  15.4 4.0 %collective-permute-start.1 = (bf16[2,2,128,256]{3,2,1,0:T(8,128)(2,1)}, bf16[2,2,128,256]{3,2,1,0:T(8,128)(2,1)}, u32[]{:S(2)}, u32[]{:S(2)}) collective-permute-start(bf16[2,2,128,256]{3,2,1,0:T(8,128)(2,1)} %get-tuple-element.41), channel_id=1, source_target_pairs={{1,2},{2,1},{3,4},{4,3},{5,6},{6,5},{7,8},{8,7},{9,10},{10,9},{11,... | collective-permute-start | bytes 786440 | tf_op jit(solution)/shard_map/ppermute | solution.py:36
  19.4 0.7 collective-permute-done.2.refs_2_
  20.1 3.3 %step_0_shot_0.1 = (f32[2,4,128,256]{3,2,1,0:T(8,128)S(1)}, f32[4,128,256]{2,1,0:T(8,128)S(1)}, f32[4,128,256]{2,1,0:T(8,128)S(1)}) custom-call(f32[2,2,2,4,128,256]{5,4,3,2,1,0:T(8,128)} %refs_1_.7, f32[2,2,2,4,128,256]{5,4,3,2,1,0:T(8,128)} %refs_1_.7, bf16[2,2,128,256]{3,2,1,0:T(8,128)(2,1)S(1)} %collective-permute-done.2.refs_2_, ...), custom_call_target="tpu_custom_call" | custom-call | flops 9999999827968 | bytes 1 | tf_op jit(solution)/shard_map/step_0_shot_0/pallas_call | solution.py:453
  23.4 0.0 all-to-all-done
  23.4 1.2 %unpack_lines.1.saved_ref.refs_4_ = f32[128,256]{1,0:T(8,128)S(1)} custom-call(bf16[256,384]{1,0:T(8,128)(2,1)} %bitcast.1.got_ref), custom_call_target="tpu_custom_call" | custom-call | flops 1 | bytes 1 | tf_op jit(solution)/shard_map/unpack_lines/pallas_call | solution.py:186
  24.6 0.1 finish_first_0.1
  24.7 3.3 %collective-permute-start.7 = (bf16[2,2,128,256]{3,2,1,0:T(8,128)(2,1)S(1)}, bf16[2,2,128,256]{3,2,1,0:T(8,128)(2,1)S(1)}, u32[]{:S(2)}, u32[]{:S(2)}) collective-permute-start(bf16[2,2,128,256]{3,2,1,0:T(8,128)(2,1)S(1)} %get-tuple-element.51), channel_id=1, source_target_pairs={{1,2},{2,1},{3,4},{4,3},{5,6},{6,5},{7,8},{8,7},{9,10},{10,9},{11,... | collective-permute-start | bytes 786440 | tf_op jit(solution)/shard_map/ppermute | solution.py:36
  28.0 0.4 collective-permute-start.6
  28.4 9.1 %collective-permute-done.refs_2_ = bf16[2,2,128,256]{3,2,1,0:T(8,128)(2,1)} collective-permute-done((bf16[2,2,128,256]{3,2,1,0:T(8,128)(2,1)}, bf16[2,2,128,256]{3,2,1,0:T(8,128)(2,1)}, u32[]{:S(2)}, u32[]{:S(2)}) %collective-permute-start) | collective-permute-done | bytes 262176 | tf_op jit(solution)/shard_map/ppermute | solution.py:36
  37.5 0.0 collective-permute-done.1.refs_3_
  37.5 3.8 %step_0_shot_1.1 = (f32[2,4,128,256]{3,2,1,0:T(8,128)S(1)}, bf16[2,2,128,256]{3,2,1,0:T(8,128)(2,1)S(1)}, bf16[2,2,128,256]{3,2,1,0:T(8,128)(2,1)S(1)}, f32[4,128,256]{2,1,0:T(8,128)S(1)}, f32[4,128,256]{2,1,0:T(8,128)S(1)}) custom-call(f32[2,2,2,4,128,256]{5,4,3,2,1,0:T(8,128)} %refs_1_.7, f32[2,2,2,4,128,256]{5,4,3,2,1,0:T(8,128)} %refs_1_.7, ...), custom_call_target="tpu_custom_call" | custom-call | flops 1 | bytes 1 | tf_op jit(solution)/shard_map/step_0_shot_1/pallas_call | solution.py:453
  41.4 3.3 %collective-permute-start.5 = (bf16[2,2,128,256]{3,2,1,0:T(8,128)(2,1)S(1)}, bf16[2,2,128,256]{3,2,1,0:T(8,128)(2,1)S(1)}, u32[]{:S(2)}, u32[]{:S(2)}) collective-permute-start(bf16[2,2,128,256]{3,2,1,0:T(8,128)(2,1)S(1)} %get-tuple-element.47), channel_id=1, source_target_pairs={{1,2},{2,1},{3,4},{4,3},{5,6},{6,5},{7,8},{8,7},{9,10},{10,9},{11,... | collective-permute-start | bytes 786440 | tf_op jit(solution)/shard_map/ppermute | solution.py:36
  44.6 0.1 collective-permute-start.4
  44.7 0.0 collective-permute-done.6.refs_2_
  44.7 2.4 %step_1_shot_0.1 = (f32[2,4,128,256]{3,2,1,0:T(8,128)S(1)}, bf16[2,2,128,256]{3,2,1,0:T(8,128)(2,1)S(1)}, bf16[2,2,128,256]{3,2,1,0:T(8,128)(2,1)S(1)}, f32[4,128,256]{2,1,0:T(8,128)S(1)}) custom-call(f32[2,4,128,256]{3,2,1,0:T(8,128)S(1)} %get-tuple-element.50.refs_0_.refs_1_, f32[2,2,2,4,128,256]{5,4,3,2,1,0:T(8,128)} %refs_1_.7, ...), custom_call_target="tpu_custom_call" | custom-call | flops 1 | bytes 1 | tf_op jit(solution)/shard_map/step_1_shot_0/pallas_call | solution.py:453
  47.1 2.9 %collective-permute-start.11 = (bf16[2,2,128,256]{3,2,1,0:T(8,128)(2,1)S(1)}, bf16[2,2,128,256]{3,2,1,0:T(8,128)(2,1)S(1)}, u32[]{:S(2)}, u32[]{:S(2)}) collective-permute-start(bf16[2,2,128,256]{3,2,1,0:T(8,128)(2,1)S(1)} %get-tuple-element.60), channel_id=1, source_target_pairs={{1,2},{2,1},{3,4},{4,3},{5,6},{6,5},{7,8},{8,7},{9,10},{10,9},{11,... | collective-permute-start | bytes 786440 | tf_op jit(solution)/shard_map/ppermute | solution.py:36
  50.0 1.4 %collective-permute-start.10 = (bf16[2,2,128,256]{3,2,1,0:T(8,128)(2,1)S(1)}, bf16[2,2,128,256]{3,2,1,0:T(8,128)(2,1)S(1)}, u32[]{:S(2)}, u32[]{:S(2)}) collective-permute-start(bf16[2,2,128,256]{3,2,1,0:T(8,128)(2,1)S(1)} %get-tuple-element.54.refs_9_), channel_id=1, source_target_pairs={{0,1},{1,0},{2,3},{3,2},{4,5},{5,4},{6,7},{7,6},{8,9},{9,8},{10,11... | collective-permute-start | bytes 786440 | tf_op jit(solution)/shard_map/ppermute | solution.py:36
  51.4 0.0 collective-permute-done.5.refs_3_
  51.4 11.3 %collective-permute-done.4.refs_2_ = bf16[2,2,128,256]{3,2,1,0:T(8,128)(2,1)S(1)} collective-permute-done((bf16[2,2,128,256]{3,2,1,0:T(8,128)(2,1)S(1)}, bf16[2,2,128,256]{3,2,1,0:T(8,128)(2,1)S(1)}, u32[]{:S(2)}, u32[]{:S(2)}) %collective-permute-start.4) | collective-permute-done | bytes 262176 | tf_op jit(solution)/shard_map/ppermute | solution.py:36
  62.8 2.5 %step_1_shot_1.1 = (f32[2,4,128,256]{3,2,1,0:T(8,128)S(1)}, bf16[2,2,128,256]{3,2,1,0:T(8,128)(2,1)S(1)}, bf16[2,2,128,256]{3,2,1,0:T(8,128)(2,1)S(1)}, f32[4,128,256]{2,1,0:T(8,128)S(1)}) custom-call(f32[2,4,128,256]{3,2,1,0:T(8,128)S(1)} %get-tuple-element.45.refs_0_.refs_1_, f32[2,2,2,4,128,256]{5,4,3,2,1,0:T(8,128)} %refs_1_.7, ...), custom_call_target="tpu_custom_call" | custom-call | flops 1 | bytes 1 | tf_op jit(solution)/shard_map/step_1_shot_1/pallas_call | solution.py:453
  65.3 2.9 %collective-permute-start.9 = (bf16[2,2,128,256]{3,2,1,0:T(8,128)(2,1)S(1)}, bf16[2,2,128,256]{3,2,1,0:T(8,128)(2,1)S(1)}, u32[]{:S(2)}, u32[]{:S(2)}) collective-permute-start(bf16[2,2,128,256]{3,2,1,0:T(8,128)(2,1)S(1)} %get-tuple-element.57), channel_id=1, source_target_pairs={{1,2},{2,1},{3,4},{4,3},{5,6},{6,5},{7,8},{8,7},{9,10},{10,9},{11,... | collective-permute-start | bytes 786440 | tf_op jit(solution)/shard_map/ppermute | solution.py:36
  68.2 0.1 collective-permute-start.8
  68.3 0.1 collective-permute-done.10.refs_2_
  68.4 1.2 %step_2_shot_0.1 = (f32[2,4,128,256]{3,2,1,0:T(8,128)S(1)}, bf16[2,2,128,256]{3,2,1,0:T(8,128)(2,1)S(1)}, bf16[2,2,128,256]{3,2,1,0:T(8,128)(2,1)S(1)}, f32[4,128,256]{2,1,0:T(8,128)S(1)}) custom-call(f32[2,4,128,256]{3,2,1,0:T(8,128)S(1)} %get-tuple-element.59.refs_0_.refs_1_, f32[2,4,128,256]{3,2,1,0:T(8,128)S(1)} %get-tuple-element.50.refs_0_.refs_1_, ...), custom_call_target="tpu_custom_call" | custom-call | flops 1 | bytes 1 | tf_op jit(solution)/shard_map/step_2_shot_0/pallas_call | solution.py:453
  69.6 3.1 %collective-permute-start.17 = (bf16[2,2,128,256]{3,2,1,0:T(8,128)(2,1)S(1)}, bf16[2,2,128,256]{3,2,1,0:T(8,128)(2,1)S(1)}, u32[]{:S(2)}, u32[]{:S(2)}) collective-permute-start(bf16[2,2,128,256]{3,2,1,0:T(8,128)(2,1)S(1)} %get-tuple-element.70), channel_id=1, source_target_pairs={{1,2},{2,1},{3,4},{4,3},{5,6},{6,5},{7,8},{8,7},{9,10},{10,9},{11,... | collective-permute-start | bytes 786440 | tf_op jit(solution)/shard_map/ppermute | solution.py:36
  72.8 1.4 %collective-permute-start.16 = (bf16[2,2,128,256]{3,2,1,0:T(8,128)(2,1)S(1)}, bf16[2,2,128,256]{3,2,1,0:T(8,128)(2,1)S(1)}, u32[]{:S(2)}, u32[]{:S(2)}) collective-permute-start(bf16[2,2,128,256]{3,2,1,0:T(8,128)(2,1)S(1)} %get-tuple-element.62.refs_9_), channel_id=1, source_target_pairs={{0,1},{1,0},{2,3},{3,2},{4,5},{5,4},{6,7},{7,6},{8,9},{9,8},{10,11... | collective-permute-start | bytes 786440 | tf_op jit(solution)/shard_map/ppermute | solution.py:36
  74.2 1.1 %collective-permute-done.9.refs_3_ = bf16[2,2,128,256]{3,2,1,0:T(8,128)(2,1)S(1)} collective-permute-done((bf16[2,2,128,256]{3,2,1,0:T(8,128)(2,1)S(1)}, bf16[2,2,128,256]{3,2,1,0:T(8,128)(2,1)S(1)}, u32[]{:S(2)}, u32[]{:S(2)}) %collective-permute-start.9) | collective-permute-done | bytes 262176 | tf_op jit(solution)/shard_map/ppermute | solution.py:36
  75.3 11.0 %collective-permute-done.8.refs_2_ = bf16[2,2,128,256]{3,2,1,0:T(8,128)(2,1)S(1)} collective-permute-done((bf16[2,2,128,256]{3,2,1,0:T(8,128)(2,1)S(1)}, bf16[2,2,128,256]{3,2,1,0:T(8,128)(2,1)S(1)}, u32[]{:S(2)}, u32[]{:S(2)}) %collective-permute-start.8) | collective-permute-done | bytes 262176 | tf_op jit(solution)/shard_map/ppermute | solution.py:36
  86.3 1.2 %step_2_shot_1.1 = (f32[2,4,128,256]{3,2,1,0:T(8,128)S(1)}, bf16[1,2,128,256]{3,2,1,0:T(8,128)(2,1)S(1)}, bf16[1,2,128,256]{3,2,1,0:T(8,128)(2,1)S(1)}, bf16[1,2...) custom-call(f32[2,4,128,256]{3,2,1,0:T(8,128)S(1)} %get-tuple-element.55.refs_0_.refs_, ...), custom_call_target="tpu_custom_call" | custom-call | flops 1 | bytes 1 | tf_op jit(solution)/shard_map/step_2_shot_1/pallas_call | solution.py:453
  87.5 3.3 %collective-permute-start.15 = (bf16[1,2,128,256]{3,2,1,0:T(8,128)(2,1)S(1)}, bf16[1,2,128,256]{3,2,1,0:T(8,128)(2,1)S(1)}, u32[]{:S(2)}, u32[]{:S(2)}) collective-permute-start(bf16[1,2,128,256]{3,2,1,0:T(8,128)(2,1)S(1)} %get-tuple-element.67), channel_id=1, source_target_pairs={{1,2},{2,1},{3,4},{4,3},{5,6},{6,5},{7,8},{8,7},{9,10},{10,9},{11,... | collective-permute-start | bytes 393224 | tf_op jit(solution)/shard_map/ppermute | solution.py:36
  90.8 0.1 collective-permute-start.14
  90.9 1.5 %collective-permute-start.12 = (bf16[1,2,128,256]{3,2,1,0:T(8,128)(2,1)S(1)}, bf16[1,2,128,256]{3,2,1,0:T(8,128)(2,1)S(1)}, u32[]{:S(2)}, u32[]{:S(2)}) collective-permute-start(bf16[1,2,128,256]{3,2,1,0:T(8,128)(2,1)S(1)} %get-tuple-element.64), channel_id=1, source_target_pairs={{0,1},{1,0},{2,3},{3,2},{4,5},{5,4},{6,7},{7,6},{8,9},{9,8},{10,11... | collective-permute-start | bytes 393224 | tf_op jit(solution)/shard_map/ppermute | solution.py:36
  92.4 0.0 collective-permute-done.17.refs_3_
  92.4 2.9 %collective-permute-start.13 = (bf16[1,2,128,256]{3,2,1,0:T(8,128)(2,1)S(1)}, bf16[1,2,128,256]{3,2,1,0:T(8,128)(2,1)S(1)}, u32[]{:S(2)}, u32[]{:S(2)}) collective-permute-start(bf16[1,2,128,256]{3,2,1,0:T(8,128)(2,1)S(1)} %get-tuple-element.65), channel_id=1, source_target_pairs={{1,2},{2,1},{3,4},{4,3},{5,6},{6,5},{7,8},{8,7},{9,10},{10,9},{11,... | collective-permute-start | bytes 393224 | tf_op jit(solution)/shard_map/ppermute | solution.py:36
  95.3 3.1 %step_3_shot_0.1 = (f32[2,2,2,4,128,256]{5,4,3,2,1,0:T(8,128)}, f32[4,192,256]{2,1,0:T(8,128)S(1)}) custom-call(f32[2,4,128,256]{3,2,1,0:T(8,128)S(1)} %get-tuple-element.69.refs_0_.refs_10_, f32[2,4,128,256]{3,2,1,0:T(8,128)S(1)} %get-tuple-element.59.refs_0_.refs_1_, bf16[2,2,128,256]{3,2,1,0:T(8,128)(2,1)S(1)} %collective-permute-done.16.refs_2_, ...), custom_call_target="tpu_custom_call" | custom-call | flops 1 | bytes 1 | tf_op jit(solution)/shard_map/step_3_shot_0/pallas_call | solution.py:453
  98.4 2.2 %collective-permute-done.14.refs_2_ = bf16[1,2,128,256]{3,2,1,0:T(8,128)(2,1)S(1)} collective-permute-done((bf16[1,2,128,256]{3,2,1,0:T(8,128)(2,1)S(1)}, bf16[1,2,128,256]{3,2,1,0:T(8,128)(2,1)S(1)}, u32[]{:S(2)}, u32[]{:S(2)}) %collective-permute-start.14) | collective-permute-done | bytes 131104 | tf_op jit(solution)/shard_map/ppermute | solution.py:36
  100.5 2.8 %step_3_shot_1.2 = (f32[4,128,256]{2,1,0:T(8,128)S(1)}, f32[4,192,256]{2,1,0:T(8,128)}) custom-call(f32[2,4,128,256]{3,2,1,0:T(8,128)S(1)} %get-tuple-element.63.refs_11_.refs_0_, f32[2,4,128,256]{3,2,1,0:T(8,128)S(1)} %get-tuple-element.55.refs_0_.refs_1_, bf16[1,2,128,256]{3,2,1,0:T(8,128)(2,1)S(1)} %collective-permute-done.14.refs_2_, ...), custom_call_target="tpu_custom_call" | custom-call | flops 1 | bytes 1 | tf_op jit(solution)/shard_map/step_3_shot_1/pallas_call | solution.py:453
  103.3 0.6 collective-permute-start.18
  103.9 1.4 %step_3_shot_1.3.after_ref = f32[2,2,2,4,128,256]{5,4,3,2,1,0:T(8,128)} custom-call(f32[2,4,128,256]{3,2,1,0:T(8,128)S(1)} %get-tuple-element.63.refs_11_.refs_0_, f32[2,4,128,256]{3,2,1,0:T(8,128)S(1)} %get-tuple-element.55.refs_0_.refs_1_, bf16[1,2,128,256]{3,2,1,0:T(8,128)(2,1)S(1)} %collective-permute-done.12.refs_2_, ...), custom_call_target="tpu_custom_call", output_to_operand_aliasing={{}: (8, {})} | custom-call | flops 9999999827968 | bytes 1 | tf_op jit(solution)/shard_map/step_3_shot_1/pallas_call | solution.py:453
  105.3 0.9 collective-permute-done.18.other_ref
  106.2 2.3 %sum_frames.1 = f32[4,192,256]{2,1,0:T(8,128)} custom-call(f32[4,192,256]{2,1,0:T(8,128)} %get-tuple-element.74.refs_7_.own_ref, f32[4,192,256]{2,1,0:T(8,128)} %collective-permute-done.18.other_ref, f32[2,2,2,4,128,256]{5,4,3,2,1,0:T(8,128)} %step_3_shot_1.3.after_ref), custom_call_target="tpu_custom_call" | custom-call | flops 1 | bytes 1 | tf_op jit(solution)/shard_map/sum_frames/pallas_call | solution.py:484
  (19 shorter events, 0.0 us)
Async XLA Ops:
  0.6 5.7 %copy-start.5 = (s32[2,128]{1,0:T(2,128)S(1)}, s32[2,128]{1,0:T(2,128)}, u32[]{:S(2)}) copy-start(s32[2,128]{1,0:T(2,128)} %ids_ref.1) | copy-start | bytes 3076
  0.6 5.7 %copy-start.2 = (bf16[2,128,256]{2,1,0:T(8,128)(2,1)S(1)}, bf16[2,128,256]{2,1,0:T(8,128)(2,1)}, u32[]{:S(2)}) copy-start(bf16[2,128,256]{2,1,0:T(8,128)(2,1)} %lines_ref.1) | copy-start | bytes 393220
  0.7 19.4 %copy-start.1 = (f32[2,4,64]{2,1,0:T(4,128)S(1)}, f32[2,4,64]{2,1,0:T(4,128)}, u32[]{:S(2)}) copy-start(f32[2,4,64]{2,1,0:T(4,128)} %refs_5_.15) | copy-start | bytes 6148
  0.7 19.4 %copy-start.3 = (s32[2,64]{1,0:T(2,128)S(1)}, s32[2,64]{1,0:T(2,128)}, u32[]{:S(2)}) copy-start(s32[2,64]{1,0:T(2,128)} %refs_4_.3) | copy-start | bytes 1540
  0.7 19.4 %copy-start.4 = (s32[2]{0:T(128)S(1)}, s32[2]{0:T(128)}, u32[]{:S(2)}) copy-start(s32[2]{0:T(128)} %refs_6_.15) | copy-start | bytes 28
  0.7 19.4 %copy-start = (f32[4,192,256]{2,1,0:T(8,128)S(1)}, f32[4,192,256]{2,1,0:T(8,128)}, u32[]{:S(2)}) copy-start(f32[4,192,256]{2,1,0:T(8,128)} %refs_8_.1) | copy-start | bytes 2359300
  2.0 17.3 %collective-permute-start.3 = (bf16[2,2,128,256]{3,2,1,0:T(8,128)(2,1)S(1)}, bf16[2,2,128,256]{3,2,1,0:T(8,128)(2,1)S(1)}, u32[]{:S(2)}, u32[]{:S(2)}) collective-permute-start(bf16[2,2,128,256]{3,2,1,0:T(8,128)(2,1)S(1)} %get-tuple-element.42), channel_id=1, source_target_pairs={{1,2},{2,1},{3,4},{4,3},{5,6},{6,5},{7,8},{8,7},{9,10},{10,9},{11,... | collective-permute-start | bytes 786440 | tf_op jit(solution)/shard_map/ppermute | solution.py:36
  5.2 14.9 %collective-permute-start.2 = (bf16[2,2,128,256]{3,2,1,0:T(8,128)(2,1)S(1)}, bf16[2,2,128,256]{3,2,1,0:T(8,128)(2,1)S(1)}, u32[]{:S(2)}, u32[]{:S(2)}) collective-permute-start(bf16[2,2,128,256]{3,2,1,0:T(8,128)(2,1)S(1)} %get-tuple-element.39.after_ref), channel_id=1, source_target_pairs={{0,1},{1,0},{2,3},{3,2},{4,5},{5,4},{6,7},{7,6},{8,9},{9,8},{10,11... | collective-permute-start | bytes 786440 | tf_op jit(solution)/shard_map/ppermute | solution.py:36
  7.3 16.0 %all-to-all-start = ((bf16[16,16,384]{2,1,0:T(8,128)(2,1)}), bf16[16,16,384]{2,1,0:T(8,128)(2,1)}, u32[]{:S(2)}, u32[]{:S(2)}) async-start(bf16[16,16,384]{2,1,0:T(8,128)(2,1)} %bitcast), calls=%async_computation | async-start | bytes 393216 | tf_op jit(solution)/shard_map/all_to_all | solution.py:185
  15.0 22.5 %collective-permute-start = (bf16[2,2,128,256]{3,2,1,0:T(8,128)(2,1)}, bf16[2,2,128,256]{3,2,1,0:T(8,128)(2,1)}, u32[]{:S(2)}, u32[]{:S(2)}) collective-permute-start(bf16[2,2,128,256]{3,2,1,0:T(8,128)(2,1)} %get-tuple-element.40), channel_id=1, source_target_pairs={{0,1},{1,0},{2,3},{3,2},{4,5},{5,4},{6,7},{7,6},{8,9},{9,8},{10,11... | collective-permute-start | bytes 786440 | tf_op jit(solution)/shard_map/ppermute | solution.py:36
  15.4 22.2 %collective-permute-start.1 = (bf16[2,2,128,256]{3,2,1,0:T(8,128)(2,1)}, bf16[2,2,128,256]{3,2,1,0:T(8,128)(2,1)}, u32[]{:S(2)}, u32[]{:S(2)}) collective-permute-start(bf16[2,2,128,256]{3,2,1,0:T(8,128)(2,1)} %get-tuple-element.41), channel_id=1, source_target_pairs={{1,2},{2,1},{3,4},{4,3},{5,6},{6,5},{7,8},{8,7},{9,10},{10,9},{11,... | collective-permute-start | bytes 786440 | tf_op jit(solution)/shard_map/ppermute | solution.py:36
  24.7 20.0 %collective-permute-start.7 = (bf16[2,2,128,256]{3,2,1,0:T(8,128)(2,1)S(1)}, bf16[2,2,128,256]{3,2,1,0:T(8,128)(2,1)S(1)}, u32[]{:S(2)}, u32[]{:S(2)}) collective-permute-start(bf16[2,2,128,256]{3,2,1,0:T(8,128)(2,1)S(1)} %get-tuple-element.51), channel_id=1, source_target_pairs={{1,2},{2,1},{3,4},{4,3},{5,6},{6,5},{7,8},{8,7},{9,10},{10,9},{11,... | collective-permute-start | bytes 786440 | tf_op jit(solution)/shard_map/ppermute | solution.py:36
  28.0 16.7 %collective-permute-start.6 = (bf16[2,2,128,256]{3,2,1,0:T(8,128)(2,1)S(1)}, bf16[2,2,128,256]{3,2,1,0:T(8,128)(2,1)S(1)}, u32[]{:S(2)}, u32[]{:S(2)}) collective-permute-start(bf16[2,2,128,256]{3,2,1,0:T(8,128)(2,1)S(1)} %get-tuple-element.44.refs_9_), channel_id=1, source_target_pairs={{0,1},{1,0},{2,3},{3,2},{4,5},{5,4},{6,7},{7,6},{8,9},{9,8},{10,11... | collective-permute-start | bytes 786440 | tf_op jit(solution)/shard_map/ppermute | solution.py:36
  41.4 10.1 %collective-permute-start.5 = (bf16[2,2,128,256]{3,2,1,0:T(8,128)(2,1)S(1)}, bf16[2,2,128,256]{3,2,1,0:T(8,128)(2,1)S(1)}, u32[]{:S(2)}, u32[]{:S(2)}) collective-permute-start(bf16[2,2,128,256]{3,2,1,0:T(8,128)(2,1)S(1)} %get-tuple-element.47), channel_id=1, source_target_pairs={{1,2},{2,1},{3,4},{4,3},{5,6},{6,5},{7,8},{8,7},{9,10},{10,9},{11,... | collective-permute-start | bytes 786440 | tf_op jit(solution)/shard_map/ppermute | solution.py:36
  44.6 18.1 %collective-permute-start.4 = (bf16[2,2,128,256]{3,2,1,0:T(8,128)(2,1)S(1)}, bf16[2,2,128,256]{3,2,1,0:T(8,128)(2,1)S(1)}, u32[]{:S(2)}, u32[]{:S(2)}) collective-permute-start(bf16[2,2,128,256]{3,2,1,0:T(8,128)(2,1)S(1)} %get-tuple-element.46.refs_9_), channel_id=1, source_target_pairs={{0,1},{1,0},{2,3},{3,2},{4,5},{5,4},{6,7},{7,6},{8,9},{9,8},{10,11... | collective-permute-start | bytes 786440 | tf_op jit(solution)/shard_map/ppermute | solution.py:36
  47.1 21.1 %collective-permute-start.11 = (bf16[2,2,128,256]{3,2,1,0:T(8,128)(2,1)S(1)}, bf16[2,2,128,256]{3,2,1,0:T(8,128)(2,1)S(1)}, u32[]{:S(2)}, u32[]{:S(2)}) collective-permute-start(bf16[2,2,128,256]{3,2,1,0:T(8,128)(2,1)S(1)} %get-tuple-element.60), channel_id=1, source_target_pairs={{1,2},{2,1},{3,4},{4,3},{5,6},{6,5},{7,8},{8,7},{9,10},{10,9},{11,... | collective-permute-start | bytes 786440 | tf_op jit(solution)/shard_map/ppermute | solution.py:36
  50.0 18.4 %collective-permute-start.10 = (bf16[2,2,128,256]{3,2,1,0:T(8,128)(2,1)S(1)}, bf16[2,2,128,256]{3,2,1,0:T(8,128)(2,1)S(1)}, u32[]{:S(2)}, u32[]{:S(2)}) collective-permute-start(bf16[2,2,128,256]{3,2,1,0:T(8,128)(2,1)S(1)} %get-tuple-element.54.refs_9_), channel_id=1, source_target_pairs={{0,1},{1,0},{2,3},{3,2},{4,5},{5,4},{6,7},{7,6},{8,9},{9,8},{10,11... | collective-permute-start | bytes 786440 | tf_op jit(solution)/shard_map/ppermute | solution.py:36
  65.3 10.1 %collective-permute-start.9 = (bf16[2,2,128,256]{3,2,1,0:T(8,128)(2,1)S(1)}, bf16[2,2,128,256]{3,2,1,0:T(8,128)(2,1)S(1)}, u32[]{:S(2)}, u32[]{:S(2)}) collective-permute-start(bf16[2,2,128,256]{3,2,1,0:T(8,128)(2,1)S(1)} %get-tuple-element.57), channel_id=1, source_target_pairs={{1,2},{2,1},{3,4},{4,3},{5,6},{6,5},{7,8},{8,7},{9,10},{10,9},{11,... | collective-permute-start | bytes 786440 | tf_op jit(solution)/shard_map/ppermute | solution.py:36
  68.2 18.1 %collective-permute-start.8 = (bf16[2,2,128,256]{3,2,1,0:T(8,128)(2,1)S(1)}, bf16[2,2,128,256]{3,2,1,0:T(8,128)(2,1)S(1)}, u32[]{:S(2)}, u32[]{:S(2)}) collective-permute-start(bf16[2,2,128,256]{3,2,1,0:T(8,128)(2,1)S(1)} %get-tuple-element.56.refs_9_), channel_id=1, source_target_pairs={{0,1},{1,0},{2,3},{3,2},{4,5},{5,4},{6,7},{7,6},{8,9},{9,8},{10,11... | collective-permute-start | bytes 786440 | tf_op jit(solution)/shard_map/ppermute | solution.py:36
  69.6 22.7 %collective-permute-start.17 = (bf16[2,2,128,256]{3,2,1,0:T(8,128)(2,1)S(1)}, bf16[2,2,128,256]{3,2,1,0:T(8,128)(2,1)S(1)}, u32[]{:S(2)}, u32[]{:S(2)}) collective-permute-start(bf16[2,2,128,256]{3,2,1,0:T(8,128)(2,1)S(1)} %get-tuple-element.70), channel_id=1, source_target_pairs={{1,2},{2,1},{3,4},{4,3},{5,6},{6,5},{7,8},{8,7},{9,10},{10,9},{11,... | collective-permute-start | bytes 786440 | tf_op jit(solution)/shard_map/ppermute | solution.py:36
  72.8 22.5 %collective-permute-start.16 = (bf16[2,2,128,256]{3,2,1,0:T(8,128)(2,1)S(1)}, bf16[2,2,128,256]{3,2,1,0:T(8,128)(2,1)S(1)}, u32[]{:S(2)}, u32[]{:S(2)}) collective-permute-start(bf16[2,2,128,256]{3,2,1,0:T(8,128)(2,1)S(1)} %get-tuple-element.62.refs_9_), channel_id=1, source_target_pairs={{0,1},{1,0},{2,3},{3,2},{4,5},{5,4},{6,7},{7,6},{8,9},{9,8},{10,11... | collective-permute-start | bytes 786440 | tf_op jit(solution)/shard_map/ppermute | solution.py:36
  87.5 10.8 %collective-permute-start.15 = (bf16[1,2,128,256]{3,2,1,0:T(8,128)(2,1)S(1)}, bf16[1,2,128,256]{3,2,1,0:T(8,128)(2,1)S(1)}, u32[]{:S(2)}, u32[]{:S(2)}) collective-permute-start(bf16[1,2,128,256]{3,2,1,0:T(8,128)(2,1)S(1)} %get-tuple-element.67), channel_id=1, source_target_pairs={{1,2},{2,1},{3,4},{4,3},{5,6},{6,5},{7,8},{8,7},{9,10},{10,9},{11,... | collective-permute-start | bytes 393224 | tf_op jit(solution)/shard_map/ppermute | solution.py:36
  90.8 9.7 %collective-permute-start.14 = (bf16[1,2,128,256]{3,2,1,0:T(8,128)(2,1)S(1)}, bf16[1,2,128,256]{3,2,1,0:T(8,128)(2,1)S(1)}, u32[]{:S(2)}, u32[]{:S(2)}) collective-permute-start(bf16[1,2,128,256]{3,2,1,0:T(8,128)(2,1)S(1)} %get-tuple-element.66.refs_12_), channel_id=1, source_target_pairs={{0,1},{1,0},{2,3},{3,2},{4,5},{5,4},{6,7},{7,6},{8,9},{9,8},{10,11... | collective-permute-start | bytes 393224 | tf_op jit(solution)/shard_map/ppermute | solution.py:36
  90.9 13.0 %collective-permute-start.12 = (bf16[1,2,128,256]{3,2,1,0:T(8,128)(2,1)S(1)}, bf16[1,2,128,256]{3,2,1,0:T(8,128)(2,1)S(1)}, u32[]{:S(2)}, u32[]{:S(2)}) collective-permute-start(bf16[1,2,128,256]{3,2,1,0:T(8,128)(2,1)S(1)} %get-tuple-element.64), channel_id=1, source_target_pairs={{0,1},{1,0},{2,3},{3,2},{4,5},{5,4},{6,7},{7,6},{8,9},{9,8},{10,11... | collective-permute-start | bytes 393224 | tf_op jit(solution)/shard_map/ppermute | solution.py:36
  92.4 11.6 %collective-permute-start.13 = (bf16[1,2,128,256]{3,2,1,0:T(8,128)(2,1)S(1)}, bf16[1,2,128,256]{3,2,1,0:T(8,128)(2,1)S(1)}, u32[]{:S(2)}, u32[]{:S(2)}) collective-permute-start(bf16[1,2,128,256]{3,2,1,0:T(8,128)(2,1)S(1)} %get-tuple-element.65), channel_id=1, source_target_pairs={{1,2},{2,1},{3,4},{4,3},{5,6},{6,5},{7,8},{8,7},{9,10},{10,9},{11,... | collective-permute-start | bytes 393224 | tf_op jit(solution)/shard_map/ppermute | solution.py:36
  103.3 2.9 %collective-permute-start.18 = (f32[4,192,256]{2,1,0:T(8,128)}, f32[4,192,256]{2,1,0:T(8,128)}, u32[]{:S(2)}, u32[]{:S(2)}) collective-permute-start(f32[4,192,256]{2,1,0:T(8,128)} %get-tuple-element.74.refs_7_.own_ref), channel_id=1, source_target_pairs={{0,16},{16,0},{1,17},{17,1},{2,18},{18,2},{3,19},{19,3},{4,20},{20... | collective-permute-start | bytes 2359304 | tf_op jit(solution)/shard_map/ppermute | solution.py:572

commit v6 on v5

--- a/solution.py
+++ b/solution.py
@@ -54,7 +54,7 @@
     return pl.multiple_of(start, 8), offset - start
 
 
-def add_window(target_ref, layer, part, offset):
+def put_window(target_ref, layer, part, offset):
     rows_y, cells_z = part.shape
     groups = rows_y // 8
     start = pl.multiple_of(lax.div(offset, 8) * 8, 8)
@@ -63,13 +63,8 @@
     before = lax.broadcasted_iota(jnp.int32, (8, cells_z), 0) < gap
     body = [jnp.where(before, 0.0, turned[0])]
     body += [jnp.where(before, turned[at - 1], turned[at]) for at in range(1, groups)]
-    at = pl.ds(start, rows_y)
-    target_ref[layer, at, :] = target_ref[layer, at, :] + jnp.concatenate(body, axis=0)
-
-    @pl.when(gap > 0)
-    def _():
-        rest = pl.ds(pl.multiple_of(start + rows_y, 8), 8)
-        target_ref[layer, rest, :] = target_ref[layer, rest, :] + jnp.where(before, turned[-1], 0.0)
+    body.append(jnp.where(before, turned[-1], 0.0))
+    target_ref[layer, pl.ds(start, rows_y + 8), :] = jnp.concatenate(body, axis=0)
 
 
 def is_odd():
@@ -231,7 +226,7 @@
     )(new, saved)
 
 
-def step_kernel(shot, step, comps, got_groups, send_groups, create, framed, lines, waits, keeps, *refs):
+def step_kernel(shot, step, comps, got_groups, send_groups, create, lines, waits, keeps, *refs):
     refs = list(refs)
 
     def take(count):
@@ -252,7 +247,6 @@
     [offsets_ref] = take(1) if first or framing else [None]
     [speed_from] = take(1)
     [contrib_from] = take(1) if with_image and not first else [None]
-    [frame_from] = take(1) if framing and framed else [None]
     keep_refs = take(len(keeps))
     held = last and comps == (1,)
     [field_from] = take(1) if last and comps == (0,) else [None]
@@ -269,6 +263,7 @@
     [speed_out] = take(1) if first else [None]
     if last and not held:
         new_ref, out_sems = take(2)
+    [terms_ref] = take(1) if framing else [None]
     loads = []
     if first:
         state_ref, load_sems = take(2)
@@ -354,17 +349,17 @@
                 if not first:
                     term = contrib_from[layer] + term
                 if framing:
-                    if not framed:
-                        contrib_ref[layer] = jnp.zeros_like(contrib_ref[layer])
-                    else:
-                        contrib_ref[layer] = frame_from[layer]
-                    add_window(contrib_ref, layer, term, offsets_ref[shot])
+                    terms_ref[layer] = term
                 else:
                     contrib_ref[layer] = term
             elif lines:
                 take_lines(new_ref, saved_ref, shot, step, layer)
             if last and not held:
                 store(new_ref.at[comp, layer], out_ref.at[shot, 0, comp, layer])
+    if framing:
+        contrib_ref[...] = jnp.zeros_like(contrib_ref)
+        for layer in range(layers):
+            put_window(contrib_ref, layer, terms_ref[layer], offsets_ref[shot])
     for started in stores:
         started.wait()
     if not last:
@@ -373,7 +368,7 @@
 
 def one_step(
     shot, step, comps, got_groups, send_groups,
-    wavefields, offsets, now, later, got, saved, pos, traces, speed, contrib, frame, out, after, heavy, model_y, keeps=(), field=None,
+    wavefields, offsets, now, later, got, saved, pos, traces, speed, contrib, out, after, heavy, model_y, keeps=(), field=None,
 ):
     first, last = step == 0, step == STEPS - 1
     with_image = 1 in comps
@@ -407,9 +402,6 @@
     if with_image and not first:
         args.append(contrib)
         specs.append(vmem)
-    if framing and frame is not None:
-        args.append(frame)
-        specs.append(vmem)
     args += [value for _, value in keeps]
     specs += [vmem] * len(keeps)
     held = last and comps == (1,)
@@ -439,7 +431,7 @@
             outs += [half, half]
         out_specs = [vmem] * len(outs)
     if framing:
-        outs.append(jax.ShapeDtypeStruct((layers, model_y, cells_z), jnp.float32))
+        outs.append(jax.ShapeDtypeStruct((layers, model_y + 8, cells_z), jnp.float32))
         out_specs.append(vmem)
     elif with_image:
         outs.append(image)
@@ -447,13 +439,15 @@
     if first:
         outs.append(image)
         out_specs.append(vmem)
+    if framing:
+        scratch.append(pltpu.VMEM(image.shape, jnp.float32))
     if step < 2:
         lead = (2,) if first else ()
         scratch = [pltpu.VMEM(lead + state.shape, jnp.float32), pltpu.SemaphoreType.DMA((1,))]
     return pl.pallas_call(
         functools.partial(
-            step_kernel, shot, step, comps, got_groups, send_groups, out is None, frame is not None,
-            lines, len(after), tuple(keep for keep, _ in keeps),
+            step_kernel, shot, step, comps, got_groups, send_groups, out is None, lines,
+            len(after), tuple(keep for keep, _ in keeps),
         ),
         in_specs=specs,
         out_specs=out_specs,
@@ -466,11 +460,18 @@
     )(*args)
 
 
-def sum_kernel(scale, own_ref, other_ref, after_ref, image_ref, sum_ref, sems):
-    del after_ref
+def sum_kernel(scale, *refs):
+    image_ref, sum_ref, sems = refs[-3:]
+    frame_refs = refs[:-4]
+    layers, model_y, _ = sum_ref.shape
     stores = []
-    for layer in range(sum_ref.shape[0]):
-        sum_ref[layer] = (own_ref[layer] + other_ref[layer]) * scale
+    for layer in range(layers):
+        total = None
+        for at in range(0, len(frame_refs), 2):
+            own_ref, other_ref = frame_refs[at : at + 2]
+            pair = own_ref[layer, :model_y] + other_ref[layer, :model_y]
+            total = pair if total is None else total + pair
+        sum_ref[layer] = total * scale
         stores.append(
             pltpu.make_async_copy(sum_ref.at[layer], image_ref.at[layer], sems.at[layer])
         )
@@ -479,21 +480,24 @@
         started.wait()
 
 
-def sum_frames(own, other, scale, after):
+def sum_frames(frames, others, scale, model_y, after):
+    layers, _, cells_z = frames[0].shape
     vmem, hbm = pl.BlockSpec(memory_space=VMEM), pl.BlockSpec(memory_space=HBM)
+    args = [value for pair in zip(frames, others) for value in pair]
+    shape_out = jax.ShapeDtypeStruct((layers, model_y, cells_z), jnp.float32)
     return pl.pallas_call(
         functools.partial(sum_kernel, scale),
-        in_specs=[vmem, vmem, hbm],
+        in_specs=[vmem] * len(args) + [hbm],
         out_specs=hbm,
-        out_shape=jax.ShapeDtypeStruct(own.shape, jnp.float32),
+        out_shape=shape_out,
         scratch_shapes=[
-            pltpu.VMEM(own.shape, jnp.float32),
-            pltpu.SemaphoreType.DMA((own.shape[0],)),
+            pltpu.VMEM(shape_out.shape, jnp.float32),
+            pltpu.SemaphoreType.DMA((layers,)),
         ],
         compiler_params=params(),
         cost_estimate=cost(),
         name="sum_frames",
-    )(own, other, pltpu.with_memory_space_constraint(after, HBM))
+    )(*args, pltpu.with_memory_space_constraint(after, HBM))
 
 
 def body(wavefields, courant, offsets, strip_lines, strip_ids, receiver_pos, traces):
@@ -523,7 +527,7 @@
     contrib = [None] * shots
     speed = [courant] * shots
     out = None
-    frame = None
+    frames = []
     after = []
     for step in range(STEPS):
         for shot in range(shots):
@@ -535,7 +539,7 @@
                 early = step == 0 and shot == 0
                 made = one_step(
                     shot, step, BOTH[0], groups[shot], () if early else send_groups, *common,
-                    got[shot], None if early else saved, *fixed, contrib[shot], None, None, after, early,
+                    got[shot], None if early else saved, *fixed, contrib[shot], None, after, early,
                     model_y,
                 )
                 later[shot], now[shot] = now[shot], made[0]
@@ -557,7 +561,7 @@
             for group in groups[shot]:
                 made = one_step(
                     shot, step, group, (group,), (), *common, got[shot][:1], saved, *fixed,
-                    contrib[shot], frame, out, after, group == (0,), model_y,
+                    contrib[shot], out, after, group == (0,), model_y,
                     () if group == (1,) else keeps, field,
                 )
                 got[shot] = got[shot][1:]
@@ -566,12 +570,13 @@
                 else:
                     out = made[0]
                 if 1 in group:
-                    frame = made[1]
-                    after = [frame]
+                    frames.append(made[1])
+                    after = [made[1]]
     if shot_devices == 2:
-        other = lax.ppermute(frame, "shot", [(0, 1), (1, 0)])
-        image = sum_frames(frame, other, scale, out)
+        others = [lax.ppermute(frame, "shot", [(0, 1), (1, 0)]) for frame in frames]
+        image = sum_frames(frames, others, scale, model_y, out)
     else:
+        frame = sum(frames)[:, :model_y]
         image = lax.psum(frame, "shot") * scale
     return (out, image)
 

time: 109 us -> 109 us (level)
  waiting for transfers between devices: 36.5 us -> 34.4 us
  starting transfers between devices: 41.4 us -> 43.1 us
    ppermute x18, waiting for transfers between devices: 35.6 us -> 33.7 us  [swap_pairs(): return lax.ppermute(value, 'space', routes)]
    ppermute x1 -> x2, starting transfers between devices: 0.6 us -> 2.36 us  [body(): others = [lax.ppermute(frame, 'shot', [(0, 1), (1, 0)]) for frame in frames]]
  transfers between devices with their start and end apart: 20 -> 21, of which waited for: 8 -> 8; matrix products, arithmetic and copies ran while one was open for 0% -> 0% of each run, Pallas kernels for 24% -> 24%
where the time goes in v6:
time: 109 us; the launch traced here: 108 us
  starting transfers between devices  43.1 us (40%)
  waiting for transfers between devices  34.4 us (32%)
  Pallas kernels  30 us (28%)
    ppermute x18, starting transfers between devices, swap_pairs(): return lax.ppermute(value, 'space', routes)  35.1 us
    ppermute x18, waiting for transfers between devices, swap_pairs(): return lax.ppermute(value, 'space', routes)  33.7 us
    pallas_call x9, Pallas kernels, one_step(): pl.pallas_call(functools.partial(step_kernel, shot, step, comps, got_grou...  21.4 us
    all_to_all x1, starting transfers between devices, deliver(): got = lax.all_to_all(message, 'space', 0, 0, tiled=False)  5.63 us
    pallas_call x2, Pallas kernels, pack_halo(): pl.pallas_call(functools.partial(pack_kernel, shot), in_specs=[pl.BlockSp...  3.36 us
    pallas_call x1, Pallas kernels, sum_frames(): pl.pallas_call(functools.partial(sum_kernel, scale), in_specs=[vmem] * le...  2.83 us
    ppermute x2, starting transfers between devices, body(): others = [lax.ppermute(frame, 'shot', [(0, 1), (1, 0)]) for frame in frames]  2.36 us
  transfers between devices with their start and end apart: 21, of which 8 were waited for; matrix products, arithmetic and copies ran while one was open for 0% of the time, Pallas kernels for 24%

profile of v6, /device:TPU:19, one launch (start us, length us, event | category | flops | bytes accessed | tf_op | source)
XLA Modules:
  0.0 108.5 jit_solution(910781338694330682)
XLA Ops:
  0.7 1.3 %pack_halo.2 = (bf16[2,2,128,256]{3,2,1,0:T(8,128)(2,1)S(1)}, bf16[2,2,128,256]{3,2,1,0:T(8,128)(2,1)S(1)}) custom-call(f32[2,2,2,4,128,256]{5,4,3,2,1,0:T(8,128)} %refs_1_.7), custom_call_target="tpu_custom_call" | custom-call | flops 1 | bytes 1 | tf_op jit(solution)/shard_map/pack_halo/pallas_call | solution.py:103
  2.0 3.1 %collective-permute-start.3 = (bf16[2,2,128,256]{3,2,1,0:T(8,128)(2,1)S(1)}, bf16[2,2,128,256]{3,2,1,0:T(8,128)(2,1)S(1)}, u32[]{:S(2)}, u32[]{:S(2)}) collective-permute-start(bf16[2,2,128,256]{3,2,1,0:T(8,128)(2,1)S(1)} %get-tuple-element.42), channel_id=1, source_target_pairs={{1,2},{2,1},{3,4},{4,3},{5,6},{6,5},{7,8},{8,7},{9,10},{10,9},{11,... | collective-permute-start | bytes 786440 | tf_op jit(solution)/shard_map/ppermute | solution.py:36
  5.2 1.2 %collective-permute-start.2 = (bf16[2,2,128,256]{3,2,1,0:T(8,128)(2,1)S(1)}, bf16[2,2,128,256]{3,2,1,0:T(8,128)(2,1)S(1)}, u32[]{:S(2)}, u32[]{:S(2)}) collective-permute-start(bf16[2,2,128,256]{3,2,1,0:T(8,128)(2,1)S(1)} %get-tuple-element.39.after_ref), channel_id=1, source_target_pairs={{0,1},{1,0},{2,3},{3,2},{4,5},{5,4},{6,7},{7,6},{8,9},{9,8},{10,11... | collective-permute-start | bytes 786440 | tf_op jit(solution)/shard_map/ppermute | solution.py:36
  6.3 1.0 pack_lines.1.refs_0_
  7.3 5.6 %all-to-all-start = ((bf16[16,16,384]{2,1,0:T(8,128)(2,1)}), bf16[16,16,384]{2,1,0:T(8,128)(2,1)}, u32[]{:S(2)}, u32[]{:S(2)}) async-start(bf16[16,16,384]{2,1,0:T(8,128)(2,1)} %bitcast), calls=%async_computation | async-start | bytes 393216 | tf_op jit(solution)/shard_map/all_to_all | solution.py:180
  13.0 2.0 %pack_halo.3 = (bf16[2,2,128,256]{3,2,1,0:T(8,128)(2,1)}, bf16[2,2,128,256]{3,2,1,0:T(8,128)(2,1)}) custom-call(f32[2,2,2,4,128,256]{5,4,3,2,1,0:T(8,128)} %refs_1_.7, bf16[256,384]{1,0:T(8,128)(2,1)} %pack_lines.1.refs_0_), custom_call_target="tpu_custom_call" | custom-call | flops 1 | bytes 1 | tf_op jit(solution)/shard_map/pack_halo/pallas_call | solution.py:103
  15.0 0.3 collective-permute-start
  15.4 4.0 %collective-permute-start.1 = (bf16[2,2,128,256]{3,2,1,0:T(8,128)(2,1)}, bf16[2,2,128,256]{3,2,1,0:T(8,128)(2,1)}, u32[]{:S(2)}, u32[]{:S(2)}) collective-permute-start(bf16[2,2,128,256]{3,2,1,0:T(8,128)(2,1)} %get-tuple-element.41), channel_id=1, source_target_pairs={{1,2},{2,1},{3,4},{4,3},{5,6},{6,5},{7,8},{8,7},{9,10},{10,9},{11,... | collective-permute-start | bytes 786440 | tf_op jit(solution)/shard_map/ppermute | solution.py:36
  19.3 0.0 collective-permute-done.3.refs_3_
  19.4 0.7 collective-permute-done.2.refs_2_
  20.1 3.3 %step_0_shot_0.1 = (f32[2,4,128,256]{3,2,1,0:T(8,128)S(1)}, f32[4,128,256]{2,1,0:T(8,128)S(1)}, f32[4,128,256]{2,1,0:T(8,128)S(1)}) custom-call(f32[2,2,2,4,128,256]{5,4,3,2,1,0:T(8,128)} %refs_1_.7, f32[2,2,2,4,128,256]{5,4,3,2,1,0:T(8,128)} %refs_1_.7, bf16[2,2,128,256]{3,2,1,0:T(8,128)(2,1)S(1)} %collective-permute-done.2.refs_2_, ...), custom_call_target="tpu_custom_call" | custom-call | flops 9999999827968 | bytes 1 | tf_op jit(solution)/shard_map/step_0_shot_0/pallas_call | solution.py:447
  23.4 0.0 all-to-all-done
  23.4 1.2 %unpack_lines.1.saved_ref.refs_4_ = f32[128,256]{1,0:T(8,128)S(1)} custom-call(bf16[256,384]{1,0:T(8,128)(2,1)} %bitcast.1.got_ref), custom_call_target="tpu_custom_call" | custom-call | flops 1 | bytes 1 | tf_op jit(solution)/shard_map/unpack_lines/pallas_call | solution.py:181
  24.6 0.1 finish_first_0.1
  24.7 3.3 %collective-permute-start.7 = (bf16[2,2,128,256]{3,2,1,0:T(8,128)(2,1)S(1)}, bf16[2,2,128,256]{3,2,1,0:T(8,128)(2,1)S(1)}, u32[]{:S(2)}, u32[]{:S(2)}) collective-permute-start(bf16[2,2,128,256]{3,2,1,0:T(8,128)(2,1)S(1)} %get-tuple-element.51), channel_id=1, source_target_pairs={{1,2},{2,1},{3,4},{4,3},{5,6},{6,5},{7,8},{8,7},{9,10},{10,9},{11,... | collective-permute-start | bytes 786440 | tf_op jit(solution)/shard_map/ppermute | solution.py:36
  28.0 0.4 collective-permute-start.6
  28.4 9.1 %collective-permute-done.refs_2_ = bf16[2,2,128,256]{3,2,1,0:T(8,128)(2,1)} collective-permute-done((bf16[2,2,128,256]{3,2,1,0:T(8,128)(2,1)}, bf16[2,2,128,256]{3,2,1,0:T(8,128)(2,1)}, u32[]{:S(2)}, u32[]{:S(2)}) %collective-permute-start) | collective-permute-done | bytes 262176 | tf_op jit(solution)/shard_map/ppermute | solution.py:36
  37.5 3.8 %step_0_shot_1.1 = (f32[2,4,128,256]{3,2,1,0:T(8,128)S(1)}, bf16[2,2,128,256]{3,2,1,0:T(8,128)(2,1)S(1)}, bf16[2,2,128,256]{3,2,1,0:T(8,128)(2,1)S(1)}, f32[4,128,256]{2,1,0:T(8,128)S(1)}, f32[4,128,256]{2,1,0:T(8,128)S(1)}) custom-call(f32[2,2,2,4,128,256]{5,4,3,2,1,0:T(8,128)} %refs_1_.7, f32[2,2,2,4,128,256]{5,4,3,2,1,0:T(8,128)} %refs_1_.7, ...), custom_call_target="tpu_custom_call" | custom-call | flops 1 | bytes 1 | tf_op jit(solution)/shard_map/step_0_shot_1/pallas_call | solution.py:447
  41.4 3.3 %collective-permute-start.5 = (bf16[2,2,128,256]{3,2,1,0:T(8,128)(2,1)S(1)}, bf16[2,2,128,256]{3,2,1,0:T(8,128)(2,1)S(1)}, u32[]{:S(2)}, u32[]{:S(2)}) collective-permute-start(bf16[2,2,128,256]{3,2,1,0:T(8,128)(2,1)S(1)} %get-tuple-element.47), channel_id=1, source_target_pairs={{1,2},{2,1},{3,4},{4,3},{5,6},{6,5},{7,8},{8,7},{9,10},{10,9},{11,... | collective-permute-start | bytes 786440 | tf_op jit(solution)/shard_map/ppermute | solution.py:36
  44.7 0.1 collective-permute-start.4
  44.8 2.4 %step_1_shot_0.1 = (f32[2,4,128,256]{3,2,1,0:T(8,128)S(1)}, bf16[2,2,128,256]{3,2,1,0:T(8,128)(2,1)S(1)}, bf16[2,2,128,256]{3,2,1,0:T(8,128)(2,1)S(1)}, f32[4,128,256]{2,1,0:T(8,128)S(1)}) custom-call(f32[2,4,128,256]{3,2,1,0:T(8,128)S(1)} %get-tuple-element.50.refs_0_.refs_1_, f32[2,2,2,4,128,256]{5,4,3,2,1,0:T(8,128)} %refs_1_.7, ...), custom_call_target="tpu_custom_call" | custom-call | flops 1 | bytes 1 | tf_op jit(solution)/shard_map/step_1_shot_0/pallas_call | solution.py:447
  47.1 2.9 %collective-permute-start.11 = (bf16[2,2,128,256]{3,2,1,0:T(8,128)(2,1)S(1)}, bf16[2,2,128,256]{3,2,1,0:T(8,128)(2,1)S(1)}, u32[]{:S(2)}, u32[]{:S(2)}) collective-permute-start(bf16[2,2,128,256]{3,2,1,0:T(8,128)(2,1)S(1)} %get-tuple-element.60), channel_id=1, source_target_pairs={{1,2},{2,1},{3,4},{4,3},{5,6},{6,5},{7,8},{8,7},{9,10},{10,9},{11,... | collective-permute-start | bytes 786440 | tf_op jit(solution)/shard_map/ppermute | solution.py:36
  50.1 1.4 %collective-permute-start.10 = (bf16[2,2,128,256]{3,2,1,0:T(8,128)(2,1)S(1)}, bf16[2,2,128,256]{3,2,1,0:T(8,128)(2,1)S(1)}, u32[]{:S(2)}, u32[]{:S(2)}) collective-permute-start(bf16[2,2,128,256]{3,2,1,0:T(8,128)(2,1)S(1)} %get-tuple-element.54.refs_9_), channel_id=1, source_target_pairs={{0,1},{1,0},{2,3},{3,2},{4,5},{5,4},{6,7},{7,6},{8,9},{9,8},{10,11... | collective-permute-start | bytes 786440 | tf_op jit(solution)/shard_map/ppermute | solution.py:36
  51.4 11.3 %collective-permute-done.4.refs_2_ = bf16[2,2,128,256]{3,2,1,0:T(8,128)(2,1)S(1)} collective-permute-done((bf16[2,2,128,256]{3,2,1,0:T(8,128)(2,1)S(1)}, bf16[2,2,128,256]{3,2,1,0:T(8,128)(2,1)S(1)}, u32[]{:S(2)}, u32[]{:S(2)}) %collective-permute-start.4) | collective-permute-done | bytes 262176 | tf_op jit(solution)/shard_map/ppermute | solution.py:36
  62.8 2.5 %step_1_shot_1.1 = (f32[2,4,128,256]{3,2,1,0:T(8,128)S(1)}, bf16[2,2,128,256]{3,2,1,0:T(8,128)(2,1)S(1)}, bf16[2,2,128,256]{3,2,1,0:T(8,128)(2,1)S(1)}, f32[4,128,256]{2,1,0:T(8,128)S(1)}) custom-call(f32[2,4,128,256]{3,2,1,0:T(8,128)S(1)} %get-tuple-element.45.refs_0_.refs_1_, f32[2,2,2,4,128,256]{5,4,3,2,1,0:T(8,128)} %refs_1_.7, ...), custom_call_target="tpu_custom_call" | custom-call | flops 1 | bytes 1 | tf_op jit(solution)/shard_map/step_1_shot_1/pallas_call | solution.py:447
  65.3 2.9 %collective-permute-start.9 = (bf16[2,2,128,256]{3,2,1,0:T(8,128)(2,1)S(1)}, bf16[2,2,128,256]{3,2,1,0:T(8,128)(2,1)S(1)}, u32[]{:S(2)}, u32[]{:S(2)}) collective-permute-start(bf16[2,2,128,256]{3,2,1,0:T(8,128)(2,1)S(1)} %get-tuple-element.57), channel_id=1, source_target_pairs={{1,2},{2,1},{3,4},{4,3},{5,6},{6,5},{7,8},{8,7},{9,10},{10,9},{11,... | collective-permute-start | bytes 786440 | tf_op jit(solution)/shard_map/ppermute | solution.py:36
  68.2 0.1 collective-permute-start.8
  68.3 0.1 collective-permute-done.10.refs_2_
  68.4 1.2 %step_2_shot_0.1 = (f32[2,4,128,256]{3,2,1,0:T(8,128)S(1)}, bf16[2,2,128,256]{3,2,1,0:T(8,128)(2,1)S(1)}, bf16[2,2,128,256]{3,2,1,0:T(8,128)(2,1)S(1)}, f32[4,128,256]{2,1,0:T(8,128)S(1)}) custom-call(f32[2,4,128,256]{3,2,1,0:T(8,128)S(1)} %get-tuple-element.59.refs_0_.refs_1_, f32[2,4,128,256]{3,2,1,0:T(8,128)S(1)} %get-tuple-element.50.refs_0_.refs_1_, ...), custom_call_target="tpu_custom_call" | custom-call | flops 1 | bytes 1 | tf_op jit(solution)/shard_map/step_2_shot_0/pallas_call | solution.py:447
  69.6 3.1 %collective-permute-start.17 = (bf16[2,2,128,256]{3,2,1,0:T(8,128)(2,1)S(1)}, bf16[2,2,128,256]{3,2,1,0:T(8,128)(2,1)S(1)}, u32[]{:S(2)}, u32[]{:S(2)}) collective-permute-start(bf16[2,2,128,256]{3,2,1,0:T(8,128)(2,1)S(1)} %get-tuple-element.70), channel_id=1, source_target_pairs={{1,2},{2,1},{3,4},{4,3},{5,6},{6,5},{7,8},{8,7},{9,10},{10,9},{11,... | collective-permute-start | bytes 786440 | tf_op jit(solution)/shard_map/ppermute | solution.py:36
  72.8 1.4 %collective-permute-start.16 = (bf16[2,2,128,256]{3,2,1,0:T(8,128)(2,1)S(1)}, bf16[2,2,128,256]{3,2,1,0:T(8,128)(2,1)S(1)}, u32[]{:S(2)}, u32[]{:S(2)}) collective-permute-start(bf16[2,2,128,256]{3,2,1,0:T(8,128)(2,1)S(1)} %get-tuple-element.62.refs_9_), channel_id=1, source_target_pairs={{0,1},{1,0},{2,3},{3,2},{4,5},{5,4},{6,7},{7,6},{8,9},{9,8},{10,11... | collective-permute-start | bytes 786440 | tf_op jit(solution)/shard_map/ppermute | solution.py:36
  74.2 1.2 %collective-permute-done.9.refs_3_ = bf16[2,2,128,256]{3,2,1,0:T(8,128)(2,1)S(1)} collective-permute-done((bf16[2,2,128,256]{3,2,1,0:T(8,128)(2,1)S(1)}, bf16[2,2,128,256]{3,2,1,0:T(8,128)(2,1)S(1)}, u32[]{:S(2)}, u32[]{:S(2)}) %collective-permute-start.9) | collective-permute-done | bytes 262176 | tf_op jit(solution)/shard_map/ppermute | solution.py:36
  75.3 11.0 %collective-permute-done.8.refs_2_ = bf16[2,2,128,256]{3,2,1,0:T(8,128)(2,1)S(1)} collective-permute-done((bf16[2,2,128,256]{3,2,1,0:T(8,128)(2,1)S(1)}, bf16[2,2,128,256]{3,2,1,0:T(8,128)(2,1)S(1)}, u32[]{:S(2)}, u32[]{:S(2)}) %collective-permute-start.8) | collective-permute-done | bytes 262176 | tf_op jit(solution)/shard_map/ppermute | solution.py:36
  86.3 1.2 %step_2_shot_1.1 = (f32[2,4,128,256]{3,2,1,0:T(8,128)S(1)}, bf16[1,2,128,256]{3,2,1,0:T(8,128)(2,1)S(1)}, bf16[1,2,128,256]{3,2,1,0:T(8,128)(2,1)S(1)}, bf16[1,2...) custom-call(f32[2,4,128,256]{3,2,1,0:T(8,128)S(1)} %get-tuple-element.55.refs_0_.refs_, ...), custom_call_target="tpu_custom_call" | custom-call | flops 1 | bytes 1 | tf_op jit(solution)/shard_map/step_2_shot_1/pallas_call | solution.py:447
  87.6 3.3 %collective-permute-start.15 = (bf16[1,2,128,256]{3,2,1,0:T(8,128)(2,1)S(1)}, bf16[1,2,128,256]{3,2,1,0:T(8,128)(2,1)S(1)}, u32[]{:S(2)}, u32[]{:S(2)}) collective-permute-start(bf16[1,2,128,256]{3,2,1,0:T(8,128)(2,1)S(1)} %get-tuple-element.67), channel_id=1, source_target_pairs={{1,2},{2,1},{3,4},{4,3},{5,6},{6,5},{7,8},{8,7},{9,10},{10,9},{11,... | collective-permute-start | bytes 393224 | tf_op jit(solution)/shard_map/ppermute | solution.py:36
  90.8 0.1 collective-permute-start.14
  90.9 1.5 %collective-permute-start.12 = (bf16[1,2,128,256]{3,2,1,0:T(8,128)(2,1)S(1)}, bf16[1,2,128,256]{3,2,1,0:T(8,128)(2,1)S(1)}, u32[]{:S(2)}, u32[]{:S(2)}) collective-permute-start(bf16[1,2,128,256]{3,2,1,0:T(8,128)(2,1)S(1)} %get-tuple-element.64), channel_id=1, source_target_pairs={{0,1},{1,0},{2,3},{3,2},{4,5},{5,4},{6,7},{7,6},{8,9},{9,8},{10,11... | collective-permute-start | bytes 393224 | tf_op jit(solution)/shard_map/ppermute | solution.py:36
  92.4 2.9 %collective-permute-start.13 = (bf16[1,2,128,256]{3,2,1,0:T(8,128)(2,1)S(1)}, bf16[1,2,128,256]{3,2,1,0:T(8,128)(2,1)S(1)}, u32[]{:S(2)}, u32[]{:S(2)}) collective-permute-start(bf16[1,2,128,256]{3,2,1,0:T(8,128)(2,1)S(1)} %get-tuple-element.65), channel_id=1, source_target_pairs={{1,2},{2,1},{3,4},{4,3},{5,6},{6,5},{7,8},{8,7},{9,10},{10,9},{11,... | collective-permute-start | bytes 393224 | tf_op jit(solution)/shard_map/ppermute | solution.py:36
  95.3 3.4 %step_3_shot_0.1 = (f32[2,2,2,4,128,256]{5,4,3,2,1,0:T(8,128)}, f32[4,200,256]{2,1,0:T(8,128)}) custom-call(f32[2,4,128,256]{3,2,1,0:T(8,128)S(1)} %get-tuple-element.69.refs_0_.refs_10_, f32[2,4,128,256]{3,2,1,0:T(8,128)S(1)} %get-tuple-element.59.refs_0_.refs_1_, bf16[2,2,128,256]{3,2,1,0:T(8,128)(2,1)S(1)} %collective-permute-done.16.refs_2_, ...), custom_call_target="tpu_custom_call" | custom-call | flops 1 | bytes 1 | tf_op jit(solution)/shard_map/step_3_shot_0/pallas_call | solution.py:447
  98.7 1.8 %collective-permute-start.18 = (f32[4,200,256]{2,1,0:T(8,128)}, f32[4,200,256]{2,1,0:T(8,128)}, u32[]{:S(2)}, u32[]{:S(2)}) collective-permute-start(f32[4,200,256]{2,1,0:T(8,128)} %get-tuple-element.72.refs_9_.refs_0_), channel_id=1, source_target_pairs={{0,16},{16,0},{1,17},{17,1},{2,18},{18,2},{3,19},{19,3},{4,20},{20... | collective-permute-start | bytes 2457608 | tf_op jit(solution)/shard_map/ppermute | solution.py:576
  100.5 0.0 collective-permute-done.14.refs_2_
  100.6 2.2 %step_3_shot_1.2 = (f32[4,128,256]{2,1,0:T(8,128)S(1)}, f32[4,200,256]{2,1,0:T(8,128)}) custom-call(f32[2,4,128,256]{3,2,1,0:T(8,128)S(1)} %get-tuple-element.63.refs_11_.refs_0_, f32[2,4,128,256]{3,2,1,0:T(8,128)S(1)} %get-tuple-element.55.refs_0_.refs_1_, bf16[1,2,128,256]{3,2,1,0:T(8,128)(2,1)S(1)} %collective-permute-done.14.refs_2_, ...), custom_call_target="tpu_custom_call" | custom-call | flops 1 | bytes 1 | tf_op jit(solution)/shard_map/step_3_shot_1/pallas_call | solution.py:447
  102.8 0.6 collective-permute-start.19
  103.3 0.0 collective-permute-done.12.refs_2_
  103.4 0.2 collective-permute-done.13.refs_3_
  103.6 1.4 %step_3_shot_1.3.refs_4_ = f32[2,2,2,4,128,256]{5,4,3,2,1,0:T(8,128)} custom-call(f32[2,4,128,256]{3,2,1,0:T(8,128)S(1)} %get-tuple-element.63.refs_11_.refs_0_, f32[2,4,128,256]{3,2,1,0:T(8,128)S(1)} %get-tuple-element.55.refs_0_.refs_1_, bf16[1,2,128,256]{3,2,1,0:T(8,128)(2,1)S(1)} %collective-permute-done.12.refs_2_, ...), custom_call_target="tpu_custom_call", output_to_operand_aliasing={{}: (8, {})} | custom-call | flops 9999999827968 | bytes 1 | tf_op jit(solution)/shard_map/step_3_shot_1/pallas_call | solution.py:447
  105.0 0.7 collective-permute-done.19.refs_3_
  105.7 2.8 %sum_frames.1 = f32[4,192,256]{2,1,0:T(8,128)} custom-call(f32[4,200,256]{2,1,0:T(8,128)} %get-tuple-element.72.refs_9_.refs_0_, f32[4,200,256]{2,1,0:T(8,128)} %collective-permute-done.18.refs_1_, f32[4,200,256]{2,1,0:T(8,128)} %get-tuple-element.74.refs_7_.refs_2_, f32[4,200,256]{2,1,0:T(8,128)} %collective-permute-done.19.refs_3_, ...), custom_call_target="tpu_custom_call" | custom-call | flops 1 | bytes 1 | tf_op jit(solution)/shard_map/sum_frames/pallas_call | solution.py:488
  (21 shorter events, 0.0 us)
Async XLA Ops:
  0.6 5.7 %copy-start.5 = (s32[2,128]{1,0:T(2,128)S(1)}, s32[2,128]{1,0:T(2,128)}, u32[]{:S(2)}) copy-start(s32[2,128]{1,0:T(2,128)} %ids_ref.1) | copy-start | bytes 3076
  0.6 5.7 %copy-start.2 = (bf16[2,128,256]{2,1,0:T(8,128)(2,1)S(1)}, bf16[2,128,256]{2,1,0:T(8,128)(2,1)}, u32[]{:S(2)}) copy-start(bf16[2,128,256]{2,1,0:T(8,128)(2,1)} %lines_ref.1) | copy-start | bytes 393220
  0.7 19.4 %copy-start.1 = (f32[2,4,64]{2,1,0:T(4,128)S(1)}, f32[2,4,64]{2,1,0:T(4,128)}, u32[]{:S(2)}) copy-start(f32[2,4,64]{2,1,0:T(4,128)} %refs_5_.15) | copy-start | bytes 6148
  0.7 19.4 %copy-start.3 = (s32[2,64]{1,0:T(2,128)S(1)}, s32[2,64]{1,0:T(2,128)}, u32[]{:S(2)}) copy-start(s32[2,64]{1,0:T(2,128)} %refs_4_.3) | copy-start | bytes 1540
  0.7 19.4 %copy-start.4 = (s32[2]{0:T(128)S(1)}, s32[2]{0:T(128)}, u32[]{:S(2)}) copy-start(s32[2]{0:T(128)} %refs_6_.15) | copy-start | bytes 28
  0.7 19.4 %copy-start = (f32[4,192,256]{2,1,0:T(8,128)S(1)}, f32[4,192,256]{2,1,0:T(8,128)}, u32[]{:S(2)}) copy-start(f32[4,192,256]{2,1,0:T(8,128)} %refs_8_.1) | copy-start | bytes 2359300
  2.0 17.3 %collective-permute-start.3 = (bf16[2,2,128,256]{3,2,1,0:T(8,128)(2,1)S(1)}, bf16[2,2,128,256]{3,2,1,0:T(8,128)(2,1)S(1)}, u32[]{:S(2)}, u32[]{:S(2)}) collective-permute-start(bf16[2,2,128,256]{3,2,1,0:T(8,128)(2,1)S(1)} %get-tuple-element.42), channel_id=1, source_target_pairs={{1,2},{2,1},{3,4},{4,3},{5,6},{6,5},{7,8},{8,7},{9,10},{10,9},{11,... | collective-permute-start | bytes 786440 | tf_op jit(solution)/shard_map/ppermute | solution.py:36
  5.2 14.9 %collective-permute-start.2 = (bf16[2,2,128,256]{3,2,1,0:T(8,128)(2,1)S(1)}, bf16[2,2,128,256]{3,2,1,0:T(8,128)(2,1)S(1)}, u32[]{:S(2)}, u32[]{:S(2)}) collective-permute-start(bf16[2,2,128,256]{3,2,1,0:T(8,128)(2,1)S(1)} %get-tuple-element.39.after_ref), channel_id=1, source_target_pairs={{0,1},{1,0},{2,3},{3,2},{4,5},{5,4},{6,7},{7,6},{8,9},{9,8},{10,11... | collective-permute-start | bytes 786440 | tf_op jit(solution)/shard_map/ppermute | solution.py:36
  7.3 16.0 %all-to-all-start = ((bf16[16,16,384]{2,1,0:T(8,128)(2,1)}), bf16[16,16,384]{2,1,0:T(8,128)(2,1)}, u32[]{:S(2)}, u32[]{:S(2)}) async-start(bf16[16,16,384]{2,1,0:T(8,128)(2,1)} %bitcast), calls=%async_computation | async-start | bytes 393216 | tf_op jit(solution)/shard_map/all_to_all | solution.py:180
  15.0 22.5 %collective-permute-start = (bf16[2,2,128,256]{3,2,1,0:T(8,128)(2,1)}, bf16[2,2,128,256]{3,2,1,0:T(8,128)(2,1)}, u32[]{:S(2)}, u32[]{:S(2)}) collective-permute-start(bf16[2,2,128,256]{3,2,1,0:T(8,128)(2,1)} %get-tuple-element.40), channel_id=1, source_target_pairs={{0,1},{1,0},{2,3},{3,2},{4,5},{5,4},{6,7},{7,6},{8,9},{9,8},{10,11... | collective-permute-start | bytes 786440 | tf_op jit(solution)/shard_map/ppermute | solution.py:36
  15.4 22.2 %collective-permute-start.1 = (bf16[2,2,128,256]{3,2,1,0:T(8,128)(2,1)}, bf16[2,2,128,256]{3,2,1,0:T(8,128)(2,1)}, u32[]{:S(2)}, u32[]{:S(2)}) collective-permute-start(bf16[2,2,128,256]{3,2,1,0:T(8,128)(2,1)} %get-tuple-element.41), channel_id=1, source_target_pairs={{1,2},{2,1},{3,4},{4,3},{5,6},{6,5},{7,8},{8,7},{9,10},{10,9},{11,... | collective-permute-start | bytes 786440 | tf_op jit(solution)/shard_map/ppermute | solution.py:36
  24.7 20.0 %collective-permute-start.7 = (bf16[2,2,128,256]{3,2,1,0:T(8,128)(2,1)S(1)}, bf16[2,2,128,256]{3,2,1,0:T(8,128)(2,1)S(1)}, u32[]{:S(2)}, u32[]{:S(2)}) collective-permute-start(bf16[2,2,128,256]{3,2,1,0:T(8,128)(2,1)S(1)} %get-tuple-element.51), channel_id=1, source_target_pairs={{1,2},{2,1},{3,4},{4,3},{5,6},{6,5},{7,8},{8,7},{9,10},{10,9},{11,... | collective-permute-start | bytes 786440 | tf_op jit(solution)/shard_map/ppermute | solution.py:36
  28.0 16.7 %collective-permute-start.6 = (bf16[2,2,128,256]{3,2,1,0:T(8,128)(2,1)S(1)}, bf16[2,2,128,256]{3,2,1,0:T(8,128)(2,1)S(1)}, u32[]{:S(2)}, u32[]{:S(2)}) collective-permute-start(bf16[2,2,128,256]{3,2,1,0:T(8,128)(2,1)S(1)} %get-tuple-element.44.refs_9_), channel_id=1, source_target_pairs={{0,1},{1,0},{2,3},{3,2},{4,5},{5,4},{6,7},{7,6},{8,9},{9,8},{10,11... | collective-permute-start | bytes 786440 | tf_op jit(solution)/shard_map/ppermute | solution.py:36
  41.4 10.1 %collective-permute-start.5 = (bf16[2,2,128,256]{3,2,1,0:T(8,128)(2,1)S(1)}, bf16[2,2,128,256]{3,2,1,0:T(8,128)(2,1)S(1)}, u32[]{:S(2)}, u32[]{:S(2)}) collective-permute-start(bf16[2,2,128,256]{3,2,1,0:T(8,128)(2,1)S(1)} %get-tuple-element.47), channel_id=1, source_target_pairs={{1,2},{2,1},{3,4},{4,3},{5,6},{6,5},{7,8},{8,7},{9,10},{10,9},{11,... | collective-permute-start | bytes 786440 | tf_op jit(solution)/shard_map/ppermute | solution.py:36
  44.7 18.1 %collective-permute-start.4 = (bf16[2,2,128,256]{3,2,1,0:T(8,128)(2,1)S(1)}, bf16[2,2,128,256]{3,2,1,0:T(8,128)(2,1)S(1)}, u32[]{:S(2)}, u32[]{:S(2)}) collective-permute-start(bf16[2,2,128,256]{3,2,1,0:T(8,128)(2,1)S(1)} %get-tuple-element.46.refs_9_), channel_id=1, source_target_pairs={{0,1},{1,0},{2,3},{3,2},{4,5},{5,4},{6,7},{7,6},{8,9},{9,8},{10,11... | collective-permute-start | bytes 786440 | tf_op jit(solution)/shard_map/ppermute | solution.py:36
  47.1 21.1 %collective-permute-start.11 = (bf16[2,2,128,256]{3,2,1,0:T(8,128)(2,1)S(1)}, bf16[2,2,128,256]{3,2,1,0:T(8,128)(2,1)S(1)}, u32[]{:S(2)}, u32[]{:S(2)}) collective-permute-start(bf16[2,2,128,256]{3,2,1,0:T(8,128)(2,1)S(1)} %get-tuple-element.60), channel_id=1, source_target_pairs={{1,2},{2,1},{3,4},{4,3},{5,6},{6,5},{7,8},{8,7},{9,10},{10,9},{11,... | collective-permute-start | bytes 786440 | tf_op jit(solution)/shard_map/ppermute | solution.py:36
  50.1 18.4 %collective-permute-start.10 = (bf16[2,2,128,256]{3,2,1,0:T(8,128)(2,1)S(1)}, bf16[2,2,128,256]{3,2,1,0:T(8,128)(2,1)S(1)}, u32[]{:S(2)}, u32[]{:S(2)}) collective-permute-start(bf16[2,2,128,256]{3,2,1,0:T(8,128)(2,1)S(1)} %get-tuple-element.54.refs_9_), channel_id=1, source_target_pairs={{0,1},{1,0},{2,3},{3,2},{4,5},{5,4},{6,7},{7,6},{8,9},{9,8},{10,11... | collective-permute-start | bytes 786440 | tf_op jit(solution)/shard_map/ppermute | solution.py:36
  65.3 10.1 %collective-permute-start.9 = (bf16[2,2,128,256]{3,2,1,0:T(8,128)(2,1)S(1)}, bf16[2,2,128,256]{3,2,1,0:T(8,128)(2,1)S(1)}, u32[]{:S(2)}, u32[]{:S(2)}) collective-permute-start(bf16[2,2,128,256]{3,2,1,0:T(8,128)(2,1)S(1)} %get-tuple-element.57), channel_id=1, source_target_pairs={{1,2},{2,1},{3,4},{4,3},{5,6},{6,5},{7,8},{8,7},{9,10},{10,9},{11,... | collective-permute-start | bytes 786440 | tf_op jit(solution)/shard_map/ppermute | solution.py:36
  68.2 18.1 %collective-permute-start.8 = (bf16[2,2,128,256]{3,2,1,0:T(8,128)(2,1)S(1)}, bf16[2,2,128,256]{3,2,1,0:T(8,128)(2,1)S(1)}, u32[]{:S(2)}, u32[]{:S(2)}) collective-permute-start(bf16[2,2,128,256]{3,2,1,0:T(8,128)(2,1)S(1)} %get-tuple-element.56.refs_9_), channel_id=1, source_target_pairs={{0,1},{1,0},{2,3},{3,2},{4,5},{5,4},{6,7},{7,6},{8,9},{9,8},{10,11... | collective-permute-start | bytes 786440 | tf_op jit(solution)/shard_map/ppermute | solution.py:36
  69.6 22.7 %collective-permute-start.17 = (bf16[2,2,128,256]{3,2,1,0:T(8,128)(2,1)S(1)}, bf16[2,2,128,256]{3,2,1,0:T(8,128)(2,1)S(1)}, u32[]{:S(2)}, u32[]{:S(2)}) collective-permute-start(bf16[2,2,128,256]{3,2,1,0:T(8,128)(2,1)S(1)} %get-tuple-element.70), channel_id=1, source_target_pairs={{1,2},{2,1},{3,4},{4,3},{5,6},{6,5},{7,8},{8,7},{9,10},{10,9},{11,... | collective-permute-start | bytes 786440 | tf_op jit(solution)/shard_map/ppermute | solution.py:36
  72.8 22.5 %collective-permute-start.16 = (bf16[2,2,128,256]{3,2,1,0:T(8,128)(2,1)S(1)}, bf16[2,2,128,256]{3,2,1,0:T(8,128)(2,1)S(1)}, u32[]{:S(2)}, u32[]{:S(2)}) collective-permute-start(bf16[2,2,128,256]{3,2,1,0:T(8,128)(2,1)S(1)} %get-tuple-element.62.refs_9_), channel_id=1, source_target_pairs={{0,1},{1,0},{2,3},{3,2},{4,5},{5,4},{6,7},{7,6},{8,9},{9,8},{10,11... | collective-permute-start | bytes 786440 | tf_op jit(solution)/shard_map/ppermute | solution.py:36
  87.6 13.0 %collective-permute-start.15 = (bf16[1,2,128,256]{3,2,1,0:T(8,128)(2,1)S(1)}, bf16[1,2,128,256]{3,2,1,0:T(8,128)(2,1)S(1)}, u32[]{:S(2)}, u32[]{:S(2)}) collective-permute-start(bf16[1,2,128,256]{3,2,1,0:T(8,128)(2,1)S(1)} %get-tuple-element.67), channel_id=1, source_target_pairs={{1,2},{2,1},{3,4},{4,3},{5,6},{6,5},{7,8},{8,7},{9,10},{10,9},{11,... | collective-permute-start | bytes 393224 | tf_op jit(solution)/shard_map/ppermute | solution.py:36
  90.8 9.7 %collective-permute-start.14 = (bf16[1,2,128,256]{3,2,1,0:T(8,128)(2,1)S(1)}, bf16[1,2,128,256]{3,2,1,0:T(8,128)(2,1)S(1)}, u32[]{:S(2)}, u32[]{:S(2)}) collective-permute-start(bf16[1,2,128,256]{3,2,1,0:T(8,128)(2,1)S(1)} %get-tuple-element.66.refs_12_), channel_id=1, source_target_pairs={{0,1},{1,0},{2,3},{3,2},{4,5},{5,4},{6,7},{7,6},{8,9},{9,8},{10,11... | collective-permute-start | bytes 393224 | tf_op jit(solution)/shard_map/ppermute | solution.py:36
  90.9 12.4 %collective-permute-start.12 = (bf16[1,2,128,256]{3,2,1,0:T(8,128)(2,1)S(1)}, bf16[1,2,128,256]{3,2,1,0:T(8,128)(2,1)S(1)}, u32[]{:S(2)}, u32[]{:S(2)}) collective-permute-start(bf16[1,2,128,256]{3,2,1,0:T(8,128)(2,1)S(1)} %get-tuple-element.64), channel_id=1, source_target_pairs={{0,1},{1,0},{2,3},{3,2},{4,5},{5,4},{6,7},{7,6},{8,9},{9,8},{10,11... | collective-permute-start | bytes 393224 | tf_op jit(solution)/shard_map/ppermute | solution.py:36
  92.4 11.2 %collective-permute-start.13 = (bf16[1,2,128,256]{3,2,1,0:T(8,128)(2,1)S(1)}, bf16[1,2,128,256]{3,2,1,0:T(8,128)(2,1)S(1)}, u32[]{:S(2)}, u32[]{:S(2)}) collective-permute-start(bf16[1,2,128,256]{3,2,1,0:T(8,128)(2,1)S(1)} %get-tuple-element.65), channel_id=1, source_target_pairs={{1,2},{2,1},{3,4},{4,3},{5,6},{6,5},{7,8},{8,7},{9,10},{10,9},{11,... | collective-permute-start | bytes 393224 | tf_op jit(solution)/shard_map/ppermute | solution.py:36
  98.7 6.9 %collective-permute-start.18 = (f32[4,200,256]{2,1,0:T(8,128)}, f32[4,200,256]{2,1,0:T(8,128)}, u32[]{:S(2)}, u32[]{:S(2)}) collective-permute-start(f32[4,200,256]{2,1,0:T(8,128)} %get-tuple-element.72.refs_9_.refs_0_), channel_id=1, source_target_pairs={{0,16},{16,0},{1,17},{17,1},{2,18},{18,2},{3,19},{19,3},{4,20},{20... | collective-permute-start | bytes 2457608 | tf_op jit(solution)/shard_map/ppermute | solution.py:576
  102.8 2.9 %collective-permute-start.19 = (f32[4,200,256]{2,1,0:T(8,128)}, f32[4,200,256]{2,1,0:T(8,128)}, u32[]{:S(2)}, u32[]{:S(2)}) collective-permute-start(f32[4,200,256]{2,1,0:T(8,128)} %get-tuple-element.74.refs_7_.refs_2_), channel_id=1, source_target_pairs={{0,16},{16,0},{1,17},{17,1},{2,18},{18,2},{3,19},{19,3},{4,20},{20... | collective-permute-start | bytes 2457608 | tf_op jit(solution)/shard_map/ppermute | solution.py:576

commit v7 on v6

--- a/solution.py
+++ b/solution.py
@@ -54,17 +54,19 @@
     return pl.multiple_of(start, 8), offset - start
 
 
-def put_window(target_ref, layer, part, offset):
-    rows_y, cells_z = part.shape
-    groups = rows_y // 8
+def put_window(target_ref, layer, part_ref, offset):
+    _, rows_y, cells_z = part_ref.shape
     start = pl.multiple_of(lax.div(offset, 8) * 8, 8)
     gap = lax.rem(offset, 8)
-    turned = pltpu.roll(part.reshape(groups, 8, cells_z), gap, 1)
     before = lax.broadcasted_iota(jnp.int32, (8, cells_z), 0) < gap
-    body = [jnp.where(before, 0.0, turned[0])]
-    body += [jnp.where(before, turned[at - 1], turned[at]) for at in range(1, groups)]
-    body.append(jnp.where(before, turned[-1], 0.0))
-    target_ref[layer, pl.ds(start, rows_y + 8), :] = jnp.concatenate(body, axis=0)
+    last = jnp.zeros((8, cells_z), jnp.float32)
+    for at in range(0, rows_y + 8, 8):
+        turned = jnp.zeros((8, cells_z), jnp.float32)
+        if at < rows_y:
+            turned = pltpu.roll(part_ref[layer, at : at + 8], gap, 0)
+        here = pl.ds(pl.multiple_of(start + at, 8), 8)
+        target_ref[layer, here, :] = jnp.where(before, last, turned)
+        last = turned
 
 
 def is_odd():
@@ -359,7 +361,7 @@
     if framing:
         contrib_ref[...] = jnp.zeros_like(contrib_ref)
         for layer in range(layers):
-            put_window(contrib_ref, layer, terms_ref[layer], offsets_ref[shot])
+            put_window(contrib_ref, layer, terms_ref, offsets_ref[shot])
     for started in stores:
         started.wait()
     if not last:
@@ -466,12 +468,13 @@
     layers, model_y, _ = sum_ref.shape
     stores = []
     for layer in range(layers):
-        total = None
-        for at in range(0, len(frame_refs), 2):
-            own_ref, other_ref = frame_refs[at : at + 2]
-            pair = own_ref[layer, :model_y] + other_ref[layer, :model_y]
-            total = pair if total is None else total + pair
-        sum_ref[layer] = total * scale
+        for row in range(0, model_y, 16):
+            rows = slice(row, row + 16)
+            total = None
+            for at in range(0, len(frame_refs), 2):
+                pair = frame_refs[at][layer, rows] + frame_refs[at + 1][layer, rows]
+                total = pair if total is None else total + pair
+            sum_ref[layer, rows] = total * scale
         stores.append(
             pltpu.make_async_copy(sum_ref.at[layer], image_ref.at[layer], sems.at[layer])
         )

time: 109 us -> 109 us (level)
  no operation moved by 1% of the time
where the time goes in v7:
time: 109 us; the launch traced here: 108 us
  starting transfers between devices  43.1 us (40%)
  waiting for transfers between devices  34.4 us (32%)
  Pallas kernels  30 us (28%)
    ppermute x18, starting transfers between devices, swap_pairs(): return lax.ppermute(value, 'space', routes)  35.1 us
    ppermute x18, waiting for transfers between devices, swap_pairs(): return lax.ppermute(value, 'space', routes)  33.7 us
    pallas_call x9, Pallas kernels, one_step(): pl.pallas_call(functools.partial(step_kernel, shot, step, comps, got_grou...  21.5 us
    all_to_all x1, starting transfers between devices, deliver(): got = lax.all_to_all(message, 'space', 0, 0, tiled=False)  5.63 us
    pallas_call x2, Pallas kernels, pack_halo(): pl.pallas_call(functools.partial(pack_kernel, shot), in_specs=[pl.BlockSp...  3.36 us
    pallas_call x1, Pallas kernels, sum_frames(): pl.pallas_call(functools.partial(sum_kernel, scale), in_specs=[vmem] * le...  2.83 us
    ppermute x2, starting transfers between devices, body(): others = [lax.ppermute(frame, 'shot', [(0, 1), (1, 0)]) for frame in frames]  2.36 us
  transfers between devices with their start and end apart: 21, of which 8 were waited for; matrix products, arithmetic and copies ran while one was open for 0% of the time, Pallas kernels for 24%

profile of v7, /device:TPU:19, one launch (start us, length us, event | category | flops | bytes accessed | tf_op | source)
XLA Modules:
  0.0 108.5 jit_solution(3966564084614188873)
XLA Ops:
  0.7 1.3 %pack_halo.2 = (bf16[2,2,128,256]{3,2,1,0:T(8,128)(2,1)S(1)}, bf16[2,2,128,256]{3,2,1,0:T(8,128)(2,1)S(1)}) custom-call(f32[2,2,2,4,128,256]{5,4,3,2,1,0:T(8,128)} %refs_1_.7), custom_call_target="tpu_custom_call" | custom-call | flops 1 | bytes 1 | tf_op jit(solution)/shard_map/pack_halo/pallas_call | solution.py:105
  2.0 3.1 %collective-permute-start.3 = (bf16[2,2,128,256]{3,2,1,0:T(8,128)(2,1)S(1)}, bf16[2,2,128,256]{3,2,1,0:T(8,128)(2,1)S(1)}, u32[]{:S(2)}, u32[]{:S(2)}) collective-permute-start(bf16[2,2,128,256]{3,2,1,0:T(8,128)(2,1)S(1)} %get-tuple-element.42), channel_id=1, source_target_pairs={{1,2},{2,1},{3,4},{4,3},{5,6},{6,5},{7,8},{8,7},{9,10},{10,9},{11,... | collective-permute-start | bytes 786440 | tf_op jit(solution)/shard_map/ppermute | solution.py:36
  5.2 1.2 %collective-permute-start.2 = (bf16[2,2,128,256]{3,2,1,0:T(8,128)(2,1)S(1)}, bf16[2,2,128,256]{3,2,1,0:T(8,128)(2,1)S(1)}, u32[]{:S(2)}, u32[]{:S(2)}) collective-permute-start(bf16[2,2,128,256]{3,2,1,0:T(8,128)(2,1)S(1)} %get-tuple-element.39.after_ref), channel_id=1, source_target_pairs={{0,1},{1,0},{2,3},{3,2},{4,5},{5,4},{6,7},{7,6},{8,9},{9,8},{10,11... | collective-permute-start | bytes 786440 | tf_op jit(solution)/shard_map/ppermute | solution.py:36
  6.3 1.0 pack_lines.1.refs_0_
  7.3 5.6 %all-to-all-start = ((bf16[16,16,384]{2,1,0:T(8,128)(2,1)}), bf16[16,16,384]{2,1,0:T(8,128)(2,1)}, u32[]{:S(2)}, u32[]{:S(2)}) async-start(bf16[16,16,384]{2,1,0:T(8,128)(2,1)} %bitcast), calls=%async_computation | async-start | bytes 393216 | tf_op jit(solution)/shard_map/all_to_all | solution.py:182
  13.0 2.0 %pack_halo.3 = (bf16[2,2,128,256]{3,2,1,0:T(8,128)(2,1)}, bf16[2,2,128,256]{3,2,1,0:T(8,128)(2,1)}) custom-call(f32[2,2,2,4,128,256]{5,4,3,2,1,0:T(8,128)} %refs_1_.7, bf16[256,384]{1,0:T(8,128)(2,1)} %pack_lines.1.refs_0_), custom_call_target="tpu_custom_call" | custom-call | flops 1 | bytes 1 | tf_op jit(solution)/shard_map/pack_halo/pallas_call | solution.py:105
  15.0 0.3 collective-permute-start
  15.4 4.0 %collective-permute-start.1 = (bf16[2,2,128,256]{3,2,1,0:T(8,128)(2,1)}, bf16[2,2,128,256]{3,2,1,0:T(8,128)(2,1)}, u32[]{:S(2)}, u32[]{:S(2)}) collective-permute-start(bf16[2,2,128,256]{3,2,1,0:T(8,128)(2,1)} %get-tuple-element.41), channel_id=1, source_target_pairs={{1,2},{2,1},{3,4},{4,3},{5,6},{6,5},{7,8},{8,7},{9,10},{10,9},{11,... | collective-permute-start | bytes 786440 | tf_op jit(solution)/shard_map/ppermute | solution.py:36
  19.3 0.0 collective-permute-done.3.refs_3_
  19.4 0.7 collective-permute-done.2.refs_2_
  20.1 3.3 %step_0_shot_0.1 = (f32[2,4,128,256]{3,2,1,0:T(8,128)S(1)}, f32[4,128,256]{2,1,0:T(8,128)S(1)}, f32[4,128,256]{2,1,0:T(8,128)S(1)}) custom-call(f32[2,2,2,4,128,256]{5,4,3,2,1,0:T(8,128)} %refs_1_.7, f32[2,2,2,4,128,256]{5,4,3,2,1,0:T(8,128)} %refs_1_.7, bf16[2,2,128,256]{3,2,1,0:T(8,128)(2,1)S(1)} %collective-permute-done.2.refs_2_, ...), custom_call_target="tpu_custom_call" | custom-call | flops 9999999827968 | bytes 1 | tf_op jit(solution)/shard_map/step_0_shot_0/pallas_call | solution.py:449
  23.4 1.2 %unpack_lines.1.saved_ref.refs_4_ = f32[128,256]{1,0:T(8,128)S(1)} custom-call(bf16[256,384]{1,0:T(8,128)(2,1)} %bitcast.1.got_ref), custom_call_target="tpu_custom_call" | custom-call | flops 1 | bytes 1 | tf_op jit(solution)/shard_map/unpack_lines/pallas_call | solution.py:183
  24.6 0.1 finish_first_0.1
  24.7 3.3 %collective-permute-start.7 = (bf16[2,2,128,256]{3,2,1,0:T(8,128)(2,1)S(1)}, bf16[2,2,128,256]{3,2,1,0:T(8,128)(2,1)S(1)}, u32[]{:S(2)}, u32[]{:S(2)}) collective-permute-start(bf16[2,2,128,256]{3,2,1,0:T(8,128)(2,1)S(1)} %get-tuple-element.51), channel_id=1, source_target_pairs={{1,2},{2,1},{3,4},{4,3},{5,6},{6,5},{7,8},{8,7},{9,10},{10,9},{11,... | collective-permute-start | bytes 786440 | tf_op jit(solution)/shard_map/ppermute | solution.py:36
  28.0 0.4 collective-permute-start.6
  28.4 9.1 %collective-permute-done.refs_2_ = bf16[2,2,128,256]{3,2,1,0:T(8,128)(2,1)} collective-permute-done((bf16[2,2,128,256]{3,2,1,0:T(8,128)(2,1)}, bf16[2,2,128,256]{3,2,1,0:T(8,128)(2,1)}, u32[]{:S(2)}, u32[]{:S(2)}) %collective-permute-start) | collective-permute-done | bytes 262176 | tf_op jit(solution)/shard_map/ppermute | solution.py:36
  37.5 3.8 %step_0_shot_1.1 = (f32[2,4,128,256]{3,2,1,0:T(8,128)S(1)}, bf16[2,2,128,256]{3,2,1,0:T(8,128)(2,1)S(1)}, bf16[2,2,128,256]{3,2,1,0:T(8,128)(2,1)S(1)}, f32[4,128,256]{2,1,0:T(8,128)S(1)}, f32[4,128,256]{2,1,0:T(8,128)S(1)}) custom-call(f32[2,2,2,4,128,256]{5,4,3,2,1,0:T(8,128)} %refs_1_.7, f32[2,2,2,4,128,256]{5,4,3,2,1,0:T(8,128)} %refs_1_.7, ...), custom_call_target="tpu_custom_call" | custom-call | flops 1 | bytes 1 | tf_op jit(solution)/shard_map/step_0_shot_1/pallas_call | solution.py:449
  41.4 3.3 %collective-permute-start.5 = (bf16[2,2,128,256]{3,2,1,0:T(8,128)(2,1)S(1)}, bf16[2,2,128,256]{3,2,1,0:T(8,128)(2,1)S(1)}, u32[]{:S(2)}, u32[]{:S(2)}) collective-permute-start(bf16[2,2,128,256]{3,2,1,0:T(8,128)(2,1)S(1)} %get-tuple-element.47), channel_id=1, source_target_pairs={{1,2},{2,1},{3,4},{4,3},{5,6},{6,5},{7,8},{8,7},{9,10},{10,9},{11,... | collective-permute-start | bytes 786440 | tf_op jit(solution)/shard_map/ppermute | solution.py:36
  44.7 0.1 collective-permute-start.4
  44.7 0.0 collective-permute-done.7.refs_3_
  44.8 2.4 %step_1_shot_0.1 = (f32[2,4,128,256]{3,2,1,0:T(8,128)S(1)}, bf16[2,2,128,256]{3,2,1,0:T(8,128)(2,1)S(1)}, bf16[2,2,128,256]{3,2,1,0:T(8,128)(2,1)S(1)}, f32[4,128,256]{2,1,0:T(8,128)S(1)}) custom-call(f32[2,4,128,256]{3,2,1,0:T(8,128)S(1)} %get-tuple-element.50.refs_0_.refs_1_, f32[2,2,2,4,128,256]{5,4,3,2,1,0:T(8,128)} %refs_1_.7, ...), custom_call_target="tpu_custom_call" | custom-call | flops 1 | bytes 1 | tf_op jit(solution)/shard_map/step_1_shot_0/pallas_call | solution.py:449
  47.1 2.9 %collective-permute-start.11 = (bf16[2,2,128,256]{3,2,1,0:T(8,128)(2,1)S(1)}, bf16[2,2,128,256]{3,2,1,0:T(8,128)(2,1)S(1)}, u32[]{:S(2)}, u32[]{:S(2)}) collective-permute-start(bf16[2,2,128,256]{3,2,1,0:T(8,128)(2,1)S(1)} %get-tuple-element.60), channel_id=1, source_target_pairs={{1,2},{2,1},{3,4},{4,3},{5,6},{6,5},{7,8},{8,7},{9,10},{10,9},{11,... | collective-permute-start | bytes 786440 | tf_op jit(solution)/shard_map/ppermute | solution.py:36
  50.1 1.4 %collective-permute-start.10 = (bf16[2,2,128,256]{3,2,1,0:T(8,128)(2,1)S(1)}, bf16[2,2,128,256]{3,2,1,0:T(8,128)(2,1)S(1)}, u32[]{:S(2)}, u32[]{:S(2)}) collective-permute-start(bf16[2,2,128,256]{3,2,1,0:T(8,128)(2,1)S(1)} %get-tuple-element.54.refs_9_), channel_id=1, source_target_pairs={{0,1},{1,0},{2,3},{3,2},{4,5},{5,4},{6,7},{7,6},{8,9},{9,8},{10,11... | collective-permute-start | bytes 786440 | tf_op jit(solution)/shard_map/ppermute | solution.py:36
  51.4 11.3 %collective-permute-done.4.refs_2_ = bf16[2,2,128,256]{3,2,1,0:T(8,128)(2,1)S(1)} collective-permute-done((bf16[2,2,128,256]{3,2,1,0:T(8,128)(2,1)S(1)}, bf16[2,2,128,256]{3,2,1,0:T(8,128)(2,1)S(1)}, u32[]{:S(2)}, u32[]{:S(2)}) %collective-permute-start.4) | collective-permute-done | bytes 262176 | tf_op jit(solution)/shard_map/ppermute | solution.py:36
  62.8 2.5 %step_1_shot_1.1 = (f32[2,4,128,256]{3,2,1,0:T(8,128)S(1)}, bf16[2,2,128,256]{3,2,1,0:T(8,128)(2,1)S(1)}, bf16[2,2,128,256]{3,2,1,0:T(8,128)(2,1)S(1)}, f32[4,128,256]{2,1,0:T(8,128)S(1)}) custom-call(f32[2,4,128,256]{3,2,1,0:T(8,128)S(1)} %get-tuple-element.45.refs_0_.refs_1_, f32[2,2,2,4,128,256]{5,4,3,2,1,0:T(8,128)} %refs_1_.7, ...), custom_call_target="tpu_custom_call" | custom-call | flops 1 | bytes 1 | tf_op jit(solution)/shard_map/step_1_shot_1/pallas_call | solution.py:449
  65.3 2.9 %collective-permute-start.9 = (bf16[2,2,128,256]{3,2,1,0:T(8,128)(2,1)S(1)}, bf16[2,2,128,256]{3,2,1,0:T(8,128)(2,1)S(1)}, u32[]{:S(2)}, u32[]{:S(2)}) collective-permute-start(bf16[2,2,128,256]{3,2,1,0:T(8,128)(2,1)S(1)} %get-tuple-element.57), channel_id=1, source_target_pairs={{1,2},{2,1},{3,4},{4,3},{5,6},{6,5},{7,8},{8,7},{9,10},{10,9},{11,... | collective-permute-start | bytes 786440 | tf_op jit(solution)/shard_map/ppermute | solution.py:36
  68.2 0.1 collective-permute-start.8
  68.3 0.1 collective-permute-done.10.refs_2_
  68.4 1.2 %step_2_shot_0.1 = (f32[2,4,128,256]{3,2,1,0:T(8,128)S(1)}, bf16[2,2,128,256]{3,2,1,0:T(8,128)(2,1)S(1)}, bf16[2,2,128,256]{3,2,1,0:T(8,128)(2,1)S(1)}, f32[4,128,256]{2,1,0:T(8,128)S(1)}) custom-call(f32[2,4,128,256]{3,2,1,0:T(8,128)S(1)} %get-tuple-element.59.refs_0_.refs_1_, f32[2,4,128,256]{3,2,1,0:T(8,128)S(1)} %get-tuple-element.50.refs_0_.refs_1_, ...), custom_call_target="tpu_custom_call" | custom-call | flops 1 | bytes 1 | tf_op jit(solution)/shard_map/step_2_shot_0/pallas_call | solution.py:449
  69.6 3.1 %collective-permute-start.17 = (bf16[2,2,128,256]{3,2,1,0:T(8,128)(2,1)S(1)}, bf16[2,2,128,256]{3,2,1,0:T(8,128)(2,1)S(1)}, u32[]{:S(2)}, u32[]{:S(2)}) collective-permute-start(bf16[2,2,128,256]{3,2,1,0:T(8,128)(2,1)S(1)} %get-tuple-element.70), channel_id=1, source_target_pairs={{1,2},{2,1},{3,4},{4,3},{5,6},{6,5},{7,8},{8,7},{9,10},{10,9},{11,... | collective-permute-start | bytes 786440 | tf_op jit(solution)/shard_map/ppermute | solution.py:36
  72.8 1.4 %collective-permute-start.16 = (bf16[2,2,128,256]{3,2,1,0:T(8,128)(2,1)S(1)}, bf16[2,2,128,256]{3,2,1,0:T(8,128)(2,1)S(1)}, u32[]{:S(2)}, u32[]{:S(2)}) collective-permute-start(bf16[2,2,128,256]{3,2,1,0:T(8,128)(2,1)S(1)} %get-tuple-element.62.refs_9_), channel_id=1, source_target_pairs={{0,1},{1,0},{2,3},{3,2},{4,5},{5,4},{6,7},{7,6},{8,9},{9,8},{10,11... | collective-permute-start | bytes 786440 | tf_op jit(solution)/shard_map/ppermute | solution.py:36
  74.2 1.2 %collective-permute-done.9.refs_3_ = bf16[2,2,128,256]{3,2,1,0:T(8,128)(2,1)S(1)} collective-permute-done((bf16[2,2,128,256]{3,2,1,0:T(8,128)(2,1)S(1)}, bf16[2,2,128,256]{3,2,1,0:T(8,128)(2,1)S(1)}, u32[]{:S(2)}, u32[]{:S(2)}) %collective-permute-start.9) | collective-permute-done | bytes 262176 | tf_op jit(solution)/shard_map/ppermute | solution.py:36
  75.3 11.0 %collective-permute-done.8.refs_2_ = bf16[2,2,128,256]{3,2,1,0:T(8,128)(2,1)S(1)} collective-permute-done((bf16[2,2,128,256]{3,2,1,0:T(8,128)(2,1)S(1)}, bf16[2,2,128,256]{3,2,1,0:T(8,128)(2,1)S(1)}, u32[]{:S(2)}, u32[]{:S(2)}) %collective-permute-start.8) | collective-permute-done | bytes 262176 | tf_op jit(solution)/shard_map/ppermute | solution.py:36
  86.3 1.2 %step_2_shot_1.1 = (f32[2,4,128,256]{3,2,1,0:T(8,128)S(1)}, bf16[1,2,128,256]{3,2,1,0:T(8,128)(2,1)S(1)}, bf16[1,2,128,256]{3,2,1,0:T(8,128)(2,1)S(1)}, bf16[1,2...) custom-call(f32[2,4,128,256]{3,2,1,0:T(8,128)S(1)} %get-tuple-element.55.refs_0_.refs_, ...), custom_call_target="tpu_custom_call" | custom-call | flops 1 | bytes 1 | tf_op jit(solution)/shard_map/step_2_shot_1/pallas_call | solution.py:449
  87.6 3.3 %collective-permute-start.15 = (bf16[1,2,128,256]{3,2,1,0:T(8,128)(2,1)S(1)}, bf16[1,2,128,256]{3,2,1,0:T(8,128)(2,1)S(1)}, u32[]{:S(2)}, u32[]{:S(2)}) collective-permute-start(bf16[1,2,128,256]{3,2,1,0:T(8,128)(2,1)S(1)} %get-tuple-element.67), channel_id=1, source_target_pairs={{1,2},{2,1},{3,4},{4,3},{5,6},{6,5},{7,8},{8,7},{9,10},{10,9},{11,... | collective-permute-start | bytes 393224 | tf_op jit(solution)/shard_map/ppermute | solution.py:36
  90.8 0.1 collective-permute-start.14
  90.9 1.5 %collective-permute-start.12 = (bf16[1,2,128,256]{3,2,1,0:T(8,128)(2,1)S(1)}, bf16[1,2,128,256]{3,2,1,0:T(8,128)(2,1)S(1)}, u32[]{:S(2)}, u32[]{:S(2)}) collective-permute-start(bf16[1,2,128,256]{3,2,1,0:T(8,128)(2,1)S(1)} %get-tuple-element.64), channel_id=1, source_target_pairs={{0,1},{1,0},{2,3},{3,2},{4,5},{5,4},{6,7},{7,6},{8,9},{9,8},{10,11... | collective-permute-start | bytes 393224 | tf_op jit(solution)/shard_map/ppermute | solution.py:36
  92.4 2.9 %collective-permute-start.13 = (bf16[1,2,128,256]{3,2,1,0:T(8,128)(2,1)S(1)}, bf16[1,2,128,256]{3,2,1,0:T(8,128)(2,1)S(1)}, u32[]{:S(2)}, u32[]{:S(2)}) collective-permute-start(bf16[1,2,128,256]{3,2,1,0:T(8,128)(2,1)S(1)} %get-tuple-element.65), channel_id=1, source_target_pairs={{1,2},{2,1},{3,4},{4,3},{5,6},{6,5},{7,8},{8,7},{9,10},{10,9},{11,... | collective-permute-start | bytes 393224 | tf_op jit(solution)/shard_map/ppermute | solution.py:36
  95.3 3.5 %step_3_shot_0.1 = (f32[2,2,2,4,128,256]{5,4,3,2,1,0:T(8,128)}, f32[4,200,256]{2,1,0:T(8,128)}) custom-call(f32[2,4,128,256]{3,2,1,0:T(8,128)S(1)} %get-tuple-element.69.refs_0_.refs_10_, f32[2,4,128,256]{3,2,1,0:T(8,128)S(1)} %get-tuple-element.59.refs_0_.refs_1_, bf16[2,2,128,256]{3,2,1,0:T(8,128)(2,1)S(1)} %collective-permute-done.16.refs_2_, ...), custom_call_target="tpu_custom_call" | custom-call | flops 1 | bytes 1 | tf_op jit(solution)/shard_map/step_3_shot_0/pallas_call | solution.py:449
  98.8 1.8 %collective-permute-start.18 = (f32[4,200,256]{2,1,0:T(8,128)}, f32[4,200,256]{2,1,0:T(8,128)}, u32[]{:S(2)}, u32[]{:S(2)}) collective-permute-start(f32[4,200,256]{2,1,0:T(8,128)} %get-tuple-element.72.refs_9_.refs_0_), channel_id=1, source_target_pairs={{0,16},{16,0},{1,17},{17,1},{2,18},{18,2},{3,19},{19,3},{4,20},{20... | collective-permute-start | bytes 2457608 | tf_op jit(solution)/shard_map/ppermute | solution.py:579
  100.5 0.0 collective-permute-done.14.refs_2_
  100.6 2.2 %step_3_shot_1.2 = (f32[4,128,256]{2,1,0:T(8,128)S(1)}, f32[4,200,256]{2,1,0:T(8,128)}) custom-call(f32[2,4,128,256]{3,2,1,0:T(8,128)S(1)} %get-tuple-element.63.refs_11_.refs_0_, f32[2,4,128,256]{3,2,1,0:T(8,128)S(1)} %get-tuple-element.55.refs_0_.refs_1_, bf16[1,2,128,256]{3,2,1,0:T(8,128)(2,1)S(1)} %collective-permute-done.14.refs_2_, ...), custom_call_target="tpu_custom_call" | custom-call | flops 1 | bytes 1 | tf_op jit(solution)/shard_map/step_3_shot_1/pallas_call | solution.py:449
  102.8 0.6 collective-permute-start.19
  103.4 0.0 collective-permute-done.12.refs_2_
  103.4 0.2 collective-permute-done.13.refs_3_
  103.6 1.4 %step_3_shot_1.3.refs_4_ = f32[2,2,2,4,128,256]{5,4,3,2,1,0:T(8,128)} custom-call(f32[2,4,128,256]{3,2,1,0:T(8,128)S(1)} %get-tuple-element.63.refs_11_.refs_0_, f32[2,4,128,256]{3,2,1,0:T(8,128)S(1)} %get-tuple-element.55.refs_0_.refs_1_, bf16[1,2,128,256]{3,2,1,0:T(8,128)(2,1)S(1)} %collective-permute-done.12.refs_2_, ...), custom_call_target="tpu_custom_call", output_to_operand_aliasing={{}: (8, {})} | custom-call | flops 9999999827968 | bytes 1 | tf_op jit(solution)/shard_map/step_3_shot_1/pallas_call | solution.py:449
  105.0 0.7 collective-permute-done.19.refs_3_
  105.7 2.8 %sum_frames.1 = f32[4,192,256]{2,1,0:T(8,128)} custom-call(f32[4,200,256]{2,1,0:T(8,128)} %get-tuple-element.72.refs_9_.refs_0_, f32[4,200,256]{2,1,0:T(8,128)} %collective-permute-done.18.refs_1_, f32[4,200,256]{2,1,0:T(8,128)} %get-tuple-element.74.refs_7_.refs_2_, f32[4,200,256]{2,1,0:T(8,128)} %collective-permute-done.19.refs_3_, ...), custom_call_target="tpu_custom_call" | custom-call | flops 1 | bytes 1 | tf_op jit(solution)/shard_map/sum_frames/pallas_call | solution.py:491
  (21 shorter events, 0.0 us)
Async XLA Ops:
  0.6 5.7 %copy-start.5 = (s32[2,128]{1,0:T(2,128)S(1)}, s32[2,128]{1,0:T(2,128)}, u32[]{:S(2)}) copy-start(s32[2,128]{1,0:T(2,128)} %ids_ref.1) | copy-start | bytes 3076
  0.6 5.7 %copy-start.2 = (bf16[2,128,256]{2,1,0:T(8,128)(2,1)S(1)}, bf16[2,128,256]{2,1,0:T(8,128)(2,1)}, u32[]{:S(2)}) copy-start(bf16[2,128,256]{2,1,0:T(8,128)(2,1)} %lines_ref.1) | copy-start | bytes 393220
  0.7 19.4 %copy-start.1 = (f32[2,4,64]{2,1,0:T(4,128)S(1)}, f32[2,4,64]{2,1,0:T(4,128)}, u32[]{:S(2)}) copy-start(f32[2,4,64]{2,1,0:T(4,128)} %refs_5_.15) | copy-start | bytes 6148
  0.7 19.4 %copy-start.3 = (s32[2,64]{1,0:T(2,128)S(1)}, s32[2,64]{1,0:T(2,128)}, u32[]{:S(2)}) copy-start(s32[2,64]{1,0:T(2,128)} %refs_4_.3) | copy-start | bytes 1540
  0.7 19.4 %copy-start.4 = (s32[2]{0:T(128)S(1)}, s32[2]{0:T(128)}, u32[]{:S(2)}) copy-start(s32[2]{0:T(128)} %refs_6_.15) | copy-start | bytes 28
  0.7 19.4 %copy-start = (f32[4,192,256]{2,1,0:T(8,128)S(1)}, f32[4,192,256]{2,1,0:T(8,128)}, u32[]{:S(2)}) copy-start(f32[4,192,256]{2,1,0:T(8,128)} %refs_8_.1) | copy-start | bytes 2359300
  2.0 17.3 %collective-permute-start.3 = (bf16[2,2,128,256]{3,2,1,0:T(8,128)(2,1)S(1)}, bf16[2,2,128,256]{3,2,1,0:T(8,128)(2,1)S(1)}, u32[]{:S(2)}, u32[]{:S(2)}) collective-permute-start(bf16[2,2,128,256]{3,2,1,0:T(8,128)(2,1)S(1)} %get-tuple-element.42), channel_id=1, source_target_pairs={{1,2},{2,1},{3,4},{4,3},{5,6},{6,5},{7,8},{8,7},{9,10},{10,9},{11,... | collective-permute-start | bytes 786440 | tf_op jit(solution)/shard_map/ppermute | solution.py:36
  5.2 14.9 %collective-permute-start.2 = (bf16[2,2,128,256]{3,2,1,0:T(8,128)(2,1)S(1)}, bf16[2,2,128,256]{3,2,1,0:T(8,128)(2,1)S(1)}, u32[]{:S(2)}, u32[]{:S(2)}) collective-permute-start(bf16[2,2,128,256]{3,2,1,0:T(8,128)(2,1)S(1)} %get-tuple-element.39.after_ref), channel_id=1, source_target_pairs={{0,1},{1,0},{2,3},{3,2},{4,5},{5,4},{6,7},{7,6},{8,9},{9,8},{10,11... | collective-permute-start | bytes 786440 | tf_op jit(solution)/shard_map/ppermute | solution.py:36
  7.3 16.0 %all-to-all-start = ((bf16[16,16,384]{2,1,0:T(8,128)(2,1)}), bf16[16,16,384]{2,1,0:T(8,128)(2,1)}, u32[]{:S(2)}, u32[]{:S(2)}) async-start(bf16[16,16,384]{2,1,0:T(8,128)(2,1)} %bitcast), calls=%async_computation | async-start | bytes 393216 | tf_op jit(solution)/shard_map/all_to_all | solution.py:182
  15.0 22.5 %collective-permute-start = (bf16[2,2,128,256]{3,2,1,0:T(8,128)(2,1)}, bf16[2,2,128,256]{3,2,1,0:T(8,128)(2,1)}, u32[]{:S(2)}, u32[]{:S(2)}) collective-permute-start(bf16[2,2,128,256]{3,2,1,0:T(8,128)(2,1)} %get-tuple-element.40), channel_id=1, source_target_pairs={{0,1},{1,0},{2,3},{3,2},{4,5},{5,4},{6,7},{7,6},{8,9},{9,8},{10,11... | collective-permute-start | bytes 786440 | tf_op jit(solution)/shard_map/ppermute | solution.py:36
  15.4 22.2 %collective-permute-start.1 = (bf16[2,2,128,256]{3,2,1,0:T(8,128)(2,1)}, bf16[2,2,128,256]{3,2,1,0:T(8,128)(2,1)}, u32[]{:S(2)}, u32[]{:S(2)}) collective-permute-start(bf16[2,2,128,256]{3,2,1,0:T(8,128)(2,1)} %get-tuple-element.41), channel_id=1, source_target_pairs={{1,2},{2,1},{3,4},{4,3},{5,6},{6,5},{7,8},{8,7},{9,10},{10,9},{11,... | collective-permute-start | bytes 786440 | tf_op jit(solution)/shard_map/ppermute | solution.py:36
  24.7 20.0 %collective-permute-start.7 = (bf16[2,2,128,256]{3,2,1,0:T(8,128)(2,1)S(1)}, bf16[2,2,128,256]{3,2,1,0:T(8,128)(2,1)S(1)}, u32[]{:S(2)}, u32[]{:S(2)}) collective-permute-start(bf16[2,2,128,256]{3,2,1,0:T(8,128)(2,1)S(1)} %get-tuple-element.51), channel_id=1, source_target_pairs={{1,2},{2,1},{3,4},{4,3},{5,6},{6,5},{7,8},{8,7},{9,10},{10,9},{11,... | collective-permute-start | bytes 786440 | tf_op jit(solution)/shard_map/ppermute | solution.py:36
  28.0 16.7 %collective-permute-start.6 = (bf16[2,2,128,256]{3,2,1,0:T(8,128)(2,1)S(1)}, bf16[2,2,128,256]{3,2,1,0:T(8,128)(2,1)S(1)}, u32[]{:S(2)}, u32[]{:S(2)}) collective-permute-start(bf16[2,2,128,256]{3,2,1,0:T(8,128)(2,1)S(1)} %get-tuple-element.44.refs_9_), channel_id=1, source_target_pairs={{0,1},{1,0},{2,3},{3,2},{4,5},{5,4},{6,7},{7,6},{8,9},{9,8},{10,11... | collective-permute-start | bytes 786440 | tf_op jit(solution)/shard_map/ppermute | solution.py:36
  41.4 10.1 %collective-permute-start.5 = (bf16[2,2,128,256]{3,2,1,0:T(8,128)(2,1)S(1)}, bf16[2,2,128,256]{3,2,1,0:T(8,128)(2,1)S(1)}, u32[]{:S(2)}, u32[]{:S(2)}) collective-permute-start(bf16[2,2,128,256]{3,2,1,0:T(8,128)(2,1)S(1)} %get-tuple-element.47), channel_id=1, source_target_pairs={{1,2},{2,1},{3,4},{4,3},{5,6},{6,5},{7,8},{8,7},{9,10},{10,9},{11,... | collective-permute-start | bytes 786440 | tf_op jit(solution)/shard_map/ppermute | solution.py:36
  44.7 18.1 %collective-permute-start.4 = (bf16[2,2,128,256]{3,2,1,0:T(8,128)(2,1)S(1)}, bf16[2,2,128,256]{3,2,1,0:T(8,128)(2,1)S(1)}, u32[]{:S(2)}, u32[]{:S(2)}) collective-permute-start(bf16[2,2,128,256]{3,2,1,0:T(8,128)(2,1)S(1)} %get-tuple-element.46.refs_9_), channel_id=1, source_target_pairs={{0,1},{1,0},{2,3},{3,2},{4,5},{5,4},{6,7},{7,6},{8,9},{9,8},{10,11... | collective-permute-start | bytes 786440 | tf_op jit(solution)/shard_map/ppermute | solution.py:36
  47.1 21.1 %collective-permute-start.11 = (bf16[2,2,128,256]{3,2,1,0:T(8,128)(2,1)S(1)}, bf16[2,2,128,256]{3,2,1,0:T(8,128)(2,1)S(1)}, u32[]{:S(2)}, u32[]{:S(2)}) collective-permute-start(bf16[2,2,128,256]{3,2,1,0:T(8,128)(2,1)S(1)} %get-tuple-element.60), channel_id=1, source_target_pairs={{1,2},{2,1},{3,4},{4,3},{5,6},{6,5},{7,8},{8,7},{9,10},{10,9},{11,... | collective-permute-start | bytes 786440 | tf_op jit(solution)/shard_map/ppermute | solution.py:36
  50.1 18.4 %collective-permute-start.10 = (bf16[2,2,128,256]{3,2,1,0:T(8,128)(2,1)S(1)}, bf16[2,2,128,256]{3,2,1,0:T(8,128)(2,1)S(1)}, u32[]{:S(2)}, u32[]{:S(2)}) collective-permute-start(bf16[2,2,128,256]{3,2,1,0:T(8,128)(2,1)S(1)} %get-tuple-element.54.refs_9_), channel_id=1, source_target_pairs={{0,1},{1,0},{2,3},{3,2},{4,5},{5,4},{6,7},{7,6},{8,9},{9,8},{10,11... | collective-permute-start | bytes 786440 | tf_op jit(solution)/shard_map/ppermute | solution.py:36
  65.3 10.1 %collective-permute-start.9 = (bf16[2,2,128,256]{3,2,1,0:T(8,128)(2,1)S(1)}, bf16[2,2,128,256]{3,2,1,0:T(8,128)(2,1)S(1)}, u32[]{:S(2)}, u32[]{:S(2)}) collective-permute-start(bf16[2,2,128,256]{3,2,1,0:T(8,128)(2,1)S(1)} %get-tuple-element.57), channel_id=1, source_target_pairs={{1,2},{2,1},{3,4},{4,3},{5,6},{6,5},{7,8},{8,7},{9,10},{10,9},{11,... | collective-permute-start | bytes 786440 | tf_op jit(solution)/shard_map/ppermute | solution.py:36
  68.2 18.1 %collective-permute-start.8 = (bf16[2,2,128,256]{3,2,1,0:T(8,128)(2,1)S(1)}, bf16[2,2,128,256]{3,2,1,0:T(8,128)(2,1)S(1)}, u32[]{:S(2)}, u32[]{:S(2)}) collective-permute-start(bf16[2,2,128,256]{3,2,1,0:T(8,128)(2,1)S(1)} %get-tuple-element.56.refs_9_), channel_id=1, source_target_pairs={{0,1},{1,0},{2,3},{3,2},{4,5},{5,4},{6,7},{7,6},{8,9},{9,8},{10,11... | collective-permute-start | bytes 786440 | tf_op jit(solution)/shard_map/ppermute | solution.py:36
  69.6 22.7 %collective-permute-start.17 = (bf16[2,2,128,256]{3,2,1,0:T(8,128)(2,1)S(1)}, bf16[2,2,128,256]{3,2,1,0:T(8,128)(2,1)S(1)}, u32[]{:S(2)}, u32[]{:S(2)}) collective-permute-start(bf16[2,2,128,256]{3,2,1,0:T(8,128)(2,1)S(1)} %get-tuple-element.70), channel_id=1, source_target_pairs={{1,2},{2,1},{3,4},{4,3},{5,6},{6,5},{7,8},{8,7},{9,10},{10,9},{11,... | collective-permute-start | bytes 786440 | tf_op jit(solution)/shard_map/ppermute | solution.py:36
  72.8 22.5 %collective-permute-start.16 = (bf16[2,2,128,256]{3,2,1,0:T(8,128)(2,1)S(1)}, bf16[2,2,128,256]{3,2,1,0:T(8,128)(2,1)S(1)}, u32[]{:S(2)}, u32[]{:S(2)}) collective-permute-start(bf16[2,2,128,256]{3,2,1,0:T(8,128)(2,1)S(1)} %get-tuple-element.62.refs_9_), channel_id=1, source_target_pairs={{0,1},{1,0},{2,3},{3,2},{4,5},{5,4},{6,7},{7,6},{8,9},{9,8},{10,11... | collective-permute-start | bytes 786440 | tf_op jit(solution)/shard_map/ppermute | solution.py:36
  87.6 13.0 %collective-permute-start.15 = (bf16[1,2,128,256]{3,2,1,0:T(8,128)(2,1)S(1)}, bf16[1,2,128,256]{3,2,1,0:T(8,128)(2,1)S(1)}, u32[]{:S(2)}, u32[]{:S(2)}) collective-permute-start(bf16[1,2,128,256]{3,2,1,0:T(8,128)(2,1)S(1)} %get-tuple-element.67), channel_id=1, source_target_pairs={{1,2},{2,1},{3,4},{4,3},{5,6},{6,5},{7,8},{8,7},{9,10},{10,9},{11,... | collective-permute-start | bytes 393224 | tf_op jit(solution)/shard_map/ppermute | solution.py:36
  90.8 9.7 %collective-permute-start.14 = (bf16[1,2,128,256]{3,2,1,0:T(8,128)(2,1)S(1)}, bf16[1,2,128,256]{3,2,1,0:T(8,128)(2,1)S(1)}, u32[]{:S(2)}, u32[]{:S(2)}) collective-permute-start(bf16[1,2,128,256]{3,2,1,0:T(8,128)(2,1)S(1)} %get-tuple-element.66.refs_12_), channel_id=1, source_target_pairs={{0,1},{1,0},{2,3},{3,2},{4,5},{5,4},{6,7},{7,6},{8,9},{9,8},{10,11... | collective-permute-start | bytes 393224 | tf_op jit(solution)/shard_map/ppermute | solution.py:36
  90.9 12.4 %collective-permute-start.12 = (bf16[1,2,128,256]{3,2,1,0:T(8,128)(2,1)S(1)}, bf16[1,2,128,256]{3,2,1,0:T(8,128)(2,1)S(1)}, u32[]{:S(2)}, u32[]{:S(2)}) collective-permute-start(bf16[1,2,128,256]{3,2,1,0:T(8,128)(2,1)S(1)} %get-tuple-element.64), channel_id=1, source_target_pairs={{0,1},{1,0},{2,3},{3,2},{4,5},{5,4},{6,7},{7,6},{8,9},{9,8},{10,11... | collective-permute-start | bytes 393224 | tf_op jit(solution)/shard_map/ppermute | solution.py:36
  92.4 11.2 %collective-permute-start.13 = (bf16[1,2,128,256]{3,2,1,0:T(8,128)(2,1)S(1)}, bf16[1,2,128,256]{3,2,1,0:T(8,128)(2,1)S(1)}, u32[]{:S(2)}, u32[]{:S(2)}) collective-permute-start(bf16[1,2,128,256]{3,2,1,0:T(8,128)(2,1)S(1)} %get-tuple-element.65), channel_id=1, source_target_pairs={{1,2},{2,1},{3,4},{4,3},{5,6},{6,5},{7,8},{8,7},{9,10},{10,9},{11,... | collective-permute-start | bytes 393224 | tf_op jit(solution)/shard_map/ppermute | solution.py:36
  98.8 6.9 %collective-permute-start.18 = (f32[4,200,256]{2,1,0:T(8,128)}, f32[4,200,256]{2,1,0:T(8,128)}, u32[]{:S(2)}, u32[]{:S(2)}) collective-permute-start(f32[4,200,256]{2,1,0:T(8,128)} %get-tuple-element.72.refs_9_.refs_0_), channel_id=1, source_target_pairs={{0,16},{16,0},{1,17},{17,1},{2,18},{18,2},{3,19},{19,3},{4,20},{20... | collective-permute-start | bytes 2457608 | tf_op jit(solution)/shard_map/ppermute | solution.py:579
  102.8 2.9 %collective-permute-start.19 = (f32[4,200,256]{2,1,0:T(8,128)}, f32[4,200,256]{2,1,0:T(8,128)}, u32[]{:S(2)}, u32[]{:S(2)}) collective-permute-start(f32[4,200,256]{2,1,0:T(8,128)} %get-tuple-element.74.refs_7_.refs_2_), channel_id=1, source_target_pairs={{0,16},{16,0},{1,17},{17,1},{2,18},{18,2},{3,19},{19,3},{4,20},{20... | collective-permute-start | bytes 2457608 | tf_op jit(solution)/shard_map/ppermute | solution.py:579

commit v8 on v7

--- a/solution.py
+++ b/solution.py
@@ -73,16 +73,36 @@
     return lax.rem(lax.axis_index("space"), 2) == 1
 
 
+def halo_shape(group, rows_y, cells_z):
+    rows = sum(2 * (rows_y if comp == 1 else rows_y - EDGE) for comp in group)
+    return jax.ShapeDtypeStruct((rows, cells_z), jnp.bfloat16)
+
+
+def halo_layer(halo, group, rows_y, comp, at):
+    if comp == 1:
+        return halo[at * rows_y : (at + 1) * rows_y]
+    kept = rows_y - EDGE
+    base = (2 * rows_y if 1 in group else 0) + at * kept
+    edge = jnp.zeros((EDGE // 2, halo.shape[1]), halo.dtype)
+    return jnp.concatenate([edge, halo[base : base + kept], edge], axis=0)
+
+
 def write_sends(field_ref, groups, send_refs):
     odd = is_odd()
+    _, layers, rows_y, _ = field_ref.shape
+
+    def pieces(group, first):
+        made = []
+        for comp in sorted(group, reverse=True):
+            for at in (first, first + 1):
+                layer = field_ref[comp, at]
+                made.append(layer if comp == 1 else layer[EDGE // 2 : rows_y - EDGE // 2])
+        return jnp.concatenate(made, axis=0)
+
     for at_group, group in enumerate(groups):
-        send0_ref, send1_ref = send_refs[2 * at_group : 2 * at_group + 2]
-        for place, comp in enumerate(group):
-            for at in range(2):
-                low = field_ref[comp, at]
-                high = field_ref[comp, at + field_ref.shape[-3] - 2]
-                send0_ref[place, at] = jnp.where(odd, low, high).astype(jnp.bfloat16)
-                send1_ref[place, at] = jnp.where(odd, high, low).astype(jnp.bfloat16)
+        low, high = pieces(group, 0), pieces(group, layers - 2)
+        send_refs[2 * at_group][...] = jnp.where(odd, low, high).astype(jnp.bfloat16)
+        send_refs[2 * at_group + 1][...] = jnp.where(odd, high, low).astype(jnp.bfloat16)
 
 
 def pack_kernel(shot, field_ref, *refs):
@@ -94,14 +114,14 @@
     ]
     for load in loads:
         load.start()
-    for comp, load in enumerate(loads):
+    for load in loads:
         load.wait()
-        write_sends(own_ref, ((comp,),), (send0_ref.at[comp : comp + 1], send1_ref.at[comp : comp + 1]))
+    write_sends(own_ref, BOTH, (send0_ref, send1_ref))
 
 
 def pack_halo(wavefields, shot, after):
     _, _, comps, layers, rows_y, cells_z = wavefields.shape
-    half = jax.ShapeDtypeStruct((comps, 2, rows_y, cells_z), jnp.bfloat16)
+    half = halo_shape(BOTH[0], rows_y, cells_z)
     return pl.pallas_call(
         functools.partial(pack_kernel, shot),
         in_specs=[pl.BlockSpec(memory_space=HBM)] + [pl.BlockSpec(memory_space=pl.ANY)] * len(after),
@@ -214,7 +234,7 @@
 
 def finish_first(shot, new, saved):
     comps, _, rows_y, cells_z = new.shape
-    half = jax.ShapeDtypeStruct((comps, 2, rows_y, cells_z), jnp.bfloat16)
+    half = halo_shape(BOTH[0], rows_y, cells_z)
     vmem = pl.BlockSpec(memory_space=VMEM)
     return pl.pallas_call(
         functools.partial(finish_kernel, shot),
@@ -241,8 +261,8 @@
     got_of = {}
     for group in got_groups:
         got0_ref, got1_ref = take(2)
-        for place, comp in enumerate(group):
-            got_of[comp] = (got0_ref, got1_ref, place)
+        for comp in group:
+            got_of[comp] = (got0_ref, got1_ref, group)
     [saved_ref] = take(1) if lines else [None]
     pos_ref, traces_ref = take(2) if with_image else (None, None)
     framing = last and with_image
@@ -304,17 +324,16 @@
         load.wait()
 
     for comp in comps:
-        got0_ref, got1_ref, place = got_of[comp]
+        got0_ref, got1_ref, group = got_of[comp]
+        got0, got1 = got0_ref[...].astype(jnp.float32), got1_ref[...].astype(jnp.float32)
+        below, above = jnp.where(odd, got0, got1), jnp.where(odd, got1, got0)
 
         def layer_of(at):
             if at < 0:
-                both = (got1_ref[place, 2 + at], got0_ref[place, 2 + at])
-            elif at >= layers:
-                both = (got0_ref[place, at - layers], got1_ref[place, at - layers])
-            else:
-                return now_ref[comp, at]
-            even_one, odd_one = (part.astype(jnp.float32) for part in both)
-            return jnp.where(odd, odd_one, even_one)
+                return halo_layer(below, group, rows_y, comp, 2 + at)
+            if at >= layers:
+                return halo_layer(above, group, rows_y, comp, at - layers)
+            return now_ref[comp, at]
 
         for layer in range(layers):
             if first and comp == comps[0]:
@@ -429,7 +448,7 @@
     else:
         outs = [state]
         for group in send_groups:
-            half = jax.ShapeDtypeStruct((len(group), 2, rows_y, cells_z), jnp.bfloat16)
+            half = halo_shape(group, rows_y, cells_z)
             outs += [half, half]
         out_specs = [vmem] * len(outs)
     if framing:

time: 109 us -> 109 us (level)
  waiting for transfers between devices: 34.4 us -> 32.9 us
    ppermute x18, waiting for transfers between devices: 33.7 us -> 32 us  [swap_pairs(): return lax.ppermute(value, 'space', routes)]
  transfers between devices with their start and end apart: 21 -> 21, of which waited for: 8 -> 7; matrix products, arithmetic and copies ran while one was open for 0% -> 0% of each run, Pallas kernels for 24% -> 25%
where the time goes in v8:
time: 109 us; the launch traced here: 108 us
  starting transfers between devices  43.3 us (40%)
  waiting for transfers between devices  32.9 us (30%)
  Pallas kernels  30.7 us (28%)
  between operations  1.1 us (1%)
    ppermute x18, starting transfers between devices, swap_pairs(): return lax.ppermute(value, 'space', routes)  35.4 us
    ppermute x18, waiting for transfers between devices, swap_pairs(): return lax.ppermute(value, 'space', routes)  32 us
    pallas_call x9, Pallas kernels, one_step(): pl.pallas_call(functools.partial(step_kernel, shot, step, comps, got_grou...  22 us
    all_to_all x1, starting transfers between devices, deliver(): got = lax.all_to_all(message, 'space', 0, 0, tiled=False)  5.63 us
    pallas_call x2, Pallas kernels, pack_halo(): pl.pallas_call(functools.partial(pack_kernel, shot), in_specs=[pl.BlockSp...  3.48 us
    pallas_call x1, Pallas kernels, sum_frames(): pl.pallas_call(functools.partial(sum_kernel, scale), in_specs=[vmem] * le...  2.83 us
    ppermute x2, starting transfers between devices, body(): others = [lax.ppermute(frame, 'shot', [(0, 1), (1, 0)]) for frame in frames]  2.22 us
  transfers between devices with their start and end apart: 21, of which 7 were waited for; matrix products, arithmetic and copies ran while one was open for 0% of the time, Pallas kernels for 25%

profile of v8, /device:TPU:19, one launch (start us, length us, event | category | flops | bytes accessed | tf_op | source)
XLA Modules:
  0.0 108.0 jit_solution(9566281970191641220)
XLA Ops:
  0.7 1.4 %pack_halo.2 = (bf16[504,256]{1,0:T(8,128)(2,1)S(1)}, bf16[504,256]{1,0:T(8,128)(2,1)S(1)}) custom-call(f32[2,2,2,4,128,256]{5,4,3,2,1,0:T(8,128)} %refs_1_.7), custom_call_target="tpu_custom_call" | custom-call | flops 1 | bytes 1 | tf_op jit(solution)/shard_map/pack_halo/pallas_call | solution.py:125
  2.1 3.1 %collective-permute-start.3 = (bf16[504,256]{1,0:T(8,128)(2,1)S(1)}, bf16[504,256]{1,0:T(8,128)(2,1)S(1)}, u32[]{:S(2)}, u32[]{:S(2)}) collective-permute-start(bf16[504,256]{1,0:T(8,128)(2,1)S(1)} %get-tuple-element.42), channel_id=1, source_target_pairs={{1,2},{2,1},{3,4},{4,3},{5,6},{6,5},{7,8},{8,7},{9,10},{10,9},{11,... | collective-permute-start | bytes 774152 | tf_op jit(solution)/shard_map/ppermute | solution.py:36
  5.2 1.2 %collective-permute-start.2 = (bf16[504,256]{1,0:T(8,128)(2,1)S(1)}, bf16[504,256]{1,0:T(8,128)(2,1)S(1)}, u32[]{:S(2)}, u32[]{:S(2)}) collective-permute-start(bf16[504,256]{1,0:T(8,128)(2,1)S(1)} %get-tuple-element.39.after_ref), channel_id=1, source_target_pairs={{0,1},{1,0},{2,3},{3,2},{4,5},{5,4},{6,7},{7,6},{8,9},{9,8},{10,11... | collective-permute-start | bytes 774152 | tf_op jit(solution)/shard_map/ppermute | solution.py:36
  6.4 1.0 pack_lines.1.refs_0_
  7.4 5.6 %all-to-all-start = ((bf16[16,16,384]{2,1,0:T(8,128)(2,1)}), bf16[16,16,384]{2,1,0:T(8,128)(2,1)}, u32[]{:S(2)}, u32[]{:S(2)}) async-start(bf16[16,16,384]{2,1,0:T(8,128)(2,1)} %bitcast), calls=%async_computation | async-start | bytes 393216 | tf_op jit(solution)/shard_map/all_to_all | solution.py:202
  13.0 2.1 %pack_halo.3 = (bf16[504,256]{1,0:T(8,128)(2,1)}, bf16[504,256]{1,0:T(8,128)(2,1)}) custom-call(f32[2,2,2,4,128,256]{5,4,3,2,1,0:T(8,128)} %refs_1_.7, bf16[256,384]{1,0:T(8,128)(2,1)} %pack_lines.1.refs_0_), custom_call_target="tpu_custom_call" | custom-call | flops 1 | bytes 1 | tf_op jit(solution)/shard_map/pack_halo/pallas_call | solution.py:125
  15.1 0.3 collective-permute-start
  15.5 4.0 %collective-permute-start.1 = (bf16[504,256]{1,0:T(8,128)(2,1)}, bf16[504,256]{1,0:T(8,128)(2,1)}, u32[]{:S(2)}, u32[]{:S(2)}) collective-permute-start(bf16[504,256]{1,0:T(8,128)(2,1)} %get-tuple-element.41), channel_id=1, source_target_pairs={{1,2},{2,1},{3,4},{4,3},{5,6},{6,5},{7,8},{8,7},{9,10},{10,9},{11,... | collective-permute-start | bytes 774152 | tf_op jit(solution)/shard_map/ppermute | solution.py:36
  19.5 0.0 collective-permute-done.3.refs_3_
  19.5 0.5 collective-permute-done.2.refs_2_
  20.0 3.3 %step_0_shot_0.1 = (f32[2,4,128,256]{3,2,1,0:T(8,128)S(1)}, f32[4,128,256]{2,1,0:T(8,128)S(1)}, f32[4,128,256]{2,1,0:T(8,128)S(1)}) custom-call(f32[2,2,2,4,128,256]{5,4,3,2,1,0:T(8,128)} %refs_1_.7, f32[2,2,2,4,128,256]{5,4,3,2,1,0:T(8,128)} %refs_1_.7, bf16[504,256]{1,0:T(8,128)(2,1)S(1)} %collective-permute-done.2.refs_2_, ...), custom_call_target="tpu_custom_call" | custom-call | flops 9999999827968 | bytes 1 | tf_op jit(solution)/shard_map/step_0_shot_0/pallas_call | solution.py:468
  23.3 0.0 all-to-all-done
  23.3 1.2 %unpack_lines.1.saved_ref.refs_4_ = f32[128,256]{1,0:T(8,128)S(1)} custom-call(bf16[256,384]{1,0:T(8,128)(2,1)} %bitcast.1.got_ref), custom_call_target="tpu_custom_call" | custom-call | flops 1 | bytes 1 | tf_op jit(solution)/shard_map/unpack_lines/pallas_call | solution.py:203
  24.6 0.2 finish_first_0.1
  24.8 3.3 %collective-permute-start.7 = (bf16[504,256]{1,0:T(8,128)(2,1)S(1)}, bf16[504,256]{1,0:T(8,128)(2,1)S(1)}, u32[]{:S(2)}, u32[]{:S(2)}) collective-permute-start(bf16[504,256]{1,0:T(8,128)(2,1)S(1)} %get-tuple-element.51), channel_id=1, source_target_pairs={{1,2},{2,1},{3,4},{4,3},{5,6},{6,5},{7,8},{8,7},{9,10},{10,9},{11,... | collective-permute-start | bytes 774152 | tf_op jit(solution)/shard_map/ppermute | solution.py:36
  28.1 0.5 collective-permute-start.6
  28.6 8.5 %collective-permute-done.refs_2_ = bf16[504,256]{1,0:T(8,128)(2,1)} collective-permute-done((bf16[504,256]{1,0:T(8,128)(2,1)}, bf16[504,256]{1,0:T(8,128)(2,1)}, u32[]{:S(2)}, u32[]{:S(2)}) %collective-permute-start) | collective-permute-done | bytes 258080 | tf_op jit(solution)/shard_map/ppermute | solution.py:36
  37.2 4.0 %step_0_shot_1.1 = (f32[2,4,128,256]{3,2,1,0:T(8,128)S(1)}, bf16[504,256]{1,0:T(8,128)(2,1)S(1)}, bf16[504,256]{1,0:T(8,128)(2,1)S(1)}, f32[4,128,256]{2,1,0:T(8,128)S(1)}, f32[4,128,256]{2,1,0:T(8,128)S(1)}) custom-call(f32[2,2,2,4,128,256]{5,4,3,2,1,0:T(8,128)} %refs_1_.7, f32[2,2,2,4,128,256]{5,4,3,2,1,0:T(8,128)} %refs_1_.7, ...), custom_call_target="tpu_custom_call" | custom-call | flops 1 | bytes 1 | tf_op jit(solution)/shard_map/step_0_shot_1/pallas_call | solution.py:468
  41.1 3.3 %collective-permute-start.5 = (bf16[504,256]{1,0:T(8,128)(2,1)S(1)}, bf16[504,256]{1,0:T(8,128)(2,1)S(1)}, u32[]{:S(2)}, u32[]{:S(2)}) collective-permute-start(bf16[504,256]{1,0:T(8,128)(2,1)S(1)} %get-tuple-element.47), channel_id=1, source_target_pairs={{1,2},{2,1},{3,4},{4,3},{5,6},{6,5},{7,8},{8,7},{9,10},{10,9},{11,... | collective-permute-start | bytes 774152 | tf_op jit(solution)/shard_map/ppermute | solution.py:36
  44.4 0.1 collective-permute-start.4
  44.5 0.0 collective-permute-done.7.refs_3_
  44.5 2.4 %step_1_shot_0.1 = (f32[2,4,128,256]{3,2,1,0:T(8,128)S(1)}, bf16[504,256]{1,0:T(8,128)(2,1)S(1)}, bf16[504,256]{1,0:T(8,128)(2,1)S(1)}, f32[4,128,256]{2,1,0:T(8,128)S(1)}) custom-call(f32[2,4,128,256]{3,2,1,0:T(8,128)S(1)} %get-tuple-element.50.refs_0_.refs_1_, f32[2,2,2,4,128,256]{5,4,3,2,1,0:T(8,128)} %refs_1_.7, ...), custom_call_target="tpu_custom_call" | custom-call | flops 1 | bytes 1 | tf_op jit(solution)/shard_map/step_1_shot_0/pallas_call | solution.py:468
  46.9 2.9 %collective-permute-start.11 = (bf16[504,256]{1,0:T(8,128)(2,1)S(1)}, bf16[504,256]{1,0:T(8,128)(2,1)S(1)}, u32[]{:S(2)}, u32[]{:S(2)}) collective-permute-start(bf16[504,256]{1,0:T(8,128)(2,1)S(1)} %get-tuple-element.60), channel_id=1, source_target_pairs={{1,2},{2,1},{3,4},{4,3},{5,6},{6,5},{7,8},{8,7},{9,10},{10,9},{11,... | collective-permute-start | bytes 774152 | tf_op jit(solution)/shard_map/ppermute | solution.py:36
  49.9 1.4 %collective-permute-start.10 = (bf16[504,256]{1,0:T(8,128)(2,1)S(1)}, bf16[504,256]{1,0:T(8,128)(2,1)S(1)}, u32[]{:S(2)}, u32[]{:S(2)}) collective-permute-start(bf16[504,256]{1,0:T(8,128)(2,1)S(1)} %get-tuple-element.54.refs_9_), channel_id=1, source_target_pairs={{0,1},{1,0},{2,3},{3,2},{4,5},{5,4},{6,7},{7,6},{8,9},{9,8},{10,11... | collective-permute-start | bytes 774152 | tf_op jit(solution)/shard_map/ppermute | solution.py:36
  51.2 11.0 %collective-permute-done.4.refs_2_ = bf16[504,256]{1,0:T(8,128)(2,1)S(1)} collective-permute-done((bf16[504,256]{1,0:T(8,128)(2,1)S(1)}, bf16[504,256]{1,0:T(8,128)(2,1)S(1)}, u32[]{:S(2)}, u32[]{:S(2)}) %collective-permute-start.4) | collective-permute-done | bytes 258080 | tf_op jit(solution)/shard_map/ppermute | solution.py:36
  62.3 2.5 %step_1_shot_1.1 = (f32[2,4,128,256]{3,2,1,0:T(8,128)S(1)}, bf16[504,256]{1,0:T(8,128)(2,1)S(1)}, bf16[504,256]{1,0:T(8,128)(2,1)S(1)}, f32[4,128,256]{2,1,0:T(8,128)S(1)}) custom-call(f32[2,4,128,256]{3,2,1,0:T(8,128)S(1)} %get-tuple-element.45.refs_0_.refs_1_, f32[2,2,2,4,128,256]{5,4,3,2,1,0:T(8,128)} %refs_1_.7, ...), custom_call_target="tpu_custom_call" | custom-call | flops 1 | bytes 1 | tf_op jit(solution)/shard_map/step_1_shot_1/pallas_call | solution.py:468
  64.8 2.8 %collective-permute-start.9 = (bf16[504,256]{1,0:T(8,128)(2,1)S(1)}, bf16[504,256]{1,0:T(8,128)(2,1)S(1)}, u32[]{:S(2)}, u32[]{:S(2)}) collective-permute-start(bf16[504,256]{1,0:T(8,128)(2,1)S(1)} %get-tuple-element.57), channel_id=1, source_target_pairs={{1,2},{2,1},{3,4},{4,3},{5,6},{6,5},{7,8},{8,7},{9,10},{10,9},{11,... | collective-permute-start | bytes 774152 | tf_op jit(solution)/shard_map/ppermute | solution.py:36
  67.6 0.1 collective-permute-start.8
  67.7 0.0 collective-permute-done.11.refs_3_
  67.7 0.1 collective-permute-done.10.refs_2_
  67.8 1.3 %step_2_shot_0.1 = (f32[2,4,128,256]{3,2,1,0:T(8,128)S(1)}, bf16[504,256]{1,0:T(8,128)(2,1)S(1)}, bf16[504,256]{1,0:T(8,128)(2,1)S(1)}, f32[4,128,256]{2,1,0:T(8,128)S(1)}) custom-call(f32[2,4,128,256]{3,2,1,0:T(8,128)S(1)} %get-tuple-element.59.refs_0_.refs_1_, f32[2,4,128,256]{3,2,1,0:T(8,128)S(1)} %get-tuple-element.50.refs_0_.refs_1_, ...), custom_call_target="tpu_custom_call" | custom-call | flops 1 | bytes 1 | tf_op jit(solution)/shard_map/step_2_shot_0/pallas_call | solution.py:468
  69.1 3.3 %collective-permute-start.17 = (bf16[504,256]{1,0:T(8,128)(2,1)S(1)}, bf16[504,256]{1,0:T(8,128)(2,1)S(1)}, u32[]{:S(2)}, u32[]{:S(2)}) collective-permute-start(bf16[504,256]{1,0:T(8,128)(2,1)S(1)} %get-tuple-element.70), channel_id=1, source_target_pairs={{1,2},{2,1},{3,4},{4,3},{5,6},{6,5},{7,8},{8,7},{9,10},{10,9},{11,... | collective-permute-start | bytes 774152 | tf_op jit(solution)/shard_map/ppermute | solution.py:36
  72.4 1.3 %collective-permute-start.16 = (bf16[504,256]{1,0:T(8,128)(2,1)S(1)}, bf16[504,256]{1,0:T(8,128)(2,1)S(1)}, u32[]{:S(2)}, u32[]{:S(2)}) collective-permute-start(bf16[504,256]{1,0:T(8,128)(2,1)S(1)} %get-tuple-element.62.refs_9_), channel_id=1, source_target_pairs={{0,1},{1,0},{2,3},{3,2},{4,5},{5,4},{6,7},{7,6},{8,9},{9,8},{10,11... | collective-permute-start | bytes 774152 | tf_op jit(solution)/shard_map/ppermute | solution.py:36
  73.7 1.1 collective-permute-done.9.refs_3_
  74.8 10.7 %collective-permute-done.8.refs_2_ = bf16[504,256]{1,0:T(8,128)(2,1)S(1)} collective-permute-done((bf16[504,256]{1,0:T(8,128)(2,1)S(1)}, bf16[504,256]{1,0:T(8,128)(2,1)S(1)}, u32[]{:S(2)}, u32[]{:S(2)}) %collective-permute-start.8) | collective-permute-done | bytes 258080 | tf_op jit(solution)/shard_map/ppermute | solution.py:36
  85.5 1.3 %step_2_shot_1.1 = (f32[2,4,128,256]{3,2,1,0:T(8,128)S(1)}, bf16[256,256]{1,0:T(8,128)(2,1)S(1)}, bf16[256,256]{1,0:T(8,128)(2,1)S(1)}, bf16[248,256]{1,0:T(8,12...) custom-call(f32[2,4,128,256]{3,2,1,0:T(8,128)S(1)} %get-tuple-element.55.refs_0_.refs_1_, ...), custom_call_target="tpu_custom_call" | custom-call | flops 1 | bytes 1 | tf_op jit(solution)/shard_map/step_2_shot_1/pallas_call | solution.py:468
  86.8 3.4 %collective-permute-start.15 = (bf16[256,256]{1,0:T(8,128)(2,1)S(1)}, bf16[256,256]{1,0:T(8,128)(2,1)S(1)}, u32[]{:S(2)}, u32[]{:S(2)}) collective-permute-start(bf16[256,256]{1,0:T(8,128)(2,1)S(1)} %get-tuple-element.67), channel_id=1, source_target_pairs={{1,2},{2,1},{3,4},{4,3},{5,6},{6,5},{7,8},{8,7},{9,10},{10,9},{11,... | collective-permute-start | bytes 393224 | tf_op jit(solution)/shard_map/ppermute | solution.py:36
  90.2 0.1 collective-permute-start.14
  90.3 1.5 %collective-permute-start.12 = (bf16[248,256]{1,0:T(8,128)(2,1)S(1)}, bf16[248,256]{1,0:T(8,128)(2,1)S(1)}, u32[]{:S(2)}, u32[]{:S(2)}) collective-permute-start(bf16[248,256]{1,0:T(8,128)(2,1)S(1)} %get-tuple-element.64), channel_id=1, source_target_pairs={{0,1},{1,0},{2,3},{3,2},{4,5},{5,4},{6,7},{7,6},{8,9},{9,8},{10,11... | collective-permute-start | bytes 380936 | tf_op jit(solution)/shard_map/ppermute | solution.py:36
  91.8 2.9 %collective-permute-start.13 = (bf16[248,256]{1,0:T(8,128)(2,1)S(1)}, bf16[248,256]{1,0:T(8,128)(2,1)S(1)}, u32[]{:S(2)}, u32[]{:S(2)}) collective-permute-start(bf16[248,256]{1,0:T(8,128)(2,1)S(1)} %get-tuple-element.65), channel_id=1, source_target_pairs={{1,2},{2,1},{3,4},{4,3},{5,6},{6,5},{7,8},{8,7},{9,10},{10,9},{11,... | collective-permute-start | bytes 380936 | tf_op jit(solution)/shard_map/ppermute | solution.py:36
  94.7 0.0 collective-permute-done.16.refs_2_
  94.7 3.5 %step_3_shot_0.1 = (f32[2,2,2,4,128,256]{5,4,3,2,1,0:T(8,128)}, f32[4,200,256]{2,1,0:T(8,128)}) custom-call(f32[2,4,128,256]{3,2,1,0:T(8,128)S(1)} %get-tuple-element.69.refs_0_.refs_10_, f32[2,4,128,256]{3,2,1,0:T(8,128)S(1)} %get-tuple-element.59.refs_0_.refs_1_, bf16[504,256]{1,0:T(8,128)(2,1)S(1)} %collective-permute-done.16.refs_2_, ...), custom_call_target="tpu_custom_call" | custom-call | flops 1 | bytes 1 | tf_op jit(solution)/shard_map/step_3_shot_0/pallas_call | solution.py:468
  98.2 1.8 %collective-permute-start.18 = (f32[4,200,256]{2,1,0:T(8,128)}, f32[4,200,256]{2,1,0:T(8,128)}, u32[]{:S(2)}, u32[]{:S(2)}) collective-permute-start(f32[4,200,256]{2,1,0:T(8,128)} %get-tuple-element.72.refs_9_.refs_0_), channel_id=1, source_target_pairs={{0,16},{16,0},{1,17},{17,1},{2,18},{18,2},{3,19},{19,3},{4,20},{20... | collective-permute-start | bytes 2457608 | tf_op jit(solution)/shard_map/ppermute | solution.py:598
  100.0 2.3 %step_3_shot_1.2 = (f32[4,128,256]{2,1,0:T(8,128)S(1)}, f32[4,200,256]{2,1,0:T(8,128)}) custom-call(f32[2,4,128,256]{3,2,1,0:T(8,128)S(1)} %get-tuple-element.63.refs_11_.refs_0_, f32[2,4,128,256]{3,2,1,0:T(8,128)S(1)} %get-tuple-element.55.refs_0_.refs_1_, bf16[256,256]{1,0:T(8,128)(2,1)S(1)} %collective-permute-done.14.refs_2_, ...), custom_call_target="tpu_custom_call" | custom-call | flops 1 | bytes 1 | tf_op jit(solution)/shard_map/step_3_shot_1/pallas_call | solution.py:468
  102.2 0.4 collective-permute-start.19
  102.7 1.4 %step_3_shot_1.3.refs_4_ = f32[2,2,2,4,128,256]{5,4,3,2,1,0:T(8,128)} custom-call(f32[2,4,128,256]{3,2,1,0:T(8,128)S(1)} %get-tuple-element.63.refs_11_.refs_0_, f32[2,4,128,256]{3,2,1,0:T(8,128)S(1)} %get-tuple-element.55.refs_0_.refs_1_, bf16[248,256]{1,0:T(8,128)(2,1)S(1)} %collective-permute-done.12.refs_2_, ...), custom_call_target="tpu_custom_call", output_to_operand_aliasing={{}: (8, {})} | custom-call | flops 9999999827968 | bytes 1 | tf_op jit(solution)/shard_map/step_3_shot_1/pallas_call | solution.py:468
  104.1 0.9 collective-permute-done.19.refs_3_
  105.0 2.8 %sum_frames.1 = f32[4,192,256]{2,1,0:T(8,128)} custom-call(f32[4,200,256]{2,1,0:T(8,128)} %get-tuple-element.72.refs_9_.refs_0_, f32[4,200,256]{2,1,0:T(8,128)} %collective-permute-done.18.refs_1_, f32[4,200,256]{2,1,0:T(8,128)} %get-tuple-element.74.refs_7_.refs_2_, f32[4,200,256]{2,1,0:T(8,128)} %collective-permute-done.19.refs_3_, ...), custom_call_target="tpu_custom_call" | custom-call | flops 1 | bytes 1 | tf_op jit(solution)/shard_map/sum_frames/pallas_call | solution.py:510
  (21 shorter events, 0.0 us)
Async XLA Ops:
  0.6 5.8 %copy-start.5 = (s32[2,128]{1,0:T(2,128)S(1)}, s32[2,128]{1,0:T(2,128)}, u32[]{:S(2)}) copy-start(s32[2,128]{1,0:T(2,128)} %ids_ref.1) | copy-start | bytes 3076
  0.6 5.8 %copy-start.2 = (bf16[2,128,256]{2,1,0:T(8,128)(2,1)S(1)}, bf16[2,128,256]{2,1,0:T(8,128)(2,1)}, u32[]{:S(2)}) copy-start(bf16[2,128,256]{2,1,0:T(8,128)(2,1)} %lines_ref.1) | copy-start | bytes 393220
  0.7 19.3 %copy-start.1 = (f32[2,4,64]{2,1,0:T(4,128)S(1)}, f32[2,4,64]{2,1,0:T(4,128)}, u32[]{:S(2)}) copy-start(f32[2,4,64]{2,1,0:T(4,128)} %refs_5_.15) | copy-start | bytes 6148
  0.7 19.3 %copy-start.3 = (s32[2,64]{1,0:T(2,128)S(1)}, s32[2,64]{1,0:T(2,128)}, u32[]{:S(2)}) copy-start(s32[2,64]{1,0:T(2,128)} %refs_4_.3) | copy-start | bytes 1540
  0.7 19.3 %copy-start.4 = (s32[2]{0:T(128)S(1)}, s32[2]{0:T(128)}, u32[]{:S(2)}) copy-start(s32[2]{0:T(128)} %refs_6_.15) | copy-start | bytes 28
  0.7 19.3 %copy-start = (f32[4,192,256]{2,1,0:T(8,128)S(1)}, f32[4,192,256]{2,1,0:T(8,128)}, u32[]{:S(2)}) copy-start(f32[4,192,256]{2,1,0:T(8,128)} %refs_8_.1) | copy-start | bytes 2359300
  2.1 17.4 %collective-permute-start.3 = (bf16[504,256]{1,0:T(8,128)(2,1)S(1)}, bf16[504,256]{1,0:T(8,128)(2,1)S(1)}, u32[]{:S(2)}, u32[]{:S(2)}) collective-permute-start(bf16[504,256]{1,0:T(8,128)(2,1)S(1)} %get-tuple-element.42), channel_id=1, source_target_pairs={{1,2},{2,1},{3,4},{4,3},{5,6},{6,5},{7,8},{8,7},{9,10},{10,9},{11,... | collective-permute-start | bytes 774152 | tf_op jit(solution)/shard_map/ppermute | solution.py:36
  5.2 14.8 %collective-permute-start.2 = (bf16[504,256]{1,0:T(8,128)(2,1)S(1)}, bf16[504,256]{1,0:T(8,128)(2,1)S(1)}, u32[]{:S(2)}, u32[]{:S(2)}) collective-permute-start(bf16[504,256]{1,0:T(8,128)(2,1)S(1)} %get-tuple-element.39.after_ref), channel_id=1, source_target_pairs={{0,1},{1,0},{2,3},{3,2},{4,5},{5,4},{6,7},{7,6},{8,9},{9,8},{10,11... | collective-permute-start | bytes 774152 | tf_op jit(solution)/shard_map/ppermute | solution.py:36
  7.4 15.9 %all-to-all-start = ((bf16[16,16,384]{2,1,0:T(8,128)(2,1)}), bf16[16,16,384]{2,1,0:T(8,128)(2,1)}, u32[]{:S(2)}, u32[]{:S(2)}) async-start(bf16[16,16,384]{2,1,0:T(8,128)(2,1)} %bitcast), calls=%async_computation | async-start | bytes 393216 | tf_op jit(solution)/shard_map/all_to_all | solution.py:202
  15.1 22.0 %collective-permute-start = (bf16[504,256]{1,0:T(8,128)(2,1)}, bf16[504,256]{1,0:T(8,128)(2,1)}, u32[]{:S(2)}, u32[]{:S(2)}) collective-permute-start(bf16[504,256]{1,0:T(8,128)(2,1)} %get-tuple-element.40), channel_id=1, source_target_pairs={{0,1},{1,0},{2,3},{3,2},{4,5},{5,4},{6,7},{7,6},{8,9},{9,8},{10,11... | collective-permute-start | bytes 774152 | tf_op jit(solution)/shard_map/ppermute | solution.py:36
  15.5 21.7 %collective-permute-start.1 = (bf16[504,256]{1,0:T(8,128)(2,1)}, bf16[504,256]{1,0:T(8,128)(2,1)}, u32[]{:S(2)}, u32[]{:S(2)}) collective-permute-start(bf16[504,256]{1,0:T(8,128)(2,1)} %get-tuple-element.41), channel_id=1, source_target_pairs={{1,2},{2,1},{3,4},{4,3},{5,6},{6,5},{7,8},{8,7},{9,10},{10,9},{11,... | collective-permute-start | bytes 774152 | tf_op jit(solution)/shard_map/ppermute | solution.py:36
  24.8 19.7 %collective-permute-start.7 = (bf16[504,256]{1,0:T(8,128)(2,1)S(1)}, bf16[504,256]{1,0:T(8,128)(2,1)S(1)}, u32[]{:S(2)}, u32[]{:S(2)}) collective-permute-start(bf16[504,256]{1,0:T(8,128)(2,1)S(1)} %get-tuple-element.51), channel_id=1, source_target_pairs={{1,2},{2,1},{3,4},{4,3},{5,6},{6,5},{7,8},{8,7},{9,10},{10,9},{11,... | collective-permute-start | bytes 774152 | tf_op jit(solution)/shard_map/ppermute | solution.py:36
  28.1 16.4 %collective-permute-start.6 = (bf16[504,256]{1,0:T(8,128)(2,1)S(1)}, bf16[504,256]{1,0:T(8,128)(2,1)S(1)}, u32[]{:S(2)}, u32[]{:S(2)}) collective-permute-start(bf16[504,256]{1,0:T(8,128)(2,1)S(1)} %get-tuple-element.44.refs_9_), channel_id=1, source_target_pairs={{0,1},{1,0},{2,3},{3,2},{4,5},{5,4},{6,7},{7,6},{8,9},{9,8},{10,11... | collective-permute-start | bytes 774152 | tf_op jit(solution)/shard_map/ppermute | solution.py:36
  41.1 10.1 %collective-permute-start.5 = (bf16[504,256]{1,0:T(8,128)(2,1)S(1)}, bf16[504,256]{1,0:T(8,128)(2,1)S(1)}, u32[]{:S(2)}, u32[]{:S(2)}) collective-permute-start(bf16[504,256]{1,0:T(8,128)(2,1)S(1)} %get-tuple-element.47), channel_id=1, source_target_pairs={{1,2},{2,1},{3,4},{4,3},{5,6},{6,5},{7,8},{8,7},{9,10},{10,9},{11,... | collective-permute-start | bytes 774152 | tf_op jit(solution)/shard_map/ppermute | solution.py:36
  44.4 17.9 %collective-permute-start.4 = (bf16[504,256]{1,0:T(8,128)(2,1)S(1)}, bf16[504,256]{1,0:T(8,128)(2,1)S(1)}, u32[]{:S(2)}, u32[]{:S(2)}) collective-permute-start(bf16[504,256]{1,0:T(8,128)(2,1)S(1)} %get-tuple-element.46.refs_9_), channel_id=1, source_target_pairs={{0,1},{1,0},{2,3},{3,2},{4,5},{5,4},{6,7},{7,6},{8,9},{9,8},{10,11... | collective-permute-start | bytes 774152 | tf_op jit(solution)/shard_map/ppermute | solution.py:36
  46.9 20.7 %collective-permute-start.11 = (bf16[504,256]{1,0:T(8,128)(2,1)S(1)}, bf16[504,256]{1,0:T(8,128)(2,1)S(1)}, u32[]{:S(2)}, u32[]{:S(2)}) collective-permute-start(bf16[504,256]{1,0:T(8,128)(2,1)S(1)} %get-tuple-element.60), channel_id=1, source_target_pairs={{1,2},{2,1},{3,4},{4,3},{5,6},{6,5},{7,8},{8,7},{9,10},{10,9},{11,... | collective-permute-start | bytes 774152 | tf_op jit(solution)/shard_map/ppermute | solution.py:36
  49.9 18.0 %collective-permute-start.10 = (bf16[504,256]{1,0:T(8,128)(2,1)S(1)}, bf16[504,256]{1,0:T(8,128)(2,1)S(1)}, u32[]{:S(2)}, u32[]{:S(2)}) collective-permute-start(bf16[504,256]{1,0:T(8,128)(2,1)S(1)} %get-tuple-element.54.refs_9_), channel_id=1, source_target_pairs={{0,1},{1,0},{2,3},{3,2},{4,5},{5,4},{6,7},{7,6},{8,9},{9,8},{10,11... | collective-permute-start | bytes 774152 | tf_op jit(solution)/shard_map/ppermute | solution.py:36
  64.8 10.0 %collective-permute-start.9 = (bf16[504,256]{1,0:T(8,128)(2,1)S(1)}, bf16[504,256]{1,0:T(8,128)(2,1)S(1)}, u32[]{:S(2)}, u32[]{:S(2)}) collective-permute-start(bf16[504,256]{1,0:T(8,128)(2,1)S(1)} %get-tuple-element.57), channel_id=1, source_target_pairs={{1,2},{2,1},{3,4},{4,3},{5,6},{6,5},{7,8},{8,7},{9,10},{10,9},{11,... | collective-permute-start | bytes 774152 | tf_op jit(solution)/shard_map/ppermute | solution.py:36
  67.6 17.9 %collective-permute-start.8 = (bf16[504,256]{1,0:T(8,128)(2,1)S(1)}, bf16[504,256]{1,0:T(8,128)(2,1)S(1)}, u32[]{:S(2)}, u32[]{:S(2)}) collective-permute-start(bf16[504,256]{1,0:T(8,128)(2,1)S(1)} %get-tuple-element.56.refs_9_), channel_id=1, source_target_pairs={{0,1},{1,0},{2,3},{3,2},{4,5},{5,4},{6,7},{7,6},{8,9},{9,8},{10,11... | collective-permute-start | bytes 774152 | tf_op jit(solution)/shard_map/ppermute | solution.py:36
  69.1 22.6 %collective-permute-start.17 = (bf16[504,256]{1,0:T(8,128)(2,1)S(1)}, bf16[504,256]{1,0:T(8,128)(2,1)S(1)}, u32[]{:S(2)}, u32[]{:S(2)}) collective-permute-start(bf16[504,256]{1,0:T(8,128)(2,1)S(1)} %get-tuple-element.70), channel_id=1, source_target_pairs={{1,2},{2,1},{3,4},{4,3},{5,6},{6,5},{7,8},{8,7},{9,10},{10,9},{11,... | collective-permute-start | bytes 774152 | tf_op jit(solution)/shard_map/ppermute | solution.py:36
  72.4 22.3 %collective-permute-start.16 = (bf16[504,256]{1,0:T(8,128)(2,1)S(1)}, bf16[504,256]{1,0:T(8,128)(2,1)S(1)}, u32[]{:S(2)}, u32[]{:S(2)}) collective-permute-start(bf16[504,256]{1,0:T(8,128)(2,1)S(1)} %get-tuple-element.62.refs_9_), channel_id=1, source_target_pairs={{0,1},{1,0},{2,3},{3,2},{4,5},{5,4},{6,7},{7,6},{8,9},{9,8},{10,11... | collective-permute-start | bytes 774152 | tf_op jit(solution)/shard_map/ppermute | solution.py:36
  86.8 13.2 %collective-permute-start.15 = (bf16[256,256]{1,0:T(8,128)(2,1)S(1)}, bf16[256,256]{1,0:T(8,128)(2,1)S(1)}, u32[]{:S(2)}, u32[]{:S(2)}) collective-permute-start(bf16[256,256]{1,0:T(8,128)(2,1)S(1)} %get-tuple-element.67), channel_id=1, source_target_pairs={{1,2},{2,1},{3,4},{4,3},{5,6},{6,5},{7,8},{8,7},{9,10},{10,9},{11,... | collective-permute-start | bytes 393224 | tf_op jit(solution)/shard_map/ppermute | solution.py:36
  90.2 9.8 %collective-permute-start.14 = (bf16[256,256]{1,0:T(8,128)(2,1)S(1)}, bf16[256,256]{1,0:T(8,128)(2,1)S(1)}, u32[]{:S(2)}, u32[]{:S(2)}) collective-permute-start(bf16[256,256]{1,0:T(8,128)(2,1)S(1)} %get-tuple-element.66.refs_12_), channel_id=1, source_target_pairs={{0,1},{1,0},{2,3},{3,2},{4,5},{5,4},{6,7},{7,6},{8,9},{9,8},{10,11... | collective-permute-start | bytes 393224 | tf_op jit(solution)/shard_map/ppermute | solution.py:36
  90.3 12.4 %collective-permute-start.12 = (bf16[248,256]{1,0:T(8,128)(2,1)S(1)}, bf16[248,256]{1,0:T(8,128)(2,1)S(1)}, u32[]{:S(2)}, u32[]{:S(2)}) collective-permute-start(bf16[248,256]{1,0:T(8,128)(2,1)S(1)} %get-tuple-element.64), channel_id=1, source_target_pairs={{0,1},{1,0},{2,3},{3,2},{4,5},{5,4},{6,7},{7,6},{8,9},{9,8},{10,11... | collective-permute-start | bytes 380936 | tf_op jit(solution)/shard_map/ppermute | solution.py:36
  91.8 10.9 %collective-permute-start.13 = (bf16[248,256]{1,0:T(8,128)(2,1)S(1)}, bf16[248,256]{1,0:T(8,128)(2,1)S(1)}, u32[]{:S(2)}, u32[]{:S(2)}) collective-permute-start(bf16[248,256]{1,0:T(8,128)(2,1)S(1)} %get-tuple-element.65), channel_id=1, source_target_pairs={{1,2},{2,1},{3,4},{4,3},{5,6},{6,5},{7,8},{8,7},{9,10},{10,9},{11,... | collective-permute-start | bytes 380936 | tf_op jit(solution)/shard_map/ppermute | solution.py:36
  98.2 6.8 %collective-permute-start.18 = (f32[4,200,256]{2,1,0:T(8,128)}, f32[4,200,256]{2,1,0:T(8,128)}, u32[]{:S(2)}, u32[]{:S(2)}) collective-permute-start(f32[4,200,256]{2,1,0:T(8,128)} %get-tuple-element.72.refs_9_.refs_0_), channel_id=1, source_target_pairs={{0,16},{16,0},{1,17},{17,1},{2,18},{18,2},{3,19},{19,3},{4,20},{20... | collective-permute-start | bytes 2457608 | tf_op jit(solution)/shard_map/ppermute | solution.py:598
  102.2 2.7 %collective-permute-start.19 = (f32[4,200,256]{2,1,0:T(8,128)}, f32[4,200,256]{2,1,0:T(8,128)}, u32[]{:S(2)}, u32[]{:S(2)}) collective-permute-start(f32[4,200,256]{2,1,0:T(8,128)} %get-tuple-element.74.refs_7_.refs_2_), channel_id=1, source_target_pairs={{0,16},{16,0},{1,17},{17,1},{2,18},{18,2},{3,19},{19,3},{4,20},{20... | collective-permute-start | bytes 2457608 | tf_op jit(solution)/shard_map/ppermute | solution.py:598

commit v9 on v8

--- a/solution.py
+++ b/solution.py
@@ -54,7 +54,7 @@
     return pl.multiple_of(start, 8), offset - start
 
 
-def put_window(target_ref, layer, part_ref, offset):
+def put_window(target_ref, layer, part_ref, offset, base_ref):
     _, rows_y, cells_z = part_ref.shape
     start = pl.multiple_of(lax.div(offset, 8) * 8, 8)
     gap = lax.rem(offset, 8)
@@ -65,7 +65,10 @@
         if at < rows_y:
             turned = pltpu.roll(part_ref[layer, at : at + 8], gap, 0)
         here = pl.ds(pl.multiple_of(start + at, 8), 8)
-        target_ref[layer, here, :] = jnp.where(before, last, turned)
+        placed = jnp.where(before, last, turned)
+        if base_ref is not None:
+            placed = base_ref[layer, here, :] + placed
+        target_ref[layer, here, :] = placed
         last = turned
 
 
@@ -248,7 +251,7 @@
     )(new, saved)
 
 
-def step_kernel(shot, step, comps, got_groups, send_groups, create, lines, waits, keeps, *refs):
+def step_kernel(shot, step, comps, got_groups, send_groups, create, framed, lines, waits, keeps, *refs):
     refs = list(refs)
 
     def take(count):
@@ -269,6 +272,7 @@
     [offsets_ref] = take(1) if first or framing else [None]
     [speed_from] = take(1)
     [contrib_from] = take(1) if with_image and not first else [None]
+    [frame_from] = take(1) if framed else [None]
     keep_refs = take(len(keeps))
     held = last and comps == (1,)
     [field_from] = take(1) if last and comps == (0,) else [None]
@@ -378,9 +382,11 @@
             if last and not held:
                 store(new_ref.at[comp, layer], out_ref.at[shot, 0, comp, layer])
     if framing:
-        contrib_ref[...] = jnp.zeros_like(contrib_ref)
         for layer in range(layers):
-            put_window(contrib_ref, layer, terms_ref, offsets_ref[shot])
+            empty = jnp.zeros_like(contrib_ref[layer])
+            contrib_ref[layer] = empty if frame_from is None else frame_from[layer]
+        for layer in range(layers):
+            put_window(contrib_ref, layer, terms_ref, offsets_ref[shot], frame_from)
     for started in stores:
         started.wait()
     if not last:
@@ -389,7 +395,7 @@
 
 def one_step(
     shot, step, comps, got_groups, send_groups,
-    wavefields, offsets, now, later, got, saved, pos, traces, speed, contrib, out, after, heavy, model_y, keeps=(), field=None,
+    wavefields, offsets, now, later, got, saved, pos, traces, speed, contrib, frame, out, after, heavy, model_y, keeps=(), field=None,
 ):
     first, last = step == 0, step == STEPS - 1
     with_image = 1 in comps
@@ -422,6 +428,9 @@
     specs.append(vmem)
     if with_image and not first:
         args.append(contrib)
+        specs.append(vmem)
+    if frame is not None:
+        args.append(frame)
         specs.append(vmem)
     args += [value for _, value in keeps]
     specs += [vmem] * len(keeps)
@@ -467,7 +476,7 @@
         scratch = [pltpu.VMEM(lead + state.shape, jnp.float32), pltpu.SemaphoreType.DMA((1,))]
     return pl.pallas_call(
         functools.partial(
-            step_kernel, shot, step, comps, got_groups, send_groups, out is None, lines,
+            step_kernel, shot, step, comps, got_groups, send_groups, out is None, frame is not None, lines,
             len(after), tuple(keep for keep, _ in keeps),
         ),
         in_specs=specs,
@@ -549,7 +558,7 @@
     contrib = [None] * shots
     speed = [courant] * shots
     out = None
-    frames = []
+    frame = None
     after = []
     for step in range(STEPS):
         for shot in range(shots):
@@ -561,7 +570,7 @@
                 early = step == 0 and shot == 0
                 made = one_step(
                     shot, step, BOTH[0], groups[shot], () if early else send_groups, *common,
-                    got[shot], None if early else saved, *fixed, contrib[shot], None, after, early,
+                    got[shot], None if early else saved, *fixed, contrib[shot], None, None, after, early,
                     model_y,
                 )
                 later[shot], now[shot] = now[shot], made[0]
@@ -583,7 +592,7 @@
             for group in groups[shot]:
                 made = one_step(
                     shot, step, group, (group,), (), *common, got[shot][:1], saved, *fixed,
-                    contrib[shot], out, after, group == (0,), model_y,
+                    contrib[shot], frame if 1 in group else None, out, after, group == (0,), model_y,
                     () if group == (1,) else keeps, field,
                 )
                 got[shot] = got[shot][1:]
@@ -592,14 +601,13 @@
                 else:
                     out = made[0]
                 if 1 in group:
-                    frames.append(made[1])
+                    frame = made[1]
                     after = [made[1]]
     if shot_devices == 2:
-        others = [lax.ppermute(frame, "shot", [(0, 1), (1, 0)]) for frame in frames]
-        image = sum_frames(frames, others, scale, model_y, out)
+        other = lax.ppermute(frame, "shot", [(0, 1), (1, 0)])
+        image = sum_frames([frame], [other], scale, model_y, out)
     else:
-        frame = sum(frames)[:, :model_y]
-        image = lax.psum(frame, "shot") * scale
+        image = lax.psum(frame[:, :model_y], "shot") * scale
     return (out, image)
 
 

time: 109 us -> 108 us (level)
  waiting for transfers between devices: 32.9 us -> 35.4 us
  starting transfers between devices: 43.3 us -> 41.6 us
  Pallas kernels: 30.7 us -> 29.3 us
    ppermute x18, waiting for transfers between devices: 32 us -> 34.5 us  [swap_pairs(): return lax.ppermute(value, 'space', routes)]
    ppermute x2 -> x1, starting transfers between devices: 2.22 us -> 0.59 us  [body(): other = lax.ppermute(frame, 'shot', [(0, 1), (1, 0)])]
  transfers between devices with their start and end apart: 21 -> 20, of which waited for: 7 -> 8; matrix products, arithmetic and copies ran while one was open for 0% -> 0% of each run, Pallas kernels for 25% -> 24%
where the time goes in v9:
time: 108 us; the launch traced here: 107 us
  starting transfers between devices  41.6 us (39%)
  waiting for transfers between devices  35.4 us (33%)
  Pallas kernels  29.3 us (27%)
  between operations  1.1 us (1%)
    ppermute x18, starting transfers between devices, swap_pairs(): return lax.ppermute(value, 'space', routes)  35.4 us
    ppermute x18, waiting for transfers between devices, swap_pairs(): return lax.ppermute(value, 'space', routes)  34.5 us
    pallas_call x9, Pallas kernels, one_step(): pl.pallas_call(functools.partial(step_kernel, shot, step, comps, got_grou...  21.1 us
    all_to_all x1, starting transfers between devices, deliver(): got = lax.all_to_all(message, 'space', 0, 0, tiled=False)  5.63 us
    pallas_call x2, Pallas kernels, pack_halo(): pl.pallas_call(functools.partial(pack_kernel, shot), in_specs=[pl.BlockSp...  3.48 us
    pallas_call x1, Pallas kernels, sum_frames(): pl.pallas_call(functools.partial(sum_kernel, scale), in_specs=[vmem] * le...  2.32 us
  transfers between devices with their start and end apart: 20, of which 8 were waited for; matrix products, arithmetic and copies ran while one was open for 0% of the time, Pallas kernels for 24%

profile of v9, /device:TPU:19, one launch (start us, length us, event | category | flops | bytes accessed | tf_op | source)
XLA Modules:
  0.0 107.5 jit_solution(10307212301422709751)
XLA Ops:
  0.7 1.4 %pack_halo.2 = (bf16[504,256]{1,0:T(8,128)(2,1)S(1)}, bf16[504,256]{1,0:T(8,128)(2,1)S(1)}) custom-call(f32[2,2,2,4,128,256]{5,4,3,2,1,0:T(8,128)} %refs_1_.7), custom_call_target="tpu_custom_call" | custom-call | flops 1 | bytes 1 | tf_op jit(solution)/shard_map/pack_halo/pallas_call | solution.py:128
  2.1 3.1 %collective-permute-start.3 = (bf16[504,256]{1,0:T(8,128)(2,1)S(1)}, bf16[504,256]{1,0:T(8,128)(2,1)S(1)}, u32[]{:S(2)}, u32[]{:S(2)}) collective-permute-start(bf16[504,256]{1,0:T(8,128)(2,1)S(1)} %get-tuple-element.42), channel_id=1, source_target_pairs={{1,2},{2,1},{3,4},{4,3},{5,6},{6,5},{7,8},{8,7},{9,10},{10,9},{11,... | collective-permute-start | bytes 774152 | tf_op jit(solution)/shard_map/ppermute | solution.py:36
  5.2 1.2 %collective-permute-start.2 = (bf16[504,256]{1,0:T(8,128)(2,1)S(1)}, bf16[504,256]{1,0:T(8,128)(2,1)S(1)}, u32[]{:S(2)}, u32[]{:S(2)}) collective-permute-start(bf16[504,256]{1,0:T(8,128)(2,1)S(1)} %get-tuple-element.39.after_ref), channel_id=1, source_target_pairs={{0,1},{1,0},{2,3},{3,2},{4,5},{5,4},{6,7},{7,6},{8,9},{9,8},{10,11... | collective-permute-start | bytes 774152 | tf_op jit(solution)/shard_map/ppermute | solution.py:36
  6.4 1.0 pack_lines.1.refs_0_
  7.4 5.6 %all-to-all-start = ((bf16[16,16,384]{2,1,0:T(8,128)(2,1)}), bf16[16,16,384]{2,1,0:T(8,128)(2,1)}, u32[]{:S(2)}, u32[]{:S(2)}) async-start(bf16[16,16,384]{2,1,0:T(8,128)(2,1)} %bitcast), calls=%async_computation | async-start | bytes 393216 | tf_op jit(solution)/shard_map/all_to_all | solution.py:205
  13.0 2.1 %pack_halo.3 = (bf16[504,256]{1,0:T(8,128)(2,1)}, bf16[504,256]{1,0:T(8,128)(2,1)}) custom-call(f32[2,2,2,4,128,256]{5,4,3,2,1,0:T(8,128)} %refs_1_.7, bf16[256,384]{1,0:T(8,128)(2,1)} %pack_lines.1.refs_0_), custom_call_target="tpu_custom_call" | custom-call | flops 1 | bytes 1 | tf_op jit(solution)/shard_map/pack_halo/pallas_call | solution.py:128
  15.1 0.3 collective-permute-start
  15.5 4.0 %collective-permute-start.1 = (bf16[504,256]{1,0:T(8,128)(2,1)}, bf16[504,256]{1,0:T(8,128)(2,1)}, u32[]{:S(2)}, u32[]{:S(2)}) collective-permute-start(bf16[504,256]{1,0:T(8,128)(2,1)} %get-tuple-element.41), channel_id=1, source_target_pairs={{1,2},{2,1},{3,4},{4,3},{5,6},{6,5},{7,8},{8,7},{9,10},{10,9},{11,... | collective-permute-start | bytes 774152 | tf_op jit(solution)/shard_map/ppermute | solution.py:36
  19.5 0.0 collective-permute-done.3.refs_3_
  19.5 0.5 collective-permute-done.2.refs_2_
  20.0 3.3 %step_0_shot_0.1 = (f32[2,4,128,256]{3,2,1,0:T(8,128)S(1)}, f32[4,128,256]{2,1,0:T(8,128)S(1)}, f32[4,128,256]{2,1,0:T(8,128)S(1)}) custom-call(f32[2,2,2,4,128,256]{5,4,3,2,1,0:T(8,128)} %refs_1_.7, f32[2,2,2,4,128,256]{5,4,3,2,1,0:T(8,128)} %refs_1_.7, bf16[504,256]{1,0:T(8,128)(2,1)S(1)} %collective-permute-done.2.refs_2_, ...), custom_call_target="tpu_custom_call" | custom-call | flops 9999999827968 | bytes 1 | tf_op jit(solution)/shard_map/step_0_shot_0/pallas_call | solution.py:477
  23.3 0.0 all-to-all-done
  23.3 1.2 %unpack_lines.1.saved_ref.refs_4_ = f32[128,256]{1,0:T(8,128)S(1)} custom-call(bf16[256,384]{1,0:T(8,128)(2,1)} %bitcast.1.got_ref), custom_call_target="tpu_custom_call" | custom-call | flops 1 | bytes 1 | tf_op jit(solution)/shard_map/unpack_lines/pallas_call | solution.py:206
  24.6 0.2 finish_first_0.1
  24.8 3.3 %collective-permute-start.7 = (bf16[504,256]{1,0:T(8,128)(2,1)S(1)}, bf16[504,256]{1,0:T(8,128)(2,1)S(1)}, u32[]{:S(2)}, u32[]{:S(2)}) collective-permute-start(bf16[504,256]{1,0:T(8,128)(2,1)S(1)} %get-tuple-element.51), channel_id=1, source_target_pairs={{1,2},{2,1},{3,4},{4,3},{5,6},{6,5},{7,8},{8,7},{9,10},{10,9},{11,... | collective-permute-start | bytes 774152 | tf_op jit(solution)/shard_map/ppermute | solution.py:36
  28.1 0.5 collective-permute-start.6
  28.6 8.5 %collective-permute-done.refs_2_ = bf16[504,256]{1,0:T(8,128)(2,1)} collective-permute-done((bf16[504,256]{1,0:T(8,128)(2,1)}, bf16[504,256]{1,0:T(8,128)(2,1)}, u32[]{:S(2)}, u32[]{:S(2)}) %collective-permute-start) | collective-permute-done | bytes 258080 | tf_op jit(solution)/shard_map/ppermute | solution.py:36
  37.2 0.0 collective-permute-done.1.refs_3_
  37.2 4.0 %step_0_shot_1.1 = (f32[2,4,128,256]{3,2,1,0:T(8,128)S(1)}, bf16[504,256]{1,0:T(8,128)(2,1)S(1)}, bf16[504,256]{1,0:T(8,128)(2,1)S(1)}, f32[4,128,256]{2,1,0:T(8,128)S(1)}, f32[4,128,256]{2,1,0:T(8,128)S(1)}) custom-call(f32[2,2,2,4,128,256]{5,4,3,2,1,0:T(8,128)} %refs_1_.7, f32[2,2,2,4,128,256]{5,4,3,2,1,0:T(8,128)} %refs_1_.7, ...), custom_call_target="tpu_custom_call" | custom-call | flops 1 | bytes 1 | tf_op jit(solution)/shard_map/step_0_shot_1/pallas_call | solution.py:477
  41.1 3.3 %collective-permute-start.5 = (bf16[504,256]{1,0:T(8,128)(2,1)S(1)}, bf16[504,256]{1,0:T(8,128)(2,1)S(1)}, u32[]{:S(2)}, u32[]{:S(2)}) collective-permute-start(bf16[504,256]{1,0:T(8,128)(2,1)S(1)} %get-tuple-element.47), channel_id=1, source_target_pairs={{1,2},{2,1},{3,4},{4,3},{5,6},{6,5},{7,8},{8,7},{9,10},{10,9},{11,... | collective-permute-start | bytes 774152 | tf_op jit(solution)/shard_map/ppermute | solution.py:36
  44.4 0.1 collective-permute-start.4
  44.5 0.0 collective-permute-done.6.refs_2_
  44.5 2.4 %step_1_shot_0.1 = (f32[2,4,128,256]{3,2,1,0:T(8,128)S(1)}, bf16[504,256]{1,0:T(8,128)(2,1)S(1)}, bf16[504,256]{1,0:T(8,128)(2,1)S(1)}, f32[4,128,256]{2,1,0:T(8,128)S(1)}) custom-call(f32[2,4,128,256]{3,2,1,0:T(8,128)S(1)} %get-tuple-element.50.refs_0_.refs_1_, f32[2,2,2,4,128,256]{5,4,3,2,1,0:T(8,128)} %refs_1_.7, ...), custom_call_target="tpu_custom_call" | custom-call | flops 1 | bytes 1 | tf_op jit(solution)/shard_map/step_1_shot_0/pallas_call | solution.py:477
  46.9 2.9 %collective-permute-start.11 = (bf16[504,256]{1,0:T(8,128)(2,1)S(1)}, bf16[504,256]{1,0:T(8,128)(2,1)S(1)}, u32[]{:S(2)}, u32[]{:S(2)}) collective-permute-start(bf16[504,256]{1,0:T(8,128)(2,1)S(1)} %get-tuple-element.60), channel_id=1, source_target_pairs={{1,2},{2,1},{3,4},{4,3},{5,6},{6,5},{7,8},{8,7},{9,10},{10,9},{11,... | collective-permute-start | bytes 774152 | tf_op jit(solution)/shard_map/ppermute | solution.py:36
  49.8 1.4 %collective-permute-start.10 = (bf16[504,256]{1,0:T(8,128)(2,1)S(1)}, bf16[504,256]{1,0:T(8,128)(2,1)S(1)}, u32[]{:S(2)}, u32[]{:S(2)}) collective-permute-start(bf16[504,256]{1,0:T(8,128)(2,1)S(1)} %get-tuple-element.54.refs_9_), channel_id=1, source_target_pairs={{0,1},{1,0},{2,3},{3,2},{4,5},{5,4},{6,7},{7,6},{8,9},{9,8},{10,11... | collective-permute-start | bytes 774152 | tf_op jit(solution)/shard_map/ppermute | solution.py:36
  51.2 11.1 %collective-permute-done.4.refs_2_ = bf16[504,256]{1,0:T(8,128)(2,1)S(1)} collective-permute-done((bf16[504,256]{1,0:T(8,128)(2,1)S(1)}, bf16[504,256]{1,0:T(8,128)(2,1)S(1)}, u32[]{:S(2)}, u32[]{:S(2)}) %collective-permute-start.4) | collective-permute-done | bytes 258080 | tf_op jit(solution)/shard_map/ppermute | solution.py:36
  62.3 2.5 %step_1_shot_1.1 = (f32[2,4,128,256]{3,2,1,0:T(8,128)S(1)}, bf16[504,256]{1,0:T(8,128)(2,1)S(1)}, bf16[504,256]{1,0:T(8,128)(2,1)S(1)}, f32[4,128,256]{2,1,0:T(8,128)S(1)}) custom-call(f32[2,4,128,256]{3,2,1,0:T(8,128)S(1)} %get-tuple-element.45.refs_0_.refs_1_, f32[2,2,2,4,128,256]{5,4,3,2,1,0:T(8,128)} %refs_1_.7, ...), custom_call_target="tpu_custom_call" | custom-call | flops 1 | bytes 1 | tf_op jit(solution)/shard_map/step_1_shot_1/pallas_call | solution.py:477
  64.8 2.8 %collective-permute-start.9 = (bf16[504,256]{1,0:T(8,128)(2,1)S(1)}, bf16[504,256]{1,0:T(8,128)(2,1)S(1)}, u32[]{:S(2)}, u32[]{:S(2)}) collective-permute-start(bf16[504,256]{1,0:T(8,128)(2,1)S(1)} %get-tuple-element.57), channel_id=1, source_target_pairs={{1,2},{2,1},{3,4},{4,3},{5,6},{6,5},{7,8},{8,7},{9,10},{10,9},{11,... | collective-permute-start | bytes 774152 | tf_op jit(solution)/shard_map/ppermute | solution.py:36
  67.6 0.1 collective-permute-start.8
  67.7 0.1 collective-permute-done.10.refs_2_
  67.8 1.3 %step_2_shot_0.1 = (f32[2,4,128,256]{3,2,1,0:T(8,128)S(1)}, bf16[504,256]{1,0:T(8,128)(2,1)S(1)}, bf16[504,256]{1,0:T(8,128)(2,1)S(1)}, f32[4,128,256]{2,1,0:T(8,128)S(1)}) custom-call(f32[2,4,128,256]{3,2,1,0:T(8,128)S(1)} %get-tuple-element.59.refs_0_.refs_1_, f32[2,4,128,256]{3,2,1,0:T(8,128)S(1)} %get-tuple-element.50.refs_0_.refs_1_, ...), custom_call_target="tpu_custom_call" | custom-call | flops 1 | bytes 1 | tf_op jit(solution)/shard_map/step_2_shot_0/pallas_call | solution.py:477
  69.1 3.3 %collective-permute-start.17 = (bf16[504,256]{1,0:T(8,128)(2,1)S(1)}, bf16[504,256]{1,0:T(8,128)(2,1)S(1)}, u32[]{:S(2)}, u32[]{:S(2)}) collective-permute-start(bf16[504,256]{1,0:T(8,128)(2,1)S(1)} %get-tuple-element.70), channel_id=1, source_target_pairs={{1,2},{2,1},{3,4},{4,3},{5,6},{6,5},{7,8},{8,7},{9,10},{10,9},{11,... | collective-permute-start | bytes 774152 | tf_op jit(solution)/shard_map/ppermute | solution.py:36
  72.4 1.3 %collective-permute-start.16 = (bf16[504,256]{1,0:T(8,128)(2,1)S(1)}, bf16[504,256]{1,0:T(8,128)(2,1)S(1)}, u32[]{:S(2)}, u32[]{:S(2)}) collective-permute-start(bf16[504,256]{1,0:T(8,128)(2,1)S(1)} %get-tuple-element.62.refs_9_), channel_id=1, source_target_pairs={{0,1},{1,0},{2,3},{3,2},{4,5},{5,4},{6,7},{7,6},{8,9},{9,8},{10,11... | collective-permute-start | bytes 774152 | tf_op jit(solution)/shard_map/ppermute | solution.py:36
  73.7 1.1 %collective-permute-done.9.refs_3_ = bf16[504,256]{1,0:T(8,128)(2,1)S(1)} collective-permute-done((bf16[504,256]{1,0:T(8,128)(2,1)S(1)}, bf16[504,256]{1,0:T(8,128)(2,1)S(1)}, u32[]{:S(2)}, u32[]{:S(2)}) %collective-permute-start.9) | collective-permute-done | bytes 258080 | tf_op jit(solution)/shard_map/ppermute | solution.py:36
  74.8 10.7 %collective-permute-done.8.refs_2_ = bf16[504,256]{1,0:T(8,128)(2,1)S(1)} collective-permute-done((bf16[504,256]{1,0:T(8,128)(2,1)S(1)}, bf16[504,256]{1,0:T(8,128)(2,1)S(1)}, u32[]{:S(2)}, u32[]{:S(2)}) %collective-permute-start.8) | collective-permute-done | bytes 258080 | tf_op jit(solution)/shard_map/ppermute | solution.py:36
  85.5 1.3 %step_2_shot_1.1 = (f32[2,4,128,256]{3,2,1,0:T(8,128)S(1)}, bf16[256,256]{1,0:T(8,128)(2,1)S(1)}, bf16[256,256]{1,0:T(8,128)(2,1)S(1)}, bf16[248,256]{1,0:T(8,12...) custom-call(f32[2,4,128,256]{3,2,1,0:T(8,128)S(1)} %get-tuple-element.55.refs_0_.refs_1_, ...), custom_call_target="tpu_custom_call" | custom-call | flops 1 | bytes 1 | tf_op jit(solution)/shard_map/step_2_shot_1/pallas_call | solution.py:477
  86.8 3.4 %collective-permute-start.15 = (bf16[256,256]{1,0:T(8,128)(2,1)S(1)}, bf16[256,256]{1,0:T(8,128)(2,1)S(1)}, u32[]{:S(2)}, u32[]{:S(2)}) collective-permute-start(bf16[256,256]{1,0:T(8,128)(2,1)S(1)} %get-tuple-element.67), channel_id=1, source_target_pairs={{1,2},{2,1},{3,4},{4,3},{5,6},{6,5},{7,8},{8,7},{9,10},{10,9},{11,... | collective-permute-start | bytes 393224 | tf_op jit(solution)/shard_map/ppermute | solution.py:36
  90.2 0.1 collective-permute-start.14
  90.3 1.5 %collective-permute-start.12 = (bf16[248,256]{1,0:T(8,128)(2,1)S(1)}, bf16[248,256]{1,0:T(8,128)(2,1)S(1)}, u32[]{:S(2)}, u32[]{:S(2)}) collective-permute-start(bf16[248,256]{1,0:T(8,128)(2,1)S(1)} %get-tuple-element.64), channel_id=1, source_target_pairs={{0,1},{1,0},{2,3},{3,2},{4,5},{5,4},{6,7},{7,6},{8,9},{9,8},{10,11... | collective-permute-start | bytes 380936 | tf_op jit(solution)/shard_map/ppermute | solution.py:36
  91.7 2.9 %collective-permute-start.13 = (bf16[248,256]{1,0:T(8,128)(2,1)S(1)}, bf16[248,256]{1,0:T(8,128)(2,1)S(1)}, u32[]{:S(2)}, u32[]{:S(2)}) collective-permute-start(bf16[248,256]{1,0:T(8,128)(2,1)S(1)} %get-tuple-element.65), channel_id=1, source_target_pairs={{1,2},{2,1},{3,4},{4,3},{5,6},{6,5},{7,8},{8,7},{9,10},{10,9},{11,... | collective-permute-start | bytes 380936 | tf_op jit(solution)/shard_map/ppermute | solution.py:36
  94.7 2.6 %step_3_shot_0.1 = (f32[2,2,2,4,128,256]{5,4,3,2,1,0:T(8,128)}, f32[4,200,256]{2,1,0:T(8,128)S(1)}) custom-call(f32[2,4,128,256]{3,2,1,0:T(8,128)S(1)} %get-tuple-element.69.refs_0_.refs_10_, f32[2,4,128,256]{3,2,1,0:T(8,128)S(1)} %get-tuple-element.59.refs_0_.refs_1_, bf16[504,256]{1,0:T(8,128)(2,1)S(1)} %collective-permute-done.16.refs_2_, ...), custom_call_target="tpu_custom_call" | custom-call | flops 1 | bytes 1 | tf_op jit(solution)/shard_map/step_3_shot_0/pallas_call | solution.py:477
  97.3 2.5 %collective-permute-done.14.refs_2_ = bf16[256,256]{1,0:T(8,128)(2,1)S(1)} collective-permute-done((bf16[256,256]{1,0:T(8,128)(2,1)S(1)}, bf16[256,256]{1,0:T(8,128)(2,1)S(1)}, u32[]{:S(2)}, u32[]{:S(2)}) %collective-permute-start.14) | collective-permute-done | bytes 131104 | tf_op jit(solution)/shard_map/ppermute | solution.py:36
  99.8 2.3 %step_3_shot_1.2 = (f32[4,128,256]{2,1,0:T(8,128)S(1)}, f32[4,200,256]{2,1,0:T(8,128)}) custom-call(f32[2,4,128,256]{3,2,1,0:T(8,128)S(1)} %get-tuple-element.63.refs_11_.refs_0_, f32[2,4,128,256]{3,2,1,0:T(8,128)S(1)} %get-tuple-element.55.refs_0_.refs_1_, bf16[256,256]{1,0:T(8,128)(2,1)S(1)} %collective-permute-done.14.refs_2_, ...), custom_call_target="tpu_custom_call" | custom-call | flops 1 | bytes 1 | tf_op jit(solution)/shard_map/step_3_shot_1/pallas_call | solution.py:477
  102.1 0.6 collective-permute-start.18
  102.7 0.0 collective-permute-done.12.refs_2_
  102.7 1.4 %step_3_shot_1.3.refs_2_ = f32[2,2,2,4,128,256]{5,4,3,2,1,0:T(8,128)} custom-call(f32[2,4,128,256]{3,2,1,0:T(8,128)S(1)} %get-tuple-element.63.refs_11_.refs_0_, f32[2,4,128,256]{3,2,1,0:T(8,128)S(1)} %get-tuple-element.55.refs_0_.refs_1_, bf16[248,256]{1,0:T(8,128)(2,1)S(1)} %collective-permute-done.12.refs_2_, ...), custom_call_target="tpu_custom_call", output_to_operand_aliasing={{}: (8, {})} | custom-call | flops 9999999827968 | bytes 1 | tf_op jit(solution)/shard_map/step_3_shot_1/pallas_call | solution.py:477
  104.1 0.9 collective-permute-done.18.refs_1_
  105.0 2.3 %sum_frames.1 = f32[4,192,256]{2,1,0:T(8,128)} custom-call(f32[4,200,256]{2,1,0:T(8,128)} %get-tuple-element.74.refs_7_.refs_0_, f32[4,200,256]{2,1,0:T(8,128)} %collective-permute-done.18.refs_1_, f32[2,2,2,4,128,256]{5,4,3,2,1,0:T(8,128)} %step_3_shot_1.3.refs_2_), custom_call_target="tpu_custom_call" | custom-call | flops 1 | bytes 1 | tf_op jit(solution)/shard_map/sum_frames/pallas_call | solution.py:519
  (19 shorter events, 0.0 us)
Async XLA Ops:
  0.6 5.8 %copy-start.5 = (s32[2,128]{1,0:T(2,128)S(1)}, s32[2,128]{1,0:T(2,128)}, u32[]{:S(2)}) copy-start(s32[2,128]{1,0:T(2,128)} %ids_ref.1) | copy-start | bytes 3076
  0.6 5.8 %copy-start.2 = (bf16[2,128,256]{2,1,0:T(8,128)(2,1)S(1)}, bf16[2,128,256]{2,1,0:T(8,128)(2,1)}, u32[]{:S(2)}) copy-start(bf16[2,128,256]{2,1,0:T(8,128)(2,1)} %lines_ref.1) | copy-start | bytes 393220
  0.7 19.3 %copy-start.1 = (f32[2,4,64]{2,1,0:T(4,128)S(1)}, f32[2,4,64]{2,1,0:T(4,128)}, u32[]{:S(2)}) copy-start(f32[2,4,64]{2,1,0:T(4,128)} %refs_5_.15) | copy-start | bytes 6148
  0.7 19.3 %copy-start.3 = (s32[2,64]{1,0:T(2,128)S(1)}, s32[2,64]{1,0:T(2,128)}, u32[]{:S(2)}) copy-start(s32[2,64]{1,0:T(2,128)} %refs_4_.3) | copy-start | bytes 1540
  0.7 19.3 %copy-start.4 = (s32[2]{0:T(128)S(1)}, s32[2]{0:T(128)}, u32[]{:S(2)}) copy-start(s32[2]{0:T(128)} %refs_6_.15) | copy-start | bytes 28
  0.7 19.3 %copy-start = (f32[4,192,256]{2,1,0:T(8,128)S(1)}, f32[4,192,256]{2,1,0:T(8,128)}, u32[]{:S(2)}) copy-start(f32[4,192,256]{2,1,0:T(8,128)} %refs_8_.1) | copy-start | bytes 2359300
  2.1 17.4 %collective-permute-start.3 = (bf16[504,256]{1,0:T(8,128)(2,1)S(1)}, bf16[504,256]{1,0:T(8,128)(2,1)S(1)}, u32[]{:S(2)}, u32[]{:S(2)}) collective-permute-start(bf16[504,256]{1,0:T(8,128)(2,1)S(1)} %get-tuple-element.42), channel_id=1, source_target_pairs={{1,2},{2,1},{3,4},{4,3},{5,6},{6,5},{7,8},{8,7},{9,10},{10,9},{11,... | collective-permute-start | bytes 774152 | tf_op jit(solution)/shard_map/ppermute | solution.py:36
  5.2 14.8 %collective-permute-start.2 = (bf16[504,256]{1,0:T(8,128)(2,1)S(1)}, bf16[504,256]{1,0:T(8,128)(2,1)S(1)}, u32[]{:S(2)}, u32[]{:S(2)}) collective-permute-start(bf16[504,256]{1,0:T(8,128)(2,1)S(1)} %get-tuple-element.39.after_ref), channel_id=1, source_target_pairs={{0,1},{1,0},{2,3},{3,2},{4,5},{5,4},{6,7},{7,6},{8,9},{9,8},{10,11... | collective-permute-start | bytes 774152 | tf_op jit(solution)/shard_map/ppermute | solution.py:36
  7.4 15.9 %all-to-all-start = ((bf16[16,16,384]{2,1,0:T(8,128)(2,1)}), bf16[16,16,384]{2,1,0:T(8,128)(2,1)}, u32[]{:S(2)}, u32[]{:S(2)}) async-start(bf16[16,16,384]{2,1,0:T(8,128)(2,1)} %bitcast), calls=%async_computation | async-start | bytes 393216 | tf_op jit(solution)/shard_map/all_to_all | solution.py:205
  15.1 22.0 %collective-permute-start = (bf16[504,256]{1,0:T(8,128)(2,1)}, bf16[504,256]{1,0:T(8,128)(2,1)}, u32[]{:S(2)}, u32[]{:S(2)}) collective-permute-start(bf16[504,256]{1,0:T(8,128)(2,1)} %get-tuple-element.40), channel_id=1, source_target_pairs={{0,1},{1,0},{2,3},{3,2},{4,5},{5,4},{6,7},{7,6},{8,9},{9,8},{10,11... | collective-permute-start | bytes 774152 | tf_op jit(solution)/shard_map/ppermute | solution.py:36
  15.5 21.7 %collective-permute-start.1 = (bf16[504,256]{1,0:T(8,128)(2,1)}, bf16[504,256]{1,0:T(8,128)(2,1)}, u32[]{:S(2)}, u32[]{:S(2)}) collective-permute-start(bf16[504,256]{1,0:T(8,128)(2,1)} %get-tuple-element.41), channel_id=1, source_target_pairs={{1,2},{2,1},{3,4},{4,3},{5,6},{6,5},{7,8},{8,7},{9,10},{10,9},{11,... | collective-permute-start | bytes 774152 | tf_op jit(solution)/shard_map/ppermute | solution.py:36
  24.8 19.7 %collective-permute-start.7 = (bf16[504,256]{1,0:T(8,128)(2,1)S(1)}, bf16[504,256]{1,0:T(8,128)(2,1)S(1)}, u32[]{:S(2)}, u32[]{:S(2)}) collective-permute-start(bf16[504,256]{1,0:T(8,128)(2,1)S(1)} %get-tuple-element.51), channel_id=1, source_target_pairs={{1,2},{2,1},{3,4},{4,3},{5,6},{6,5},{7,8},{8,7},{9,10},{10,9},{11,... | collective-permute-start | bytes 774152 | tf_op jit(solution)/shard_map/ppermute | solution.py:36
  28.1 16.4 %collective-permute-start.6 = (bf16[504,256]{1,0:T(8,128)(2,1)S(1)}, bf16[504,256]{1,0:T(8,128)(2,1)S(1)}, u32[]{:S(2)}, u32[]{:S(2)}) collective-permute-start(bf16[504,256]{1,0:T(8,128)(2,1)S(1)} %get-tuple-element.44.refs_9_), channel_id=1, source_target_pairs={{0,1},{1,0},{2,3},{3,2},{4,5},{5,4},{6,7},{7,6},{8,9},{9,8},{10,11... | collective-permute-start | bytes 774152 | tf_op jit(solution)/shard_map/ppermute | solution.py:36
  41.1 10.1 %collective-permute-start.5 = (bf16[504,256]{1,0:T(8,128)(2,1)S(1)}, bf16[504,256]{1,0:T(8,128)(2,1)S(1)}, u32[]{:S(2)}, u32[]{:S(2)}) collective-permute-start(bf16[504,256]{1,0:T(8,128)(2,1)S(1)} %get-tuple-element.47), channel_id=1, source_target_pairs={{1,2},{2,1},{3,4},{4,3},{5,6},{6,5},{7,8},{8,7},{9,10},{10,9},{11,... | collective-permute-start | bytes 774152 | tf_op jit(solution)/shard_map/ppermute | solution.py:36
  44.4 17.9 %collective-permute-start.4 = (bf16[504,256]{1,0:T(8,128)(2,1)S(1)}, bf16[504,256]{1,0:T(8,128)(2,1)S(1)}, u32[]{:S(2)}, u32[]{:S(2)}) collective-permute-start(bf16[504,256]{1,0:T(8,128)(2,1)S(1)} %get-tuple-element.46.refs_9_), channel_id=1, source_target_pairs={{0,1},{1,0},{2,3},{3,2},{4,5},{5,4},{6,7},{7,6},{8,9},{9,8},{10,11... | collective-permute-start | bytes 774152 | tf_op jit(solution)/shard_map/ppermute | solution.py:36
  46.9 20.8 %collective-permute-start.11 = (bf16[504,256]{1,0:T(8,128)(2,1)S(1)}, bf16[504,256]{1,0:T(8,128)(2,1)S(1)}, u32[]{:S(2)}, u32[]{:S(2)}) collective-permute-start(bf16[504,256]{1,0:T(8,128)(2,1)S(1)} %get-tuple-element.60), channel_id=1, source_target_pairs={{1,2},{2,1},{3,4},{4,3},{5,6},{6,5},{7,8},{8,7},{9,10},{10,9},{11,... | collective-permute-start | bytes 774152 | tf_op jit(solution)/shard_map/ppermute | solution.py:36
  49.8 18.0 %collective-permute-start.10 = (bf16[504,256]{1,0:T(8,128)(2,1)S(1)}, bf16[504,256]{1,0:T(8,128)(2,1)S(1)}, u32[]{:S(2)}, u32[]{:S(2)}) collective-permute-start(bf16[504,256]{1,0:T(8,128)(2,1)S(1)} %get-tuple-element.54.refs_9_), channel_id=1, source_target_pairs={{0,1},{1,0},{2,3},{3,2},{4,5},{5,4},{6,7},{7,6},{8,9},{9,8},{10,11... | collective-permute-start | bytes 774152 | tf_op jit(solution)/shard_map/ppermute | solution.py:36
  64.8 10.0 %collective-permute-start.9 = (bf16[504,256]{1,0:T(8,128)(2,1)S(1)}, bf16[504,256]{1,0:T(8,128)(2,1)S(1)}, u32[]{:S(2)}, u32[]{:S(2)}) collective-permute-start(bf16[504,256]{1,0:T(8,128)(2,1)S(1)} %get-tuple-element.57), channel_id=1, source_target_pairs={{1,2},{2,1},{3,4},{4,3},{5,6},{6,5},{7,8},{8,7},{9,10},{10,9},{11,... | collective-permute-start | bytes 774152 | tf_op jit(solution)/shard_map/ppermute | solution.py:36
  67.6 17.9 %collective-permute-start.8 = (bf16[504,256]{1,0:T(8,128)(2,1)S(1)}, bf16[504,256]{1,0:T(8,128)(2,1)S(1)}, u32[]{:S(2)}, u32[]{:S(2)}) collective-permute-start(bf16[504,256]{1,0:T(8,128)(2,1)S(1)} %get-tuple-element.56.refs_9_), channel_id=1, source_target_pairs={{0,1},{1,0},{2,3},{3,2},{4,5},{5,4},{6,7},{7,6},{8,9},{9,8},{10,11... | collective-permute-start | bytes 774152 | tf_op jit(solution)/shard_map/ppermute | solution.py:36
  69.1 22.6 %collective-permute-start.17 = (bf16[504,256]{1,0:T(8,128)(2,1)S(1)}, bf16[504,256]{1,0:T(8,128)(2,1)S(1)}, u32[]{:S(2)}, u32[]{:S(2)}) collective-permute-start(bf16[504,256]{1,0:T(8,128)(2,1)S(1)} %get-tuple-element.70), channel_id=1, source_target_pairs={{1,2},{2,1},{3,4},{4,3},{5,6},{6,5},{7,8},{8,7},{9,10},{10,9},{11,... | collective-permute-start | bytes 774152 | tf_op jit(solution)/shard_map/ppermute | solution.py:36
  72.4 22.3 %collective-permute-start.16 = (bf16[504,256]{1,0:T(8,128)(2,1)S(1)}, bf16[504,256]{1,0:T(8,128)(2,1)S(1)}, u32[]{:S(2)}, u32[]{:S(2)}) collective-permute-start(bf16[504,256]{1,0:T(8,128)(2,1)S(1)} %get-tuple-element.62.refs_9_), channel_id=1, source_target_pairs={{0,1},{1,0},{2,3},{3,2},{4,5},{5,4},{6,7},{7,6},{8,9},{9,8},{10,11... | collective-permute-start | bytes 774152 | tf_op jit(solution)/shard_map/ppermute | solution.py:36
  86.8 10.5 %collective-permute-start.15 = (bf16[256,256]{1,0:T(8,128)(2,1)S(1)}, bf16[256,256]{1,0:T(8,128)(2,1)S(1)}, u32[]{:S(2)}, u32[]{:S(2)}) collective-permute-start(bf16[256,256]{1,0:T(8,128)(2,1)S(1)} %get-tuple-element.67), channel_id=1, source_target_pairs={{1,2},{2,1},{3,4},{4,3},{5,6},{6,5},{7,8},{8,7},{9,10},{10,9},{11,... | collective-permute-start | bytes 393224 | tf_op jit(solution)/shard_map/ppermute | solution.py:36
  90.2 9.6 %collective-permute-start.14 = (bf16[256,256]{1,0:T(8,128)(2,1)S(1)}, bf16[256,256]{1,0:T(8,128)(2,1)S(1)}, u32[]{:S(2)}, u32[]{:S(2)}) collective-permute-start(bf16[256,256]{1,0:T(8,128)(2,1)S(1)} %get-tuple-element.66.refs_12_), channel_id=1, source_target_pairs={{0,1},{1,0},{2,3},{3,2},{4,5},{5,4},{6,7},{7,6},{8,9},{9,8},{10,11... | collective-permute-start | bytes 393224 | tf_op jit(solution)/shard_map/ppermute | solution.py:36
  90.3 12.4 %collective-permute-start.12 = (bf16[248,256]{1,0:T(8,128)(2,1)S(1)}, bf16[248,256]{1,0:T(8,128)(2,1)S(1)}, u32[]{:S(2)}, u32[]{:S(2)}) collective-permute-start(bf16[248,256]{1,0:T(8,128)(2,1)S(1)} %get-tuple-element.64), channel_id=1, source_target_pairs={{0,1},{1,0},{2,3},{3,2},{4,5},{5,4},{6,7},{7,6},{8,9},{9,8},{10,11... | collective-permute-start | bytes 380936 | tf_op jit(solution)/shard_map/ppermute | solution.py:36
  91.7 10.9 %collective-permute-start.13 = (bf16[248,256]{1,0:T(8,128)(2,1)S(1)}, bf16[248,256]{1,0:T(8,128)(2,1)S(1)}, u32[]{:S(2)}, u32[]{:S(2)}) collective-permute-start(bf16[248,256]{1,0:T(8,128)(2,1)S(1)} %get-tuple-element.65), channel_id=1, source_target_pairs={{1,2},{2,1},{3,4},{4,3},{5,6},{6,5},{7,8},{8,7},{9,10},{10,9},{11,... | collective-permute-start | bytes 380936 | tf_op jit(solution)/shard_map/ppermute | solution.py:36
  102.1 2.9 %collective-permute-start.18 = (f32[4,200,256]{2,1,0:T(8,128)}, f32[4,200,256]{2,1,0:T(8,128)}, u32[]{:S(2)}, u32[]{:S(2)}) collective-permute-start(f32[4,200,256]{2,1,0:T(8,128)} %get-tuple-element.74.refs_7_.refs_0_), channel_id=1, source_target_pairs={{0,16},{16,0},{1,17},{17,1},{2,18},{18,2},{3,19},{19,3},{4,20},{20... | collective-permute-start | bytes 2457608 | tf_op jit(solution)/shard_map/ppermute | solution.py:607
